TPU v7x, 32 devices: a whole 2x2x4 slice. The times are simulated.
32 devices in a mesh: dp: 4 (over y, x), expert: 8 (over z, core).
Axes of the slice: x: 2, y: 2, z: 4, core: 2. Of those that a mesh axis runs over, the one named last changes fastest.
Arguments:
- tokens: bfloat16 [32, 197, 768], P(('dp', 'expert')), may hold values from -6 to 6
- cotangent: bfloat16 [32, 197, 768], P(('dp', 'expert')), may hold values from -6 to 6
- expert_picks: int32 [6304, 2], P(('dp', 'expert')), may hold values from 0 to 7, all different within a row
- priority: int32 [32, 197], P(('dp', 'expert')), may hold values from 0 to 196, each once within a row
- dense_master: float32 [9449472], P(('dp', 'expert')), may hold values from -2 to 2
- dense_momentum: float32 [9449472], P(('dp', 'expert')), may hold values from -1.25 to 1.25
- dense_variance: float32 [9449472], P(('dp', 'expert')), may hold values from 0.005 to 0.08
- expert_master: float32 [8, 4718592], P('expert', 'dp'), may hold values from -6 to 6
- expert_momentum: float32 [8, 4718592], P('expert', 'dp'), may hold values from -0.1875 to 0.1875
- expert_variance: float32 [8, 4718592], P('expert', 'dp'), may hold values from 5e-05 to 0.0008
Outputs:
- block_output: float32 [32, 197, 768], P(('dp', 'expert'))
- input_grad: float32 [32, 197, 768], P(('dp', 'expert'))
- dense_grad: float32 [9449472], P(('dp', 'expert'))
- expert_grad: float32 [8, 4718592], P('expert', 'dp')
- dense_update: float32 [9449472], P(('dp', 'expert'))
- momentum_dense: float32 [9449472], P(('dp', 'expert'))
- variance_dense: float32 [9449472], P(('dp', 'expert'))
- expert_update: float32 [8, 4718592], P('expert', 'dp')
- momentum_expert: float32 [8, 4718592], P('expert', 'dp')
- variance_expert: float32 [8, 4718592], P('expert', 'dp')
- gain_grads: float32 [4, 768], replicated
Inputs may be any that keep to these rules, and one draw needn't show every extreme that they name: `expert_picks`: each row names two different experts. `priority`: each row is a permutation of the ranks of one group's tokens.
All inputs are finite; a program needn't handle non-finite values.
Results may differ from a plain program's by a relative error of at most 0.02.
Values may be sent and summed in bfloat16 or wider, within the bound.
No kernel may reach another device: no remote copies, remote signals or barrier semaphores. Data moves between devices by JAX's collectives and lax.ppermute only.
A program may use at most 320 MiB of HBM per device.

v0:
```python
import math

import jax
import jax.numpy as jnp
from jax import lax
from jax.sharding import PartitionSpec as P

HEADS = 12
HEAD_DIM = 64


eps_norm = 1e-06
beta_first = 0.9
beta_second = 0.999
adam_eps = 1e-08
adam_step = 10.0


def unpack(flat_params, model_width, hidden_width, experts):
    layouts = (
        [(model_width, model_width)] * 8
        + [(model_width, hidden_width), (hidden_width, model_width), (model_width, experts)]
        + [(model_width,)] * 4
    )
    pieces = []
    offset = 0
    for layout in layouts:
        length = math.prod(layout)
        pieces.append(flat_params[offset : offset + length].reshape(layout))
        offset += length
    return pieces


def slot_places(picks, ranks, experts):
    token_count = ranks.shape[0]
    order_keys = jnp.stack([ranks, ranks + token_count], axis=1)
    expert_by_key = (
        jnp.zeros((2 * token_count,), jnp.int32).at[order_keys.reshape(-1)].set(picks.reshape(-1))
    )
    one_hot = (expert_by_key[:, None] == jnp.arange(experts, dtype=jnp.int32)[None, :]).astype(
        jnp.int32
    )
    earlier = jnp.cumsum(one_hot, axis=0) - one_hot
    place_by_key = jnp.sum(earlier * one_hot, axis=1)
    return place_by_key[order_keys]


def norm_rows(hidden):
    center = hidden - jnp.mean(hidden, axis=-1, keepdims=True)
    inverse = lax.rsqrt(jnp.mean(center * center, axis=-1, keepdims=True) + eps_norm)
    return (center * inverse, inverse)


def norm_back(upstream, normed, inverse, gain):
    scaled = upstream * gain
    gain_grad = jnp.sum(upstream * normed, axis=0)
    centered = (
        scaled
        - jnp.mean(scaled, axis=-1, keepdims=True)
        - normed * jnp.mean(scaled * normed, axis=-1, keepdims=True)
    )
    return (inverse * centered, gain_grad)


def gelu_slope(pre_act):
    normal_cdf = 0.5 * (1.0 + lax.erf(pre_act * 0.7071067811865476))
    density = jnp.exp(-0.5 * pre_act * pre_act) * 0.3989422804014327
    return normal_cdf + pre_act * density


def split_heads(row_block, images):
    return row_block.reshape(
        images, row_block.shape[0] // images, HEADS, row_block.shape[1] // HEADS
    )


def attention_scores(queries, key_rows, images):
    return jnp.einsum(
        "gqhc,gkhc->ghqk",
        split_heads(queries, images),
        split_heads(key_rows, images),
        preferred_element_type=jnp.float32,
    ) * HEAD_DIM ** (-0.5)


def attention_forward(normed_low, weights, images):
    w_query, w_key, w_value, w_out = weights
    token_count, model_width = normed_low.shape
    queries = jnp.dot(normed_low, w_query, preferred_element_type=jnp.float32).astype(jnp.bfloat16)
    key_rows = jnp.dot(normed_low, w_key, preferred_element_type=jnp.float32).astype(jnp.bfloat16)
    value_rows = jnp.dot(normed_low, w_value, preferred_element_type=jnp.float32).astype(
        jnp.bfloat16
    )
    scores = attention_scores(queries, key_rows, images)
    log_total = jax.nn.logsumexp(scores, axis=-1, keepdims=True)
    soft_weights = jnp.exp(scores - log_total).astype(jnp.bfloat16)
    mixed = jnp.einsum(
        "ghqk,gkhc->gqhc",
        soft_weights,
        split_heads(value_rows, images),
        preferred_element_type=jnp.float32,
    )
    mixed = mixed.reshape(token_count, model_width).astype(jnp.bfloat16)
    branch = jnp.dot(mixed, w_out, preferred_element_type=jnp.float32)
    return (branch, (queries, key_rows, value_rows, log_total, mixed))


def attention_backward(branch_grad, normed_low, kept_state, weights, images):
    w_query, w_key, w_value, w_out = weights
    queries, key_rows, value_rows, log_total, mixed = kept_state
    token_count, model_width = normed_low.shape
    branch_low = branch_grad.astype(jnp.bfloat16)
    out_weight_grad = jnp.dot(mixed.T, branch_low, preferred_element_type=jnp.float32)
    mixed_grad = jnp.dot(branch_low, w_out.T, preferred_element_type=jnp.float32).astype(
        jnp.bfloat16
    )
    scores = attention_scores(queries, key_rows, images)
    soft_weights = jnp.exp(scores - log_total)
    mixed_heads = split_heads(mixed_grad, images)
    weight_grad = jnp.einsum(
        "gqhc,gkhc->ghqk",
        mixed_heads,
        split_heads(value_rows, images),
        preferred_element_type=jnp.float32,
    )
    value_grad = jnp.einsum(
        "ghqk,gqhc->gkhc",
        soft_weights.astype(jnp.bfloat16),
        mixed_heads,
        preferred_element_type=jnp.float32,
    )
    value_grad = value_grad.reshape(token_count, model_width).astype(jnp.bfloat16)
    score_grad = soft_weights * (
        weight_grad - jnp.sum(weight_grad * soft_weights, axis=-1, keepdims=True)
    )
    score_grad = score_grad.astype(jnp.bfloat16)
    query_grad = jnp.einsum(
        "ghqk,gkhc->gqhc",
        score_grad,
        split_heads(key_rows, images),
        preferred_element_type=jnp.float32,
    ) * HEAD_DIM ** (-0.5)
    query_grad = query_grad.reshape(token_count, model_width).astype(jnp.bfloat16)
    key_grad = jnp.einsum(
        "ghqk,gqhc->gkhc",
        score_grad,
        split_heads(queries, images),
        preferred_element_type=jnp.float32,
    ) * HEAD_DIM ** (-0.5)
    key_grad = key_grad.reshape(token_count, model_width).astype(jnp.bfloat16)
    weight_grads = (
        jnp.dot(normed_low.T, query_grad, preferred_element_type=jnp.float32),
        jnp.dot(normed_low.T, key_grad, preferred_element_type=jnp.float32),
        jnp.dot(normed_low.T, value_grad, preferred_element_type=jnp.float32),
        out_weight_grad,
    )
    input_grad = (
        jnp.dot(query_grad, w_query.T, preferred_element_type=jnp.float32)
        + jnp.dot(key_grad, w_key.T, preferred_element_type=jnp.float32)
        + jnp.dot(value_grad, w_value.T, preferred_element_type=jnp.float32)
    )
    return (input_grad, weight_grads)


def adam_update(momentum, variance, gradient, clip_factor):
    clipped = gradient * clip_factor
    momentum_new = beta_first * momentum + (1.0 - beta_first) * clipped
    variance_new = beta_second * variance + (1.0 - beta_second) * clipped * clipped
    first_hat = momentum_new / (1.0 - beta_first**adam_step)
    second_hat = variance_new / (1.0 - beta_second**adam_step)
    return (-first_hat / (jnp.sqrt(second_hat) + adam_eps), momentum_new, variance_new)


def on_device(
    tokens,
    cotangent,
    expert_picks,
    priority,
    dense_master,
    dense_momentum,
    dense_variance,
    expert_master,
    expert_momentum,
    expert_variance,
):
    expert_ranks = lax.axis_size("expert")
    local_experts = expert_master.shape[0]
    experts = local_experts * expert_ranks
    images, seq_length, model_width = tokens.shape
    token_count = images * seq_length
    pair_count = 2 * token_count
    capacity = 2 * token_count // experts
    total_slots = experts * capacity
    dense_low = dense_master.astype(jnp.bfloat16)
    dense_flat = lax.all_gather(dense_low, ("dp", "expert"), axis=0, tiled=True)
    expert_flat = lax.all_gather(expert_master.astype(jnp.bfloat16), "dp", axis=1, tiled=True)
    hidden_width = expert_flat.shape[1] // (2 * model_width)
    pieces = unpack(dense_flat, model_width, hidden_width, experts)
    first_experts = expert_flat[:, : model_width * hidden_width].reshape(
        local_experts, model_width, hidden_width
    )
    second_experts = expert_flat[:, model_width * hidden_width :].reshape(
        local_experts, hidden_width, model_width
    )
    stream = tokens.astype(jnp.float32).reshape(token_count, model_width)
    first_normed, first_inverse = norm_rows(stream)
    first_input = (first_normed * pieces[11]).astype(jnp.bfloat16)
    first_branch, first_state = attention_forward(first_input, pieces[0:4], images)
    stream_one = stream + first_branch
    mlp_normed, mlp_inverse = norm_rows(stream_one)
    mlp_input = (mlp_normed * pieces[12]).astype(jnp.bfloat16)
    mlp_pre = jnp.dot(mlp_input, pieces[8], preferred_element_type=jnp.float32)
    mlp_act = jax.nn.gelu(mlp_pre, approximate=False).astype(jnp.bfloat16)
    stream_two = stream_one + jnp.dot(mlp_act, pieces[9], preferred_element_type=jnp.float32)
    second_normed, second_inverse = norm_rows(stream_two)
    second_input = (second_normed * pieces[13]).astype(jnp.bfloat16)
    second_branch, second_state = attention_forward(second_input, pieces[4:8], images)
    stream_three = stream_two + second_branch
    moe_normed, moe_inverse = norm_rows(stream_three)
    moe_input = (moe_normed * pieces[14]).astype(jnp.bfloat16)
    logits = jnp.dot(moe_input, pieces[10], preferred_element_type=jnp.float32)
    soft_weights = jax.nn.softmax(logits, axis=-1)
    gate_values = jnp.take_along_axis(soft_weights, expert_picks, axis=1)
    places = slot_places(expert_picks, priority[0], experts)
    pair_slots = jnp.where(places < capacity, expert_picks * capacity + places, total_slots)
    slot_pair = (
        jnp.full((total_slots + 1,), pair_count, jnp.int32)
        .at[pair_slots.reshape(-1)]
        .set(jnp.arange(pair_count, dtype=jnp.int32))[:total_slots]
    )
    slot_token = jnp.where(slot_pair < pair_count, slot_pair // 2, token_count)
    padded_input = jnp.concatenate([moe_input, jnp.zeros((1, model_width), jnp.bfloat16)], axis=0)
    outgoing = padded_input[slot_token].reshape(expert_ranks, local_experts, capacity, model_width)
    arriving = lax.all_to_all(outgoing, "expert", split_axis=0, concat_axis=0, tiled=True)
    expert_pre = jnp.einsum(
        "secd,edf->secf", arriving, first_experts, preferred_element_type=jnp.float32
    )
    expert_act = jax.nn.gelu(expert_pre, approximate=False).astype(jnp.bfloat16)
    expert_out = jnp.einsum(
        "secf,efd->secd", expert_act, second_experts, preferred_element_type=jnp.float32
    ).astype(jnp.bfloat16)
    returning = lax.all_to_all(expert_out, "expert", split_axis=0, concat_axis=0, tiled=True)
    padded_out = jnp.concatenate(
        [returning.reshape(total_slots, model_width), jnp.zeros((1, model_width), jnp.bfloat16)],
        axis=0,
    )
    pair_out = padded_out[pair_slots].astype(jnp.float32)
    output = stream_three + jnp.sum(gate_values[:, :, None] * pair_out, axis=1)
    upstream = cotangent.astype(jnp.float32).reshape(token_count, model_width)
    pair_grad = (gate_values[:, :, None] * upstream[:, None, :]).astype(jnp.bfloat16)
    gate_grad = jnp.sum(upstream[:, None, :] * pair_out, axis=-1)
    padded_pair = jnp.concatenate(
        [pair_grad.reshape(pair_count, model_width), jnp.zeros((1, model_width), jnp.bfloat16)],
        axis=0,
    )
    outgoing_grad = padded_pair[slot_pair].reshape(
        expert_ranks, local_experts, capacity, model_width
    )
    arriving_grad = lax.all_to_all(outgoing_grad, "expert", split_axis=0, concat_axis=0, tiled=True)
    act_grad = jnp.einsum(
        "secd,efd->secf", arriving_grad, second_experts, preferred_element_type=jnp.float32
    )
    second_expert_grad = jnp.einsum(
        "secf,secd->efd", expert_act, arriving_grad, preferred_element_type=jnp.float32
    )
    pre_grad = (act_grad * gelu_slope(expert_pre)).astype(jnp.bfloat16)
    first_expert_grad = jnp.einsum(
        "secd,secf->edf", arriving, pre_grad, preferred_element_type=jnp.float32
    )
    input_back = jnp.einsum(
        "secf,edf->secd", pre_grad, first_experts, preferred_element_type=jnp.float32
    ).astype(jnp.bfloat16)
    returned_grad = lax.all_to_all(input_back, "expert", split_axis=0, concat_axis=0, tiled=True)
    padded_back = jnp.concatenate(
        [
            returned_grad.reshape(total_slots, model_width),
            jnp.zeros((1, model_width), jnp.bfloat16),
        ],
        axis=0,
    )
    dispatch_grad = jnp.sum(padded_back[pair_slots].astype(jnp.float32), axis=1)
    one_hot_picks = (
        expert_picks[:, :, None] == jnp.arange(experts, dtype=jnp.int32)[None, None, :]
    ).astype(jnp.float32)
    prob_grad = jnp.sum(gate_grad[:, :, None] * one_hot_picks, axis=1)
    logit_grad = soft_weights * (
        prob_grad - jnp.sum(prob_grad * soft_weights, axis=-1, keepdims=True)
    )
    logit_grad = logit_grad.astype(jnp.bfloat16)
    router_grad = jnp.dot(moe_input.T, logit_grad, preferred_element_type=jnp.float32)
    moe_input_grad = dispatch_grad + jnp.dot(
        logit_grad, pieces[10].T, preferred_element_type=jnp.float32
    )
    addend, moe_gain_grad = norm_back(moe_input_grad, moe_normed, moe_inverse, pieces[14])
    stream_grad = upstream + addend
    attn_input_grad, second_weight_grads = attention_backward(
        stream_grad, second_input, second_state, pieces[4:8], images
    )
    addend, second_gain_grad = norm_back(attn_input_grad, second_normed, second_inverse, pieces[13])
    stream_grad = stream_grad + addend
    mlp_out_grad = stream_grad.astype(jnp.bfloat16)
    mlp_act_grad = jnp.dot(mlp_out_grad, pieces[9].T, preferred_element_type=jnp.float32)
    mlp_second_grad = jnp.dot(mlp_act.T, mlp_out_grad, preferred_element_type=jnp.float32)
    mlp_pre_grad = (mlp_act_grad * gelu_slope(mlp_pre)).astype(jnp.bfloat16)
    mlp_first_grad = jnp.dot(mlp_input.T, mlp_pre_grad, preferred_element_type=jnp.float32)
    mlp_input_grad = jnp.dot(mlp_pre_grad, pieces[8].T, preferred_element_type=jnp.float32)
    addend, mlp_gain_grad = norm_back(mlp_input_grad, mlp_normed, mlp_inverse, pieces[12])
    stream_grad = stream_grad + addend
    attn_input_grad, first_weight_grads = attention_backward(
        stream_grad, first_input, first_state, pieces[0:4], images
    )
    addend, first_gain_grad = norm_back(attn_input_grad, first_normed, first_inverse, pieces[11])
    stream_grad = stream_grad + addend
    dense_length = dense_flat.shape[0]
    used_length = model_width * (8 * model_width + 2 * hidden_width + experts + 4)
    grad_pieces = (
        list(first_weight_grads)
        + list(second_weight_grads)
        + [
            mlp_first_grad,
            mlp_second_grad,
            router_grad,
            first_gain_grad,
            mlp_gain_grad,
            second_gain_grad,
            moe_gain_grad,
        ]
    )
    flat_pieces = [piece_grad.reshape(-1) for piece_grad in grad_pieces]
    flat_pieces.append(jnp.zeros((dense_length - used_length,), jnp.float32))
    dense_local = jnp.concatenate(flat_pieces, axis=0)
    dense_grad = lax.psum_scatter(dense_local, ("dp", "expert"), scatter_dimension=0, tiled=True)
    expert_local = jnp.concatenate(
        [
            first_expert_grad.reshape(local_experts, -1),
            second_expert_grad.reshape(local_experts, -1),
        ],
        axis=1,
    )
    expert_grad = lax.psum_scatter(
        expert_local.astype(jnp.bfloat16), "dp", scatter_dimension=1, tiled=True
    ).astype(jnp.float32)
    gain_local = jnp.stack(
        [first_gain_grad, mlp_gain_grad, second_gain_grad, moe_gain_grad], axis=0
    )
    square_local = jnp.sum(dense_grad * dense_grad) + jnp.sum(expert_grad * expert_grad)
    square_sum, gain_grads = lax.psum((square_local, gain_local), ("dp", "expert"))
    param_count = (dense_master.size + expert_master.size) * lax.axis_size("dp") * expert_ranks
    clip_factor = jnp.minimum(1.0, jnp.sqrt(param_count / (square_sum + 1e-06)))
    dense_update, momentum_dense, variance_dense = adam_update(
        dense_momentum, dense_variance, dense_grad, clip_factor
    )
    expert_update, momentum_expert, variance_expert = adam_update(
        expert_momentum, expert_variance, expert_grad, clip_factor
    )
    block_output = output.reshape(images, seq_length, model_width)
    input_grad = stream_grad.reshape(images, seq_length, model_width)
    return (
        block_output,
        input_grad,
        dense_grad,
        expert_grad,
        dense_update,
        momentum_dense,
        variance_dense,
        expert_update,
        momentum_expert,
        variance_expert,
        gain_grads,
    )


def solution(mesh):
    placed = (
        P(("dp", "expert"), None, None),
        P(("dp", "expert"), None, None),
        P(("dp", "expert"), None),
        P(("dp", "expert"), None),
        P(("dp", "expert")),
        P(("dp", "expert")),
        P(("dp", "expert")),
        P("expert", "dp"),
        P("expert", "dp"),
        P("expert", "dp"),
    )
    return jax.shard_map(
        on_device,
        mesh=mesh,
        in_specs=placed,
        out_specs=(
            P(("dp", "expert"), None, None),
            P(("dp", "expert"), None, None),
            P(("dp", "expert")),
            P("expert", "dp"),
            P(("dp", "expert")),
            P(("dp", "expert")),
            P(("dp", "expert")),
            P("expert", "dp"),
            P("expert", "dp"),
            P("expert", "dp"),
            P(),
        ),
        check_vma=False,
    )
```

profile of v0, /device:TPU:0, one launch (start us, length us, event | category | flops | bytes accessed | tf_op | source)
XLA Modules:
  0.0 2158.4 jit_solution(16232257115837596912)
XLA Ops:
  8.6 7.5 reshape.937
  39.7 194.4 %all-gather.6.cloned.1.call-done = bf16[32,1,295296]{2,1,0:T(2,128)(2,1)} async-done(((bf16[1,1,295296]{2,1,0:T(2,128)(2,1)}), bf16[32,1,295296]{2,1,0:T(2,128)(2,1)}) %all-gather.6.cloned.1.call-update) | async-done | bytes 18898960 | tf_op jit(solution)/shard_map/all_gather | solution.py:195
  234.1 400.7 %reduce.13 = bf16[32,295296]{1,0:T(8,128)(2,1)} reduce(bf16[32,1,295296]{2,1,0:T(2,128)(2,1)} %all-gather.6.cloned.1.call-done, bf16[]{:T(256)} %constant.253), dimensions={1}, to_apply=%all-gather.reduce_sub_computation | reduce | bytes 37797888 | tf_op jit(solution)/shard_map/all_gather | solution.py:195
  634.9 46.6 %reshape.938 = bf16[9449472]{0:T(1024)(128)(2,1)} reshape(bf16[32,295296]{1,0:T(8,128)(2,1)} %reduce.13) | data formatting | bytes 37797888
  681.5 8.2 fusion.187
  717.6 8.6 slice.184
  726.3 9.2 slice.186
  742.5 9.5 fusion.33
  790.9 8.2 all-to-all-done
  802.7 104.5 %slice_reduce_fusion.1 = (bf16[2359296]{0:T(1024)(128)(2,1)}, bf16[2359296]{0:T(1024)(128)(2,1)}) fusion(bf16[1,4718592]{1,0:T(2,128)(2,1)} %all-gather.4.cloned.1.call-done), kind=kLoop, calls=%fused_computation.10 | loop fusion | bytes 18874368 | tf_op jit(solution)/shard_map/slice | solution.py:199
  907.2 8.2 reshape.939
  915.4 9.2 reshape.940
  950.7 16.0 fusion.25
  966.8 17.4 fusion.51
  984.2 66.7 %copy.235 = bf16[1,1,3072,768]{3,1,2,0:T(2,128)(2,1)} copy(bf16[1,1,3072,768]{3,2,1,0:T(8,128)(2,1)S(1)} %fusion.25) | data formatting | bytes 9437184
  1053.7 43.5 %copy.234 = bf16[1,1,768,3072]{3,1,2,0:T(2,128)(2,1)} copy(bf16[1,1,768,3072]{3,2,1,0:T(8,128)(2,1)S(1)} %fusion.24) | data formatting | bytes 9437184
  1102.3 61.4 %pad_maximum_fusion = bf16[1,4718592]{1,0:T(2,128)(2,1)} fusion(bf16[1,2359296]{1,0:T(2,128)(2,1)} %bitcast.319, bf16[1,2359296]{1,0:T(2,128)(2,1)} %bitcast.320), kind=kLoop, calls=%fused_computation.8 | loop fusion | flops 18874368 | bytes 18874368 | tf_op jit(solution)/shard_map/concatenate | solution.py:333
  1252.0 9.6 copy.233
  1261.6 11.0 reshape.856
  1314.4 191.7 %all-reduce.13.cloned.1.call-done = bf16[1,4718592]{1,0:T(2,128)(2,1)} async-done(((bf16[1,4718592]{1,0:T(2,128)(2,1)}), bf16[1,4718592]{1,0:T(2,128)(2,1)}) %all-reduce.13.cloned.1.call-update) | async-done | bytes 9437200
  1506.1 12.2 multiply_reduce_fusion
  1518.3 551.8 %all-reduce.11.cloned.1.call-done = f32[9449472]{0:T(1024)} async-done(((f32[9449472]{0:T(1024)}), f32[9449472]{0:T(1024)}) %all-reduce.11.cloned.1.call-update) | async-done | bytes 37797904
  2075.1 39.2 %all-reduce.7 = (f32[]{:T(128)}, f32[4,768]{1,0:T(4,128)}) all-reduce(f32[]{:T(128)S(6)} %add.276, f32[4,768]{1,0:T(4,128)S(1)} %pad_maximum_fusion.1), channel_id=1, replica_groups=mesh['dp'=4,'expert'=8] {'dp','expert'}, use_global_device_ids=true, to_apply=%region_42.43 | all-reduce | flops 3073 | bytes 24584 | tf_op jit(solution)/shard_map/psum | solution.py:347
  2119.0 32.7 %add_divide_fusion = (f32[1,1179648]{1,0:T(1,128)}, f32[1,1179648]{1,0:T(1,128)}, f32[1,1179648]{1,0:T(1,128)}) fusion(f32[1,1179648]{1,0:T(1,128)S(1)} %copy-done.8, f32[]{:T(128)S(6)} %min.3, f32[1,1179648]{1,0:T(1,128)} %param.18, f32[1,1179648]{1,0:T(1,128)} %param.19), kind=kLoop, calls=%fused_computation.50 | loop fusion | flops 15335424 | bytes 28311556 | tf_op jit(solution)/shard_map/div | solution.py:171
  (516 shorter events, 271.7 us)
Async XLA Ops:
  7.2 226.9 %all-gather.6.cloned.1.call-start = ((), (), s32[]{:S(2)}) async-start(), calls=%async_computation.5 | async-start | bytes 38979072 | tf_op jit(solution)/shard_map/all_gather | solution.py:195
  16.1 786.6 %all-gather.4.cloned.1.call-start = ((), (), s32[]{:S(2)}) async-start(), calls=%async_computation.4 | async-start | bytes 23592960 | tf_op jit(solution)/shard_map/all_gather | solution.py:196
  22.7 691.0 %copy-start.101 = (f32[197]{0:T(256)}, f32[197]{0:T(256)S(1)}, u32[]{:S(2)}) copy-start(f32[197]{0:T(256)S(1)} %broadcast_multiply_fusion.12) | copy-start | bytes 2368
  23.0 690.7 %copy-start.103 = (f32[197]{0:T(256)}, f32[197]{0:T(256)S(1)}, u32[]{:S(2)}) copy-start(f32[197]{0:T(256)S(1)} %add_rsqrt_fusion.3) | copy-start | bytes 2368
  38.8 596.1 %copy-start.83 = (s32[197,2]{1,0:T(8,128)}, s32[197,2]{1,0:T(8,128)S(1)}, u32[]{:S(2)}) copy-start(s32[197,2]{1,0:T(8,128)S(1)} %copy.195) | copy-start | bytes 4732
  700.3 13.4 copy-start.93
  700.3 42.1 %copy-start.95 = (f32[768]{0:T(1024)}, f32[768]{0:T(1024)S(1)}, u32[]{:S(2)}) copy-start(f32[768]{0:T(1024)S(1)} %get-tuple-element.109) | copy-start | bytes 9220
  700.4 53.3 %copy-start.97 = (f32[768]{0:T(1024)}, f32[768]{0:T(1024)S(1)}, u32[]{:S(2)}) copy-start(f32[768]{0:T(1024)S(1)} %get-tuple-element.108) | copy-start | bytes 9220
  700.4 72.4 %copy-start.99 = (f32[768]{0:T(1024)}, f32[768]{0:T(1024)S(1)}, u32[]{:S(2)}) copy-start(f32[768]{0:T(1024)S(1)} %get-tuple-element.107) | copy-start | bytes 9220
  704.0 36.7 %copy-start.59 = (bf16[197,768]{0,1:T(8,128)(2,1)}, bf16[197,768]{0,1:T(8,128)(2,1)S(1)}, u32[]{:S(2)}) copy-start(bf16[197,768]{0,1:T(8,128)(2,1)S(1)} %copy.184) | copy-start | bytes 907780
  717.6 24.0 %copy-start.20 = (bf16[768,768]{1,0:T(8,128)(2,1)}, bf16[768,768]{1,0:T(8,128)(2,1)S(1)}, u32[]{:S(2)}) copy-start(bf16[768,768]{1,0:T(8,128)(2,1)S(1)} %slice.181) | copy-start | bytes 3538948
  738.1 16.3 copy-start.22
  753.4 18.6 copy-start.4
  776.8 22.3 %all-to-all-start = ((bf16[8,1,49,768]{3,2,1,0:T(8,128)(2,1)}), bf16[8,1,49,768]{3,2,1,0:T(8,128)(2,1)S(1)}, u32[]{:S(2)}, u32[]{:S(2)}) async-start(bf16[8,1,49,768]{3,2,1,0:T(8,128)(2,1)} %bitcast.22), calls=%async_computation | async-start | bytes 1376256 | tf_op jit(solution)/shard_map/all_to_all | solution.py:234
  799.1 132.6 %all-to-all-start.2 = ((bf16[8,1,49,768]{3,2,1,0:T(8,128)(2,1)}), bf16[8,1,49,768]{3,2,1,0:T(8,128)(2,1)S(1)}, u32[]{:S(2)}, u32[]{:S(2)}) async-start(bf16[8,1,49,768]{3,2,1,0:T(8,128)(2,1)} %bitcast.37), calls=%async_computation.2 | async-start | bytes 1376256 | tf_op jit(solution)/shard_map/all_to_all | solution.py:259
  940.0 26.8 %slice-start.11 = ((s8[5505024]{0:T(1024)(128)(4,1)}), s8[1310720]{0:T(1024)(128)(4,1)S(1)}, s32[]{:S(2)}) async-start(s8[5505024]{0:T(1024)(128)(4,1)} %bitcast.325), calls=%async_computation.19 | async-start | bytes 2621440
  945.7 151.5 %all-to-all-start.3 = ((bf16[8,1,49,768]{3,2,1,0:T(8,128)(2,1)}), bf16[8,1,49,768]{3,2,1,0:T(8,128)(2,1)S(1)}, u32[]{:S(2)}, u32[]{:S(2)}) async-start(bf16[8,1,49,768]{3,2,1,0:T(8,128)(2,1)} %fusion.50), calls=%async_computation.3 | async-start | bytes 1376256 | tf_op jit(solution)/shard_map/all_to_all | solution.py:273
  950.7 16.1 slice-start.12
  984.2 66.7 %copy-start.127 = (bf16[8,49,3072]{2,1,0:T(8,128)(2,1)S(1)}, bf16[8,49,3072]{2,1,0:T(8,128)(2,1)}, u32[]{:S(2)}) copy-start(bf16[8,49,3072]{2,1,0:T(8,128)(2,1)} %copy-done.126) | copy-start | bytes 7225348
  1097.2 70.4 %all-to-all-start.1 = ((bf16[8,1,49,768]{3,2,1,0:T(8,128)(2,1)}), bf16[8,1,49,768]{3,2,1,0:T(8,128)(2,1)S(1)}, u32[]{:S(2)}, u32[]{:S(2)}) async-start(bf16[8,1,49,768]{3,2,1,0:T(8,128)(2,1)} %fusion.51), calls=%async_computation.1 | async-start | bytes 1376256 | tf_op jit(solution)/shard_map/all_to_all | solution.py:242
  1102.3 403.8 %all-reduce.13.cloned.1.call-start = ((), (), s32[]{:S(2)}) async-start(), calls=%async_computation.7 | async-start | bytes 37748736
  1163.8 906.3 %all-reduce.11.cloned.1.call-start = ((), (), s32[]{:S(2)}) async-start(), calls=%async_computation.6 | async-start | bytes 75595776
  1204.4 22.0 %copy-start.75 = (bf16[12,64,197]{2,1,0:T(8,128)(2,1)}, bf16[12,64,197]{2,1,0:T(8,128)(2,1)S(1)}, u32[]{:S(2)}) copy-start(bf16[12,64,197]{2,1,0:T(8,128)(2,1)S(1)} %fusion.56) | copy-start | bytes 907780
  2072.4 46.6 %copy-start.51 = (f32[295296]{0:T(1024)}, f32[295296]{0:T(1024)S(1)}, u32[]{:S(2)}) copy-start(f32[295296]{0:T(1024)S(1)} %get-tuple-element.104) | copy-start | bytes 3543556
  (127 other events, 470.9 us)
Sparse Core Ops, SparseCore 0:
  16.2 217.8 all-gather.5
  236.6 174.1 all-gather.3
  1163.9 342.1 all-reduce.12
  1513.6 556.4 all-reduce.10
where the time goes:
time: 2170 us; the launch traced here: 2160 us
  waiting for transfers between devices  946 us (44%)
  other arithmetic  536 us (25%)
  local copies, waits for them, and re-layouts  475 us (22%)
  matrix products  126 us (6%)
  blocking collectives  39.2 us (2%)
    unnamed x6, waiting for transfers between devices  744 us
    all_gather x1, other arithmetic, on_device(): dense_flat = lax.all_gather(dense_low, ('dp', 'expert'), axis=0, tiled=True)  401 us
    unnamed x308, local copies, waits for them, and re-layouts  225 us
    all_gather x1, waiting for transfers between devices, on_device(): dense_flat = lax.all_gather(dense_low, ('dp', 'expert'), axis=0, tiled=True)  194 us
    slice x1, local copies, waits for them, and re-layouts, on_device(): expert_flat[:, :model_width * hidden_width]  104 us
    concatenate x1, other arithmetic, on_device(): jnp.concatenate([first_expert_grad.reshape(local_experts, -1), second_exp...  61.4 us
    slice x15, local copies, waits for them, and re-layouts, unpack(): pieces.append(flat_params[offset:offset + length].reshape(layout))  53.4 us
  transfers between devices with their start and end apart: 8, of which 4 were waited for; matrix products, arithmetic and copies ran while one was open for 49% of the time, Pallas kernels for 0%

commit v1 on v0

v1 whole, which is shorter than its diff:
```python
import functools
import math

import jax
import jax.numpy as jnp
from jax import lax
from jax.experimental import pallas as pl
from jax.experimental.pallas import tpu as pltpu
from jax.sharding import PartitionSpec as P

HEADS = 12
HEAD_DIM = 64
LANES = 128

f32 = jnp.float32
bf16 = jnp.bfloat16

eps_norm = 1e-06
beta_first = 0.9
beta_second = 0.999
adam_eps = 1e-08
adam_step = 10.0

VMEM = pl.BlockSpec(memory_space=pltpu.VMEM)
SMEM = pl.BlockSpec(memory_space=pltpu.SMEM)


def params(mib=56):
    return pltpu.CompilerParams(vmem_limit_bytes=mib << 20)


def cost(flops, nbytes, trans=0):
    return pl.CostEstimate(flops=int(flops), bytes_accessed=int(nbytes), transcendentals=int(trans))


def dot(a, b):
    return lax.dot_general(a, b, (((1,), (0,)), ((), ())), preferred_element_type=f32)


def dot_nt(a, b):
    return lax.dot_general(a, b, (((1,), (1,)), ((), ())), preferred_element_type=f32)


def dot_tn(a, b):
    return lax.dot_general(a, b, (((0,), (0,)), ((), ())), preferred_element_type=f32)


def norm_rows(hidden):
    center = hidden - jnp.mean(hidden, axis=-1, keepdims=True)
    inverse = lax.rsqrt(jnp.mean(center * center, axis=-1, keepdims=True) + eps_norm)
    return center * inverse, inverse


def norm_back(upstream, normed, inverse, gain):
    scaled = upstream * gain
    gain_grad = jnp.sum(upstream * normed, axis=0, keepdims=True)
    centered = (
        scaled
        - jnp.mean(scaled, axis=-1, keepdims=True)
        - normed * jnp.mean(scaled * normed, axis=-1, keepdims=True)
    )
    return inverse * centered, gain_grad


def normal_cdf(v):
    return 0.5 * (1.0 + lax.erf(v * 0.7071067811865476))


def density(v):
    return jnp.exp(-0.5 * v * v) * 0.3989422804014327


def to_rows(read, write, first_q, rows, wide, tiles):
    if wide:
        quarter = rows // 4
        for q in range(4):
            for j in range(tiles):
                write(q * quarter, quarter, j, read(first_q + tiles * q + j, quarter, 4 * tiles))
    else:
        for j in range(tiles):
            write(0, rows, j, read(first_q + j, rows, tiles))


def pack_dense_kernel(dims, k_ref, tail_ref, own_ref, out_ref, buf):
    rows, tail_rows, tail, own, step, tiles, chunks, wide_ok = dims
    buf[0:tail] = tail_ref[...]
    buf[tail : tail + own] = own_ref[...]
    buf[tail + own :] = jnp.zeros((buf.shape[0] - tail - own, LANES), f32)
    k = k_ref[0]
    start = tail - step * k

    def read(first, count, stride):
        return buf[pl.ds(first, count, stride=stride), :]

    def write(first, count, j, value):
        out_ref[first : first + count, LANES * j : LANES * (j + 1)] = value.astype(bf16)

    wide = (k >= chunks // 2) & (k < 3 * chunks // 4) & wide_ok

    @pl.when(wide)
    def _():
        to_rows(read, write, start, rows, True, tiles)

    @pl.when(jnp.logical_not(wide))
    def _():
        to_rows(read, write, start, rows, False, tiles)

    for j in range(tiles):
        write(rows, tail_rows, j, read(own + j, tail_rows, tiles))


def pack_expert_kernel(dims, wide_ref, own_ref, out_ref):
    rows, tiles = dims

    def read(first, count, stride):
        return own_ref[pl.ds(first, count, stride=stride), :]

    def write(first, count, j, value):
        out_ref[first : first + count, LANES * j : LANES * (j + 1)] = value.astype(bf16)

    wide = wide_ref[0] > 0

    @pl.when(wide)
    def _():
        to_rows(read, write, 0, rows, True, tiles)

    @pl.when(jnp.logical_not(wide))
    def _():
        to_rows(read, write, 0, rows, False, tiles)


def unpack_kernel(dims, wide_ref, rows_ref, out_ref, square_ref):
    rows, tiles = dims
    wide = wide_ref[0] > 0

    def store(is_wide):
        total = jnp.zeros((1, LANES), f32)
        quarter = rows // 4
        for q in range(4):
            for j in range(tiles):
                piece = rows_ref[q * quarter : (q + 1) * quarter, LANES * j : LANES * (j + 1)].astype(f32)
                if is_wide:
                    out_ref[pl.ds(tiles * q + j, quarter, stride=4 * tiles), :] = piece
                else:
                    out_ref[pl.ds(tiles * quarter * q + j, quarter, stride=tiles), :] = piece
                total = total + jnp.sum(piece * piece, axis=0, keepdims=True)
        square_ref[...] = total

    @pl.when(wide)
    def _():
        store(True)

    @pl.when(jnp.logical_not(wide))
    def _():
        store(False)


def shift_kernel(dims, k_ref, flat_ref, head_ref, out_ref, square_ref, buf):
    step, own = dims
    count = flat_ref.shape[0]
    buf[0:count] = flat_ref[...]
    buf[count : count + head_ref.shape[0]] = head_ref[...]
    value = buf[pl.ds(step * k_ref[0], own), :]
    out_ref[...] = value
    square_ref[...] = jnp.sum(value * value, axis=0, keepdims=True)


def adam_kernel(clip_ref, grad_ref, momentum_ref, variance_ref, update_ref, momentum_out, variance_out):
    clipped = grad_ref[...] * clip_ref[0]
    momentum_new = beta_first * momentum_ref[...] + (1.0 - beta_first) * clipped
    variance_new = beta_second * variance_ref[...] + (1.0 - beta_second) * clipped * clipped
    first_hat = momentum_new / (1.0 - beta_first**adam_step)
    second_hat = variance_new / (1.0 - beta_second**adam_step)
    update_ref[...] = -first_hat / (jnp.sqrt(second_hat) + adam_eps)
    momentum_out[...] = momentum_new
    variance_out[...] = variance_new


def adam(clip, grad, momentum, variance, block):
    count = grad.shape[0]
    spec = pl.BlockSpec((block, LANES), lambda i: (i, 0))
    shape = jax.ShapeDtypeStruct(grad.shape, f32)
    return pl.pallas_call(
        adam_kernel,
        grid=(pl.cdiv(count, block),),
        in_specs=[SMEM, spec, spec, spec],
        out_specs=[spec] * 3,
        out_shape=[shape] * 3,
        compiler_params=params(),
        cost_estimate=cost(20 * grad.size, 24 * grad.size, 2 * grad.size),
        name="adam",
    )(clip, grad, momentum, variance)


def route_kernel(experts, capacity, stride, prio_row, prio_col, picks, picks_t, cols_ref, rows_ref):
    seq = picks.shape[0]
    before = (prio_row[...] < prio_col[...]).astype(f32).astype(bf16)
    lane = lax.broadcasted_iota(jnp.int32, (seq, experts), 1)
    sub = lax.broadcasted_iota(jnp.int32, (experts, seq), 0)
    hot = [(picks[:, j : j + 1] == lane).astype(f32) for j in range(2)]
    hot_t = [(picks_t[j : j + 1, :] == sub).astype(f32) for j in range(2)]
    first = jnp.sum(hot[0], axis=0, keepdims=True)
    first_t = jnp.sum(hot_t[0], axis=1, keepdims=True)
    for j in range(2):
        earlier = dot(before, hot[j].astype(bf16)) + (first if j else 0.0)
        earlier_t = dot_nt(hot_t[j].astype(bf16), before) + (first_t if j else 0.0)
        place = jnp.sum(earlier * hot[j], axis=1, keepdims=True).astype(jnp.int32)
        place_t = jnp.sum(earlier_t * hot_t[j], axis=0, keepdims=True).astype(jnp.int32)
        cols_ref[:, j : j + 1] = jnp.where(
            place < capacity, picks[:, j : j + 1] * stride + place, -1
        )
        rows_ref[j : j + 1, :] = jnp.where(
            place_t < capacity, picks_t[j : j + 1, :] * stride + place_t, -1
        )


def head_masks():
    lane = lax.broadcasted_iota(jnp.int32, (1, 2 * HEAD_DIM), 1)
    first = (lane < HEAD_DIM).astype(f32)
    return first.astype(bf16), (1.0 - first).astype(bf16)


def soft_scores(queries, key_rows, key_ok):
    scores = dot_nt(queries, key_rows) * HEAD_DIM ** (-0.5)
    scores = jnp.where(key_ok, scores, -1e30)
    top = jnp.max(scores, axis=-1, keepdims=True)
    raised = jnp.exp(scores - top)
    return raised * (1.0 / jnp.sum(raised, axis=-1, keepdims=True))


def matrix(w_ref, index):
    per = w_ref.shape[0] // 4
    width = w_ref.shape[2]
    rows = width // per
    return w_ref[index * per : (index + 1) * per, 0:rows, :].reshape(width, width)


def quarter_in(w_ref, q):
    width = w_ref.shape[2]
    rows = width // w_ref.shape[0]
    return w_ref[:, q * rows : (q + 1) * rows, :].reshape(width, width)


def attn_fwd_kernel(seq, stream_ref, gain_ref, w_ref, out_ref, a_ref, q_ref, k_ref, v_ref, o_ref):
    normed, _ = norm_rows(stream_ref[...])
    a_ref[...] = (normed * gain_ref[...]).astype(bf16)
    for index, ref in enumerate((q_ref, k_ref, v_ref)):
        ref[...] = dot(a_ref[...], matrix(w_ref, index)).astype(bf16)
    count = stream_ref.shape[0]
    key_ok = lax.broadcasted_iota(jnp.int32, (count, count), 1) < seq
    masks = head_masks()
    for pair in range(HEADS // 2):
        lanes = slice(2 * HEAD_DIM * pair, 2 * HEAD_DIM * (pair + 1))
        mixed = None
        for mask in masks:
            soft = soft_scores(q_ref[:, lanes] * mask, k_ref[:, lanes], key_ok).astype(bf16)
            part = dot(soft, v_ref[:, lanes] * mask)
            mixed = part if mixed is None else mixed + part
        o_ref[:, lanes] = mixed.astype(bf16)
    out_ref[...] = stream_ref[...] + dot(o_ref[...], matrix(w_ref, 3))


def attn_bwd_kernel(
    seq, grad_ref, stream_ref, gain_ref, w_ref, a_ref, q_ref, k_ref, v_ref, o_ref,
    out_ref, gain_out, dw_ref, do_ref, dq_ref, dk_ref, dv_ref,
):
    width = grad_ref.shape[1]
    branch = grad_ref[...].astype(bf16)

    def put(index, value):
        per = dw_ref.shape[0] // 4
        dw_ref[index * per : (index + 1) * per] = value.astype(bf16).reshape(per, width // per, width)

    do_ref[...] = dot_nt(branch, matrix(w_ref, 3)).astype(bf16)
    put(3, dot_tn(o_ref[...], branch))
    count = grad_ref.shape[0]
    key_ok = lax.broadcasted_iota(jnp.int32, (count, count), 1) < seq
    masks = head_masks()
    scale = HEAD_DIM ** (-0.5)
    for pair in range(HEADS // 2):
        lanes = slice(2 * HEAD_DIM * pair, 2 * HEAD_DIM * (pair + 1))
        dq = dk = dv = None
        for mask in masks:
            q_h = q_ref[:, lanes] * mask
            k_h = k_ref[:, lanes] * mask
            do_h = do_ref[:, lanes] * mask
            soft = soft_scores(q_h, k_ref[:, lanes], key_ok)
            dsoft = dot_nt(do_h, v_ref[:, lanes])
            dv_h = dot_tn(soft.astype(bf16), do_h)
            inner = jnp.sum(dsoft * soft, axis=-1, keepdims=True)
            dscore = (soft * (dsoft - inner)).astype(bf16)
            dq_h = dot(dscore, k_h)
            dk_h = dot_tn(dscore, q_h)
            dq = dq_h if dq is None else dq + dq_h
            dk = dk_h if dk is None else dk + dk_h
            dv = dv_h if dv is None else dv + dv_h
        dq_ref[:, lanes] = (dq * scale).astype(bf16)
        dk_ref[:, lanes] = (dk * scale).astype(bf16)
        dv_ref[:, lanes] = dv.astype(bf16)
    back = None
    for index, ref in enumerate((dq_ref, dk_ref, dv_ref)):
        put(index, dot_tn(a_ref[...], ref[...]))
        part = dot_nt(ref[...], matrix(w_ref, index))
        back = part if back is None else back + part
    normed, inverse = norm_rows(stream_ref[...])
    addend, gain_grad = norm_back(back, normed, inverse, gain_ref[...])
    out_ref[...] = grad_ref[...] + addend
    gain_out[...] = gain_grad


def mlp_fwd_kernel(stream_ref, gain_ref, w1_ref, w2_ref, out_ref, b_ref, u_ref):
    width = stream_ref.shape[1]
    normed, _ = norm_rows(stream_ref[...])
    b_ref[...] = (normed * gain_ref[...]).astype(bf16)
    out_ref[...] = stream_ref[...]
    total = None
    for q in range(4):
        pre = dot(b_ref[...], quarter_in(w1_ref, q))
        u_ref[:, q * width : (q + 1) * width] = pre
        part = dot((pre * normal_cdf(pre)).astype(bf16), matrix(w2_ref, q))
        total = part if total is None else total + part
    out_ref[...] = stream_ref[...] + total


def mlp_bwd_kernel(
    grad_ref, stream_ref, gain_ref, w1_ref, w2_ref, b_ref, u_ref, out_ref, gain_out, dw1_ref, dw2_ref
):
    width = grad_ref.shape[1]
    upper = grad_ref[...].astype(bf16)
    back = None
    for q in range(4):
        pre = u_ref[:, q * width : (q + 1) * width]
        cdf = normal_cdf(pre)
        act = (pre * cdf).astype(bf16)
        per = dw2_ref.shape[0] // 4
        dw2_ref[q * per : (q + 1) * per] = dot_tn(act, upper).astype(bf16).reshape(per, width // per, width)
        dact = dot_nt(upper, matrix(w2_ref, q))
        dpre = (dact * (cdf + pre * density(pre))).astype(bf16)
        groups = dw1_ref.shape[0]
        rows = width // groups
        dw1_ref[:, q * rows : (q + 1) * rows, :] = (
            dot_tn(b_ref[...], dpre).astype(bf16).reshape(groups, rows, width)
        )
        part = dot_nt(dpre, quarter_in(w1_ref, q))
        back = part if back is None else back + part
    normed, inverse = norm_rows(stream_ref[...])
    addend, gain_grad = norm_back(back, normed, inverse, gain_ref[...])
    out_ref[...] = grad_ref[...] + addend
    gain_out[...] = gain_grad


def pick_hots(picks, experts):
    lane = lax.broadcasted_iota(jnp.int32, (picks.shape[0], experts), 1)
    return [(picks[:, j : j + 1] == lane).astype(f32) for j in range(2)]


def softmax_rows(logits):
    raised = jnp.exp(logits - jnp.max(logits, axis=-1, keepdims=True))
    return raised / jnp.sum(raised, axis=-1, keepdims=True)


def dispatch_kernel(
    slots, stream_ref, gain_ref, wr_ref, picks_ref, rows_ref, cot_ref, c_ref, probs_ref, x_ref, dy_ref
):
    count = stream_ref.shape[0]
    experts = wr_ref.shape[1]
    normed, _ = norm_rows(stream_ref[...])
    c_ref[...] = (normed * gain_ref[...]).astype(bf16)
    probs = softmax_rows(dot(c_ref[...], wr_ref[...]))
    probs_ref[...] = probs
    hots = pick_hots(picks_ref, experts)
    sub = lax.broadcasted_iota(jnp.int32, (slots, count), 0)
    chosen = None
    dy = None
    for j in range(2):
        gate = jnp.sum(probs * hots[j], axis=-1, keepdims=True)
        select = (rows_ref[j : j + 1, :] == sub).astype(f32).astype(bf16)
        chosen = select if chosen is None else chosen + select
        part = dot(select, (gate * cot_ref[...]).astype(bf16))
        dy = part if dy is None else dy + part
    x_ref[...] = dot(chosen, c_ref[...]).astype(bf16)
    dy_ref[...] = dy.astype(bf16)


def expert_kernel(x_ref, dy_ref, u1_ref, u2_ref, y_ref, dx_ref, act_ref, dpre_ref, y_sum, dx_sum):
    q = pl.program_id(0)
    width = x_ref.shape[1]
    first = u1_ref[...].reshape(width, width)
    pre = dot(x_ref[...], first)
    cdf = normal_cdf(pre)
    act = (pre * cdf).astype(bf16)
    act_ref[...] = act
    dact = dot_nt(dy_ref[...], u2_ref[...])
    dpre = (dact * (cdf + pre * density(pre))).astype(bf16)
    dpre_ref[...] = dpre
    y_part = dot(act, u2_ref[...])
    dx_part = dot_nt(dpre, first)

    @pl.when(q == 0)
    def _():
        y_sum[...] = y_part
        dx_sum[...] = dx_part

    @pl.when(q > 0)
    def _():
        y_sum[...] += y_part
        dx_sum[...] += dx_part

    @pl.when(q == pl.num_programs(0) - 1)
    def _():
        y_ref[...] = y_sum[...].astype(bf16)
        dx_ref[...] = dx_sum[...].astype(bf16)


def expert_grad_kernel(x_ref, dy_ref, act_ref, dpre_ref, out_ref):
    q = pl.program_id(0)
    groups, _, rows, width = out_ref.shape
    half = groups // 2
    out_ref[0:half, q] = dot_tn(x_ref[...], dpre_ref[...]).astype(bf16).reshape(half, rows, width)
    second = dot_tn(act_ref[...], dy_ref[...]).astype(bf16)
    per = width // rows
    for part in range(per):
        flat = q * per + part
        out_ref[half + flat // 4, flat % 4] = second[part * rows : (part + 1) * rows]


def combine_kernel(
    stream_ref, gain_ref, wr_ref, picks_ref, cols_ref, cot_ref, c_ref, probs_ref, y_ref, dx_ref,
    out_ref, grad_ref, gain_out, router_out,
):
    count = stream_ref.shape[0]
    slots = y_ref.shape[0]
    experts = wr_ref.shape[1]
    probs = probs_ref[...]
    hots = pick_hots(picks_ref, experts)
    lane = lax.broadcasted_iota(jnp.int32, (count, slots), 1)
    cot = cot_ref[...]
    total = stream_ref[...]
    chosen = None
    prob_grad = None
    for j in range(2):
        select = (cols_ref[:, j : j + 1] == lane).astype(f32).astype(bf16)
        chosen = select if chosen is None else chosen + select
        pair_out = dot(select, y_ref[...])
        gate = jnp.sum(probs * hots[j], axis=-1, keepdims=True)
        total = total + gate * pair_out
        part = jnp.sum(cot * pair_out, axis=-1, keepdims=True) * hots[j]
        prob_grad = part if prob_grad is None else prob_grad + part
    out_ref[...] = total
    logit_grad = probs * (prob_grad - jnp.sum(prob_grad * probs, axis=-1, keepdims=True))
    logit_grad = logit_grad.astype(bf16)
    router_out[...] = dot_tn(c_ref[...], logit_grad)
    back = dot(chosen, dx_ref[...]) + dot_nt(logit_grad, wr_ref[...])
    normed, inverse = norm_rows(stream_ref[...])
    addend, gain_grad = norm_back(back, normed, inverse, gain_ref[...])
    grad_ref[...] = cot + addend
    gain_out[...] = gain_grad


def all_sum(value, axes):
    for axis in axes:
        size = lax.axis_size(axis)
        hop = 1
        while hop < size:
            value = value + lax.ppermute(value, axis, [(i, i ^ hop) for i in range(size)])
            hop *= 2
    return value


def shape(dims, dtype=f32):
    return jax.ShapeDtypeStruct(dims, dtype)


def on_device(
    tokens,
    cotangent,
    expert_picks,
    priority,
    dense_master,
    dense_momentum,
    dense_variance,
    expert_master,
    expert_momentum,
    expert_variance,
):
    both = ("dp", "expert")
    dp_ranks = lax.axis_size("dp")
    expert_ranks = lax.axis_size("expert")
    devices = dp_ranks * expert_ranks
    local_experts = expert_master.shape[0]
    experts = local_experts * expert_ranks
    images, seq, width = tokens.shape
    assert local_experts == 1 and images == 1
    tiles = width // LANES
    me = lax.axis_index("dp") * expert_ranks + lax.axis_index("expert")
    me_arr = me.reshape(1).astype(jnp.int32)

    own = dense_master.shape[0] // LANES
    expert_flat = expert_master.shape[1] // LANES
    hidden = expert_master.shape[1] * dp_ranks // (2 * width)
    matrix_rows = 8 * width + 2 * hidden
    rows = matrix_rows // devices
    step = own - rows * tiles
    tail = step * devices
    tail_rows = -(-tail // (16 * tiles)) * 16
    wide_ok = rows % 64 == 0
    expert_rows = expert_flat // tiles

    dense_flat = dense_master.reshape(own, LANES)
    forward_ring = [(i, (i + 1) % devices) for i in range(devices)]
    backward_ring = [((i + 1) % devices, i) for i in range(devices)]
    tail_from = lax.ppermute(dense_flat[own - tail :], both, forward_ring)
    buf_rows = -(-(own + max(tail, tail_rows * tiles)) // 8) * 8
    chunk = pl.pallas_call(
        functools.partial(
            pack_dense_kernel, (rows, tail_rows, tail, own, step, tiles, devices, wide_ok)
        ),
        in_specs=[SMEM, VMEM, VMEM],
        out_specs=VMEM,
        out_shape=shape((rows + tail_rows, width), bf16),
        scratch_shapes=[pltpu.VMEM((buf_rows, LANES), f32)],
        compiler_params=params(),
        cost_estimate=cost(0, 6 * dense_master.size),
        name="pack_dense",
    )(me_arr, tail_from, dense_flat)
    gathered = lax.all_gather(chunk, both, axis=0, tiled=True)
    gathered = gathered.reshape(devices, rows + tail_rows, width)

    expert_wide = (lax.axis_index("dp") < dp_ranks // 2).astype(jnp.int32).reshape(1)
    expert_chunk = pl.pallas_call(
        functools.partial(pack_expert_kernel, (expert_rows, tiles)),
        in_specs=[SMEM, VMEM],
        out_specs=VMEM,
        out_shape=shape((expert_rows, width), bf16),
        compiler_params=params(),
        cost_estimate=cost(0, 6 * expert_master.size),
        name="pack_expert",
    )(expert_wide, expert_master.reshape(expert_flat, LANES))
    expert_all = lax.all_gather(expert_chunk, "dp", axis=0, tiled=True)

    capacity = 2 * seq // experts
    stride = -(-capacity // 8) * 8
    slots = experts * stride
    padded = -(-seq // 16) * 16
    cols, rows_slots = pl.pallas_call(
        functools.partial(route_kernel, experts, capacity, stride),
        in_specs=[VMEM] * 4,
        out_specs=[VMEM] * 2,
        out_shape=[shape((seq, 2), jnp.int32), shape((2, seq), jnp.int32)],
        compiler_params=params(),
        cost_estimate=cost(2e6, 1e5),
        name="route",
    )(priority, priority.reshape(seq, 1), expert_picks, expert_picks.T)
    fill = padded - seq
    cols = jnp.pad(cols, ((0, fill), (0, 0)), constant_values=-1)
    rows_slots = jnp.pad(rows_slots, ((0, 0), (0, fill)), constant_values=-1)
    picks = jnp.pad(expert_picks, ((0, fill), (0, 0)))
    stream = jnp.pad(tokens.reshape(seq, width).astype(f32), ((0, fill), (0, 0)))
    cot = jnp.pad(cotangent.reshape(seq, width).astype(f32), ((0, fill), (0, 0)))

    tail_flat = gathered[devices - 1, rows:, :].reshape(-1)
    router = tail_flat[: width * experts].reshape(width, experts)
    gains = tail_flat[width * experts : width * (experts + 4)].reshape(4, width).astype(f32)
    gain = [gains[i : i + 1] for i in range(4)]

    per = devices // 4
    dense_block = (per, rows + tail_rows, width)

    def layer_spec(index):
        return pl.BlockSpec(dense_block, lambda *_: (index, 0, 0), pipeline_mode=pl.Buffered(1))

    if wide_ok:
        first_in, first_spec, first_shape = gathered, layer_spec(2), (per, rows, width)
    else:
        first_in = gathered[2 * per : 3 * per, :rows].reshape(width, 4, width)
        first_in = first_in.transpose(1, 0, 2).reshape(1, 4 * width, width)
        first_spec, first_shape = VMEM, (1, 4 * width, width)

    act_shape = shape((padded, width), bf16)
    stream_shape = shape((padded, width), f32)
    gain_shape = shape((1, width), f32)
    tok_flops = 2 * padded * width * width
    weight_bytes = 2 * width * width

    def call(kernel, ins, in_specs, outs, name, flops, nbytes, trans=0, scratch=()):
        whole = [pl.BlockSpec(a.shape, lambda *_, n=len(a.shape): (0,) * n) for a in outs]
        specs = [
            s if s is not None else pl.BlockSpec(a.shape, lambda *_, n=a.ndim: (0,) * n)
            for a, s in zip(ins, in_specs, strict=True)
        ]
        return pl.pallas_call(
            kernel,
            grid=(1,),
            in_specs=specs,
            out_specs=whole,
            out_shape=outs,
            scratch_shapes=list(scratch),
            compiler_params=params(),
            cost_estimate=cost(flops, nbytes, trans),
            name=name,
        )(*ins)

    def attn_fwd(value, layer, which):
        return call(
            functools.partial(attn_fwd_kernel, seq),
            (value, gain[which], gathered),
            (None, None, layer_spec(layer)),
            [stream_shape] + [act_shape] * 5,
            "attn_fwd",
            5 * tok_flops,
            4 * weight_bytes,
        )

    def attn_bwd(grad, value, kept, layer, which):
        return call(
            functools.partial(attn_bwd_kernel, seq),
            (grad, value, gain[which], gathered, *kept),
            (None, None, None, layer_spec(layer)) + (None,) * 5,
            [stream_shape, gain_shape, shape((per, rows, width), bf16)],
            "attn_bwd",
            11 * tok_flops,
            8 * weight_bytes,
            scratch=[pltpu.VMEM((padded, width), bf16)] * 4,
        )

    stream_one, *kept_one = attn_fwd(stream, 0, 0)
    stream_two, mlp_in, mlp_pre = call(
        mlp_fwd_kernel,
        (stream_one, gain[1], first_in, gathered),
        (None, None, first_spec, layer_spec(3)),
        [stream_shape, act_shape, shape((padded, hidden), f32)],
        "mlp_fwd",
        8 * tok_flops,
        8 * weight_bytes,
    )
    stream_three, *kept_two = attn_fwd(stream_two, 1, 2)
    moe_in, probs, outgoing, outgoing_grad = call(
        functools.partial(dispatch_kernel, slots),
        (stream_three, gain[3], router, picks, rows_slots, cot),
        (None,) * 6,
        [act_shape, shape((padded, experts)), shape((slots, width), bf16), shape((slots, width), bf16)],
        "dispatch",
        3 * 2 * padded * slots * width,
        4e6,
    )

    def exchange(value):
        value = value.reshape(expert_ranks, slots // expert_ranks, width)
        value = lax.all_to_all(value, "expert", split_axis=0, concat_axis=0, tiled=True)
        return value.reshape(slots, width)

    arriving = exchange(outgoing)
    arriving_grad = exchange(outgoing_grad)

    quarter = expert_rows // 4
    half = dp_ranks // 2
    expert_flops = 2 * slots * width * width
    expert_out, input_back, expert_act, pre_grad = pl.pallas_call(
        expert_kernel,
        grid=(4,),
        in_specs=[
            pl.BlockSpec((slots, width), lambda q: (0, 0)),
            pl.BlockSpec((slots, width), lambda q: (0, 0)),
            pl.BlockSpec((half, 1, quarter, width), lambda q: (0, q, 0, 0)),
            pl.BlockSpec((width, width), lambda q: (4 + q, 0)),
        ],
        out_specs=[
            pl.BlockSpec((slots, width), lambda q: (0, 0)),
            pl.BlockSpec((slots, width), lambda q: (0, 0)),
            pl.BlockSpec((slots, width), lambda q: (0, q)),
            pl.BlockSpec((slots, width), lambda q: (0, q)),
        ],
        out_shape=[
            shape((slots, width), bf16),
            shape((slots, width), bf16),
            shape((slots, hidden), bf16),
            shape((slots, hidden), bf16),
        ],
        scratch_shapes=[pltpu.VMEM((slots, width), f32)] * 2,
        compiler_params=params(),
        cost_estimate=cost(16 * expert_flops, 8 * weight_bytes),
        name="expert",
    )(
        arriving,
        arriving_grad,
        expert_all.reshape(dp_ranks, 4, quarter, width),
        expert_all,
    )
    returned = exchange(expert_out)
    returned_grad = exchange(input_back)
    expert_local = pl.pallas_call(
        expert_grad_kernel,
        grid=(4,),
        in_specs=[
            pl.BlockSpec((slots, width), lambda q: (0, 0)),
            pl.BlockSpec((slots, width), lambda q: (0, 0)),
            pl.BlockSpec((slots, width), lambda q: (0, q)),
            pl.BlockSpec((slots, width), lambda q: (0, q)),
        ],
        out_specs=pl.BlockSpec((dp_ranks, 4, quarter, width), lambda q: (0, 0, 0, 0)),
        out_shape=shape((dp_ranks, 4, quarter, width), bf16),
        compiler_params=params(),
        cost_estimate=cost(8 * expert_flops, 8 * weight_bytes),
        name="expert_grad",
    )(arriving, arriving_grad, expert_act, pre_grad)
    expert_sum = lax.psum_scatter(
        expert_local.reshape(dp_ranks * expert_rows, width), "dp", scatter_dimension=0, tiled=True
    )

    output, grad, gain_four, router_grad = call(
        combine_kernel,
        (stream_three, gain[3], router, picks, cols, cot, moe_in, probs, returned, returned_grad),
        (None,) * 10,
        [stream_shape, stream_shape, gain_shape, shape((width, experts))],
        "combine",
        3 * 2 * padded * slots * width,
        6e6,
    )
    grad, gain_three, second_dw = attn_bwd(grad, stream_two, kept_two, 1, 2)
    grad, gain_two, first_dw1, second_dw2 = call(
        mlp_bwd_kernel,
        (grad, stream_one, gain[1], first_in, gathered, mlp_in, mlp_pre),
        (None, None, None, first_spec, layer_spec(3), None, None),
        [stream_shape, gain_shape, shape(first_shape, bf16), shape((per, rows, width), bf16)],
        "mlp_bwd",
        16 * tok_flops,
        16 * weight_bytes,
    )
    grad, gain_one, first_dw = attn_bwd(grad, stream, kept_one, 0, 0)
    if not wide_ok:
        first_dw1 = first_dw1.reshape(4, width, width).transpose(1, 0, 2)
    dense_local = jnp.concatenate(
        [part.reshape(-1, width) for part in (first_dw, second_dw, first_dw1, second_dw2)], axis=0
    )
    dense_sum = lax.psum_scatter(dense_local, both, scatter_dimension=0, tiled=True)

    small = jnp.concatenate(
        [router_grad.reshape(-1)] + [g.reshape(-1) for g in (gain_one, gain_two, gain_three, gain_four)]
    )
    small = jnp.pad(small, (0, tail * LANES - small.shape[0])).reshape(tail, LANES)
    small = all_sum(small, ("expert", "dp"))
    gain_at = width * experts
    gain_grads = small.reshape(-1)[gain_at : gain_at + 4 * width].reshape(4, width)

    dense_wide = (me >= devices // 2) & (me < 3 * devices // 4) & wide_ok
    dense_rows, _ = pl.pallas_call(
        functools.partial(unpack_kernel, (rows, tiles)),
        in_specs=[SMEM, VMEM],
        out_specs=[VMEM, VMEM],
        out_shape=[shape((rows * tiles, LANES)), shape((1, LANES))],
        compiler_params=params(),
        cost_estimate=cost(0, 6 * rows * width),
        name="unpack_dense",
    )(dense_wide.astype(jnp.int32).reshape(1), dense_sum)
    head = lax.ppermute(dense_rows[:tail], both, backward_ring)
    head = jnp.where(me == devices - 1, small, head)
    dense_grad, dense_square = pl.pallas_call(
        functools.partial(shift_kernel, (step, own)),
        in_specs=[SMEM, VMEM, VMEM],
        out_specs=[VMEM, VMEM],
        out_shape=[shape((own, LANES)), shape((1, LANES))],
        scratch_shapes=[pltpu.VMEM((-(-(rows * tiles + tail) // 8) * 8, LANES), f32)],
        compiler_params=params(),
        cost_estimate=cost(0, 8 * rows * width),
        name="shift_dense",
    )(me_arr, dense_rows, head)
    expert_grad, expert_square = pl.pallas_call(
        functools.partial(unpack_kernel, (expert_rows, tiles)),
        in_specs=[SMEM, VMEM],
        out_specs=[VMEM, VMEM],
        out_shape=[shape((expert_flat, LANES)), shape((1, LANES))],
        compiler_params=params(),
        cost_estimate=cost(0, 6 * expert_rows * width),
        name="unpack_expert",
    )(expert_wide, expert_sum)

    square = all_sum(dense_square + expert_square, ("expert", "dp"))
    square_sum = jnp.sum(square)
    param_count = (dense_master.size + expert_master.size) * devices
    clip_factor = jnp.minimum(1.0, jnp.sqrt(param_count / (square_sum + 1e-06))).reshape(1)

    dense_update, momentum_dense, variance_dense = adam(
        clip_factor,
        dense_grad,
        dense_momentum.reshape(own, LANES),
        dense_variance.reshape(own, LANES),
        own,
    )
    expert_update, momentum_expert, variance_expert = adam(
        clip_factor,
        expert_grad,
        expert_momentum.reshape(expert_flat, LANES),
        expert_variance.reshape(expert_flat, LANES),
        expert_flat // 8,
    )
    image = (1, seq, width)
    return (
        output[:seq].reshape(image),
        grad[:seq].reshape(image),
        dense_grad.reshape(dense_master.shape),
        expert_grad.reshape(expert_master.shape),
        dense_update.reshape(dense_master.shape),
        momentum_dense.reshape(dense_master.shape),
        variance_dense.reshape(dense_master.shape),
        expert_update.reshape(expert_master.shape),
        momentum_expert.reshape(expert_master.shape),
        variance_expert.reshape(expert_master.shape),
        gain_grads,
    )


def solution(mesh):
    tokens = P(("dp", "expert"), None, None)
    flat = P(("dp", "expert"))
    pairs = P(("dp", "expert"), None)
    expert = P("expert", "dp")
    return jax.shard_map(
        on_device,
        mesh=mesh,
        in_specs=(tokens, tokens, pairs, pairs, flat, flat, flat, expert, expert, expert),
        out_specs=(tokens, tokens, flat, expert, flat, flat, flat, expert, expert, expert, P()),
        check_vma=False,
    )
```

time: 2170 us -> 730 us (0.34)
  other arithmetic: 536 us -> 28 us
  waiting for transfers between devices: 946 us -> 470 us
  local copies, waits for them, and re-layouts: 475 us -> 14.5 us
  Pallas kernels: 0 us -> 133 us
  matrix products: 126 us -> 0 us
    unnamed x6 -> x4, waiting for transfers between devices: 744 us -> 0.07 us
    all_gather x1 -> x0, other arithmetic: 401 us -> none  [on_device(): dense_flat = lax.all_gather(dense_low, ('dp', 'expert'), axis=0, tiled=True)]
    reduce_scatter x0 -> x2, waiting for transfers between devices: none -> 267 us  [the longest x1 175 us: on_device(): lax.psum_scatter(dense_local, both, scatter_dimension=0, tiled=True)]
    unnamed x308 -> x39, local copies, waits for them, and re-layouts: 225 us -> 6.35 us
    slice x17 -> x5, local copies, waits for them, and re-layouts: 158 us -> 2.94 us  [the longest x1 0.82 us: on_device(): tail_from = lax.ppermute(dense_flat[own - tail:], both, forward_ring)]
    pallas_call x0 -> x18, Pallas kernels: none -> 133 us  [the longest x8 71.8 us: call(): pl.pallas_call(kernel, grid=(1,), in_specs=specs, out_specs=whole, out_sh...]
    dot_general x51 -> x0, matrix products: 126 us -> none  [the longest x1 17.4 us: on_device(): jnp.einsum('secf,efd->secd', expert_act, second_experts, preferred_elemen...]
    all_to_all x0 -> x2, blocking collectives: none -> 46.6 us  [exchange(): lax.all_to_all(value, 'expert', split_axis=0, concat_axis=0, tiled=True)]
  transfers between devices with their start and end apart: 8 -> 18, of which waited for: 4 -> 14; matrix products, arithmetic and copies ran while one was open for 49% -> 2% of each run, Pallas kernels for 0% -> 7%
where the time goes in v1:
time: 730 us; the launch traced here: 726 us
  waiting for transfers between devices  470 us (64%)
  Pallas kernels  133 us (18%)
  blocking collectives  46.6 us (6%)
  other arithmetic  28 us (4%)
  starting transfers between devices  18.9 us (3%)
  between operations  15 us (2%)
  local copies, waits for them, and re-layouts  14.5 us (2%)
    reduce_scatter x1, waiting for transfers between devices, on_device(): lax.psum_scatter(dense_local, both, scatter_dimension=0, tiled=True)  175 us
    all_gather x1, waiting for transfers between devices, on_device(): gathered = lax.all_gather(chunk, both, axis=0, tiled=True)  115 us
    reduce_scatter x1, waiting for transfers between devices, on_device(): lax.psum_scatter(expert_local.reshape(dp_ranks * expert_rows, width), 'dp...  91.9 us
    pallas_call x8, Pallas kernels, call(): pl.pallas_call(kernel, grid=(1,), in_specs=specs, out_specs=whole, out_sh...  71.8 us
    all_to_all x2, blocking collectives, exchange(): lax.all_to_all(value, 'expert', split_axis=0, concat_axis=0, tiled=True)  46.6 us
    all_gather x1, waiting for transfers between devices, on_device(): expert_all = lax.all_gather(expert_chunk, 'dp', axis=0, tiled=True)  41.2 us
    concatenate x1, other arithmetic, on_device(): jnp.concatenate([part.reshape(-1, width) for part in (first_dw, second_dw...  23.6 us
    ppermute x10, waiting for transfers between devices, all_sum(): lax.ppermute(value, axis, [(i, i ^ hop) for i in range(size)])  20.4 us
  transfers between devices with their start and end apart: 18, of which 14 were waited for; matrix products, arithmetic and copies ran while one was open for 2% of the time, Pallas kernels for 7%

profile of v1, /device:TPU:0, one launch (start us, length us, event | category | flops | bytes accessed | tf_op | source)
XLA Modules:
  0.0 726.1 jit_solution(4597974762928370452)
XLA Ops:
  8.5 7.7 %collective-permute-done.tail_ref = f32[96,128]{1,0:T(8,128)S(1)} collective-permute-done((f32[96,128]{1,0:T(8,128)S(1)}, f32[96,128]{1,0:T(8,128)S(1)}, u32[]{:S(2)}, u32[]{:S(2)}) %collective-permute-start) | collective-permute-done | bytes 49184 | tf_op jit(solution)/shard_map/ppermute | solution.py:512
  19.2 5.0 pack_expert.1
  30.9 114.8 %all-gather.3.cloned.1.call-done = bf16[12800,768]{1,0:T(8,128)(2,1)} async-done(((bf16[400,768]{1,0:T(8,128)(2,1)}), bf16[12800,768]{1,0:T(8,128)(2,1)}) %all-gather.3.cloned.1.call-update) | async-done | bytes 19660816 | tf_op jit(solution)/shard_map/all_gather | solution.py:526
  148.7 6.5 attn_fwd.2
  155.2 9.1 %mlp_fwd.1 = (f32[208,768]{1,0:T(8,128)}, bf16[208,768]{1,0:T(8,128)(2,1)}, f32[208,3072]{1,0:T(8,128)}) custom-call(f32[208,768]{1,0:T(8,128)} %get-tuple-element.61.stream_ref, f32[1,768]{1,0:T(1,128)} %get-tuple-element.137.gain_ref, bf16[32,400,768]{2,1,0:T(8,128)(2,1)} %bitcast.60, bf16[32,400,768]{2,1,0:T(8,128)(2,1)} %bitcast.61), custom_call_target="tpu_custom_call" | custom-call | flops 1962934272 | bytes 9437184 | tf_op jit(solution)/shard_map/mlp_fwd/pallas_call | solution.py:591
  164.3 6.5 attn_fwd.3
  174.6 23.0 %all_to_all.20 = bf16[8,56,768]{2,1,0:T(8,128)(2,1)} all-to-all(bf16[8,56,768]{2,1,0:T(8,128)(2,1)} %bitcast.88), channel_id=1, replica_groups=mesh['dp'=4,'expert'=8] {'expert'}, dimensions={0} | all-to-all | bytes 1376256 | tf_op jit(solution)/shard_map/all_to_all | solution.py:649
  201.4 41.2 %all-gather.5.cloned.1.call-done.u2_ref = bf16[6144,768]{1,0:T(8,128)(2,1)} async-done(((bf16[1536,768]{1,0:T(8,128)(2,1)}), bf16[6144,768]{1,0:T(8,128)(2,1)}) %all-gather.5.cloned.1.call-update) | async-done | bytes 9437200 | tf_op jit(solution)/shard_map/all_gather | solution.py:539
  243.5 14.4 %expert.1 = (bf16[448,768]{1,0:T(8,128)(2,1)}, bf16[448,768]{1,0:T(8,128)(2,1)}, bf16[448,3072]{1,0:T(8,128)(2,1)}, bf16[448,3072]{1,0:T(8,128)(2,1)}) custom-call(bf16[448,768]{1,0:T(8,128)(2,1)} %bitcast.76, bf16[448,768]{1,0:T(8,128)(2,1)} %bitcast.78, bf16[4,4,384,768]{3,2,1,0:T(8,128)(2,1)} %bitcast.94, ...), custom_call_target="tpu_custom_call" | custom-call | flops 8455716864 | bytes 9437184 | tf_op jit(solution)/shard_map/expert/pallas_call | solution.py:658
  257.9 23.6 %all_to_all.21 = bf16[8,56,768]{2,1,0:T(8,128)(2,1)} all-to-all(bf16[8,56,768]{2,1,0:T(8,128)(2,1)} %bitcast.89), channel_id=1, replica_groups=mesh['dp'=4,'expert'=8] {'expert'}, dimensions={0} | all-to-all | bytes 1376256 | tf_op jit(solution)/shard_map/all_to_all | solution.py:649
  285.7 18.1 %all-to-all-done.3 = bf16[8,56,768]{2,1,0:T(8,128)(2,1)S(1)} async-done(((bf16[8,56,768]{2,1,0:T(8,128)(2,1)}), bf16[8,56,768]{2,1,0:T(8,128)(2,1)S(1)}, u32[]{:S(2)}, u32[]{:S(2)}) %all-to-all-start.3) | async-done | bytes 688160 | tf_op jit(solution)/shard_map/all_to_all | solution.py:649
  304.6 4.7 combine.1
  309.4 13.2 %attn_bwd.2 = (f32[208,768]{1,0:T(8,128)}, f32[1,768]{1,0:T(1,128)}, bf16[8,384,768]{2,1,0:T(8,128)(2,1)}) custom-call(f32[208,768]{1,0:T(8,128)} %get-tuple-element.73.grad_ref, f32[208,768]{1,0:T(8,128)} %get-tuple-element.62.stream_ref, f32[1,768]{1,0:T(1,128)} %get-tuple-element.136.gain_ref, bf16[32,400,768]{2,1,0:T(8,128)(2,1)} %bitcast.63, ...), custom_call_target="tpu_custom_call" | custom-call | flops 2699034624 | bytes 9437184 | tf_op jit(solution)/shard_map/attn_bwd/pallas_call | solution.py:591
  322.6 14.8 %mlp_bwd.1 = (f32[208,768]{1,0:T(8,128)}, f32[1,768]{1,0:T(1,128)}, bf16[8,384,768]{2,1,0:T(8,128)(2,1)}, bf16[8,384,768]{2,1,0:T(8,128)(2,1)}) custom-call(f32[208,768]{1,0:T(8,128)} %get-tuple-element.79.grad_ref, f32[208,768]{1,0:T(8,128)} %get-tuple-element.61.stream_ref, f32[1,768]{1,0:T(1,128)} %get-tuple-element.137.gain_ref, ...), custom_call_target="tpu_custom_call" | custom-call | flops 3925868544 | bytes 18874368 | tf_op jit(solution)/shard_map/mlp_bwd/pallas_call | solution.py:591
  337.4 13.2 %attn_bwd.3 = (f32[208,768]{1,0:T(8,128)}, f32[1,768]{1,0:T(1,128)}, bf16[8,384,768]{2,1,0:T(8,128)(2,1)}) custom-call(f32[208,768]{1,0:T(8,128)} %get-tuple-element.82.grad_ref, f32[208,768]{1,0:T(8,128)} %pad_convert_fusion.1.stream_ref, f32[1,768]{1,0:T(1,128)} %get-tuple-element.138.gain_ref, bf16[32,400,768]{2,1,0:T(8,128)(2,1)} %bitcast.66, ...), custom_call_target="tpu_custom_call" | custom-call | flops 2699034624 | bytes 9437184 | tf_op jit(solution)/shard_map/attn_bwd/pallas_call | solution.py:591
  350.5 23.6 %pad_maximum_fusion = bf16[12288,768]{1,0:T(8,128)(2,1)} fusion(bf16[3072,768]{1,0:T(8,128)(2,1)} %bitcast.70, bf16[3072,768]{1,0:T(8,128)(2,1)} %bitcast.69, bf16[3072,768]{1,0:T(8,128)(2,1)} %bitcast.68, bf16[3072,768]{1,0:T(8,128)(2,1)} %bitcast.71), kind=kLoop, calls=%fused_computation | loop fusion | flops 75497472 | bytes 37748736 | tf_op jit(solution)/shard_map/concatenate | solution.py:732
  374.3 11.6 %expert_grad.1 = bf16[4,4,384,768]{3,2,1,0:T(8,128)(2,1)} custom-call(bf16[448,768]{1,0:T(8,128)(2,1)} %bitcast.77, bf16[448,768]{1,0:T(8,128)(2,1)} %bitcast.79, bf16[448,3072]{1,0:T(8,128)(2,1)} %get-tuple-element.100.act_ref, bf16[448,3072]{1,0:T(8,128)(2,1)} %get-tuple-element.101.dpre_ref), custom_call_target="tpu_custom_call" | custom-call | flops 4227858432 | bytes 9437184 | tf_op jit(solution)/shard_map/expert_grad/pallas_call | solution.py:691
  388.7 4.1 collective-permute-done.2
  392.9 5.0 collective-permute-done.3
  403.5 175.4 %reduce-scatter.3.cloned.1.call-done.rows_ref = bf16[384,768]{1,0:T(8,128)(2,1)} async-done(((bf16[12288,768]{1,0:T(8,128)(2,1)}), bf16[384,768]{1,0:T(8,128)(2,1)}) %reduce-scatter.3.cloned.1.call-update) | async-done | bytes 589840 | tf_op jit(solution)/shard_map/reduce_scatter | solution.py:735
  583.9 91.9 %reduce-scatter.5.cloned.1.call-done.rows_ref = bf16[1536,768]{1,0:T(8,128)(2,1)} async-done(((bf16[6144,768]{1,0:T(8,128)(2,1)}), bf16[1536,768]{1,0:T(8,128)(2,1)}) %reduce-scatter.5.cloned.1.call-update) | async-done | bytes 2359312 | tf_op jit(solution)/shard_map/reduce_scatter | solution.py:706
  675.9 5.2 unpack_expert.1
  702.9 12.3 %adam.3 = (f32[9216,128]{1,0:T(8,128)}, f32[9216,128]{1,0:T(8,128)}, f32[9216,128]{1,0:T(8,128)}) custom-call(f32[1]{0:T(128)} %bitcast.34.clip_ref, f32[9216,128]{1,0:T(8,128)} %get-tuple-element.102.grad_ref, f32[9216,128]{1,0:T(8,128)} %bitcast.73, f32[9216,128]{1,0:T(8,128)} %bitcast.74), custom_call_target="tpu_custom_call" | custom-call | flops 23592960 | bytes 28311552 | tf_op jit(solution)/shard_map/adam/pallas_call | solution.py:183
  715.2 4.2 adam.2
  (110 shorter events, 62.1 us)
Async XLA Ops:
  7.2 138.5 %all-gather.3.cloned.1.call-start = ((), (), s32[]{:S(2)}) async-start(), calls=%async_computation.6 | async-start | bytes 20275200 | tf_op jit(solution)/shard_map/all_gather | solution.py:526
  8.0 8.1 %collective-permute-start = (f32[96,128]{1,0:T(8,128)S(1)}, f32[96,128]{1,0:T(8,128)S(1)}, u32[]{:S(2)}, u32[]{:S(2)}) collective-permute-start(f32[96,128]{1,0:T(8,128)S(1)} %slice_bitcast_fusion.2), channel_id=1, source_target_pairs={{0,1},{1,2},{2,3},{3,4},{4,5},{5,6},{6,7},{7,8},{8,9},{9,10},{10,1... | collective-permute-start | bytes 147464 | tf_op jit(solution)/shard_map/ppermute | solution.py:512
  19.1 223.5 %all-gather.5.cloned.1.call-start = ((), (), s32[]{:S(2)}) async-start(), calls=%async_computation.7 | async-start | bytes 11796480 | tf_op jit(solution)/shard_map/all_gather | solution.py:539
  19.2 5.2 copy-start.11
  19.2 10.0 %copy-start.6 = (bf16[1,197,768]{2,1,0:T(8,128)(2,1)S(1)}, bf16[1,197,768]{2,1,0:T(8,128)(2,1)}, u32[]{:S(2)}) copy-start(bf16[1,197,768]{2,1,0:T(8,128)(2,1)} %param.10) | copy-start | bytes 907780
  19.2 10.8 %copy-start.7 = (bf16[1,197,768]{2,1,0:T(8,128)(2,1)S(1)}, bf16[1,197,768]{2,1,0:T(8,128)(2,1)}, u32[]{:S(2)}) copy-start(bf16[1,197,768]{2,1,0:T(8,128)(2,1)} %param.11) | copy-start | bytes 907780
  197.7 45.0 %all-to-all-start.1 = ((bf16[8,56,768]{2,1,0:T(8,128)(2,1)}), bf16[8,56,768]{2,1,0:T(8,128)(2,1)S(1)}, u32[]{:S(2)}, u32[]{:S(2)}) async-start(bf16[8,56,768]{2,1,0:T(8,128)(2,1)} %bitcast.87), calls=%async_computation.1 | async-start | bytes 1376256 | tf_op jit(solution)/shard_map/all_to_all | solution.py:649
  243.5 41.6 %copy-start.8 = (s32[197,2]{1,0:T(8,128)S(1)}, s32[197,2]{1,0:T(8,128)}, u32[]{:S(2)}) copy-start(s32[197,2]{1,0:T(8,128)} %get-tuple-element.64) | copy-start | bytes 4732
  281.5 22.3 %all-to-all-start.3 = ((bf16[8,56,768]{2,1,0:T(8,128)(2,1)}), bf16[8,56,768]{2,1,0:T(8,128)(2,1)S(1)}, u32[]{:S(2)}, u32[]{:S(2)}) async-start(bf16[8,56,768]{2,1,0:T(8,128)(2,1)} %bitcast.86), calls=%async_computation.3 | async-start | bytes 1376256 | tf_op jit(solution)/shard_map/all_to_all | solution.py:649
  285.0 293.9 %reduce-scatter.3.cloned.1.call-start = ((), (), s32[]{:S(2)}) async-start(), calls=%async_computation.8 | async-start | bytes 19464192 | tf_op jit(solution)/shard_map/reduce_scatter | solution.py:735
  374.1 301.7 %reduce-scatter.5.cloned.1.call-start = ((), (), s32[]{:S(2)}) async-start(), calls=%async_computation.9 | async-start | bytes 11796480 | tf_op jit(solution)/shard_map/reduce_scatter | solution.py:706
  386.0 309.4 %copy-start.4 = (f32[208,768]{1,0:T(8,128)S(1)}, f32[208,768]{1,0:T(8,128)}, u32[]{:S(2)}) copy-start(f32[208,768]{1,0:T(8,128)} %get-tuple-element.88) | copy-start | bytes 1916932
  386.0 312.1 %copy-start.3 = (f32[208,768]{1,0:T(8,128)S(1)}, f32[208,768]{1,0:T(8,128)}, u32[]{:S(2)}) copy-start(f32[208,768]{1,0:T(8,128)} %get-tuple-element.72) | copy-start | bytes 1916932
  387.4 1.3 collective-permute-start.1
  388.7 4.1 collective-permute-start.2
  392.8 5.1 collective-permute-start.3
  397.9 4.2 collective-permute-start.4
  402.0 279.1 %collective-permute-start.5 = (f32[96,128]{1,0:T(8,128)S(1)}, f32[96,128]{1,0:T(8,128)S(1)}, u32[]{:S(2)}, u32[]{:S(2)}) collective-permute-start(f32[96,128]{1,0:T(8,128)S(1)} %add.59), channel_id=1, source_target_pairs={{0,16},{8,24},{16,0},{24,8},{1,17},{9,25},{17,1},{25,9},{2,18},{10... | collective-permute-start | bytes 147464 | tf_op jit(solution)/shard_map/ppermute | solution.py:465
  581.9 99.2 %collective-permute-start.6 = (f32[96,128]{1,0:T(8,128)S(1)}, f32[96,128]{1,0:T(8,128)S(1)}, u32[]{:S(2)}, u32[]{:S(2)}) collective-permute-start(f32[96,128]{1,0:T(8,128)S(1)} %slice.76), channel_id=1, source_target_pairs={{1,0},{2,1},{3,2},{4,3},{5,4},{6,5},{7,6},{8,7},{9,8},{10,9},{11,1... | collective-permute-start | bytes 147464 | tf_op jit(solution)/shard_map/ppermute | solution.py:755
  684.9 1.1 collective-permute-start.7
  686.0 3.5 collective-permute-start.8
  689.5 4.4 collective-permute-start.9
  694.0 3.5 collective-permute-start.10
  697.5 4.1 collective-permute-start.11
  (10 other events, 15.0 us)
Sparse Core Ops, SparseCore 0:
  19.3 126.4 all-gather.2
  148.1 94.4 all-gather.4
  374.2 204.6 reduce-scatter.2
  581.9 93.9 reduce-scatter.4

commit v2 on v1

--- a/solution.py
+++ b/solution.py
@@ -71,14 +71,14 @@
 
 
 def to_rows(read, write, first_q, rows, wide, tiles):
-    if wide:
-        quarter = rows // 4
-        for q in range(4):
-            for j in range(tiles):
-                write(q * quarter, quarter, j, read(first_q + tiles * q + j, quarter, 4 * tiles))
-    else:
+    blocks = 4 if rows % 64 == 0 else 1
+    count = rows // blocks
+    for b in range(blocks):
         for j in range(tiles):
-            write(0, rows, j, read(first_q + j, rows, tiles))
+            if wide:
+                write(b * count, count, j, read(first_q + tiles * b + j, count, 4 * tiles))
+            else:
+                write(b * count, count, j, read(first_q + tiles * count * b + j, count, tiles))
 
 
 def pack_dense_kernel(dims, k_ref, tail_ref, own_ref, out_ref, buf):
@@ -97,9 +97,11 @@
 
     wide = (k >= chunks // 2) & (k < 3 * chunks // 4) & wide_ok
 
-    @pl.when(wide)
-    def _():
-        to_rows(read, write, start, rows, True, tiles)
+    if wide_ok:
+
+        @pl.when(wide)
+        def _():
+            to_rows(read, write, start, rows, True, tiles)
 
     @pl.when(jnp.logical_not(wide))
     def _():
@@ -109,14 +111,16 @@
         write(rows, tail_rows, j, read(own + j, tail_rows, tiles))
 
 
-def pack_expert_kernel(dims, wide_ref, own_ref, out_ref):
+def pack_expert_kernel(dims, wide_ref, own_ref, *out_refs):
     rows, tiles = dims
+    half = rows // 2
 
     def read(first, count, stride):
         return own_ref[pl.ds(first, count, stride=stride), :]
 
     def write(first, count, j, value):
-        out_ref[first : first + count, LANES * j : LANES * (j + 1)] = value.astype(bf16)
+        at = first % half
+        out_refs[first // half][at : at + count, LANES * j : LANES * (j + 1)] = value.astype(bf16)
 
     wide = wide_ref[0] > 0
 
@@ -129,8 +133,13 @@
         to_rows(read, write, 0, rows, False, tiles)
 
 
-def unpack_kernel(dims, wide_ref, rows_ref, out_ref, square_ref):
+def unpack_kernel(dims, wide_ref, *refs):
     rows, tiles = dims
+    piece_refs, (out_ref, square_ref, rows_ref) = refs[:-3], refs[-3:]
+    at = 0
+    for ref in piece_refs:
+        rows_ref[at : at + ref.shape[0]] = ref[...].astype(f32)
+        at += ref.shape[0]
     wide = wide_ref[0] > 0
 
     def store(is_wide):
@@ -138,7 +147,7 @@
         quarter = rows // 4
         for q in range(4):
             for j in range(tiles):
-                piece = rows_ref[q * quarter : (q + 1) * quarter, LANES * j : LANES * (j + 1)].astype(f32)
+                piece = rows_ref[q * quarter : (q + 1) * quarter, LANES * j : LANES * (j + 1)]
                 if is_wide:
                     out_ref[pl.ds(tiles * q + j, quarter, stride=4 * tiles), :] = piece
                 else:
@@ -192,11 +201,11 @@
     )(clip, grad, momentum, variance)
 
 
-def route_kernel(experts, capacity, stride, prio_row, prio_col, picks, picks_t, cols_ref, rows_ref):
-    seq = picks.shape[0]
+def route_kernel(experts, capacity, stride, prio_row, prio_col, picks, picks_t, cot, cols_ref, rows_ref, g_ref):
+    count = picks.shape[0]
     before = (prio_row[...] < prio_col[...]).astype(f32).astype(bf16)
-    lane = lax.broadcasted_iota(jnp.int32, (seq, experts), 1)
-    sub = lax.broadcasted_iota(jnp.int32, (experts, seq), 0)
+    lane = lax.broadcasted_iota(jnp.int32, (count, experts), 1)
+    sub = lax.broadcasted_iota(jnp.int32, (experts, count), 0)
     hot = [(picks[:, j : j + 1] == lane).astype(f32) for j in range(2)]
     hot_t = [(picks_t[j : j + 1, :] == sub).astype(f32) for j in range(2)]
     first = jnp.sum(hot[0], axis=0, keepdims=True)
@@ -212,6 +221,28 @@
         rows_ref[j : j + 1, :] = jnp.where(
             place_t < capacity, picks_t[j : j + 1, :] * stride + place_t, -1
         )
+    first, second = slot_selects(rows_ref, g_ref.shape[0])
+    g_ref[...] = dot(first + second, cot[...]).astype(bf16)
+
+
+def slot_selects(rows_ref, slots):
+    sub = lax.broadcasted_iota(jnp.int32, (slots, rows_ref.shape[1]), 0)
+    return [(rows_ref[j : j + 1, :] == sub).astype(f32).astype(bf16) for j in range(2)]
+
+
+def token_selects(cols_ref, slots):
+    lane = lax.broadcasted_iota(jnp.int32, (cols_ref.shape[0], slots), 1)
+    return [(cols_ref[:, j : j + 1] == lane).astype(f32).astype(bf16) for j in range(2)]
+
+
+def split_lanes(column):
+    high = column.astype(bf16).astype(f32)
+    rest = column - high
+    middle = rest.astype(bf16).astype(f32)
+    low = rest - middle
+    lane = lax.broadcasted_iota(jnp.int32, (column.shape[0], LANES), 1)
+    wide = jnp.where(lane == 0, high, jnp.where(lane == 1, middle, jnp.where(lane == 2, low, 0.0)))
+    return wide.astype(bf16)
 
 
 def head_masks():
@@ -226,6 +257,21 @@
     top = jnp.max(scores, axis=-1, keepdims=True)
     raised = jnp.exp(scores - top)
     return raised * (1.0 / jnp.sum(raised, axis=-1, keepdims=True))
+
+
+def put_chunk(scratch, low, chunk, value, first=0):
+    place = chunk ^ low
+    scratch[place & 1, place >> 1, first : first + value.shape[0], :] = value
+
+
+def flush(scratch, keep_ref, send_ref, sems):
+    copies = [
+        pltpu.make_async_copy(scratch.at[i], ref, sems.at[i]) for i, ref in enumerate((keep_ref, send_ref))
+    ]
+    for copy in copies:
+        copy.start()
+    for copy in copies:
+        copy.wait()
 
 
 def matrix(w_ref, index):
@@ -261,15 +307,18 @@
 
 
 def attn_bwd_kernel(
-    seq, grad_ref, stream_ref, gain_ref, w_ref, a_ref, q_ref, k_ref, v_ref, o_ref,
-    out_ref, gain_out, dw_ref, do_ref, dq_ref, dk_ref, dv_ref,
+    seq, low_ref, grad_ref, stream_ref, gain_ref, w_ref, a_ref, q_ref, k_ref, v_ref, o_ref,
+    out_ref, gain_out, keep_ref, send_ref, dw, do_ref, dq_ref, dk_ref, dv_ref, sems,
 ):
     width = grad_ref.shape[1]
     branch = grad_ref[...].astype(bf16)
+    low = low_ref[0]
 
     def put(index, value):
-        per = dw_ref.shape[0] // 4
-        dw_ref[index * per : (index + 1) * per] = value.astype(bf16).reshape(per, width // per, width)
+        rows = dw.shape[2]
+        per = width // rows
+        for i in range(per):
+            put_chunk(dw, low, index * per + i, value[i * rows : (i + 1) * rows].astype(bf16))
 
     do_ref[...] = dot_nt(branch, matrix(w_ref, 3)).astype(bf16)
     put(3, dot_tn(o_ref[...], branch))
@@ -302,6 +351,7 @@
         put(index, dot_tn(a_ref[...], ref[...]))
         part = dot_nt(ref[...], matrix(w_ref, index))
         back = part if back is None else back + part
+    flush(dw, keep_ref, send_ref, sems)
     normed, inverse = norm_rows(stream_ref[...])
     addend, gain_grad = norm_back(back, normed, inverse, gain_ref[...])
     out_ref[...] = grad_ref[...] + addend
@@ -323,26 +373,42 @@
 
 
 def mlp_bwd_kernel(
-    grad_ref, stream_ref, gain_ref, w1_ref, w2_ref, b_ref, u_ref, out_ref, gain_out, dw1_ref, dw2_ref
+    by_core, low_ref, grad_ref, stream_ref, gain_ref, w1_ref, w2_ref, b_ref, u_ref,
+    out_ref, gain_out, keep2_ref, send2_ref, *refs,
 ):
+    if by_core:
+        keep1_ref, send1_ref, dw2, dw1, sems = refs
+    else:
+        dw1_ref, dw2, sems = refs
     width = grad_ref.shape[1]
     upper = grad_ref[...].astype(bf16)
+    low = low_ref[0]
     back = None
     for q in range(4):
         pre = u_ref[:, q * width : (q + 1) * width]
         cdf = normal_cdf(pre)
         act = (pre * cdf).astype(bf16)
-        per = dw2_ref.shape[0] // 4
-        dw2_ref[q * per : (q + 1) * per] = dot_tn(act, upper).astype(bf16).reshape(per, width // per, width)
+        rows = dw2.shape[2]
+        per = width // rows
+        second = dot_tn(act, upper)
+        for i in range(per):
+            put_chunk(dw2, low, q * per + i, second[i * rows : (i + 1) * rows].astype(bf16))
         dact = dot_nt(upper, matrix(w2_ref, q))
         dpre = (dact * (cdf + pre * density(pre))).astype(bf16)
-        groups = dw1_ref.shape[0]
+        first = dot_tn(b_ref[...], dpre).astype(bf16)
+        groups = w1_ref.shape[0]
         rows = width // groups
-        dw1_ref[:, q * rows : (q + 1) * rows, :] = (
-            dot_tn(b_ref[...], dpre).astype(bf16).reshape(groups, rows, width)
-        )
+        for i in range(groups):
+            piece = first[i * rows : (i + 1) * rows]
+            if by_core:
+                put_chunk(dw1, low, i, piece, q * rows)
+            else:
+                dw1_ref[i, q * rows : (q + 1) * rows, :] = piece
         part = dot_nt(dpre, quarter_in(w1_ref, q))
         back = part if back is None else back + part
+    flush(dw2, keep2_ref, send2_ref, sems)
+    if by_core:
+        flush(dw1, keep1_ref, send1_ref, sems)
     normed, inverse = norm_rows(stream_ref[...])
     addend, gain_grad = norm_back(back, normed, inverse, gain_ref[...])
     out_ref[...] = grad_ref[...] + addend
@@ -359,41 +425,75 @@
     return raised / jnp.sum(raised, axis=-1, keepdims=True)
 
 
-def dispatch_kernel(
-    slots, stream_ref, gain_ref, wr_ref, picks_ref, rows_ref, cot_ref, c_ref, probs_ref, x_ref, dy_ref
-):
-    count = stream_ref.shape[0]
+def dispatch_kernel(stream_ref, gain_ref, wr_ref, picks_ref, rows_ref, c_ref, probs_ref, x_ref):
+    width = stream_ref.shape[1]
     experts = wr_ref.shape[1]
     normed, _ = norm_rows(stream_ref[...])
     c_ref[...] = (normed * gain_ref[...]).astype(bf16)
     probs = softmax_rows(dot(c_ref[...], wr_ref[...]))
     probs_ref[...] = probs
     hots = pick_hots(picks_ref, experts)
-    sub = lax.broadcasted_iota(jnp.int32, (slots, count), 0)
-    chosen = None
-    dy = None
+    selects = slot_selects(rows_ref, x_ref.shape[0])
+    gates = None
     for j in range(2):
-        gate = jnp.sum(probs * hots[j], axis=-1, keepdims=True)
-        select = (rows_ref[j : j + 1, :] == sub).astype(f32).astype(bf16)
-        chosen = select if chosen is None else chosen + select
-        part = dot(select, (gate * cot_ref[...]).astype(bf16))
-        dy = part if dy is None else dy + part
-    x_ref[...] = dot(chosen, c_ref[...]).astype(bf16)
-    dy_ref[...] = dy.astype(bf16)
-
-
-def expert_kernel(x_ref, dy_ref, u1_ref, u2_ref, y_ref, dx_ref, act_ref, dpre_ref, y_sum, dx_sum):
+        part = dot(selects[j], split_lanes(jnp.sum(probs * hots[j], axis=-1, keepdims=True)))
+        gates = part if gates is None else gates + part
+    x_ref[:, 0:width] = dot(selects[0] + selects[1], c_ref[...]).astype(bf16)
+    x_ref[:, width:] = gates.astype(bf16)
+
+
+def add_lanes(wide):
+    wide = wide.astype(f32)
+    return wide[:, 0:1] + wide[:, 1:2] + wide[:, 2:3]
+
+
+def expert_kernel(dims, dp_ref, x_ref, g_ref, *refs):
+    parts, quarter = dims
+    weight_refs, refs = refs[: 2 * parts], refs[2 * parts :]
+    y_ref, dx_ref, dy_ref, act_ref, dpre_ref, weights, y_sum, dx_sum, sems = refs
     q = pl.program_id(0)
-    width = x_ref.shape[1]
-    first = u1_ref[...].reshape(width, width)
-    pre = dot(x_ref[...], first)
+    width = g_ref.shape[1]
+    half = parts // 2
+    rows = weights.shape[1] // 2
+    me = dp_ref[0]
+
+    def copies(side):
+        return [
+            pltpu.make_async_copy(
+                weight_refs[side * parts + r],
+                weights.at[r ^ me, side * rows : (side + 1) * rows],
+                sems.at[side * parts + r],
+            )
+            for r in range(parts)
+        ]
+
+    @pl.when(q == 0)
+    def _():
+        for side in range(2):
+            for copy in copies(side):
+                copy.start()
+        dy_ref[...] = (add_lanes(x_ref[:, width:]) * g_ref[...].astype(f32)).astype(bf16)
+        for side in range(2):
+            for copy in copies(side):
+                copy.wait()
+
+    first = weights[0:half, pl.ds(pl.multiple_of(q * quarter, 16), quarter), :].reshape(width, width)
+    if 4 * quarter >= width:
+        per = 4 * quarter // width
+        at = pl.ds(pl.multiple_of(lax.rem(q, per) * width, 16), width)
+        second = weights[half + q // per, at, :]
+    else:
+        per = width // (4 * quarter)
+        second = weights[pl.ds(half + q * per, per)].reshape(width, width)
+    x = x_ref[:, 0:width]
+    pre = dot(x, first)
     cdf = normal_cdf(pre)
     act = (pre * cdf).astype(bf16)
     act_ref[...] = act
-    dact = dot_nt(dy_ref[...], u2_ref[...])
+    dact = dot_nt(dy_ref[...], second)
     dpre = (dact * (cdf + pre * density(pre))).astype(bf16)
     dpre_ref[...] = dpre
-    y_part = dot(act, u2_ref[...])
+    y_part = dot(act, second)
     dx_part = dot_nt(dpre, first)
 
     @pl.when(q == 0)
@@ -408,63 +508,137 @@
 
     @pl.when(q == pl.num_programs(0) - 1)
     def _():
-        y_ref[...] = y_sum[...].astype(bf16)
-        dx_ref[...] = dx_sum[...].astype(bf16)
-
-
-def expert_grad_kernel(x_ref, dy_ref, act_ref, dpre_ref, out_ref):
+        y = y_sum[...].astype(bf16)
+        y_ref[...] = y
+        dx_ref[:, 0:width] = dx_sum[...].astype(bf16)
+        gate_grad = jnp.sum(g_ref[...].astype(f32) * y.astype(f32), axis=-1, keepdims=True)
+        dx_ref[:, width:] = split_lanes(gate_grad)
+
+
+def expert_grad_kernel(dims, dp_ref, x_ref, dy_ref, act_ref, dpre_ref, *refs):
+    parts, quarter = dims
+    out_refs, scratch, sems = refs[:4], refs[4], refs[5]
     q = pl.program_id(0)
-    groups, _, rows, width = out_ref.shape
-    half = groups // 2
-    out_ref[0:half, q] = dot_tn(x_ref[...], dpre_ref[...]).astype(bf16).reshape(half, rows, width)
+    me = dp_ref[0]
+    width = dy_ref.shape[1]
+    half = parts // 2
+    rows = scratch.shape[1]
+    first = dot_tn(x_ref[:, 0:width], dpre_ref[...]).astype(bf16)
+    count = width // half
+    for i in range(half):
+        at = pl.ds(pl.multiple_of(q * quarter, 16), quarter)
+        scratch[i ^ me, at, :] = first[i * count : (i + 1) * count]
     second = dot_tn(act_ref[...], dy_ref[...]).astype(bf16)
-    per = width // rows
-    for part in range(per):
-        flat = q * per + part
-        out_ref[half + flat // 4, flat % 4] = second[part * rows : (part + 1) * rows]
+    if rows >= width:
+        per = rows // width
+        at = pl.ds(pl.multiple_of(lax.rem(q, per) * width, 16), width)
+        scratch[(half + q // per) ^ me, at, :] = second
+    else:
+        per = width // rows
+        for i in range(per):
+            scratch[(half + q * per + i) ^ me] = second[i * rows : (i + 1) * rows]
+
+    @pl.when(q == pl.num_programs(0) - 1)
+    def _():
+        copies = []
+        for side, bit in ((0, 1), (1, parts // 2)):
+            lists = [r for r in range(parts) if r & bit], [r for r in range(parts) if not r & bit]
+            for which, group in enumerate(lists):
+                for i, r in enumerate(group):
+                    copies.append(
+                        pltpu.make_async_copy(
+                            scratch.at[r, side * rows // 2 : (side + 1) * rows // 2],
+                            out_refs[2 * side + which].at[i],
+                            sems.at[side * parts + r],
+                        )
+                    )
+        for copy in copies:
+            copy.start()
+        for copy in copies:
+            copy.wait()
 
 
 def combine_kernel(
-    stream_ref, gain_ref, wr_ref, picks_ref, cols_ref, cot_ref, c_ref, probs_ref, y_ref, dx_ref,
-    out_ref, grad_ref, gain_out, router_out,
+    stream_ref, gain_ref, wr_ref, picks_ref, cols_ref, cot_ref, c_ref, probs_ref, dx_ref,
+    grad_ref, gain_out, router_out,
 ):
-    count = stream_ref.shape[0]
-    slots = y_ref.shape[0]
+    width = stream_ref.shape[1]
     experts = wr_ref.shape[1]
     probs = probs_ref[...]
     hots = pick_hots(picks_ref, experts)
-    lane = lax.broadcasted_iota(jnp.int32, (count, slots), 1)
-    cot = cot_ref[...]
-    total = stream_ref[...]
-    chosen = None
+    selects = token_selects(cols_ref, dx_ref.shape[0])
     prob_grad = None
     for j in range(2):
-        select = (cols_ref[:, j : j + 1] == lane).astype(f32).astype(bf16)
-        chosen = select if chosen is None else chosen + select
-        pair_out = dot(select, y_ref[...])
-        gate = jnp.sum(probs * hots[j], axis=-1, keepdims=True)
-        total = total + gate * pair_out
-        part = jnp.sum(cot * pair_out, axis=-1, keepdims=True) * hots[j]
+        part = add_lanes(dot(selects[j], dx_ref[:, width:])) * hots[j]
         prob_grad = part if prob_grad is None else prob_grad + part
-    out_ref[...] = total
     logit_grad = probs * (prob_grad - jnp.sum(prob_grad * probs, axis=-1, keepdims=True))
     logit_grad = logit_grad.astype(bf16)
     router_out[...] = dot_tn(c_ref[...], logit_grad)
-    back = dot(chosen, dx_ref[...]) + dot_nt(logit_grad, wr_ref[...])
+    back = dot(selects[0] + selects[1], dx_ref[:, 0:width]) + dot_nt(logit_grad, wr_ref[...])
     normed, inverse = norm_rows(stream_ref[...])
     addend, gain_grad = norm_back(back, normed, inverse, gain_ref[...])
-    grad_ref[...] = cot + addend
+    grad_ref[...] = cot_ref[...].astype(f32) + addend
     gain_out[...] = gain_grad
 
 
-def all_sum(value, axes):
+def output_kernel(stream_ref, picks_ref, cols_ref, probs_ref, y_ref, out_ref):
+    seq = out_ref.shape[0]
+    probs = probs_ref[...]
+    hots = pick_hots(picks_ref, probs.shape[1])
+    selects = token_selects(cols_ref, y_ref.shape[0])
+    total = stream_ref[...]
+    for j in range(2):
+        gate = jnp.sum(probs * hots[j], axis=-1, keepdims=True)
+        total = total + gate * dot(selects[j], y_ref[...])
+    out_ref[...] = total[0:seq]
+
+
+def swap(value, axes, bit):
+    size = 1
     for axis in axes:
-        size = lax.axis_size(axis)
-        hop = 1
-        while hop < size:
-            value = value + lax.ppermute(value, axis, [(i, i ^ hop) for i in range(size)])
-            hop *= 2
+        size *= lax.axis_size(axis)
+    return lax.ppermute(value, axes, [(i, i ^ (1 << bit)) for i in range(size)])
+
+
+def all_sum(value, axes, bits):
+    for bit in range(bits):
+        value = value + swap(value, axes, bit)
     return value
+
+
+def gather_parts(value, axes, order):
+    parts = {0: value}
+    for bit in order:
+        parts.update({at | (1 << bit): swap(part, axes, bit) for at, part in list(parts.items())})
+    return [parts[at] for at in sorted(parts)]
+
+
+def reduce_low(value, axes, bits):
+    for bit in bits:
+        pairs = value.reshape((value.shape[0] // 2, 2) + value.shape[1:])
+        value = pairs[:, 0] + swap(pairs[:, 1], axes, bit)
+    return value[0]
+
+
+def reduce_high(value, axes, bits):
+    for bit in reversed(bits):
+        pairs = value.reshape((2, value.shape[0] // 2) + value.shape[1:])
+        value = pairs[0] + swap(pairs[1], axes, bit)
+    return value[0]
+
+
+def reduce_layers(layers, axes, bits, me, low_first):
+    grid = [[layers[0], layers[1]], [layers[2], layers[3]]]
+    if not low_first:
+        grid = [list(column) for column in zip(*grid)]
+    first, second = (bits[0], bits[1]) if low_first else (bits[1], bits[0])
+    own = (me >> first) & 1
+    keep = [jnp.where(own == 0, row[0], row[1]) for row in grid]
+    send = [jnp.where(own == 0, row[1], row[0]) for row in grid]
+    arrived = swap(jnp.stack(send), axes, first)
+    sums = [keep[i] + arrived[i] for i in range(2)]
+    own = (me >> second) & 1
+    return jnp.where(own == 0, sums[0], sums[1]) + swap(jnp.where(own == 0, sums[1], sums[0]), axes, second)
 
 
 def shape(dims, dtype=f32):
@@ -491,9 +665,14 @@
     experts = local_experts * expert_ranks
     images, seq, width = tokens.shape
     assert local_experts == 1 and images == 1
+    assert devices & (devices - 1) == 0 and dp_ranks >= 4
     tiles = width // LANES
-    me = lax.axis_index("dp") * expert_ranks + lax.axis_index("expert")
-    me_arr = me.reshape(1).astype(jnp.int32)
+    dp_me = lax.axis_index("dp").astype(jnp.int32)
+    me = dp_me * expert_ranks + lax.axis_index("expert").astype(jnp.int32)
+    me_arr = me.reshape(1)
+    dp_arr = dp_me.reshape(1)
+    dp_bits = dp_ranks.bit_length() - 1
+    all_bits = devices.bit_length() - 1
 
     own = dense_master.shape[0] // LANES
     expert_flat = expert_master.shape[1] // LANES
@@ -526,37 +705,52 @@
     gathered = lax.all_gather(chunk, both, axis=0, tiled=True)
     gathered = gathered.reshape(devices, rows + tail_rows, width)
 
-    expert_wide = (lax.axis_index("dp") < dp_ranks // 2).astype(jnp.int32).reshape(1)
-    expert_chunk = pl.pallas_call(
+    expert_wide = (dp_me < dp_ranks // 2).astype(jnp.int32).reshape(1)
+    half_shape = shape((expert_rows // 2, width), bf16)
+    halves = pl.pallas_call(
         functools.partial(pack_expert_kernel, (expert_rows, tiles)),
         in_specs=[SMEM, VMEM],
-        out_specs=VMEM,
-        out_shape=shape((expert_rows, width), bf16),
+        out_specs=[VMEM, VMEM],
+        out_shape=[half_shape, half_shape],
         compiler_params=params(),
         cost_estimate=cost(0, 6 * expert_master.size),
         name="pack_expert",
     )(expert_wide, expert_master.reshape(expert_flat, LANES))
-    expert_all = lax.all_gather(expert_chunk, "dp", axis=0, tiled=True)
+    dp_axis = ("dp",)
+    dp_order = list(range(dp_bits))
+    expert_parts = gather_parts(halves[0], dp_axis, dp_order)
+    expert_parts += gather_parts(halves[1], dp_axis, dp_order[::-1])
 
     capacity = 2 * seq // experts
     stride = -(-capacity // 8) * 8
     slots = experts * stride
     padded = -(-seq // 16) * 16
-    cols, rows_slots = pl.pallas_call(
+    fill = padded - seq
+    ranks = jnp.pad(priority, ((0, 0), (0, fill)), constant_values=1 << 20)
+    picks = jnp.pad(expert_picks, ((0, fill), (0, 0)), constant_values=-1)
+    cot = jnp.pad(cotangent.reshape(seq, width), ((0, fill), (0, 0)))
+    stream = jnp.pad(tokens.reshape(seq, width).astype(f32), ((0, fill), (0, 0)))
+    cols, rows_slots, outgoing_cot = pl.pallas_call(
         functools.partial(route_kernel, experts, capacity, stride),
-        in_specs=[VMEM] * 4,
-        out_specs=[VMEM] * 2,
-        out_shape=[shape((seq, 2), jnp.int32), shape((2, seq), jnp.int32)],
+        in_specs=[VMEM] * 5,
+        out_specs=[VMEM] * 3,
+        out_shape=[
+            shape((padded, 2), jnp.int32),
+            shape((2, padded), jnp.int32),
+            shape((slots, width), bf16),
+        ],
         compiler_params=params(),
-        cost_estimate=cost(2e6, 1e5),
+        cost_estimate=cost(2 * padded * slots * width, 1e6),
         name="route",
-    )(priority, priority.reshape(seq, 1), expert_picks, expert_picks.T)
-    fill = padded - seq
-    cols = jnp.pad(cols, ((0, fill), (0, 0)), constant_values=-1)
-    rows_slots = jnp.pad(rows_slots, ((0, 0), (0, fill)), constant_values=-1)
-    picks = jnp.pad(expert_picks, ((0, fill), (0, 0)))
-    stream = jnp.pad(tokens.reshape(seq, width).astype(f32), ((0, fill), (0, 0)))
-    cot = jnp.pad(cotangent.reshape(seq, width).astype(f32), ((0, fill), (0, 0)))
+    )(ranks, ranks.reshape(padded, 1), picks, picks.T, cot)
+
+    def exchange(value):
+        dims = value.shape
+        value = value.reshape(expert_ranks, slots // expert_ranks, dims[1])
+        value = lax.all_to_all(value, "expert", split_axis=0, concat_axis=0, tiled=True)
+        return value.reshape(dims)
+
+    arriving_cot = exchange(outgoing_cot)
 
     tail_flat = gathered[devices - 1, rows:, :].reshape(-1)
     router = tail_flat[: width * experts].reshape(width, experts)
@@ -565,38 +759,41 @@
 
     per = devices // 4
     dense_block = (per, rows + tail_rows, width)
+    low = me & (per - 1)
+    low_arr = low.reshape(1)
 
     def layer_spec(index):
         return pl.BlockSpec(dense_block, lambda *_: (index, 0, 0), pipeline_mode=pl.Buffered(1))
 
     if wide_ok:
-        first_in, first_spec, first_shape = gathered, layer_spec(2), (per, rows, width)
+        first_in, first_spec = gathered, layer_spec(2)
     else:
         first_in = gathered[2 * per : 3 * per, :rows].reshape(width, 4, width)
         first_in = first_in.transpose(1, 0, 2).reshape(1, 4 * width, width)
-        first_spec, first_shape = VMEM, (1, 4 * width, width)
+        first_spec = None
 
     act_shape = shape((padded, width), bf16)
     stream_shape = shape((padded, width), f32)
     gain_shape = shape((1, width), f32)
     tok_flops = 2 * padded * width * width
     weight_bytes = 2 * width * width
-
-    def call(kernel, ins, in_specs, outs, name, flops, nbytes, trans=0, scratch=()):
-        whole = [pl.BlockSpec(a.shape, lambda *_, n=len(a.shape): (0,) * n) for a in outs]
-        specs = [
-            s if s is not None else pl.BlockSpec(a.shape, lambda *_, n=a.ndim: (0,) * n)
-            for a, s in zip(ins, in_specs, strict=True)
-        ]
+    ANY = pl.BlockSpec(memory_space=pl.ANY)
+
+    def call(kernel, ins, in_specs, outs, name, flops, nbytes, out_specs=None, scratch=()):
+        out_specs = out_specs or [None] * len(outs)
+
+        def whole(a):
+            return pl.BlockSpec(a.shape, lambda *_, n=len(a.shape): (0,) * n)
+
         return pl.pallas_call(
             kernel,
             grid=(1,),
-            in_specs=specs,
-            out_specs=whole,
+            in_specs=[s or whole(a) for a, s in zip(ins, in_specs, strict=True)],
+            out_specs=[s or whole(a) for a, s in zip(outs, out_specs, strict=True)],
             out_shape=outs,
             scratch_shapes=list(scratch),
             compiler_params=params(),
-            cost_estimate=cost(flops, nbytes, trans),
+            cost_estimate=cost(flops, nbytes),
             name=name,
         )(*ins)
 
@@ -611,16 +808,21 @@
             4 * weight_bytes,
         )
 
+    core_shape = shape((per // 2, rows, width), bf16)
+    by_core = pltpu.VMEM((2, per // 2, rows, width), bf16)
+    two_sems = pltpu.SemaphoreType.DMA((2,))
+
     def attn_bwd(grad, value, kept, layer, which):
         return call(
             functools.partial(attn_bwd_kernel, seq),
-            (grad, value, gain[which], gathered, *kept),
-            (None, None, None, layer_spec(layer)) + (None,) * 5,
-            [stream_shape, gain_shape, shape((per, rows, width), bf16)],
+            (low_arr, grad, value, gain[which], gathered, *kept),
+            (SMEM, None, None, None, layer_spec(layer)) + (None,) * 5,
+            [stream_shape, gain_shape, core_shape, core_shape],
             "attn_bwd",
             11 * tok_flops,
             8 * weight_bytes,
-            scratch=[pltpu.VMEM((padded, width), bf16)] * 4,
+            out_specs=[None, None, ANY, ANY],
+            scratch=[by_core] + [pltpu.VMEM((padded, width), bf16)] * 4 + [two_sems],
         )
 
     stream_one, *kept_one = attn_fwd(stream, 0, 0)
@@ -634,124 +836,154 @@
         8 * weight_bytes,
     )
     stream_three, *kept_two = attn_fwd(stream_two, 1, 2)
-    moe_in, probs, outgoing, outgoing_grad = call(
-        functools.partial(dispatch_kernel, slots),
-        (stream_three, gain[3], router, picks, rows_slots, cot),
-        (None,) * 6,
-        [act_shape, shape((padded, experts)), shape((slots, width), bf16), shape((slots, width), bf16)],
+    moe_in, probs, outgoing = call(
+        dispatch_kernel,
+        (stream_three, gain[3], router, picks, rows_slots),
+        (None,) * 5,
+        [act_shape, shape((padded, experts)), shape((slots, width + LANES), bf16)],
         "dispatch",
-        3 * 2 * padded * slots * width,
+        2 * padded * slots * width,
         4e6,
     )
-
-    def exchange(value):
-        value = value.reshape(expert_ranks, slots // expert_ranks, width)
-        value = lax.all_to_all(value, "expert", split_axis=0, concat_axis=0, tiled=True)
-        return value.reshape(slots, width)
-
     arriving = exchange(outgoing)
-    arriving_grad = exchange(outgoing_grad)
 
     quarter = expert_rows // 4
-    half = dp_ranks // 2
     expert_flops = 2 * slots * width * width
-    expert_out, input_back, expert_act, pre_grad = pl.pallas_call(
-        expert_kernel,
+    slot_spec = pl.BlockSpec((slots, width), lambda q: (0, 0))
+    wide_spec = pl.BlockSpec((slots, width + LANES), lambda q: (0, 0))
+    hidden_spec = pl.BlockSpec((slots, width), lambda q: (0, q))
+    expert_out, input_back, slot_grad, expert_act, pre_grad = pl.pallas_call(
+        functools.partial(expert_kernel, (dp_ranks, quarter)),
         grid=(4,),
-        in_specs=[
-            pl.BlockSpec((slots, width), lambda q: (0, 0)),
-            pl.BlockSpec((slots, width), lambda q: (0, 0)),
-            pl.BlockSpec((half, 1, quarter, width), lambda q: (0, q, 0, 0)),
-            pl.BlockSpec((width, width), lambda q: (4 + q, 0)),
-        ],
-        out_specs=[
-            pl.BlockSpec((slots, width), lambda q: (0, 0)),
-            pl.BlockSpec((slots, width), lambda q: (0, 0)),
-            pl.BlockSpec((slots, width), lambda q: (0, q)),
-            pl.BlockSpec((slots, width), lambda q: (0, q)),
-        ],
+        in_specs=[SMEM, wide_spec, slot_spec] + [ANY] * (2 * dp_ranks),
+        out_specs=[slot_spec, wide_spec, slot_spec, hidden_spec, hidden_spec],
         out_shape=[
             shape((slots, width), bf16),
+            shape((slots, width + LANES), bf16),
             shape((slots, width), bf16),
             shape((slots, hidden), bf16),
             shape((slots, hidden), bf16),
         ],
-        scratch_shapes=[pltpu.VMEM((slots, width), f32)] * 2,
+        scratch_shapes=[
+            pltpu.VMEM((dp_ranks, expert_rows, width), bf16),
+            pltpu.VMEM((slots, width), f32),
+            pltpu.VMEM((slots, width), f32),
+            pltpu.SemaphoreType.DMA((2 * dp_ranks,)),
+        ],
         compiler_params=params(),
         cost_estimate=cost(16 * expert_flops, 8 * weight_bytes),
         name="expert",
-    )(
-        arriving,
-        arriving_grad,
-        expert_all.reshape(dp_ranks, 4, quarter, width),
-        expert_all,
-    )
-    returned = exchange(expert_out)
+    )(dp_arr, arriving, arriving_cot, *expert_parts)
     returned_grad = exchange(input_back)
-    expert_local = pl.pallas_call(
-        expert_grad_kernel,
+    part_shape = shape((dp_ranks // 2, expert_rows // 2, width), bf16)
+    expert_parts = pl.pallas_call(
+        functools.partial(expert_grad_kernel, (dp_ranks, quarter)),
         grid=(4,),
-        in_specs=[
-            pl.BlockSpec((slots, width), lambda q: (0, 0)),
-            pl.BlockSpec((slots, width), lambda q: (0, 0)),
-            pl.BlockSpec((slots, width), lambda q: (0, q)),
-            pl.BlockSpec((slots, width), lambda q: (0, q)),
+        in_specs=[SMEM, wide_spec, slot_spec, hidden_spec, hidden_spec],
+        out_specs=[ANY] * 4,
+        out_shape=[part_shape] * 4,
+        scratch_shapes=[
+            pltpu.VMEM((dp_ranks, expert_rows, width), bf16),
+            pltpu.SemaphoreType.DMA((2 * dp_ranks,)),
         ],
-        out_specs=pl.BlockSpec((dp_ranks, 4, quarter, width), lambda q: (0, 0, 0, 0)),
-        out_shape=shape((dp_ranks, 4, quarter, width), bf16),
         compiler_params=params(),
         cost_estimate=cost(8 * expert_flops, 8 * weight_bytes),
         name="expert_grad",
-    )(arriving, arriving_grad, expert_act, pre_grad)
-    expert_sum = lax.psum_scatter(
-        expert_local.reshape(dp_ranks * expert_rows, width), "dp", scatter_dimension=0, tiled=True
+    )(dp_arr, arriving, slot_grad, expert_act, pre_grad)
+    expert_first = expert_parts[1] + swap(expert_parts[0], dp_axis, 0)
+    expert_second = expert_parts[3] + swap(expert_parts[2], dp_axis, dp_bits - 1)
+    expert_sums = (
+        reduce_low(expert_first, dp_axis, dp_order[1:]),
+        reduce_high(expert_second, dp_axis, dp_order[:-1]),
     )
 
-    output, grad, gain_four, router_grad = call(
+    grad, gain_four, router_grad = call(
         combine_kernel,
-        (stream_three, gain[3], router, picks, cols, cot, moe_in, probs, returned, returned_grad),
-        (None,) * 10,
-        [stream_shape, stream_shape, gain_shape, shape((width, experts))],
+        (stream_three, gain[3], router, picks, cols, cot, moe_in, probs, returned_grad),
+        (None,) * 9,
+        [stream_shape, gain_shape, shape((width, experts))],
         "combine",
-        3 * 2 * padded * slots * width,
+        2 * padded * slots * width,
         6e6,
     )
-    grad, gain_three, second_dw = attn_bwd(grad, stream_two, kept_two, 1, 2)
-    grad, gain_two, first_dw1, second_dw2 = call(
-        mlp_bwd_kernel,
-        (grad, stream_one, gain[1], first_in, gathered, mlp_in, mlp_pre),
-        (None, None, None, first_spec, layer_spec(3), None, None),
-        [stream_shape, gain_shape, shape(first_shape, bf16), shape((per, rows, width), bf16)],
+    grad, gain_three, *second_dw = attn_bwd(grad, stream_two, kept_two, 1, 2)
+    mlp_out = [core_shape, core_shape]
+    mlp_scratch = [by_core]
+    if wide_ok:
+        mlp_out, mlp_scratch = mlp_out * 2, mlp_scratch * 2
+    else:
+        mlp_out = mlp_out + [shape((1, 4 * width, width), bf16)]
+    grad, gain_two, *mlp_dw = call(
+        functools.partial(mlp_bwd_kernel, wide_ok),
+        (low_arr, grad, stream_one, gain[1], first_in, gathered, mlp_in, mlp_pre),
+        (SMEM, None, None, None, first_spec, layer_spec(3), None, None),
+        [stream_shape, gain_shape] + mlp_out,
         "mlp_bwd",
         16 * tok_flops,
         16 * weight_bytes,
+        out_specs=[None, None] + [ANY if len(o.shape) == 3 and o.shape == core_shape.shape else None for o in mlp_out],
+        scratch=mlp_scratch + [two_sems],
     )
-    grad, gain_one, first_dw = attn_bwd(grad, stream, kept_one, 0, 0)
     if not wide_ok:
-        first_dw1 = first_dw1.reshape(4, width, width).transpose(1, 0, 2)
-    dense_local = jnp.concatenate(
-        [part.reshape(-1, width) for part in (first_dw, second_dw, first_dw1, second_dw2)], axis=0
-    )
-    dense_sum = lax.psum_scatter(dense_local, both, scatter_dimension=0, tiled=True)
+        wide_grad = mlp_dw[2].reshape(4, width, width).transpose(1, 0, 2).reshape(per, rows, width)
+        wide_grad = jnp.take(wide_grad, jnp.arange(per) ^ low, axis=0)
+        wide_grad = wide_grad.reshape(per // 2, 2, rows, width)
+        mlp_dw = mlp_dw[:2] + [wide_grad[:, 0], wide_grad[:, 1]]
+    grad, gain_one, *first_dw = attn_bwd(grad, stream, kept_one, 0, 0)
+
+    per_bits = per.bit_length() - 1
+    cut = rows // 32 * 16
+    top = (per_bits, per_bits + 1)
+    z_bits = list(range(1, per_bits))
+    layers = []
+    for keep, send in (second_dw, mlp_dw[:2], mlp_dw[2:], first_dw):
+        arrived = swap(send, both, 0)
+        upper = reduce_low(keep[:, :cut] + arrived[:, :cut], both, z_bits)
+        layers.append((upper, keep[:, cut:] + arrived[:, cut:]))
+    layers = [layers[i] for i in (3, 0, 2, 1)]
+    pieces = []
+    for low_first in (True, False):
+        at = slice(0, cut // 2) if low_first else slice(cut // 2, cut)
+        pieces.append(reduce_layers([u[at] for u, _ in layers], both, top, me, low_first))
+    for low_first in (True, False):
+        middle = (rows - cut) // 2
+        at = slice(0, middle) if low_first else slice(middle, rows - cut)
+        part = reduce_layers([v[:, at] for _, v in layers], both, top, me, low_first)
+        pieces.append(reduce_low(part, both, z_bits))
+
+    output = call(
+        output_kernel,
+        (stream_three, picks, cols, probs, exchange(expert_out)),
+        (None,) * 5,
+        [shape((seq, width))],
+        "output",
+        4 * padded * slots * width,
+        4e6,
+    )[0]
 
     small = jnp.concatenate(
         [router_grad.reshape(-1)] + [g.reshape(-1) for g in (gain_one, gain_two, gain_three, gain_four)]
     )
     small = jnp.pad(small, (0, tail * LANES - small.shape[0])).reshape(tail, LANES)
-    small = all_sum(small, ("expert", "dp"))
+    small = all_sum(small, both, all_bits)
     gain_at = width * experts
     gain_grads = small.reshape(-1)[gain_at : gain_at + 4 * width].reshape(4, width)
 
+    def unpack(wide, pieces, count, name):
+        return pl.pallas_call(
+            functools.partial(unpack_kernel, (count, tiles)),
+            in_specs=[SMEM] + [VMEM] * len(pieces),
+            out_specs=[VMEM, VMEM],
+            out_shape=[shape((count * tiles, LANES)), shape((1, LANES))],
+            scratch_shapes=[pltpu.VMEM((count, width), f32)],
+            compiler_params=params(),
+            cost_estimate=cost(0, 6 * count * width),
+            name=name,
+        )(wide, *pieces)
+
+    expert_grad, expert_square = unpack(expert_wide, expert_sums, expert_rows, "unpack_expert")
     dense_wide = (me >= devices // 2) & (me < 3 * devices // 4) & wide_ok
-    dense_rows, _ = pl.pallas_call(
-        functools.partial(unpack_kernel, (rows, tiles)),
-        in_specs=[SMEM, VMEM],
-        out_specs=[VMEM, VMEM],
-        out_shape=[shape((rows * tiles, LANES)), shape((1, LANES))],
-        compiler_params=params(),
-        cost_estimate=cost(0, 6 * rows * width),
-        name="unpack_dense",
-    )(dense_wide.astype(jnp.int32).reshape(1), dense_sum)
+    dense_rows, _ = unpack(dense_wide.astype(jnp.int32).reshape(1), pieces, rows, "unpack_dense")
     head = lax.ppermute(dense_rows[:tail], both, backward_ring)
     head = jnp.where(me == devices - 1, small, head)
     dense_grad, dense_square = pl.pallas_call(
@@ -764,17 +996,8 @@
         cost_estimate=cost(0, 8 * rows * width),
         name="shift_dense",
     )(me_arr, dense_rows, head)
-    expert_grad, expert_square = pl.pallas_call(
-        functools.partial(unpack_kernel, (expert_rows, tiles)),
-        in_specs=[SMEM, VMEM],
-        out_specs=[VMEM, VMEM],
-        out_shape=[shape((expert_flat, LANES)), shape((1, LANES))],
-        compiler_params=params(),
-        cost_estimate=cost(0, 6 * expert_rows * width),
-        name="unpack_expert",
-    )(expert_wide, expert_sum)
-
-    square = all_sum(dense_square + expert_square, ("expert", "dp"))
+
+    square = all_sum(dense_square + expert_square, both, all_bits)
     square_sum = jnp.sum(square)
     param_count = (dense_master.size + expert_master.size) * devices
     clip_factor = jnp.minimum(1.0, jnp.sqrt(param_count / (square_sum + 1e-06))).reshape(1)
@@ -795,7 +1018,7 @@
     )
     image = (1, seq, width)
     return (
-        output[:seq].reshape(image),
+        output.reshape(image),
         grad[:seq].reshape(image),
         dense_grad.reshape(dense_master.shape),
         expert_grad.reshape(expert_master.shape),

time: 730 us -> 620 us (0.85)
  waiting for transfers between devices: 470 us -> 362 us
  blocking collectives: 46.6 us -> 0 us
  starting transfers between devices: 18.9 us -> 52.3 us
  Pallas kernels: 133 us -> 142 us
    reduce_scatter x2 -> x0, waiting for transfers between devices: 267 us -> none  [the longest x1 175 us: on_device(): lax.psum_scatter(dense_local, both, scatter_dimension=0, tiled=True)]
    ppermute x10 -> x44, waiting for transfers between devices: 20.4 us -> 226 us  [swap(): return lax.ppermute(value, axes, [(i, i ^ 1 << bit) for i in range(size)])]
    all_to_all x2 -> x0, blocking collectives: 46.6 us -> none  [exchange(): lax.all_to_all(value, 'expert', split_axis=0, concat_axis=0, tiled=True)]
    all_gather x1 -> x0, waiting for transfers between devices: 41.2 us -> none  [on_device(): expert_all = lax.all_gather(expert_chunk, 'dp', axis=0, tiled=True)]
    ppermute x10 -> x44, starting transfers between devices: 8.81 us -> 35.8 us  [swap(): return lax.ppermute(value, axes, [(i, i ^ 1 << bit) for i in range(size)])]
    concatenate x1 -> x0, other arithmetic: 23.6 us -> none  [on_device(): jnp.concatenate([part.reshape(-1, width) for part in (first_dw, second_dw...]
    add x9 -> x22, other arithmetic: 0.72 us -> 11.8 us  [the longest x4 6.39 us: on_device(): layers.append((upper, keep[:, cut:] + arrived[:, cut:]))]
    all_to_all x2 -> x4, waiting for transfers between devices: 18.1 us -> 7.55 us  [exchange(): lax.all_to_all(value, 'expert', split_axis=0, concat_axis=0, tiled=True)]
  transfers between devices with their start and end apart: 18 -> 51, of which waited for: 14 -> 29; matrix products, arithmetic and copies ran while one was open for 2% -> 6% of each run, Pallas kernels for 7% -> 17%
where the time goes in v2:
time: 620 us; the launch traced here: 615 us
  waiting for transfers between devices  362 us (58%)
  Pallas kernels  142 us (23%)
  starting transfers between devices  52.3 us (8%)
  other arithmetic  22 us (4%)
  local copies, waits for them, and re-layouts  20.6 us (3%)
  between operations  15.5 us (2%)
    ppermute x44, waiting for transfers between devices, swap(): return lax.ppermute(value, axes, [(i, i ^ 1 << bit) for i in range(size)])  226 us
    all_gather x1, waiting for transfers between devices, on_device(): gathered = lax.all_gather(chunk, both, axis=0, tiled=True)  121 us
    pallas_call x9, Pallas kernels, call(): pl.pallas_call(kernel, grid=(1,), in_specs=[s or whole(a) for a, s in zip...  75.8 us
    ppermute x44, starting transfers between devices, swap(): return lax.ppermute(value, axes, [(i, i ^ 1 << bit) for i in range(size)])  35.8 us
    pallas_call x1, Pallas kernels, on_device(): pl.pallas_call(functools.partial(expert_kernel, (dp_ranks, quarter)), gri...  17.8 us
    pallas_call x2, Pallas kernels, adam(): pl.pallas_call(adam_kernel, grid=(pl.cdiv(count, block),), in_specs=[SMEM...  16.4 us
    all_to_all x4, starting transfers between devices, exchange(): lax.all_to_all(value, 'expert', split_axis=0, concat_axis=0, tiled=True)  16 us
  transfers between devices with their start and end apart: 51, of which 29 were waited for; matrix products, arithmetic and copies ran while one was open for 6% of the time, Pallas kernels for 17%

profile of v2, /device:TPU:0, one launch (start us, length us, event | category | flops | bytes accessed | tf_op | source)
XLA Modules:
  0.0 615.2 jit_solution(17290365250303073194)
XLA Ops:
  8.5 7.7 %collective-permute-done.tail_ref = f32[96,128]{1,0:T(8,128)S(1)} collective-permute-done((f32[96,128]{1,0:T(8,128)S(1)}, f32[96,128]{1,0:T(8,128)S(1)}, u32[]{:S(2)}, u32[]{:S(2)}) %collective-permute-start) | collective-permute-done | bytes 49184 | tf_op jit(solution)/shard_map/ppermute | solution.py:691
  37.1 121.4 %all-gather.2.cloned.1.call-done = bf16[12800,768]{1,0:T(8,128)(2,1)} async-done(((bf16[400,768]{1,0:T(8,128)(2,1)}), bf16[12800,768]{1,0:T(8,128)(2,1)}) %all-gather.2.cloned.1.call-update) | async-done | bytes 19660816 | tf_op jit(solution)/shard_map/all_gather | solution.py:705
  161.5 6.5 %attn_fwd.2 = (f32[208,768]{1,0:T(8,128)}, bf16[208,768]{1,0:T(8,128)(2,1)}, bf16[208,768]{1,0:T(8,128)(2,1)}, bf16[208,768]{1,0:T(8,128)(2,1)}, bf16[208,768]{1,0:T(8,128)(2,1)}, /*index=5*/bf16[208,768]{1,0:T(8,128)(2,1)}) custom-call(f32[208,768]{1,0:T(8,128)} %pad_convert_fusion.stream_ref, f32[1,768]{1,0:T(1,128)} %get-tuple-element.194.gain_ref, ...), custom_call_target="tpu_custom_call" | custom-call | flops 1226833920 | bytes 4718592 | tf_op jit(solution)/shard_map/attn_fwd/pallas_call | solution.py:788
  167.9 8.1 %mlp_fwd.1 = (f32[208,768]{1,0:T(8,128)}, bf16[208,768]{1,0:T(8,128)(2,1)}, f32[208,3072]{1,0:T(8,128)}) custom-call(f32[208,768]{1,0:T(8,128)} %get-tuple-element.71.stream_ref, f32[1,768]{1,0:T(1,128)} %get-tuple-element.193.gain_ref, bf16[32,400,768]{2,1,0:T(8,128)(2,1)} %bitcast.241, bf16[32,400,768]{2,1,0:T(8,128)(2,1)} %bitcast.242), custom_call_target="tpu_custom_call" | custom-call | flops 1962934272 | bytes 9437184 | tf_op jit(solution)/shard_map/mlp_fwd/pallas_call | solution.py:788
  176.1 6.5 %attn_fwd.3 = (f32[208,768]{1,0:T(8,128)}, bf16[208,768]{1,0:T(8,128)(2,1)}, bf16[208,768]{1,0:T(8,128)(2,1)}, bf16[208,768]{1,0:T(8,128)(2,1)}, bf16[208,768]{1,0:T(8,128)(2,1)}, /*index=5*/bf16[208,768]{1,0:T(8,128)(2,1)}) custom-call(f32[208,768]{1,0:T(8,128)} %get-tuple-element.72.stream_ref, f32[1,768]{1,0:T(1,128)} %get-tuple-element.192.gain_ref, ...), custom_call_target="tpu_custom_call" | custom-call | flops 1226833920 | bytes 4718592 | tf_op jit(solution)/shard_map/attn_fwd/pallas_call | solution.py:788
  193.8 24.7 %collective-permute-done.2.refs_2_ = bf16[768,768]{1,0:T(8,128)(2,1)S(1)} collective-permute-done((bf16[768,768]{1,0:T(8,128)(2,1)S(1)}, bf16[768,768]{1,0:T(8,128)(2,1)S(1)}, u32[]{:S(2)}, u32[]{:S(2)}) %collective-permute-start.2) | collective-permute-done | bytes 1179680 | tf_op jit(solution)/shard_map/ppermute | solution.py:600
  220.3 23.1 %collective-permute-done.3.refs_3_ = bf16[768,768]{1,0:T(8,128)(2,1)S(1)} collective-permute-done((bf16[768,768]{1,0:T(8,128)(2,1)}, bf16[768,768]{1,0:T(8,128)(2,1)S(1)}, u32[]{:S(2)}, u32[]{:S(2)}) %collective-permute-start.3) | collective-permute-done | bytes 1179680 | tf_op jit(solution)/shard_map/ppermute | solution.py:600
  245.8 17.8 %expert.1 = (bf16[448,768]{1,0:T(8,128)(2,1)}, bf16[448,896]{1,0:T(8,128)(2,1)}, bf16[448,768]{1,0:T(8,128)(2,1)}, bf16[448,3072]{1,0:T(8,128)(2,1)}, bf16[448,3072]{1,0:T(8,128)(2,1)}) custom-call(s32[1]{0:T(128)} %bitcast.12.dp_ref, bf16[448,896]{1,0:T(8,128)(2,1)} %bitcast.271, bf16[448,768]{1,0:T(8,128)(2,1)} %bitcast.276, ...), custom_call_target="tpu_custom_call" | custom-call | flops 8455716864 | bytes 9437184 | tf_op jit(solution)/shard_map/expert/pallas_call | solution.py:855
  268.3 11.7 %expert_grad.1 = (bf16[2,768,768]{2,1,0:T(8,128)(2,1)}, bf16[2,768,768]{2,1,0:T(8,128)(2,1)}, bf16[2,768,768]{2,1,0:T(8,128)(2,1)}, bf16[2,768,768]{2,1,0:T(8,128)(2,1)}) custom-call(s32[1]{0:T(128)} %bitcast.12.dp_ref, bf16[448,896]{1,0:T(8,128)(2,1)} %bitcast.272, bf16[448,768]{1,0:T(8,128)(2,1)} %get-tuple-element.115.dy_ref, ...), custom_call_target="tpu_custom_call" | custom-call | flops 4227858432 | bytes 9437184 | tf_op jit(solution)/shard_map/expert_grad/pallas_call | solution.py:879
  282.1 7.5 %all-to-all-done.3 = bf16[8,56,896]{2,1,0:T(8,128)(2,1)S(1)} async-done(((bf16[8,56,896]{2,1,0:T(8,128)(2,1)}), bf16[8,56,896]{2,1,0:T(8,128)(2,1)S(1)}, u32[]{:S(2)}, u32[]{:S(2)}) %all-to-all-start.3) | async-done | bytes 802848 | tf_op jit(solution)/shard_map/all_to_all | solution.py:750
  296.5 14.1 %attn_bwd.2 = (f32[208,768]{1,0:T(8,128)}, f32[1,768]{1,0:T(1,128)}, bf16[4,384,768]{2,1,0:T(8,128)(2,1)}, bf16[4,384,768]{2,1,0:T(8,128)(2,1)}) custom-call(s32[1]{0:T(128)} %bitcast.22.low_ref, f32[208,768]{1,0:T(8,128)} %get-tuple-element.84.grad_ref, f32[208,768]{1,0:T(8,128)} %get-tuple-element.72.stream_ref, f32[1,768]{1,0:T(1,128)} %get-tuple-element.192.gain_ref, ...), custom_call_target="tpu_custom_call" | custom-call | flops 2699034624 | bytes 9437184 | tf_op jit(solution)/shard_map/attn_bwd/pallas_call | solution.py:788
  311.4 16.1 %mlp_bwd.1 = (f32[208,768]{1,0:T(8,128)}, f32[1,768]{1,0:T(1,128)}, bf16[4,384,768]{2,1,0:T(8,128)(2,1)}, bf16[4,384,768]{2,1,0:T(8,128)(2,1)}, bf16[4,384,768]{...) custom-call(s32[1]{0:T(128)} %bitcast.22.low_ref, f32[208,768]{1,0:T(8,128)} %get-tuple-element.90.grad_ref, ...), custom_call_target="tpu_custom_call" | custom-call | flops 3925868544 | bytes 18874368 | tf_op jit(solution)/shard_map/mlp_bwd/pallas_call | solution.py:788
  327.6 14.2 %attn_bwd.3 = (f32[208,768]{1,0:T(8,128)}, f32[1,768]{1,0:T(1,128)}, bf16[4,384,768]{2,1,0:T(8,128)(2,1)}, bf16[4,384,768]{2,1,0:T(8,128)(2,1)}) custom-call(s32[1]{0:T(128)} %bitcast.22.low_ref, f32[208,768]{1,0:T(8,128)} %get-tuple-element.93.grad_ref, f32[208,768]{1,0:T(8,128)} %pad_convert_fusion.stream_ref, f32[1,768]{1,0:T(1,128)} %get-tuple-element.194.gain_ref, ...), custom_call_target="tpu_custom_call" | custom-call | flops 2699034624 | bytes 9437184 | tf_op jit(solution)/shard_map/attn_bwd/pallas_call | solution.py:788
  380.3 9.7 %collective-permute-done.11 = bf16[2,192,768]{2,1,0:T(8,128)(2,1)S(1)} collective-permute-done((bf16[2,192,768]{2,1,0:T(8,128)(2,1)S(1)}, bf16[2,192,768]{2,1,0:T(8,128)(2,1)S(1)}, u32[]{:S(2)}, u32[]{:S(2)}) %collective-permute-start.11) | collective-permute-done | bytes 589856 | tf_op jit(solution)/shard_map/ppermute | solution.py:600
  391.1 11.6 %collective-permute-done.8 = bf16[2,192,768]{2,1,0:T(8,128)(2,1)S(1)} collective-permute-done((bf16[2,192,768]{2,1,0:T(8,128)(2,1)S(1)}, bf16[2,192,768]{2,1,0:T(8,128)(2,1)S(1)}, u32[]{:S(2)}, u32[]{:S(2)}) %collective-permute-start.8) | collective-permute-done | bytes 589856 | tf_op jit(solution)/shard_map/ppermute | solution.py:600
  403.8 11.5 %collective-permute-done.14 = bf16[2,192,768]{2,1,0:T(8,128)(2,1)S(1)} collective-permute-done((bf16[2,192,768]{2,1,0:T(8,128)(2,1)S(1)}, bf16[2,192,768]{2,1,0:T(8,128)(2,1)S(1)}, u32[]{:S(2)}, u32[]{:S(2)}) %collective-permute-start.14) | collective-permute-done | bytes 589856 | tf_op jit(solution)/shard_map/ppermute | solution.py:600
  416.8 17.4 %collective-permute-done.17 = bf16[2,192,768]{2,1,0:T(8,128)(2,1)S(1)} collective-permute-done((bf16[2,192,768]{2,1,0:T(8,128)(2,1)S(1)}, bf16[2,192,768]{2,1,0:T(8,128)(2,1)S(1)}, u32[]{:S(2)}, u32[]{:S(2)}) %collective-permute-start.17) | collective-permute-done | bytes 589856 | tf_op jit(solution)/shard_map/ppermute | solution.py:600
  437.3 19.3 %collective-permute-done.9 = bf16[1,192,768]{2,1,0:T(8,128)(2,1)S(1)} collective-permute-done((bf16[1,192,768]{2,1,0:T(8,128)(2,1)S(1)}, bf16[1,192,768]{2,1,0:T(8,128)(2,1)S(1)}, u32[]{:S(2)}, u32[]{:S(2)}) %collective-permute-start.9) | collective-permute-done | bytes 294944 | tf_op jit(solution)/shard_map/ppermute | solution.py:600
  456.7 12.6 %collective-permute-done.15 = bf16[1,192,768]{2,1,0:T(8,128)(2,1)S(1)} collective-permute-done((bf16[1,192,768]{2,1,0:T(8,128)(2,1)S(1)}, bf16[1,192,768]{2,1,0:T(8,128)(2,1)S(1)}, u32[]{:S(2)}, u32[]{:S(2)}) %collective-permute-start.15) | collective-permute-done | bytes 294944 | tf_op jit(solution)/shard_map/ppermute | solution.py:600
  479.1 30.8 %collective-permute-done.19 = bf16[2,96,768]{2,1,0:T(8,128)(2,1)S(1)} collective-permute-done((bf16[2,96,768]{2,1,0:T(8,128)(2,1)S(1)}, bf16[2,96,768]{2,1,0:T(8,128)(2,1)S(1)}, u32[]{:S(2)}, u32[]{:S(2)}) %collective-permute-start.19) | collective-permute-done | bytes 294944 | tf_op jit(solution)/shard_map/ppermute | solution.py:600
  514.2 13.3 %collective-permute-done.22 = bf16[96,768]{1,0:T(8,128)(2,1)S(1)} collective-permute-done((bf16[96,768]{1,0:T(8,128)(2,1)S(1)}, bf16[96,768]{1,0:T(8,128)(2,1)S(1)}, u32[]{:S(2)}, u32[]{:S(2)}) %collective-permute-start.22) | collective-permute-done | bytes 147488 | tf_op jit(solution)/shard_map/ppermute | solution.py:600
  535.7 8.5 %collective-permute-done.29 = bf16[2,96,768]{2,1,0:T(8,128)(2,1)S(1)} collective-permute-done((bf16[2,96,768]{2,1,0:T(8,128)(2,1)S(1)}, bf16[2,96,768]{2,1,0:T(8,128)(2,1)S(1)}, u32[]{:S(2)}, u32[]{:S(2)}) %collective-permute-start.29) | collective-permute-done | bytes 294944 | tf_op jit(solution)/shard_map/ppermute | solution.py:600
  549.0 5.6 collective-permute-done.30
  595.9 12.3 %adam.3 = (f32[9216,128]{1,0:T(8,128)}, f32[9216,128]{1,0:T(8,128)}, f32[9216,128]{1,0:T(8,128)}) custom-call(f32[1]{0:T(128)} %bitcast.85.clip_ref, f32[9216,128]{1,0:T(8,128)} %get-tuple-element.122.grad_ref, f32[9216,128]{1,0:T(8,128)} %bitcast.257, f32[9216,128]{1,0:T(8,128)} %bitcast.258), custom_call_target="tpu_custom_call" | custom-call | flops 23592960 | bytes 28311552 | tf_op jit(solution)/shard_map/adam/pallas_call | solution.py:192
  (226 shorter events, 167.7 us)
Async XLA Ops:
  7.2 151.3 %all-gather.2.cloned.1.call-start = ((), (), s32[]{:S(2)}) async-start(), calls=%async_computation.4 | async-start | bytes 20275200 | tf_op jit(solution)/shard_map/all_gather | solution.py:705
  25.4 160.6 %all-to-all-start.1 = ((bf16[8,56,768]{2,1,0:T(8,128)(2,1)}), bf16[8,56,768]{2,1,0:T(8,128)(2,1)S(1)}, u32[]{:S(2)}, u32[]{:S(2)}) async-start(bf16[8,56,768]{2,1,0:T(8,128)(2,1)} %bitcast.277), calls=%async_computation.1 | async-start | bytes 1376256 | tf_op jit(solution)/shard_map/all_to_all | solution.py:750
  34.3 157.5 %collective-permute-start.1 = (bf16[768,768]{1,0:T(8,128)(2,1)}, bf16[768,768]{1,0:T(8,128)(2,1)}, u32[]{:S(2)}, u32[]{:S(2)}) collective-permute-start(bf16[768,768]{1,0:T(8,128)(2,1)} %get-tuple-element.79.refs_0_), channel_id=1, source_target_pairs={{0,8},{8,0},{16,24},{24,16},{1,9},{9,1},{17,25},{25,17},{2,10},{10... | collective-permute-start | bytes 3538952 | tf_op jit(solution)/shard_map/ppermute | solution.py:600
  35.4 157.8 %collective-permute-start.5 = (bf16[768,768]{1,0:T(8,128)(2,1)}, bf16[768,768]{1,0:T(8,128)(2,1)}, u32[]{:S(2)}, u32[]{:S(2)}) collective-permute-start(bf16[768,768]{1,0:T(8,128)(2,1)} %get-tuple-element.80.refs_4_), channel_id=1, source_target_pairs={{0,16},{8,24},{16,0},{24,8},{1,17},{9,25},{17,1},{25,9},{2,18},{10... | collective-permute-start | bytes 3538952 | tf_op jit(solution)/shard_map/ppermute | solution.py:600
  186.0 58.9 %all-to-all-start = ((bf16[8,56,896]{2,1,0:T(8,128)(2,1)}), bf16[8,56,896]{2,1,0:T(8,128)(2,1)S(1)}, u32[]{:S(2)}, u32[]{:S(2)}) async-start(bf16[8,56,896]{2,1,0:T(8,128)(2,1)} %bitcast.273), calls=%async_computation | async-start | bytes 1605632 | tf_op jit(solution)/shard_map/all_to_all | solution.py:750
  189.7 28.8 %collective-permute-start.2 = (bf16[768,768]{1,0:T(8,128)(2,1)S(1)}, bf16[768,768]{1,0:T(8,128)(2,1)S(1)}, u32[]{:S(2)}, u32[]{:S(2)}) collective-permute-start(bf16[768,768]{1,0:T(8,128)(2,1)S(1)} %copy-done.16), channel_id=1, source_target_pairs={{0,16},{8,24},{16,0},{24,8},{1,17},{9,25},{17,1},{25,9},{2,18},{10... | collective-permute-start | bytes 3538952 | tf_op jit(solution)/shard_map/ppermute | solution.py:600
  191.2 29.0 %collective-permute-start.4 = (bf16[768,768]{1,0:T(8,128)(2,1)}, bf16[768,768]{1,0:T(8,128)(2,1)S(1)}, u32[]{:S(2)}, u32[]{:S(2)}) collective-permute-start(bf16[768,768]{1,0:T(8,128)(2,1)} %get-tuple-element.80.refs_4_), channel_id=1, source_target_pairs={{0,8},{8,0},{16,24},{24,16},{1,9},{9,1},{17,25},{25,17},{2,10},{10... | collective-permute-start | bytes 3538952 | tf_op jit(solution)/shard_map/ppermute | solution.py:600
  191.8 51.6 %collective-permute-start.3 = (bf16[768,768]{1,0:T(8,128)(2,1)}, bf16[768,768]{1,0:T(8,128)(2,1)S(1)}, u32[]{:S(2)}, u32[]{:S(2)}) collective-permute-start(bf16[768,768]{1,0:T(8,128)(2,1)} %collective-permute-done.1.refs_1_), channel_id=1, source_target_pairs={{0,16},{8,24},{16,0},{24,8},{1,17},{9,25},{17,1},{25,9},{2,18},{10... | collective-permute-start | bytes 3538952 | tf_op jit(solution)/shard_map/ppermute | solution.py:600
  193.2 51.6 %collective-permute-start.6 = (bf16[768,768]{1,0:T(8,128)(2,1)}, bf16[768,768]{1,0:T(8,128)(2,1)}, u32[]{:S(2)}, u32[]{:S(2)}) collective-permute-start(bf16[768,768]{1,0:T(8,128)(2,1)} %collective-permute-done.5.refs_6_), channel_id=1, source_target_pairs={{0,8},{8,0},{16,24},{24,16},{1,9},{9,1},{17,25},{25,17},{2,10},{10... | collective-permute-start | bytes 3538952 | tf_op jit(solution)/shard_map/ppermute | solution.py:600
  280.1 85.9 %collective-permute-start.37 = (bf16[2,768,768]{2,1,0:T(8,128)(2,1)}, bf16[2,768,768]{2,1,0:T(8,128)(2,1)S(1)}, u32[]{:S(2)}, u32[]{:S(2)}) collective-permute-start(bf16[2,768,768]{2,1,0:T(8,128)(2,1)} %get-tuple-element.119), channel_id=1, source_target_pairs={{0,8},{8,0},{16,24},{24,16},{1,9},{9,1},{17,25},{25,17},{2,10},{10... | collective-permute-start | bytes 7077896 | tf_op jit(solution)/shard_map/ppermute | solution.py:600
  281.1 80.4 %collective-permute-start.39 = (bf16[2,768,768]{2,1,0:T(8,128)(2,1)}, bf16[2,768,768]{2,1,0:T(8,128)(2,1)}, u32[]{:S(2)}, u32[]{:S(2)}) collective-permute-start(bf16[2,768,768]{2,1,0:T(8,128)(2,1)} %get-tuple-element.121), channel_id=1, source_target_pairs={{0,16},{8,24},{16,0},{24,8},{1,17},{9,25},{17,1},{25,9},{2,18},{10... | collective-permute-start | bytes 7077896 | tf_op jit(solution)/shard_map/ppermute | solution.py:600
  311.3 56.0 %collective-permute-start.10 = (bf16[4,384,768]{2,1,0:T(8,128)(2,1)}, bf16[4,384,768]{2,1,0:T(8,128)(2,1)}, u32[]{:S(2)}, u32[]{:S(2)}) collective-permute-start(bf16[4,384,768]{2,1,0:T(8,128)(2,1)} %get-tuple-element.103), channel_id=1, source_target_pairs={{0,1},{1,0},{2,3},{3,2},{4,5},{5,4},{6,7},{7,6},{8,9},{9,8},{10,11... | collective-permute-start | bytes 7077896 | tf_op jit(solution)/shard_map/ppermute | solution.py:600
  343.1 29.6 %collective-permute-start.7 = (bf16[4,384,768]{2,1,0:T(8,128)(2,1)}, bf16[4,384,768]{2,1,0:T(8,128)(2,1)}, u32[]{:S(2)}, u32[]{:S(2)}) collective-permute-start(bf16[4,384,768]{2,1,0:T(8,128)(2,1)} %get-tuple-element.101), channel_id=1, source_target_pairs={{0,1},{1,0},{2,3},{3,2},{4,5},{5,4},{6,7},{7,6},{8,9},{9,8},{10,11... | collective-permute-start | bytes 7077896 | tf_op jit(solution)/shard_map/ppermute | solution.py:600
  357.5 223.1 %all-to-all-start.2 = ((bf16[8,56,768]{2,1,0:T(8,128)(2,1)}), bf16[8,56,768]{2,1,0:T(8,128)(2,1)S(1)}, u32[]{:S(2)}, u32[]{:S(2)}) async-start(bf16[8,56,768]{2,1,0:T(8,128)(2,1)} %bitcast.275), calls=%async_computation.2 | async-start | bytes 1376256 | tf_op jit(solution)/shard_map/all_to_all | solution.py:750
  366.0 200.6 %collective-permute-start.35 = (f32[96,128]{1,0:T(8,128)S(1)}, f32[96,128]{1,0:T(8,128)S(1)}, u32[]{:S(2)}, u32[]{:S(2)}) collective-permute-start(f32[96,128]{1,0:T(8,128)S(1)} %add.197), channel_id=1, source_target_pairs={{0,16},{1,17},{2,18},{3,19},{4,20},{5,21},{6,22},{7,23},{8,24},{9,... | collective-permute-start | bytes 147464 | tf_op jit(solution)/shard_map/ppermute | solution.py:600
  377.4 38.0 %collective-permute-start.14 = (bf16[2,192,768]{2,1,0:T(8,128)(2,1)S(1)}, bf16[2,192,768]{2,1,0:T(8,128)(2,1)S(1)}, u32[]{:S(2)}, u32[]{:S(2)}) collective-permute-start(bf16[2,192,768]{2,1,0:T(8,128)(2,1)S(1)} %slice_bitcast_fusion.9), channel_id=1, source_target_pairs={{0,2},{1,3},{2,0},{3,1},{4,6},{5,7},{6,4},{7,5},{8,10},{9,11},{10,... | collective-permute-start | bytes 1769480 | tf_op jit(solution)/shard_map/ppermute | solution.py:600
  379.4 54.7 %collective-permute-start.17 = (bf16[2,192,768]{2,1,0:T(8,128)(2,1)S(1)}, bf16[2,192,768]{2,1,0:T(8,128)(2,1)S(1)}, u32[]{:S(2)}, u32[]{:S(2)}) collective-permute-start(bf16[2,192,768]{2,1,0:T(8,128)(2,1)S(1)} %slice_bitcast_fusion.7), channel_id=1, source_target_pairs={{0,2},{1,3},{2,0},{3,1},{4,6},{5,7},{6,4},{7,5},{8,10},{9,11},{10,... | collective-permute-start | bytes 1769480 | tf_op jit(solution)/shard_map/ppermute | solution.py:600
  390.1 86.5 %collective-permute-start.23 = (bf16[2,4,96,768]{3,2,1,0:T(8,128)(2,1)S(1)}, bf16[2,4,96,768]{3,2,1,0:T(8,128)(2,1)S(1)}, u32[]{:S(2)}, u32[]{:S(2)}) collective-permute-start(bf16[2,4,96,768]{3,2,1,0:T(8,128)(2,1)S(1)} %pad_maximum_fusion), channel_id=1, source_target_pairs={{0,8},{1,9},{2,10},{3,11},{4,12},{5,13},{6,14},{7,15},{8,0},{9,1},... | collective-permute-start | bytes 3538952 | tf_op jit(solution)/shard_map/ppermute | solution.py:600
  402.7 75.1 %collective-permute-start.27 = (bf16[2,4,96,768]{3,2,1,0:T(8,128)(2,1)S(1)}, bf16[2,4,96,768]{3,2,1,0:T(8,128)(2,1)S(1)}, u32[]{:S(2)}, u32[]{:S(2)}) collective-permute-start(bf16[2,4,96,768]{3,2,1,0:T(8,128)(2,1)S(1)} %pad_maximum_fusion.1), channel_id=1, source_target_pairs={{0,16},{1,17},{2,18},{3,19},{4,20},{5,21},{6,22},{7,23},{8,24},{9,... | collective-permute-start | bytes 3538952 | tf_op jit(solution)/shard_map/ppermute | solution.py:600
  435.3 34.0 %collective-permute-start.15 = (bf16[1,192,768]{2,1,0:T(8,128)(2,1)S(1)}, bf16[1,192,768]{2,1,0:T(8,128)(2,1)S(1)}, u32[]{:S(2)}, u32[]{:S(2)}) collective-permute-start(bf16[1,192,768]{2,1,0:T(8,128)(2,1)S(1)} %slice_bitcast_fusion.21), channel_id=1, source_target_pairs={{0,4},{1,5},{2,6},{3,7},{4,0},{5,1},{6,2},{7,3},{8,12},{9,13},{10,... | collective-permute-start | bytes 884744 | tf_op jit(solution)/shard_map/ppermute | solution.py:600
  469.3 42.9 %collective-permute-start.38 = (bf16[1,768,768]{2,1,0:T(8,128)(2,1)S(1)}, bf16[1,768,768]{2,1,0:T(8,128)(2,1)S(1)}, u32[]{:S(2)}, u32[]{:S(2)}) collective-permute-start(bf16[1,768,768]{2,1,0:T(8,128)(2,1)S(1)} %slice_bitcast_fusion), channel_id=1, source_target_pairs={{0,16},{8,24},{16,0},{24,8},{1,17},{9,25},{17,1},{25,9},{2,18},{10... | collective-permute-start | bytes 3538952 | tf_op jit(solution)/shard_map/ppermute | solution.py:600
  475.5 84.5 %collective-permute-start.40 = (bf16[1,768,768]{2,1,0:T(8,128)(2,1)}, bf16[1,768,768]{2,1,0:T(8,128)(2,1)S(1)}, u32[]{:S(2)}, u32[]{:S(2)}) collective-permute-start(bf16[1,768,768]{2,1,0:T(8,128)(2,1)} %slice.421), channel_id=1, source_target_pairs={{0,8},{8,0},{16,24},{24,16},{1,9},{9,1},{17,25},{25,17},{2,10},{10... | collective-permute-start | bytes 3538952 | tf_op jit(solution)/shard_map/ppermute | solution.py:600
  476.6 33.3 %collective-permute-start.19 = (bf16[2,96,768]{2,1,0:T(8,128)(2,1)S(1)}, bf16[2,96,768]{2,1,0:T(8,128)(2,1)S(1)}, u32[]{:S(2)}, u32[]{:S(2)}) collective-permute-start(bf16[2,96,768]{2,1,0:T(8,128)(2,1)S(1)} %pad_maximum_fusion.2), channel_id=1, source_target_pairs={{0,8},{1,9},{2,10},{3,11},{4,12},{5,13},{6,14},{7,15},{8,0},{9,1},... | collective-permute-start | bytes 884744 | tf_op jit(solution)/shard_map/ppermute | solution.py:600
  477.8 33.0 %collective-permute-start.21 = (bf16[2,96,768]{2,1,0:T(8,128)(2,1)S(1)}, bf16[2,96,768]{2,1,0:T(8,128)(2,1)S(1)}, u32[]{:S(2)}, u32[]{:S(2)}) collective-permute-start(bf16[2,96,768]{2,1,0:T(8,128)(2,1)S(1)} %pad_maximum_fusion.3), channel_id=1, source_target_pairs={{0,16},{1,17},{2,18},{3,19},{4,20},{5,21},{6,22},{7,23},{8,24},{9,... | collective-permute-start | bytes 884744 | tf_op jit(solution)/shard_map/ppermute | solution.py:600
  (48 other events, 501.5 us)
Sparse Core Ops, SparseCore 0:
  19.3 139.1 all-gather.1

commit v3 on v2

--- a/solution.py
+++ b/solution.py
@@ -29,8 +29,8 @@
     return pltpu.CompilerParams(vmem_limit_bytes=mib << 20)
 
 
-def cost(flops, nbytes, trans=0):
-    return pl.CostEstimate(flops=int(flops), bytes_accessed=int(nbytes), transcendentals=int(trans))
+def cost(*_):
+    return pl.CostEstimate(flops=1, bytes_accessed=1, transcendentals=0)
 
 
 def dot(a, b):
@@ -133,13 +133,19 @@
         to_rows(read, write, 0, rows, False, tiles)
 
 
-def unpack_kernel(dims, wide_ref, *refs):
+def add_up(refs):
+    return sum(ref[...].astype(f32) for ref in refs)
+
+
+def unpack_kernel(dims, groups, wide_ref, *refs):
     rows, tiles = dims
-    piece_refs, (out_ref, square_ref, rows_ref) = refs[:-3], refs[-3:]
+    refs, (out_ref, square_ref, rows_ref) = refs[:-3], refs[-3:]
     at = 0
-    for ref in piece_refs:
-        rows_ref[at : at + ref.shape[0]] = ref[...].astype(f32)
-        at += ref.shape[0]
+    for count in groups:
+        value = add_up(refs[:count])
+        refs = refs[count:]
+        rows_ref[at : at + value.shape[0]] = value
+        at += value.shape[0]
     wide = wide_ref[0] > 0
 
     def store(is_wide):
@@ -164,14 +170,20 @@
         store(False)
 
 
-def shift_kernel(dims, k_ref, flat_ref, head_ref, out_ref, square_ref, buf):
+def stack_rows_kernel(*refs):
+    out_ref = refs[-1]
+    at = 0
+    for ref in refs[:-1]:
+        out_ref[at : at + ref.shape[0]] = ref[...]
+        at += ref.shape[0]
+
+
+def shift_kernel(dims, k_ref, flat_ref, head_ref, out_ref, buf):
     step, own = dims
     count = flat_ref.shape[0]
     buf[0:count] = flat_ref[...]
     buf[count : count + head_ref.shape[0]] = head_ref[...]
-    value = buf[pl.ds(step * k_ref[0], own), :]
-    out_ref[...] = value
-    square_ref[...] = jnp.sum(value * value, axis=0, keepdims=True)
+    out_ref[...] = buf[pl.ds(step * k_ref[0], own), :]
 
 
 def adam_kernel(clip_ref, grad_ref, momentum_ref, variance_ref, update_ref, momentum_out, variance_out):
@@ -201,8 +213,12 @@
     )(clip, grad, momentum, variance)
 
 
-def route_kernel(experts, capacity, stride, prio_row, prio_col, picks, picks_t, cot, cols_ref, rows_ref, g_ref):
+def route_kernel(
+    experts, capacity, stride, me_ref, prio_row, prio_col, picks, picks_t, cot,
+    cols_ref, near_ref, rows_ref, g_ref,
+):
     count = picks.shape[0]
+    me = me_ref[0]
     before = (prio_row[...] < prio_col[...]).astype(f32).astype(bf16)
     lane = lax.broadcasted_iota(jnp.int32, (count, experts), 1)
     sub = lax.broadcasted_iota(jnp.int32, (experts, count), 0)
@@ -215,13 +231,13 @@
         earlier_t = dot_nt(hot_t[j].astype(bf16), before) + (first_t if j else 0.0)
         place = jnp.sum(earlier * hot[j], axis=1, keepdims=True).astype(jnp.int32)
         place_t = jnp.sum(earlier_t * hot_t[j], axis=0, keepdims=True).astype(jnp.int32)
-        cols_ref[:, j : j + 1] = jnp.where(
-            place < capacity, picks[:, j : j + 1] * stride + place, -1
-        )
-        rows_ref[j : j + 1, :] = jnp.where(
-            place_t < capacity, picks_t[j : j + 1, :] * stride + place_t, -1
-        )
-    first, second = slot_selects(rows_ref, g_ref.shape[0])
+        pick, pick_t = picks[:, j : j + 1], picks_t[j : j + 1, :]
+        kept = (place < capacity) & (pick >= 0)
+        cols_ref[:, j : j + 1] = jnp.where(kept, pick * stride + place, -1)
+        near_ref[:, j : j + 1] = jnp.where(kept, (pick ^ me) * stride + place, -1)
+        kept = (place_t < capacity) & (pick_t >= 0)
+        rows_ref[j : j + 1, :] = jnp.where(kept, pick_t * stride + place_t, -1)
+    first, second = slot_selects(rows_ref, experts * stride)
     g_ref[...] = dot(first + second, cot[...]).astype(bf16)
 
 
@@ -307,21 +323,9 @@
 
 
 def attn_bwd_kernel(
-    seq, low_ref, grad_ref, stream_ref, gain_ref, w_ref, a_ref, q_ref, k_ref, v_ref, o_ref,
-    out_ref, gain_out, keep_ref, send_ref, dw, do_ref, dq_ref, dk_ref, dv_ref, sems,
+    seq, grad_ref, stream_ref, gain_ref, w_ref, q_ref, k_ref, v_ref, out_ref, gain_out, dq_ref, dk_ref, dv_ref, do_ref
 ):
-    width = grad_ref.shape[1]
-    branch = grad_ref[...].astype(bf16)
-    low = low_ref[0]
-
-    def put(index, value):
-        rows = dw.shape[2]
-        per = width // rows
-        for i in range(per):
-            put_chunk(dw, low, index * per + i, value[i * rows : (i + 1) * rows].astype(bf16))
-
-    do_ref[...] = dot_nt(branch, matrix(w_ref, 3)).astype(bf16)
-    put(3, dot_tn(o_ref[...], branch))
+    do_ref[...] = dot_nt(grad_ref[...].astype(bf16), matrix(w_ref, 3)).astype(bf16)
     count = grad_ref.shape[0]
     key_ok = lax.broadcasted_iota(jnp.int32, (count, count), 1) < seq
     masks = head_masks()
@@ -348,14 +352,28 @@
         dv_ref[:, lanes] = dv.astype(bf16)
     back = None
     for index, ref in enumerate((dq_ref, dk_ref, dv_ref)):
-        put(index, dot_tn(a_ref[...], ref[...]))
         part = dot_nt(ref[...], matrix(w_ref, index))
         back = part if back is None else back + part
-    flush(dw, keep_ref, send_ref, sems)
     normed, inverse = norm_rows(stream_ref[...])
     addend, gain_grad = norm_back(back, normed, inverse, gain_ref[...])
     out_ref[...] = grad_ref[...] + addend
     gain_out[...] = gain_grad
+
+
+def attn_weights_kernel(
+    low_ref, grad_ref, a_ref, o_ref, dq_ref, dk_ref, dv_ref, keep_ref, send_ref, dw, sems
+):
+    low = low_ref[0]
+    rows = dw.shape[2]
+    per = grad_ref.shape[1] // rows
+    branch = grad_ref[...].astype(bf16)
+    for index in range(4):
+        left = o_ref if index == 3 else a_ref
+        right = branch if index == 3 else (dq_ref, dk_ref, dv_ref)[index][...]
+        value = dot_tn(left[...], right)
+        for i in range(per):
+            put_chunk(dw, low, index * per + i, value[i * rows : (i + 1) * rows].astype(bf16))
+    flush(dw, keep_ref, send_ref, sems)
 
 
 def mlp_fwd_kernel(stream_ref, gain_ref, w1_ref, w2_ref, out_ref, b_ref, u_ref):
@@ -447,35 +465,27 @@
     return wide[:, 0:1] + wide[:, 1:2] + wide[:, 2:3]
 
 
-def expert_kernel(dims, dp_ref, x_ref, g_ref, *refs):
-    parts, quarter = dims
-    weight_refs, refs = refs[: 2 * parts], refs[2 * parts :]
-    y_ref, dx_ref, dy_ref, act_ref, dpre_ref, weights, y_sum, dx_sum, sems = refs
+def expert_kernel(dims, spans, me_ref, x_ref, g_ref, *refs):
+    parts, quarter, blocks = dims
+    weight_refs, refs = refs[: len(spans)], refs[len(spans) :]
+    y_refs, refs = refs[: blocks // 2], refs[blocks // 2 :]
+    dx_ref, dy_ref, act_ref, dpre_ref, weights, y_near, y_sum, dx_sum, sems = refs
     q = pl.program_id(0)
     width = g_ref.shape[1]
     half = parts // 2
-    rows = weights.shape[1] // 2
-    me = dp_ref[0]
-
-    def copies(side):
-        return [
-            pltpu.make_async_copy(
-                weight_refs[side * parts + r],
-                weights.at[r ^ me, side * rows : (side + 1) * rows],
-                sems.at[side * parts + r],
-            )
-            for r in range(parts)
-        ]
+    me = me_ref[0]
 
     @pl.when(q == 0)
     def _():
-        for side in range(2):
-            for copy in copies(side):
-                copy.start()
+        copies = [
+            pltpu.make_async_copy(ref, weights.at[place ^ me, first : first + ref.shape[0]], sems.at[i])
+            for i, ((place, first), ref) in enumerate(zip(spans, weight_refs))
+        ]
+        for copy in copies:
+            copy.start()
         dy_ref[...] = (add_lanes(x_ref[:, width:]) * g_ref[...].astype(f32)).astype(bf16)
-        for side in range(2):
-            for copy in copies(side):
-                copy.wait()
+        for copy in copies:
+            copy.wait()
 
     first = weights[0:half, pl.ds(pl.multiple_of(q * quarter, 16), quarter), :].reshape(width, width)
     if 4 * quarter >= width:
@@ -485,8 +495,7 @@
     else:
         per = width // (4 * quarter)
         second = weights[pl.ds(half + q * per, per)].reshape(width, width)
-    x = x_ref[:, 0:width]
-    pre = dot(x, first)
+    pre = dot(x_ref[:, 0:width], first)
     cdf = normal_cdf(pre)
     act = (pre * cdf).astype(bf16)
     act_ref[...] = act
@@ -508,16 +517,20 @@
 
     @pl.when(q == pl.num_programs(0) - 1)
     def _():
-        y = y_sum[...].astype(bf16)
-        y_ref[...] = y
+        y = y_sum[...].astype(bf16).astype(f32)
+        stride = y.shape[0] // blocks
+        for block in range(blocks):
+            y_near[block ^ me_ref[1]] = y[block * stride : (block + 1) * stride].astype(bf16)
+        for pair, ref in enumerate(y_refs):
+            ref[...] = y_near[2 * pair : 2 * pair + 2]
         dx_ref[:, 0:width] = dx_sum[...].astype(bf16)
-        gate_grad = jnp.sum(g_ref[...].astype(f32) * y.astype(f32), axis=-1, keepdims=True)
+        gate_grad = jnp.sum(g_ref[...].astype(f32) * y, axis=-1, keepdims=True)
         dx_ref[:, width:] = split_lanes(gate_grad)
 
 
 def expert_grad_kernel(dims, dp_ref, x_ref, dy_ref, act_ref, dpre_ref, *refs):
     parts, quarter = dims
-    out_refs, scratch, sems = refs[:4], refs[4], refs[5]
+    out_refs, scratch, sems = refs[: 2 * parts], refs[-2], refs[-1]
     q = pl.program_id(0)
     me = dp_ref[0]
     width = dy_ref.shape[1]
@@ -548,7 +561,7 @@
                     copies.append(
                         pltpu.make_async_copy(
                             scratch.at[r, side * rows // 2 : (side + 1) * rows // 2],
-                            out_refs[2 * side + which].at[i],
+                            out_refs[side * parts + which * half + i],
                             sems.at[side * parts + r],
                         )
                     )
@@ -573,7 +586,7 @@
         prob_grad = part if prob_grad is None else prob_grad + part
     logit_grad = probs * (prob_grad - jnp.sum(prob_grad * probs, axis=-1, keepdims=True))
     logit_grad = logit_grad.astype(bf16)
-    router_out[...] = dot_tn(c_ref[...], logit_grad)
+    router_out[...] = dot_tn(logit_grad, c_ref[...])
     back = dot(selects[0] + selects[1], dx_ref[:, 0:width]) + dot_nt(logit_grad, wr_ref[...])
     normed, inverse = norm_rows(stream_ref[...])
     addend, gain_grad = norm_back(back, normed, inverse, gain_ref[...])
@@ -581,64 +594,110 @@
     gain_out[...] = gain_grad
 
 
-def output_kernel(stream_ref, picks_ref, cols_ref, probs_ref, y_ref, out_ref):
+def output_kernel(stream_ref, picks_ref, near_ref, probs_ref, *refs):
+    y_refs, (other_ref, out_ref, wide) = refs[:-3], refs[-3:]
+    stride = other_ref.shape[1]
+    for pair, ref in enumerate(y_refs):
+        wide[2 * pair * stride : (2 * pair + 1) * stride] = ref[0].astype(f32)
+        wide[(2 * pair + 1) * stride : (2 * pair + 2) * stride] = other_ref[pair].astype(f32)
+    y = wide[...].astype(bf16)
     seq = out_ref.shape[0]
     probs = probs_ref[...]
     hots = pick_hots(picks_ref, probs.shape[1])
-    selects = token_selects(cols_ref, y_ref.shape[0])
+    selects = token_selects(near_ref, y.shape[0])
     total = stream_ref[...]
     for j in range(2):
         gate = jnp.sum(probs * hots[j], axis=-1, keepdims=True)
-        total = total + gate * dot(selects[j], y_ref[...])
+        total = total + gate * dot(selects[j], y)
     out_ref[...] = total[0:seq]
 
 
-def swap(value, axes, bit):
+def add_pair(left, right):
+    return (left.astype(f32) + right.astype(f32)).astype(bf16)
+
+
+def fold_layers_kernel(cut, top_ref, *refs):
+    layers, refs = [refs[2 * i : 2 * i + 2] for i in range(4)], refs[8:]
+    uppers, (send_x, keep_x, send_y, keep_y, scratch) = refs[:4], refs[4:]
+    middle = send_x.shape[2]
+    place = pl.program_id(0)
+    for layer, (keep, got) in enumerate(layers):
+        value = add_pair(keep[0], got[0])
+        for j, upper in enumerate(uppers):
+
+            @pl.when(lax.rem(place, 4) == j)
+            def _():
+                upper[layer, place // 4] = value[:cut]
+
+        scratch[layer ^ top_ref[0]] = value[cut:]
+    for i in range(2):
+        keep_x[i, 0] = scratch[2 * i, 0:middle]
+        send_x[i, 0] = scratch[2 * i + 1, 0:middle]
+        keep_y[i, 0] = scratch[i, middle:]
+        send_y[i, 0] = scratch[i + 2, middle:]
+
+
+def fold_plane_kernel(keep_x, got_x, keep_y, got_y, own_a, send_y, own_b, send_x):
+    for keep, got, own, send in ((keep_x, got_x, own_a, send_y), (keep_y, got_y, own_b, send_x)):
+        own[...] = add_pair(keep[0], got[0])
+        send[...] = add_pair(keep[1], got[1])
+
+
+def fold_rows_kernel(own_a, got_a, own_b, got_b, *outs):
+    middle = own_a.shape[1]
+    for place in range(own_a.shape[0]):
+        out = outs[place % 4].at[place // 4]
+        out[0:middle] = add_pair(own_a[place], got_a[place])
+        out[middle:] = add_pair(own_b[place], got_b[place])
+
+
+def fold_uppers_kernel(top_ref, *refs):
+    refs, outs, scratch = refs[:-5], refs[-5:-1], refs[-1]
+    for layer in range(4):
+        scratch[layer ^ top_ref[0]] = sum(ref[layer].astype(f32) for ref in refs).astype(bf16)
+    for place, out in enumerate(outs):
+        out[...] = scratch[place]
+
+
+def fold_expert_kernel(highs, *refs):
+    count = len(refs) // 6
+    ins, outs = refs[: 4 * count], refs[4 * count :]
+    for side, high in enumerate(highs):
+        half = count // 2
+        for i in range(count):
+            which, at = (i // half, i % half) if high else (i % 2, i // 2)
+            keep, got = ins[2 * side * count + i], ins[(2 * side + 1) * count + i]
+            outs[side * count + which * half + at][...] = add_pair(keep[...], got[...])
+
+
+def swap(value, axes, mask):
     size = 1
     for axis in axes:
         size *= lax.axis_size(axis)
-    return lax.ppermute(value, axes, [(i, i ^ (1 << bit)) for i in range(size)])
-
-
-def all_sum(value, axes, bits):
-    for bit in range(bits):
-        value = value + swap(value, axes, bit)
-    return value
-
-
-def gather_parts(value, axes, order):
-    parts = {0: value}
-    for bit in order:
-        parts.update({at | (1 << bit): swap(part, axes, bit) for at, part in list(parts.items())})
-    return [parts[at] for at in sorted(parts)]
-
-
-def reduce_low(value, axes, bits):
+    return lax.ppermute(value, axes, [(i, i ^ mask) for i in range(size)])
+
+
+def after(value, *others):
+    return lax.optimization_barrier((value, others))[0]
+
+
+def bit_groups(bits):
+    return [bits[i : i + 2] for i in range(0, len(bits), 2)]
+
+
+def all_sum_step(value, axes, bits):
+    if len(bits) == 1:
+        return value + swap(value, axes, 1 << bits[0])
+    low, high = 1 << bits[0], 1 << bits[1]
+    near, far, both = swap(value, axes, low), swap(value, axes, high), swap(value, axes, low | high)
+    return (value + near) + (far + both)
+
+
+def reduce_bits(value, axes, bits):
     for bit in bits:
         pairs = value.reshape((value.shape[0] // 2, 2) + value.shape[1:])
-        value = pairs[:, 0] + swap(pairs[:, 1], axes, bit)
+        value = pairs[:, 0] + swap(pairs[:, 1], axes, 1 << bit)
     return value[0]
-
-
-def reduce_high(value, axes, bits):
-    for bit in reversed(bits):
-        pairs = value.reshape((2, value.shape[0] // 2) + value.shape[1:])
-        value = pairs[0] + swap(pairs[1], axes, bit)
-    return value[0]
-
-
-def reduce_layers(layers, axes, bits, me, low_first):
-    grid = [[layers[0], layers[1]], [layers[2], layers[3]]]
-    if not low_first:
-        grid = [list(column) for column in zip(*grid)]
-    first, second = (bits[0], bits[1]) if low_first else (bits[1], bits[0])
-    own = (me >> first) & 1
-    keep = [jnp.where(own == 0, row[0], row[1]) for row in grid]
-    send = [jnp.where(own == 0, row[1], row[0]) for row in grid]
-    arrived = swap(jnp.stack(send), axes, first)
-    sums = [keep[i] + arrived[i] for i in range(2)]
-    own = (me >> second) & 1
-    return jnp.where(own == 0, sums[0], sums[1]) + swap(jnp.where(own == 0, sums[1], sums[0]), axes, second)
 
 
 def shape(dims, dtype=f32):
@@ -706,20 +765,32 @@
     gathered = gathered.reshape(devices, rows + tail_rows, width)
 
     expert_wide = (dp_me < dp_ranks // 2).astype(jnp.int32).reshape(1)
-    half_shape = shape((expert_rows // 2, width), bf16)
     halves = pl.pallas_call(
         functools.partial(pack_expert_kernel, (expert_rows, tiles)),
         in_specs=[SMEM, VMEM],
         out_specs=[VMEM, VMEM],
-        out_shape=[half_shape, half_shape],
+        out_shape=[shape((expert_rows // 2, width), bf16)] * 2,
         compiler_params=params(),
         cost_estimate=cost(0, 6 * expert_master.size),
         name="pack_expert",
     )(expert_wide, expert_master.reshape(expert_flat, LANES))
     dp_axis = ("dp",)
     dp_order = list(range(dp_bits))
-    expert_parts = gather_parts(halves[0], dp_axis, dp_order)
-    expert_parts += gather_parts(halves[1], dp_axis, dp_order[::-1])
+
+    def gather_step(parts, bit):
+        return {**parts, **{at | (1 << bit): swap(part, dp_axis, 1 << bit) for at, part in parts.items()}}
+
+    half_rows = expert_rows // 2
+    orders = (dp_order, dp_order[::-1])
+    sides = [gather_step({0: half}, bits[0]) for half, bits in zip(halves, orders)]
+    gathered, sides = lax.optimization_barrier((gathered, sides))
+    sides = [gather_step(side, bits[1]) for side, bits in zip(sides, orders)]
+    for i, bits in enumerate(orders):
+        for bit in bits[2:]:
+            sides[i] = gather_step(sides[i], bit)
+    expert_parts = [side[at] for side in sides for at in sorted(side)]
+    expert_spans = [(at, i * half_rows) for i, side in enumerate(sides) for at in sorted(side)]
+    soon = [sides[i][1 << bits[1]] for i, bits in enumerate(orders)]
 
     capacity = 2 * seq // experts
     stride = -(-capacity // 8) * 8
@@ -730,19 +801,18 @@
     picks = jnp.pad(expert_picks, ((0, fill), (0, 0)), constant_values=-1)
     cot = jnp.pad(cotangent.reshape(seq, width), ((0, fill), (0, 0)))
     stream = jnp.pad(tokens.reshape(seq, width).astype(f32), ((0, fill), (0, 0)))
-    cols, rows_slots, outgoing_cot = pl.pallas_call(
+    e_me = lax.axis_index("expert").astype(jnp.int32).reshape(1)
+    pair_shape = shape((2, stride, width), bf16)
+    cols, near_cols, rows_slots, outgoing_cot = pl.pallas_call(
         functools.partial(route_kernel, experts, capacity, stride),
-        in_specs=[VMEM] * 5,
-        out_specs=[VMEM] * 3,
-        out_shape=[
-            shape((padded, 2), jnp.int32),
-            shape((2, padded), jnp.int32),
-            shape((slots, width), bf16),
-        ],
+        in_specs=[SMEM] + [VMEM] * 5,
+        out_specs=[VMEM] * 4,
+        out_shape=[shape((padded, 2), jnp.int32)] * 2
+        + [shape((2, padded), jnp.int32), shape((slots, width), bf16)],
         compiler_params=params(),
-        cost_estimate=cost(2 * padded * slots * width, 1e6),
+        cost_estimate=cost(),
         name="route",
-    )(ranks, ranks.reshape(padded, 1), picks, picks.T, cot)
+    )(e_me, ranks, ranks.reshape(padded, 1), picks, picks.T, cot)
 
     def exchange(value):
         dims = value.shape
@@ -808,21 +878,34 @@
             4 * weight_bytes,
         )
 
-    core_shape = shape((per // 2, rows, width), bf16)
-    by_core = pltpu.VMEM((2, per // 2, rows, width), bf16)
-    two_sems = pltpu.SemaphoreType.DMA((2,))
+    places = per // 2
+    core_shape = shape((places, rows, width), bf16)
+    by_core = pltpu.VMEM((2, places, rows, width), bf16)
+    sems = pltpu.SemaphoreType.DMA((2,))
 
     def attn_bwd(grad, value, kept, layer, which):
         return call(
             functools.partial(attn_bwd_kernel, seq),
-            (low_arr, grad, value, gain[which], gathered, *kept),
-            (SMEM, None, None, None, layer_spec(layer)) + (None,) * 5,
-            [stream_shape, gain_shape, core_shape, core_shape],
+            (grad, value, gain[which], gathered, *kept[1:4]),
+            (None, None, None, layer_spec(layer)) + (None,) * 3,
+            [stream_shape, gain_shape] + [act_shape] * 3,
             "attn_bwd",
-            11 * tok_flops,
-            8 * weight_bytes,
-            out_specs=[None, None, ANY, ANY],
-            scratch=[by_core] + [pltpu.VMEM((padded, width), bf16)] * 4 + [two_sems],
+            0,
+            0,
+            scratch=[pltpu.VMEM((padded, width), bf16)],
+        )
+
+    def attn_weights(grad, kept, found):
+        return call(
+            attn_weights_kernel,
+            (low_arr, grad, kept[0], kept[4], *found),
+            (SMEM,) + (None,) * 6,
+            [core_shape, core_shape],
+            "attn_weights",
+            0,
+            0,
+            out_specs=[ANY] * 2,
+            scratch=[by_core, sems],
         )
 
     stream_one, *kept_one = attn_fwd(stream, 0, 0)
@@ -836,142 +919,257 @@
         8 * weight_bytes,
     )
     stream_three, *kept_two = attn_fwd(stream_two, 1, 2)
+    stream_three = after(stream_three, soon)
     moe_in, probs, outgoing = call(
         dispatch_kernel,
         (stream_three, gain[3], router, picks, rows_slots),
         (None,) * 5,
         [act_shape, shape((padded, experts)), shape((slots, width + LANES), bf16)],
         "dispatch",
-        2 * padded * slots * width,
-        4e6,
+        0,
+        0,
     )
     arriving = exchange(outgoing)
 
     quarter = expert_rows // 4
-    expert_flops = 2 * slots * width * width
     slot_spec = pl.BlockSpec((slots, width), lambda q: (0, 0))
     wide_spec = pl.BlockSpec((slots, width + LANES), lambda q: (0, 0))
+    pair_spec = pl.BlockSpec((2, stride, width), lambda q: (0, 0, 0))
     hidden_spec = pl.BlockSpec((slots, width), lambda q: (0, q))
-    expert_out, input_back, slot_grad, expert_act, pre_grad = pl.pallas_call(
-        functools.partial(expert_kernel, (dp_ranks, quarter)),
+    pairs = experts // 2
+    *expert_out, input_back, slot_grad, expert_act, pre_grad = pl.pallas_call(
+        functools.partial(expert_kernel, (dp_ranks, quarter, experts), expert_spans),
         grid=(4,),
-        in_specs=[SMEM, wide_spec, slot_spec] + [ANY] * (2 * dp_ranks),
-        out_specs=[slot_spec, wide_spec, slot_spec, hidden_spec, hidden_spec],
-        out_shape=[
-            shape((slots, width), bf16),
-            shape((slots, width + LANES), bf16),
-            shape((slots, width), bf16),
-            shape((slots, hidden), bf16),
-            shape((slots, hidden), bf16),
-        ],
+        in_specs=[SMEM, wide_spec, slot_spec] + [ANY] * len(expert_parts),
+        out_specs=[pair_spec] * pairs + [wide_spec, slot_spec, hidden_spec, hidden_spec],
+        out_shape=[pair_shape] * pairs
+        + [shape((slots, width + LANES), bf16), shape((slots, width), bf16)]
+        + [shape((slots, hidden), bf16)] * 2,
         scratch_shapes=[
             pltpu.VMEM((dp_ranks, expert_rows, width), bf16),
+            pltpu.VMEM((experts, stride, width), bf16),
             pltpu.VMEM((slots, width), f32),
             pltpu.VMEM((slots, width), f32),
-            pltpu.SemaphoreType.DMA((2 * dp_ranks,)),
+            pltpu.SemaphoreType.DMA((len(expert_parts),)),
         ],
         compiler_params=params(),
-        cost_estimate=cost(16 * expert_flops, 8 * weight_bytes),
+        cost_estimate=cost(),
         name="expert",
-    )(dp_arr, arriving, arriving_cot, *expert_parts)
+    )(jnp.concatenate([dp_arr, e_me]), arriving, arriving_cot, *expert_parts)
     returned_grad = exchange(input_back)
-    part_shape = shape((dp_ranks // 2, expert_rows // 2, width), bf16)
-    expert_parts = pl.pallas_call(
+    part_shape = shape((expert_rows // 2, width), bf16)
+    expert_first = pl.pallas_call(
         functools.partial(expert_grad_kernel, (dp_ranks, quarter)),
         grid=(4,),
         in_specs=[SMEM, wide_spec, slot_spec, hidden_spec, hidden_spec],
-        out_specs=[ANY] * 4,
-        out_shape=[part_shape] * 4,
+        out_specs=[ANY] * (2 * dp_ranks),
+        out_shape=[part_shape] * (2 * dp_ranks),
         scratch_shapes=[
             pltpu.VMEM((dp_ranks, expert_rows, width), bf16),
             pltpu.SemaphoreType.DMA((2 * dp_ranks,)),
         ],
         compiler_params=params(),
-        cost_estimate=cost(8 * expert_flops, 8 * weight_bytes),
+        cost_estimate=cost(),
         name="expert_grad",
     )(dp_arr, arriving, slot_grad, expert_act, pre_grad)
-    expert_first = expert_parts[1] + swap(expert_parts[0], dp_axis, 0)
-    expert_second = expert_parts[3] + swap(expert_parts[2], dp_axis, dp_bits - 1)
-    expert_sums = (
-        reduce_low(expert_first, dp_axis, dp_order[1:]),
-        reduce_high(expert_second, dp_axis, dp_order[:-1]),
-    )
+    count = dp_ranks // 2
+    expert_first = [expert_first[i * count : (i + 1) * count] for i in range(4)]
+    returned_grad = after(returned_grad, expert_first)
+
+    per_bits = per.bit_length() - 1
+    cut = max(16, rows // 96 * 16)
+    middle = (rows - cut) // 2
+    top_bits = (per_bits, per_bits + 1)
+    top = (me >> per_bits).reshape(1)
+    z_bits = list(range(1, per_bits))
+    z_masks = [2 * j for j in (1, 2, 3)]
+    assert places % 4 == 0
+
+    def over_z(values):
+        return [values[0]] + [swap(value, both, mask) for value, mask in zip(values[1:], z_masks)]
+
+    def rest_of_z(values):
+        if len(z_bits) == 2:
+            return values
+        total = sum(value.astype(f32) for value in values).astype(bf16)
+        lead = total.ndim - 3
+        total = jnp.moveaxis(total, lead, 0)
+        return [reduce_bits(total, both, z_bits[2:])]
 
     grad, gain_four, router_grad = call(
         combine_kernel,
         (stream_three, gain[3], router, picks, cols, cot, moe_in, probs, returned_grad),
         (None,) * 9,
-        [stream_shape, gain_shape, shape((width, experts))],
+        [stream_shape, gain_shape, shape((experts, width))],
         "combine",
-        2 * padded * slots * width,
-        6e6,
+        0,
+        0,
     )
-    grad, gain_three, *second_dw = attn_bwd(grad, stream_two, kept_two, 1, 2)
+    def to_other_core(parts):
+        return [parts[0], swap(parts[1], both, 1)]
+
+    expert_got = [
+        [swap(value[i], dp_axis, mask) for i in range(dp_ranks // 2)]
+        for value, mask in ((expert_first[0], 1), (expert_first[2], dp_ranks // 2))
+    ]
+    upper = grad
+    grad, gain_three, *found = attn_bwd(upper, stream_two, kept_two, 1, 2)
+    second_dw = to_other_core(attn_weights(upper, kept_two, found))
+
     mlp_out = [core_shape, core_shape]
-    mlp_scratch = [by_core]
-    if wide_ok:
-        mlp_out, mlp_scratch = mlp_out * 2, mlp_scratch * 2
-    else:
-        mlp_out = mlp_out + [shape((1, 4 * width, width), bf16)]
+    mlp_out = mlp_out * 2 if wide_ok else mlp_out + [shape((1, 4 * width, width), bf16)]
     grad, gain_two, *mlp_dw = call(
         functools.partial(mlp_bwd_kernel, wide_ok),
         (low_arr, grad, stream_one, gain[1], first_in, gathered, mlp_in, mlp_pre),
         (SMEM, None, None, None, first_spec, layer_spec(3), None, None),
         [stream_shape, gain_shape] + mlp_out,
         "mlp_bwd",
-        16 * tok_flops,
-        16 * weight_bytes,
-        out_specs=[None, None] + [ANY if len(o.shape) == 3 and o.shape == core_shape.shape else None for o in mlp_out],
-        scratch=mlp_scratch + [two_sems],
+        0,
+        0,
+        out_specs=[None, None] + ([ANY] * 4 if wide_ok else [ANY] * 2 + [None]),
+        scratch=[by_core] * (2 if wide_ok else 1) + [sems],
     )
     if not wide_ok:
         wide_grad = mlp_dw[2].reshape(4, width, width).transpose(1, 0, 2).reshape(per, rows, width)
         wide_grad = jnp.take(wide_grad, jnp.arange(per) ^ low, axis=0)
-        wide_grad = wide_grad.reshape(per // 2, 2, rows, width)
+        wide_grad = wide_grad.reshape(places, 2, rows, width)
         mlp_dw = mlp_dw[:2] + [wide_grad[:, 0], wide_grad[:, 1]]
-    grad, gain_one, *first_dw = attn_bwd(grad, stream, kept_one, 0, 0)
-
-    per_bits = per.bit_length() - 1
-    cut = rows // 32 * 16
-    top = (per_bits, per_bits + 1)
-    z_bits = list(range(1, per_bits))
-    layers = []
-    for keep, send in (second_dw, mlp_dw[:2], mlp_dw[2:], first_dw):
-        arrived = swap(send, both, 0)
-        upper = reduce_low(keep[:, :cut] + arrived[:, :cut], both, z_bits)
-        layers.append((upper, keep[:, cut:] + arrived[:, cut:]))
-    layers = [layers[i] for i in (3, 0, 2, 1)]
-    pieces = []
-    for low_first in (True, False):
-        at = slice(0, cut // 2) if low_first else slice(cut // 2, cut)
-        pieces.append(reduce_layers([u[at] for u, _ in layers], both, top, me, low_first))
-    for low_first in (True, False):
-        middle = (rows - cut) // 2
-        at = slice(0, middle) if low_first else slice(middle, rows - cut)
-        part = reduce_layers([v[:, at] for _, v in layers], both, top, me, low_first)
-        pieces.append(reduce_low(part, both, z_bits))
+    mlp_dw = [to_other_core(mlp_dw[i : i + 2]) for i in (0, 2)]
+
+    upper = grad
+    grad, gain_one, *found = attn_bwd(upper, stream, kept_one, 0, 0)
+    found, expert_got = lax.optimization_barrier((found, expert_got))
+    first_dw = to_other_core(attn_weights(upper, kept_one, found))
+
+    small = call(
+        stack_rows_kernel,
+        (router_grad, gain_one, gain_two, gain_three, gain_four),
+        (None,) * 5,
+        [shape((experts + 4, width))],
+        "stack_rows",
+        0,
+        0,
+    )[0]
+    found_small = small
+    small = jnp.sum(lax.all_gather(small, both, axis=0, tiled=False), axis=0)
+
+    plane_shape = shape((2, places, middle, width), bf16)
+    plane_spec = pl.BlockSpec((2, 1, middle, width), lambda i: (0, i, 0, 0))
+    line_shape = shape((places, middle, width), bf16)
+    line_spec = pl.BlockSpec((1, middle, width), lambda i: (i, 0, 0))
+    upper_shape = shape((4, places // 4, cut, width), bf16)
+    part_spec = pl.BlockSpec((1, rows, width), lambda i: (i, 0, 0))
+    layers = (first_dw, second_dw, mlp_dw[1], mlp_dw[0])
+    *uppers, send_x, keep_x, send_y, keep_y = pl.pallas_call(
+        functools.partial(fold_layers_kernel, cut),
+        grid=(places,),
+        in_specs=[SMEM] + [part_spec] * 8,
+        out_specs=[pl.BlockSpec(upper_shape.shape, lambda i: (0, 0, 0, 0))] * 4 + [plane_spec] * 4,
+        out_shape=[upper_shape] * 4 + [plane_shape] * 4,
+        scratch_shapes=[pltpu.VMEM((4, rows - cut, width), bf16)],
+        compiler_params=params(),
+        cost_estimate=cost(),
+        name="fold_layers",
+    )(top, *[part for layer in layers for part in layer])
+    masks = [1 << bit for bit in top_bits]
+    got_x, got_y = swap(send_x, both, masks[0]), swap(send_y, both, masks[1])
+    uppers = over_z(uppers)
+    expert_ins = [part for i in (0, 1) for group in (expert_first[2 * i + 1], expert_got[i]) for part in group]
+    expert_second = call(
+        functools.partial(fold_expert_kernel, (dp_bits == 1, True)),
+        expert_ins,
+        (None,) * len(expert_ins),
+        [part_shape] * (2 * count),
+        "fold_expert",
+        0,
+        0,
+    )
+
+    uppers = [value.reshape(4, -1, cut, width) for value in uppers]
+    uppers = [value.reshape(4, cut, width) for value in rest_of_z(uppers)]
+    uppers, expert_second = lax.optimization_barrier((uppers, expert_second))
+    upper_rows = call(
+        fold_uppers_kernel,
+        (top, *uppers),
+        (SMEM,) + (None,) * len(uppers),
+        [shape((cut, width), bf16)] * 4,
+        "fold_uppers",
+        0,
+        0,
+        scratch=[pltpu.VMEM((4, cut, width), bf16)],
+    )
+    got_x, got_y, upper_rows = lax.optimization_barrier((got_x, got_y, upper_rows))
+
+    expert_out = after(expert_out, upper_rows)
+    expert_out = [expert_out[0]] + [swap(v, ("expert",), 2 * j) for j, v in enumerate(expert_out) if j]
+    own_a, send_y, own_b, send_x = pl.pallas_call(
+        fold_plane_kernel,
+        grid=(places,),
+        in_specs=[plane_spec] * 4,
+        out_specs=[line_spec] * 4,
+        out_shape=[line_shape] * 4,
+        compiler_params=params(),
+        cost_estimate=cost(),
+        name="fold_plane",
+    )(keep_x, got_x, keep_y, got_y)
+    got_y, got_x = swap(send_y, both, masks[1]), swap(send_x, both, masks[0])
+    got_x, got_y, expert_out = lax.optimization_barrier((got_x, got_y, expert_out))
+    other_out = swap(jnp.stack([value[1] for value in expert_out]), ("expert",), 1)
+    lower_rows = call(
+        fold_rows_kernel,
+        (own_a, got_y, own_b, got_x),
+        (None,) * 4,
+        [shape((places // 4, rows - cut, width), bf16)] * 4,
+        "fold_rows",
+        0,
+        0,
+    )
+    lower_rows, other_out, expert_second, _ = lax.optimization_barrier((lower_rows, other_out, expert_second, found_small))
+    lower_rows = over_z(lower_rows)
+    half = count // 2
+    expert_groups = []
+    for side, bits in enumerate(orders):
+        keep, send = (expert_second[(2 * side + i) * half : (2 * side + i + 1) * half] for i in range(2))
+        got = [swap(part, dp_axis, 1 << bits[1]) for part in send]
+        expert_groups.append([list(pair) for pair in zip(keep, got)])
+    if dp_bits > 2:
+        for side, bits in enumerate(orders):
+            value = [sum(pair) for pair in expert_groups[side]]
+            for bit in bits[2:]:
+                half = len(value) // 2
+                keep, send = (value[:half], value[half:]) if side else (value[0::2], value[1::2])
+                value = [k + swap(v, dp_axis, 1 << bit) for k, v in zip(keep, send)]
+            expert_groups[side] = [value]
+    expert_groups = [side[0] for side in expert_groups]
+    upper_rows, expert_groups = lax.optimization_barrier((upper_rows, expert_groups))
 
     output = call(
         output_kernel,
-        (stream_three, picks, cols, probs, exchange(expert_out)),
-        (None,) * 5,
+        (stream_three, picks, near_cols, probs, *expert_out, other_out),
+        (None,) * (5 + pairs),
         [shape((seq, width))],
         "output",
-        4 * padded * slots * width,
-        4e6,
+        0,
+        0,
+        scratch=[pltpu.VMEM((slots, width), f32)],
     )[0]
 
-    small = jnp.concatenate(
-        [router_grad.reshape(-1)] + [g.reshape(-1) for g in (gain_one, gain_two, gain_three, gain_four)]
-    )
-    small = jnp.pad(small, (0, tail * LANES - small.shape[0])).reshape(tail, LANES)
-    small = all_sum(small, both, all_bits)
-    gain_at = width * experts
-    gain_grads = small.reshape(-1)[gain_at : gain_at + 4 * width].reshape(4, width)
-
-    def unpack(wide, pieces, count, name):
+    lower_rows, output = lax.optimization_barrier((lower_rows, output))
+    lower_rows = rest_of_z(lower_rows)
+    upper_rows = [upper_rows[0]] + [
+        swap(value, both, masks[0] * j) for j, value in enumerate(upper_rows) if j
+    ]
+    dense_groups = [upper_rows, [value.reshape(rows - cut, width) for value in lower_rows]]
+
+    gain_grads = small[experts:]
+    small_square = jnp.sum(small * small)
+    small = jnp.concatenate([small[:experts].T.reshape(-1, LANES), gain_grads.reshape(-1, LANES)])
+    small = jnp.pad(small, ((0, tail - small.shape[0]), (0, 0)))
+
+    def unpack(wide, groups, count, name):
+        pieces = [piece for group in groups for piece in group]
         return pl.pallas_call(
-            functools.partial(unpack_kernel, (count, tiles)),
+            functools.partial(unpack_kernel, (count, tiles), [len(group) for group in groups]),
             in_specs=[SMEM] + [VMEM] * len(pieces),
             out_specs=[VMEM, VMEM],
             out_shape=[shape((count * tiles, LANES)), shape((1, LANES))],
@@ -981,24 +1179,26 @@
             name=name,
         )(wide, *pieces)
 
-    expert_grad, expert_square = unpack(expert_wide, expert_sums, expert_rows, "unpack_expert")
+    expert_grad, expert_square = unpack(expert_wide, expert_groups, expert_rows, "unpack_expert")
     dense_wide = (me >= devices // 2) & (me < 3 * devices // 4) & wide_ok
-    dense_rows, _ = unpack(dense_wide.astype(jnp.int32).reshape(1), pieces, rows, "unpack_dense")
+    dense_rows, dense_square = unpack(dense_wide.astype(jnp.int32).reshape(1), dense_groups, rows, "unpack_dense")
     head = lax.ppermute(dense_rows[:tail], both, backward_ring)
     head = jnp.where(me == devices - 1, small, head)
-    dense_grad, dense_square = pl.pallas_call(
+    dense_grad = pl.pallas_call(
         functools.partial(shift_kernel, (step, own)),
         in_specs=[SMEM, VMEM, VMEM],
-        out_specs=[VMEM, VMEM],
-        out_shape=[shape((own, LANES)), shape((1, LANES))],
+        out_specs=VMEM,
+        out_shape=shape((own, LANES)),
         scratch_shapes=[pltpu.VMEM((-(-(rows * tiles + tail) // 8) * 8, LANES), f32)],
         compiler_params=params(),
         cost_estimate=cost(0, 8 * rows * width),
         name="shift_dense",
     )(me_arr, dense_rows, head)
 
-    square = all_sum(dense_square + expert_square, both, all_bits)
-    square_sum = jnp.sum(square)
+    square = dense_square + expert_square
+    for bits in bit_groups(list(range(all_bits))):
+        square = all_sum_step(square, both, bits)
+    square_sum = jnp.sum(square) + small_square
     param_count = (dense_master.size + expert_master.size) * devices
     clip_factor = jnp.minimum(1.0, jnp.sqrt(param_count / (square_sum + 1e-06))).reshape(1)
 

time: 620 us -> 549 us (0.89)
  waiting for transfers between devices: 362 us -> 266 us
  Pallas kernels: 142 us -> 178 us
  other arithmetic: 22 us -> 6.22 us
  starting transfers between devices: 52.3 us -> 66.6 us
    ppermute x44 -> x40, waiting for transfers between devices: 226 us -> 138 us  [swap(): return lax.ppermute(value, axes, [(i, i ^ mask) for i in range(size)])]
    all_gather x1, waiting for transfers between devices: 121 us -> 102 us  [on_device(): gathered = lax.all_gather(chunk, both, axis=0, tiled=True)]
    pallas_call x3 -> x5, Pallas kernels: 25.6 us -> 45 us  [the longest x1 18 us: on_device(): pl.pallas_call(functools.partial(expert_kernel, (dp_ranks, quarter, exper...]
    pallas_call x9 -> x15, Pallas kernels: 75.8 us -> 92.5 us  [call(): pl.pallas_call(kernel, grid=(1,), in_specs=[s or whole(a) for a, s in zip...]
    all_gather x0 -> x1, waiting for transfers between devices: none -> 13.7 us  [on_device(): small = jnp.sum(lax.all_gather(small, both, axis=0, tiled=False), axis=0)]
    add x22 -> x3, other arithmetic: 11.8 us -> 0.67 us  [the longest x1 0.66 us: on_device(): square = dense_square + expert_square]
    all_to_all x4 -> x3, starting transfers between devices: 16 us -> 24.1 us  [exchange(): lax.all_to_all(value, 'expert', split_axis=0, concat_axis=0, tiled=True)]
    ppermute x44 -> x40, starting transfers between devices: 35.8 us -> 40.5 us  [swap(): return lax.ppermute(value, axes, [(i, i ^ mask) for i in range(size)])]
  transfers between devices with their start and end apart: 51 -> 47, of which waited for: 29 -> 26; matrix products, arithmetic and copies ran while one was open for 6% -> 3% of each run, Pallas kernels for 17% -> 20%
where the time goes in v3:
time: 549 us; the launch traced here: 550 us
  waiting for transfers between devices  266 us (48%)
  Pallas kernels  178 us (32%)
  starting transfers between devices  66.6 us (12%)
  local copies, waits for them, and re-layouts  17.2 us (3%)
  between operations  16 us (3%)
  other arithmetic  6.22 us (1%)
    ppermute x40, waiting for transfers between devices, swap(): return lax.ppermute(value, axes, [(i, i ^ mask) for i in range(size)])  138 us
    all_gather x1, waiting for transfers between devices, on_device(): gathered = lax.all_gather(chunk, both, axis=0, tiled=True)  102 us
    pallas_call x15, Pallas kernels, call(): pl.pallas_call(kernel, grid=(1,), in_specs=[s or whole(a) for a, s in zip...  92.5 us
    ppermute x40, starting transfers between devices, swap(): return lax.ppermute(value, axes, [(i, i ^ mask) for i in range(size)])  40.5 us
    all_to_all x3, starting transfers between devices, exchange(): lax.all_to_all(value, 'expert', split_axis=0, concat_axis=0, tiled=True)  24.1 us
    pallas_call x1, Pallas kernels, on_device(): pl.pallas_call(functools.partial(expert_kernel, (dp_ranks, quarter, exper...  18 us
    pallas_call x2, Pallas kernels, adam(): pl.pallas_call(adam_kernel, grid=(pl.cdiv(count, block),), in_specs=[SMEM...  16.5 us
    all_gather x1, waiting for transfers between devices, on_device(): small = jnp.sum(lax.all_gather(small, both, axis=0, tiled=False), axis=0)  13.7 us
  transfers between devices with their start and end apart: 47, of which 26 were waited for; matrix products, arithmetic and copies ran while one was open for 3% of the time, Pallas kernels for 20%

profile of v3, /device:TPU:0, one launch (start us, length us, event | category | flops | bytes accessed | tf_op | source)
XLA Modules:
  0.0 550.0 jit_solution(8732476461119800148)
XLA Ops:
  8.5 7.7 %collective-permute-done.tail_ref = f32[96,128]{1,0:T(8,128)S(1)} collective-permute-done((f32[96,128]{1,0:T(8,128)S(1)}, f32[96,128]{1,0:T(8,128)S(1)}, u32[]{:S(2)}, u32[]{:S(2)}) %collective-permute-start) | collective-permute-done | bytes 49184 | tf_op jit(solution)/shard_map/ppermute | solution.py:750
  36.1 16.7 %collective-permute-done.1.refs_1_ = bf16[768,768]{1,0:T(8,128)(2,1)} collective-permute-done((bf16[768,768]{1,0:T(8,128)(2,1)}, bf16[768,768]{1,0:T(8,128)(2,1)}, u32[]{:S(2)}, u32[]{:S(2)}) %collective-permute-start.1) | collective-permute-done | bytes 1179680 | tf_op jit(solution)/shard_map/ppermute | solution.py:677
  54.0 101.7 %all-gather.5.cloned.1.call-done = bf16[12800,768]{1,0:T(8,128)(2,1)} async-done(((bf16[400,768]{1,0:T(8,128)(2,1)}), bf16[12800,768]{1,0:T(8,128)(2,1)}) %all-gather.5.cloned.1.call-update) | async-done | bytes 19660816 | tf_op jit(solution)/shard_map/all_gather | solution.py:764
  159.9 6.5 %attn_fwd.2 = (f32[208,768]{1,0:T(8,128)}, bf16[208,768]{1,0:T(8,128)(2,1)}, bf16[208,768]{1,0:T(8,128)(2,1)}, bf16[208,768]{1,0:T(8,128)(2,1)}, bf16[208,768]{1,0:T(8,128)(2,1)}, /*index=5*/bf16[208,768]{1,0:T(8,128)(2,1)}) custom-call(f32[208,768]{1,0:T(8,128)} %pad_convert_fusion.stream_ref, f32[1,768]{1,0:T(1,128)} %get-tuple-element.363.gain_ref, ...), custom_call_target="tpu_custom_call" | custom-call | flops 1 | bytes 1 | tf_op jit(solution)/shard_map/attn_fwd/pallas_call | solution.py:858
  166.4 8.1 %mlp_fwd.1 = (f32[208,768]{1,0:T(8,128)}, bf16[208,768]{1,0:T(8,128)(2,1)}, f32[208,3072]{1,0:T(8,128)}) custom-call(f32[208,768]{1,0:T(8,128)} %get-tuple-element.171.stream_ref, f32[1,768]{1,0:T(1,128)} %get-tuple-element.362.gain_ref, bf16[32,400,768]{2,1,0:T(8,128)(2,1)} %bitcast.64, bf16[32,400,768]{2,1,0:T(8,128)(2,1)} %bitcast.65), custom_call_target="tpu_custom_call" | custom-call | flops 1 | bytes 1 | tf_op jit(solution)/shard_map/mlp_fwd/pallas_call | solution.py:858
  174.5 6.5 %attn_fwd.3 = (f32[208,768]{1,0:T(8,128)}, bf16[208,768]{1,0:T(8,128)(2,1)}, bf16[208,768]{1,0:T(8,128)(2,1)}, bf16[208,768]{1,0:T(8,128)(2,1)}, bf16[208,768]{1,0:T(8,128)(2,1)}, /*index=5*/bf16[208,768]{1,0:T(8,128)(2,1)}) custom-call(f32[208,768]{1,0:T(8,128)} %get-tuple-element.172.stream_ref, f32[1,768]{1,0:T(1,128)} %get-tuple-element.361.gain_ref, ...), custom_call_target="tpu_custom_call" | custom-call | flops 1 | bytes 1 | tf_op jit(solution)/shard_map/attn_fwd/pallas_call | solution.py:858
  188.4 15.3 %all-to-all-start = ((bf16[8,56,896]{2,1,0:T(8,128)(2,1)}), bf16[8,56,896]{2,1,0:T(8,128)(2,1)S(1)}, u32[]{:S(2)}, u32[]{:S(2)}) async-start(bf16[8,56,896]{2,1,0:T(8,128)(2,1)} %bitcast.86), calls=%async_computation | async-start | bytes 1605632 | tf_op jit(solution)/shard_map/all_to_all | solution.py:820
  206.4 25.7 %collective-permute-done.5.refs_3_ = bf16[768,768]{1,0:T(8,128)(2,1)S(1)} collective-permute-done((bf16[768,768]{1,0:T(8,128)(2,1)}, bf16[768,768]{1,0:T(8,128)(2,1)S(1)}, u32[]{:S(2)}, u32[]{:S(2)}) %collective-permute-start.5) | collective-permute-done | bytes 1179680 | tf_op jit(solution)/shard_map/ppermute | solution.py:677
  233.3 18.0 %expert.1 = (bf16[2,56,768]{2,1,0:T(8,128)(2,1)}, bf16[2,56,768]{2,1,0:T(8,128)(2,1)}, bf16[2,56,768]{2,1,0:T(8,128)(2,1)}, bf16[2,56,768]{2,1,0:T(8,128)(2,1)},...) custom-call(s32[2]{0:T(128)} %pad_add_fusion.me_ref, ...), custom_call_target="tpu_custom_call" | custom-call | flops 1 | bytes 1 | tf_op jit(solution)/shard_map/expert/pallas_call | solution.py:940
  256.1 11.8 %expert_grad.1 = (bf16[768,768]{1,0:T(8,128)(2,1)}, bf16[768,768]{1,0:T(8,128)(2,1)}, bf16[768,768]{1,0:T(8,128)(2,1)}, bf16[768,768]{1,0:T(8,128)(2,1)}, bf16[7...) custom-call(s32[1]{0:T(128)} %bitcast.17.dp_ref, ...), custom_call_target="tpu_custom_call" | custom-call | flops 1 | bytes 1 | tf_op jit(solution)/shard_map/expert_grad/pallas_call | solution.py:961
  282.2 10.5 %attn_bwd.2 = (f32[208,768]{1,0:T(8,128)}, f32[1,768]{1,0:T(1,128)}, bf16[208,768]{1,0:T(8,128)(2,1)}, bf16[208,768]{1,0:T(8,128)(2,1)}, bf16[208,768]{1,0:T(8,128)(2,1)}) custom-call(f32[208,768]{1,0:T(8,128)} %get-tuple-element.198.grad_ref, f32[208,768]{1,0:T(8,128)} %get-tuple-element.172.stream_ref, f32[1,768]{1,0:T(1,128)} %get-tuple-element.361.gain_ref, ...), custom_call_target="tpu_custom_call" | custom-call | flops 1 | bytes 1 | tf_op jit(solution)/shard_map/attn_bwd/pallas_call | solution.py:858
  292.7 16.0 %mlp_bwd.1 = (f32[208,768]{1,0:T(8,128)}, f32[1,768]{1,0:T(1,128)}, bf16[4,384,768]{2,1,0:T(8,128)(2,1)}, bf16[4,384,768]{2,1,0:T(8,128)(2,1)}, bf16[4,384,768]{...) custom-call(s32[1]{0:T(128)} %bitcast.1.low_ref, f32[208,768]{1,0:T(8,128)} %get-tuple-element.202.grad_ref, ...), custom_call_target="tpu_custom_call" | custom-call | flops 1 | bytes 1 | tf_op jit(solution)/shard_map/mlp_bwd/pallas_call | solution.py:858
  308.7 10.5 %attn_bwd.3 = (f32[208,768]{1,0:T(8,128)}, f32[1,768]{1,0:T(1,128)}, bf16[208,768]{1,0:T(8,128)(2,1)}, bf16[208,768]{1,0:T(8,128)(2,1)}, bf16[208,768]{1,0:T(8,128)(2,1)}) custom-call(f32[208,768]{1,0:T(8,128)} %get-tuple-element.205.grad_ref, f32[208,768]{1,0:T(8,128)} %pad_convert_fusion.stream_ref, f32[1,768]{1,0:T(1,128)} %get-tuple-element.363.gain_ref, ...), custom_call_target="tpu_custom_call" | custom-call | flops 1 | bytes 1 | tf_op jit(solution)/shard_map/attn_bwd/pallas_call | solution.py:858
  345.7 12.1 %fold_layers.1 = (bf16[4,1,64,768]{3,2,1,0:T(8,128)(2,1)}, bf16[4,1,64,768]{3,2,1,0:T(8,128)(2,1)}, bf16[4,1,64,768]{3,2,1,0:T(8,128)(2,1)}, bf16[4,1,64,768]{3,...) custom-call(s32[1]{0:T(128)} %bitcast.top_ref, ...), custom_call_target="tpu_custom_call" | custom-call | flops 1 | bytes 1 | tf_op jit(solution)/shard_map/fold_layers/pallas_call | solution.py:1063
  364.3 6.2 %fold_expert.1 = (bf16[768,768]{1,0:T(8,128)(2,1)}, bf16[768,768]{1,0:T(8,128)(2,1)}, bf16[768,768]{1,0:T(8,128)(2,1)}, bf16[768,768]{1,0:T(8,128)(2,1)}) custom-call(bf16[768,768]{1,0:T(8,128)(2,1)} %get-tuple-element.191.refs_0_, bf16[768,768]{1,0:T(8,128)(2,1)} %get-tuple-element.192.refs_1_, bf16[768,768]{1,0:T(8,128)(2,1)} %copy-done.8, ...), custom_call_target="tpu_custom_call" | custom-call | flops 1 | bytes 1 | tf_op jit(solution)/shard_map/fold_expert/pallas_call | solution.py:858
  370.4 8.1 %collective-permute-done.17 = bf16[4,1,64,768]{3,2,0,1:T(8,128)(2,1)S(1)} collective-permute-done((bf16[4,1,64,768]{3,2,0,1:T(8,128)(2,1)}, bf16[4,1,64,768]{3,2,0,1:T(8,128)(2,1)S(1)}, u32[]{:S(2)}, u32[]{:S(2)}) %collective-permute-start.17) | collective-permute-done | bytes 393248 | tf_op jit(solution)/shard_map/ppermute | solution.py:677
  378.5 13.1 %collective-permute-done.18 = bf16[4,1,64,768]{3,2,0,1:T(8,128)(2,1)S(1)} collective-permute-done((bf16[4,1,64,768]{3,2,0,1:T(8,128)(2,1)}, bf16[4,1,64,768]{3,2,0,1:T(8,128)(2,1)S(1)}, u32[]{:S(2)}, u32[]{:S(2)}) %collective-permute-start.18) | collective-permute-done | bytes 393248 | tf_op jit(solution)/shard_map/ppermute | solution.py:677
  394.8 8.3 %collective-permute-done.15.got_x = bf16[2,4,160,768]{3,2,1,0:T(8,128)(2,1)S(1)} collective-permute-done((bf16[2,4,160,768]{3,2,1,0:T(8,128)(2,1)}, bf16[2,4,160,768]{3,2,1,0:T(8,128)(2,1)S(1)}, u32[]{:S(2)}, u32[]{:S(2)}) %collective-permute-start.15) | collective-permute-done | bytes 1966112 | tf_op jit(solution)/shard_map/ppermute | solution.py:677
  405.1 5.7 %fold_plane.1 = (bf16[4,160,768]{2,1,0:T(8,128)(2,1)}, bf16[4,160,768]{2,1,0:T(8,128)(2,1)}, bf16[4,160,768]{2,1,0:T(8,128)(2,1)}, bf16[4,160,768]{2,1,0:T(8,128)(2,1)}) custom-call(bf16[2,4,160,768]{3,2,1,0:T(8,128)(2,1)} %get-tuple-element.230.keep_x, bf16[2,4,160,768]{3,2,1,0:T(8,128)(2,1)} %copy-done.5, ...), custom_call_target="tpu_custom_call" | custom-call | flops 1 | bytes 1 | tf_op jit(solution)/shard_map/fold_plane/pallas_call | solution.py:1105
  421.8 9.8 %collective-permute-done.23.refs_2_ = bf16[2,56,768]{2,1,0:T(8,128)(2,1)S(1)} collective-permute-done((bf16[2,56,768]{2,1,0:T(8,128)(2,1)S(1)}, bf16[2,56,768]{2,1,0:T(8,128)(2,1)S(1)}, u32[]{:S(2)}, u32[]{:S(2)}) %collective-permute-start.23) | collective-permute-done | bytes 172064 | tf_op jit(solution)/shard_map/ppermute | solution.py:677
  446.7 24.6 %collective-permute-done.29.refs_1_ = bf16[768,768]{1,0:T(8,128)(2,1)S(1)} collective-permute-done((bf16[768,768]{1,0:T(8,128)(2,1)}, bf16[768,768]{1,0:T(8,128)(2,1)S(1)}, u32[]{:S(2)}, u32[]{:S(2)}) %collective-permute-start.29) | collective-permute-done | bytes 1179680 | tf_op jit(solution)/shard_map/ppermute | solution.py:677
  477.2 13.7 %all-gather.7.cloned.1.call-done = f32[32,12,768]{2,1,0:T(8,128)} async-done(((f32[1,12,768]{2,1,0:T(8,128)}), f32[32,12,768]{2,1,0:T(8,128)}) %all-gather.7.cloned.1.call-update) | async-done | bytes 1179664 | tf_op jit(solution)/shard_map/all_gather | solution.py:1054
  495.4 6.1 %unpack_expert.1 = (f32[9216,128]{1,0:T(8,128)}, f32[1,128]{1,0:T(1,128)}) custom-call(s32[1]{0:T(128)} %bitcast.7.wide_ref, bf16[768,768]{1,0:T(8,128)(2,1)} %get-tuple-element.312.refs_0_, bf16[768,768]{1,0:T(8,128)(2,1)} %copy-done.9, bf16[768,768]{1,0:T(8,128)(2,1)} %get-tuple-element.314.refs_2_, bf16[768,768]{1,0:T(8,128)(2,1)} %copy-done.10), custom_call_target="tpu_custom_call" | custom-call | flops 1 | bytes 1 | tf_op jit(solution)/shard_map/unpack_expert/pallas_call | solution.py:1171
  524.1 12.3 %adam.3 = (f32[9216,128]{1,0:T(8,128)}, f32[9216,128]{1,0:T(8,128)}, f32[9216,128]{1,0:T(8,128)}) custom-call(f32[1]{0:T(128)} %bitcast.42.clip_ref, f32[9216,128]{1,0:T(8,128)} %get-tuple-element.316.grad_ref, f32[9216,128]{1,0:T(8,128)} %bitcast.76, f32[9216,128]{1,0:T(8,128)} %bitcast.77), custom_call_target="tpu_custom_call" | custom-call | flops 1 | bytes 1 | tf_op jit(solution)/shard_map/adam/pallas_call | solution.py:204
  (205 shorter events, 159.2 us)
Async XLA Ops:
  7.2 148.5 %all-gather.5.cloned.1.call-start = ((), (), s32[]{:S(2)}) async-start(), calls=%async_computation.3 | async-start | bytes 20275200 | tf_op jit(solution)/shard_map/all_gather | solution.py:764
  24.0 28.8 %collective-permute-start.1 = (bf16[768,768]{1,0:T(8,128)(2,1)}, bf16[768,768]{1,0:T(8,128)(2,1)}, u32[]{:S(2)}, u32[]{:S(2)}) collective-permute-start(bf16[768,768]{1,0:T(8,128)(2,1)} %get-tuple-element.174.refs_0_), channel_id=1, source_target_pairs={{0,8},{8,0},{16,24},{24,16},{1,9},{9,1},{17,25},{25,17},{2,10},{10... | collective-permute-start | bytes 3538952 | tf_op jit(solution)/shard_map/ppermute | solution.py:677
  25.0 29.0 %collective-permute-start.2 = (bf16[768,768]{1,0:T(8,128)(2,1)}, bf16[768,768]{1,0:T(8,128)(2,1)}, u32[]{:S(2)}, u32[]{:S(2)}) collective-permute-start(bf16[768,768]{1,0:T(8,128)(2,1)} %get-tuple-element.175.refs_4_), channel_id=1, source_target_pairs={{0,16},{8,24},{16,0},{24,8},{1,17},{9,25},{17,1},{25,9},{2,18},{10... | collective-permute-start | bytes 3538952 | tf_op jit(solution)/shard_map/ppermute | solution.py:677
  32.2 156.2 %all-to-all-start.1 = ((bf16[8,56,768]{2,1,0:T(8,128)(2,1)}), bf16[8,56,768]{2,1,0:T(8,128)(2,1)S(1)}, u32[]{:S(2)}, u32[]{:S(2)}) async-start(bf16[8,56,768]{2,1,0:T(8,128)(2,1)} %bitcast.87), calls=%async_computation.1 | async-start | bytes 1376256 | tf_op jit(solution)/shard_map/all_to_all | solution.py:820
  155.7 28.2 %collective-permute-start.3 = (bf16[768,768]{1,0:T(8,128)(2,1)S(1)}, bf16[768,768]{1,0:T(8,128)(2,1)}, u32[]{:S(2)}, u32[]{:S(2)}) collective-permute-start(bf16[768,768]{1,0:T(8,128)(2,1)S(1)} %copy-done.11), channel_id=1, source_target_pairs={{0,16},{8,24},{16,0},{24,8},{1,17},{9,25},{17,1},{25,9},{2,18},{10... | collective-permute-start | bytes 3538952 | tf_op jit(solution)/shard_map/ppermute | solution.py:677
  157.1 28.0 %collective-permute-start.4 = (bf16[768,768]{1,0:T(8,128)(2,1)S(1)}, bf16[768,768]{1,0:T(8,128)(2,1)}, u32[]{:S(2)}, u32[]{:S(2)}) collective-permute-start(bf16[768,768]{1,0:T(8,128)(2,1)S(1)} %copy-done.12), channel_id=1, source_target_pairs={{0,8},{8,0},{16,24},{24,16},{1,9},{9,1},{17,25},{25,17},{2,10},{10... | collective-permute-start | bytes 3538952 | tf_op jit(solution)/shard_map/ppermute | solution.py:677
  188.4 44.0 %all-to-all-start = ((bf16[8,56,896]{2,1,0:T(8,128)(2,1)}), bf16[8,56,896]{2,1,0:T(8,128)(2,1)S(1)}, u32[]{:S(2)}, u32[]{:S(2)}) async-start(bf16[8,56,896]{2,1,0:T(8,128)(2,1)} %bitcast.86), calls=%async_computation | async-start | bytes 1605632 | tf_op jit(solution)/shard_map/all_to_all | solution.py:820
  203.8 28.3 %collective-permute-start.5 = (bf16[768,768]{1,0:T(8,128)(2,1)}, bf16[768,768]{1,0:T(8,128)(2,1)S(1)}, u32[]{:S(2)}, u32[]{:S(2)}) collective-permute-start(bf16[768,768]{1,0:T(8,128)(2,1)} %collective-permute-done.1.refs_1_), channel_id=1, source_target_pairs={{0,16},{8,24},{16,0},{24,8},{1,17},{9,25},{17,1},{25,9},{2,18},{10... | collective-permute-start | bytes 3538952 | tf_op jit(solution)/shard_map/ppermute | solution.py:677
  204.4 28.0 %collective-permute-start.6 = (bf16[768,768]{1,0:T(8,128)(2,1)}, bf16[768,768]{1,0:T(8,128)(2,1)}, u32[]{:S(2)}, u32[]{:S(2)}) collective-permute-start(bf16[768,768]{1,0:T(8,128)(2,1)} %collective-permute-done.2.refs_6_), channel_id=1, source_target_pairs={{0,8},{8,0},{16,24},{24,16},{1,9},{9,1},{17,25},{25,17},{2,10},{10... | collective-permute-start | bytes 3538952 | tf_op jit(solution)/shard_map/ppermute | solution.py:677
  256.1 234.8 %all-gather.7.cloned.1.call-start = ((), (), s32[]{:S(2)}) async-start(), calls=%async_computation.4 | async-start | bytes 1622016 | tf_op jit(solution)/shard_map/all_gather | solution.py:1054
  267.9 51.4 %collective-permute-start.10 = (bf16[768,768]{1,0:T(8,128)(2,1)}, bf16[768,768]{1,0:T(8,128)(2,1)S(1)}, u32[]{:S(2)}, u32[]{:S(2)}) collective-permute-start(bf16[768,768]{1,0:T(8,128)(2,1)} %get-tuple-element.194), channel_id=1, source_target_pairs={{0,16},{8,24},{16,0},{24,8},{1,17},{9,25},{17,1},{25,9},{2,18},{10... | collective-permute-start | bytes 3538952 | tf_op jit(solution)/shard_map/ppermute | solution.py:677
  269.5 49.8 %collective-permute-start.7 = (bf16[768,768]{1,0:T(8,128)(2,1)}, bf16[768,768]{1,0:T(8,128)(2,1)S(1)}, u32[]{:S(2)}, u32[]{:S(2)}) collective-permute-start(bf16[768,768]{1,0:T(8,128)(2,1)} %get-tuple-element.189), channel_id=1, source_target_pairs={{0,8},{8,0},{16,24},{24,16},{1,9},{9,1},{17,25},{25,17},{2,10},{10... | collective-permute-start | bytes 3538952 | tf_op jit(solution)/shard_map/ppermute | solution.py:677
  270.0 53.1 %collective-permute-start.8 = (bf16[768,768]{1,0:T(8,128)(2,1)}, bf16[768,768]{1,0:T(8,128)(2,1)}, u32[]{:S(2)}, u32[]{:S(2)}) collective-permute-start(bf16[768,768]{1,0:T(8,128)(2,1)} %get-tuple-element.190), channel_id=1, source_target_pairs={{0,8},{8,0},{16,24},{24,16},{1,9},{9,1},{17,25},{25,17},{2,10},{10... | collective-permute-start | bytes 3538952 | tf_op jit(solution)/shard_map/ppermute | solution.py:677
  271.5 51.6 %collective-permute-start.9 = (bf16[768,768]{1,0:T(8,128)(2,1)}, bf16[768,768]{1,0:T(8,128)(2,1)}, u32[]{:S(2)}, u32[]{:S(2)}) collective-permute-start(bf16[768,768]{1,0:T(8,128)(2,1)} %get-tuple-element.193), channel_id=1, source_target_pairs={{0,16},{8,24},{16,0},{24,8},{1,17},{9,25},{17,1},{25,9},{2,18},{10... | collective-permute-start | bytes 3538952 | tf_op jit(solution)/shard_map/ppermute | solution.py:677
  357.8 45.4 %collective-permute-start.15 = (bf16[2,4,160,768]{3,2,1,0:T(8,128)(2,1)}, bf16[2,4,160,768]{3,2,1,0:T(8,128)(2,1)S(1)}, u32[]{:S(2)}, u32[]{:S(2)}) collective-permute-start(bf16[2,4,160,768]{3,2,1,0:T(8,128)(2,1)} %get-tuple-element.231), channel_id=1, source_target_pairs={{0,8},{1,9},{2,10},{3,11},{4,12},{5,13},{6,14},{7,15},{8,0},{9,1},... | collective-permute-start | bytes 5898248 | tf_op jit(solution)/shard_map/ppermute | solution.py:677
  358.4 45.0 %collective-permute-start.16 = (bf16[2,4,160,768]{3,2,1,0:T(8,128)(2,1)}, bf16[2,4,160,768]{3,2,1,0:T(8,128)(2,1)S(1)}, u32[]{:S(2)}, u32[]{:S(2)}) collective-permute-start(bf16[2,4,160,768]{3,2,1,0:T(8,128)(2,1)} %get-tuple-element.232), channel_id=1, source_target_pairs={{0,16},{1,17},{2,18},{3,19},{4,20},{5,21},{6,22},{7,23},{8,24},{9,... | collective-permute-start | bytes 5898248 | tf_op jit(solution)/shard_map/ppermute | solution.py:677
  361.6 30.0 %collective-permute-start.18 = (bf16[4,1,64,768]{3,2,0,1:T(8,128)(2,1)}, bf16[4,1,64,768]{3,2,0,1:T(8,128)(2,1)S(1)}, u32[]{:S(2)}, u32[]{:S(2)}) collective-permute-start(bf16[4,1,64,768]{3,2,0,1:T(8,128)(2,1)} %bitcast.104), channel_id=1, source_target_pairs={{0,4},{1,5},{2,6},{3,7},{4,0},{5,1},{6,2},{7,3},{8,12},{9,13},{10,... | collective-permute-start | bytes 1179656 | tf_op jit(solution)/shard_map/ppermute | solution.py:677
  440.3 31.0 %collective-permute-start.29 = (bf16[768,768]{1,0:T(8,128)(2,1)}, bf16[768,768]{1,0:T(8,128)(2,1)S(1)}, u32[]{:S(2)}, u32[]{:S(2)}) collective-permute-start(bf16[768,768]{1,0:T(8,128)(2,1)} %get-tuple-element.300), channel_id=1, source_target_pairs={{0,16},{8,24},{16,0},{24,8},{1,17},{9,25},{17,1},{25,9},{2,18},{10... | collective-permute-start | bytes 3538952 | tf_op jit(solution)/shard_map/ppermute | solution.py:677
  441.5 30.7 %collective-permute-start.30 = (bf16[768,768]{1,0:T(8,128)(2,1)}, bf16[768,768]{1,0:T(8,128)(2,1)S(1)}, u32[]{:S(2)}, u32[]{:S(2)}) collective-permute-start(bf16[768,768]{1,0:T(8,128)(2,1)} %get-tuple-element.302), channel_id=1, source_target_pairs={{0,8},{8,0},{16,24},{24,16},{1,9},{9,1},{17,25},{25,17},{2,10},{10... | collective-permute-start | bytes 3538952 | tf_op jit(solution)/shard_map/ppermute | solution.py:677
  442.3 32.0 %collective-permute-start.26 = (bf16[1,320,768]{2,1,0:T(8,128)(2,1)}, bf16[1,320,768]{2,1,0:T(8,128)(2,1)S(1)}, u32[]{:S(2)}, u32[]{:S(2)}) collective-permute-start(bf16[1,320,768]{2,1,0:T(8,128)(2,1)} %get-tuple-element.292), channel_id=1, source_target_pairs={{0,2},{1,3},{2,0},{3,1},{4,6},{5,7},{6,4},{7,5},{8,10},{9,11},{10,... | collective-permute-start | bytes 1474568 | tf_op jit(solution)/shard_map/ppermute | solution.py:677
  444.0 51.4 %collective-permute-start.27 = (bf16[1,320,768]{2,1,0:T(8,128)(2,1)}, bf16[1,320,768]{2,1,0:T(8,128)(2,1)}, u32[]{:S(2)}, u32[]{:S(2)}) collective-permute-start(bf16[1,320,768]{2,1,0:T(8,128)(2,1)} %get-tuple-element.293), channel_id=1, source_target_pairs={{0,4},{1,5},{2,6},{3,7},{4,0},{5,1},{6,2},{7,3},{8,12},{9,13},{10,... | collective-permute-start | bytes 1474568 | tf_op jit(solution)/shard_map/ppermute | solution.py:677
  446.3 49.0 %collective-permute-start.28 = (bf16[1,320,768]{2,1,0:T(8,128)(2,1)}, bf16[1,320,768]{2,1,0:T(8,128)(2,1)}, u32[]{:S(2)}, u32[]{:S(2)}) collective-permute-start(bf16[1,320,768]{2,1,0:T(8,128)(2,1)} %get-tuple-element.294), channel_id=1, source_target_pairs={{0,6},{1,7},{2,4},{3,5},{4,2},{5,3},{6,0},{7,1},{8,14},{9,15},{10,... | collective-permute-start | bytes 1474568 | tf_op jit(solution)/shard_map/ppermute | solution.py:677
  472.3 29.2 %collective-permute-start.31 = (bf16[64,768]{1,0:T(8,128)(2,1)}, bf16[64,768]{1,0:T(8,128)(2,1)}, u32[]{:S(2)}, u32[]{:S(2)}) collective-permute-start(bf16[64,768]{1,0:T(8,128)(2,1)} %get-tuple-element.304), channel_id=1, source_target_pairs={{0,8},{1,9},{2,10},{3,11},{4,12},{5,13},{6,14},{7,15},{8,0},{9,1},... | collective-permute-start | bytes 294920 | tf_op jit(solution)/shard_map/ppermute | solution.py:677
  472.7 28.8 %collective-permute-start.32 = (bf16[64,768]{1,0:T(8,128)(2,1)}, bf16[64,768]{1,0:T(8,128)(2,1)}, u32[]{:S(2)}, u32[]{:S(2)}) collective-permute-start(bf16[64,768]{1,0:T(8,128)(2,1)} %get-tuple-element.305), channel_id=1, source_target_pairs={{0,16},{1,17},{2,18},{3,19},{4,20},{5,21},{6,22},{7,23},{8,24},{9,... | collective-permute-start | bytes 294920 | tf_op jit(solution)/shard_map/ppermute | solution.py:677
  (59 other events, 969.6 us)
Sparse Core Ops, SparseCore 0:
  19.3 136.3 all-gather.4
  414.3 76.5 all-gather.6

commit v4 on v3

--- a/solution.py
+++ b/solution.py
@@ -111,16 +111,14 @@
         write(rows, tail_rows, j, read(own + j, tail_rows, tiles))
 
 
-def pack_expert_kernel(dims, wide_ref, own_ref, *out_refs):
+def pack_expert_kernel(dims, wide_ref, own_ref, out_ref):
     rows, tiles = dims
-    half = rows // 2
 
     def read(first, count, stride):
         return own_ref[pl.ds(first, count, stride=stride), :]
 
     def write(first, count, j, value):
-        at = first % half
-        out_refs[first // half][at : at + count, LANES * j : LANES * (j + 1)] = value.astype(bf16)
+        out_ref[first : first + count, LANES * j : LANES * (j + 1)] = value.astype(bf16)
 
     wide = wide_ref[0] > 0
 
@@ -178,12 +176,16 @@
         at += ref.shape[0]
 
 
-def shift_kernel(dims, k_ref, flat_ref, head_ref, out_ref, buf):
+def adam_shift_kernel(
+    dims, clip_ref, k_ref, flat_ref, head_ref, momentum_ref, variance_ref,
+    update_ref, momentum_out, variance_out, grad_ref, buf,
+):
     step, own = dims
     count = flat_ref.shape[0]
     buf[0:count] = flat_ref[...]
     buf[count : count + head_ref.shape[0]] = head_ref[...]
-    out_ref[...] = buf[pl.ds(step * k_ref[0], own), :]
+    grad_ref[...] = buf[pl.ds(step * k_ref[0], own), :]
+    adam_kernel(clip_ref, grad_ref, momentum_ref, variance_ref, update_ref, momentum_out, variance_out)
 
 
 def adam_kernel(clip_ref, grad_ref, momentum_ref, variance_ref, update_ref, momentum_out, variance_out):
@@ -208,7 +210,7 @@
         out_specs=[spec] * 3,
         out_shape=[shape] * 3,
         compiler_params=params(),
-        cost_estimate=cost(20 * grad.size, 24 * grad.size, 2 * grad.size),
+        cost_estimate=cost(),
         name="adam",
     )(clip, grad, momentum, variance)
 
@@ -280,16 +282,6 @@
     scratch[place & 1, place >> 1, first : first + value.shape[0], :] = value
 
 
-def flush(scratch, keep_ref, send_ref, sems):
-    copies = [
-        pltpu.make_async_copy(scratch.at[i], ref, sems.at[i]) for i, ref in enumerate((keep_ref, send_ref))
-    ]
-    for copy in copies:
-        copy.start()
-    for copy in copies:
-        copy.wait()
-
-
 def matrix(w_ref, index):
     per = w_ref.shape[0] // 4
     width = w_ref.shape[2]
@@ -303,9 +295,30 @@
     return w_ref[:, q * rows : (q + 1) * rows, :].reshape(width, width)
 
 
-def attn_fwd_kernel(seq, stream_ref, gain_ref, w_ref, out_ref, a_ref, q_ref, k_ref, v_ref, o_ref):
+def start_all(sources, targets, sems):
+    copies = [pltpu.make_async_copy(a, b, sems.at[i]) for i, (a, b) in enumerate(zip(sources, targets))]
+    for copy in copies:
+        copy.start()
+    return copies
+
+
+def wait_all(copies):
+    for copy in copies:
+        copy.wait()
+
+
+def layer_copies(spots, arrays, place_ref, layer, target, sems):
+    low, top = place_ref[0], place_ref[1]
+    found = []
+    for j, (array, before, behind) in enumerate(spots):
+        source = arrays[array].at[before + (layer ^ top,) + behind + (pl.ds(0, target.shape[1]),)]
+        found.append(pltpu.make_async_copy(source, target.at[j ^ low], sems.at[j ^ low]))
+    return found
+
+
+def attn_fwd(seq, stream_ref, gain, w_ref, out_ref, a_ref, q_ref, k_ref, v_ref, o_ref):
     normed, _ = norm_rows(stream_ref[...])
-    a_ref[...] = (normed * gain_ref[...]).astype(bf16)
+    a_ref[...] = (normed * gain).astype(bf16)
     for index, ref in enumerate((q_ref, k_ref, v_ref)):
         ref[...] = dot(a_ref[...], matrix(w_ref, index)).astype(bf16)
     count = stream_ref.shape[0]
@@ -322,9 +335,17 @@
     out_ref[...] = stream_ref[...] + dot(o_ref[...], matrix(w_ref, 3))
 
 
-def attn_bwd_kernel(
-    seq, grad_ref, stream_ref, gain_ref, w_ref, q_ref, k_ref, v_ref, out_ref, gain_out, dq_ref, dk_ref, dv_ref, do_ref
-):
+def attn_bwd_kernel(seq, spots, layer, place_ref, gain_ref, *refs):
+    ins, arrays, refs = refs[:5], refs[5 : 5 + len(refs) - 24], refs[len(refs) - 19 :]
+    out_ref, gain_out, *outs = refs[:5]
+    grad_ref, stream_ref, q_ref, k_ref, v_ref = refs[5:10]
+    held_out, dq_ref, dk_ref, dv_ref, do_ref, w_ref, w_sems, in_sems, out_sems = refs[10:]
+    copies = layer_copies(spots, arrays, place_ref, layer, w_ref, w_sems)
+    for copy in copies:
+        copy.start()
+    arriving = start_all(ins, (grad_ref, stream_ref, q_ref, k_ref, v_ref), in_sems)
+    wait_all(copies)
+    wait_all(arriving)
     do_ref[...] = dot_nt(grad_ref[...].astype(bf16), matrix(w_ref, 3)).astype(bf16)
     count = grad_ref.shape[0]
     key_ok = lax.broadcasted_iota(jnp.int32, (count, count), 1) < seq
@@ -350,22 +371,48 @@
         dq_ref[:, lanes] = (dq * scale).astype(bf16)
         dk_ref[:, lanes] = (dk * scale).astype(bf16)
         dv_ref[:, lanes] = dv.astype(bf16)
+    leaving = start_all((dq_ref, dk_ref, dv_ref), outs, out_sems)
     back = None
     for index, ref in enumerate((dq_ref, dk_ref, dv_ref)):
         part = dot_nt(ref[...], matrix(w_ref, index))
         back = part if back is None else back + part
     normed, inverse = norm_rows(stream_ref[...])
     addend, gain_grad = norm_back(back, normed, inverse, gain_ref[...])
-    out_ref[...] = grad_ref[...] + addend
+    held_out[...] = grad_ref[...] + addend
+    last = pltpu.make_async_copy(held_out, out_ref, out_sems.at[3])
+    last.start()
     gain_out[...] = gain_grad
-
-
-def attn_weights_kernel(
-    low_ref, grad_ref, a_ref, o_ref, dq_ref, dk_ref, dv_ref, keep_ref, send_ref, dw, sems
-):
+    wait_all(leaving)
+    last.wait()
+
+
+def leave_chunk(scratch, low, chunk, keep_ref, send_ref, sem):
+    place = chunk ^ low
+    source = scratch.at[place & 1, place >> 1]
+
+    @pl.when((place & 1) == 0)
+    def _():
+        pltpu.make_async_copy(source, keep_ref.at[place >> 1], sem).start()
+
+    @pl.when((place & 1) == 1)
+    def _():
+        pltpu.make_async_copy(source, send_ref.at[place >> 1], sem).start()
+
+
+def wait_chunks(scratch, low, keep_ref, sems):
+    for chunk in range(2 * scratch.shape[1]):
+        place = chunk ^ low
+        pltpu.make_async_copy(scratch.at[place & 1, place >> 1], keep_ref.at[place >> 1], sems.at[chunk]).wait()
+
+
+def attn_weights_kernel(low_ref, *refs):
+    ins, keep_ref, send_ref, refs = refs[:6], refs[6], refs[7], refs[8:]
+    (grad_ref, a_ref, o_ref, dq_ref, dk_ref, dv_ref), (dw, in_sems, sems) = refs[:6], refs[6:]
     low = low_ref[0]
     rows = dw.shape[2]
     per = grad_ref.shape[1] // rows
+    arriving = start_all(ins, refs[:6], in_sems)
+    wait_all(arriving)
     branch = grad_ref[...].astype(bf16)
     for index in range(4):
         left = o_ref if index == 3 else a_ref
@@ -373,14 +420,14 @@
         value = dot_tn(left[...], right)
         for i in range(per):
             put_chunk(dw, low, index * per + i, value[i * rows : (i + 1) * rows].astype(bf16))
-    flush(dw, keep_ref, send_ref, sems)
-
-
-def mlp_fwd_kernel(stream_ref, gain_ref, w1_ref, w2_ref, out_ref, b_ref, u_ref):
+            leave_chunk(dw, low, index * per + i, keep_ref, send_ref, sems.at[index * per + i])
+    wait_chunks(dw, low, keep_ref, sems)
+
+
+def mlp_fwd(stream_ref, gain, w1_ref, w2_ref, out_ref, b_ref, u_ref):
     width = stream_ref.shape[1]
     normed, _ = norm_rows(stream_ref[...])
-    b_ref[...] = (normed * gain_ref[...]).astype(bf16)
-    out_ref[...] = stream_ref[...]
+    b_ref[...] = (normed * gain).astype(bf16)
     total = None
     for q in range(4):
         pre = dot(b_ref[...], quarter_in(w1_ref, q))
@@ -390,18 +437,77 @@
     out_ref[...] = stream_ref[...] + total
 
 
-def mlp_bwd_kernel(
-    by_core, low_ref, grad_ref, stream_ref, gain_ref, w1_ref, w2_ref, b_ref, u_ref,
-    out_ref, gain_out, keep2_ref, send2_ref, *refs,
-):
+def forward_kernel(seq, spots, dims, by_core, place_ref, stream_ref, picks_ref, rows_ref, *refs):
+    rows, experts, count = dims
+    arrays, refs = refs[:count], refs[count:]
+    if not by_core:
+        w1_ref, refs = refs[0], refs[1:]
+    outs, refs = refs[:15], refs[15:]
+    gains_ref, wr_ref, c_ref, probs_ref, x_ref = refs[:5]
+    held, (weights, tails, w_sems, tail_sems, out_sems) = refs[5:20], refs[20:]
+    low, top = place_ref[0], place_ref[1]
+    per = weights.shape[1]
+    copies = {
+        layer: layer_copies(spots, arrays, place_ref, layer, weights.at[layer], w_sems.at[layer])
+        for layer in (0, 2, 3, 1)
+    }
+    tail_copies = []
+    for j, (array, before, behind) in enumerate(spots):
+        source = arrays[array].at[before + (3 ^ top,) + behind + (pl.ds(rows, tails.shape[1]),)]
+        tail_copies.append(pltpu.make_async_copy(source, tails.at[j ^ low], tail_sems.at[j]))
+    for copy in copies[0] + tail_copies:
+        copy.start()
+    for copy in copies[0] + tail_copies:
+        copy.wait()
+    for copy in copies[2] + copies[3] + copies[1]:
+        copy.start()
+    tail = tails[per - 1].astype(f32)
+    gains = [tail[experts + i : experts + i + 1] for i in range(4)]
+    gains_ref[...] = tail[experts : experts + 4]
+    leaving = []
+
+    def leave(first, last):
+        for i in range(first, last):
+            leaving.append(pltpu.make_async_copy(held[i], outs[i], out_sems.at[i]))
+            leaving[-1].start()
+
+    attn_fwd(seq, stream_ref, gains[0], weights.at[0], *held[0:6])
+    leave(0, 6)
+    for copy in copies[2] + copies[3]:
+        copy.wait()
+    mlp_fwd(held[0], gains[1], weights.at[2] if by_core else w1_ref, weights.at[3], *held[6:9])
+    leave(6, 9)
+    for copy in copies[1]:
+        copy.wait()
+    attn_fwd(seq, held[6], gains[2], weights.at[1], *held[9:15])
+    leave(9, 15)
+    wr_ref[...] = router_matrix(tail, stream_ref.shape[1], experts)
+    dispatch(held[9], gains[3], wr_ref, picks_ref, rows_ref, c_ref, probs_ref, x_ref)
+    for copy in leaving:
+        copy.wait()
+
+
+def mlp_bwd_kernel(by_core, spots, count, place_ref, gain_ref, *refs):
+    ins, arrays, refs = refs[:4], refs[4 : 4 + count], refs[4 + count :]
     if by_core:
-        keep1_ref, send1_ref, dw2, dw1, sems = refs
+        out_ref, gain_out, keep2_ref, send2_ref, keep1_ref, send1_ref, *refs = refs
+        dw2, dw1, w2_ref, w1_ref, *refs = refs
     else:
-        dw1_ref, dw2, sems = refs
+        w1_ref, out_ref, gain_out, keep2_ref, send2_ref, dw1_ref, *refs = refs
+        dw2, w2_ref, *refs = refs
+    grad_ref, stream_ref, b_ref, u_ref, held_out, w_sems, in_sems, out_sems, last_sem = refs
+    low = place_ref[0]
+    arriving = start_all(ins, (grad_ref, stream_ref, b_ref, u_ref), in_sems)
+    copies = layer_copies(spots, arrays, place_ref, 3, w2_ref, w_sems.at[0])
+    if by_core:
+        copies += layer_copies(spots, arrays, place_ref, 2, w1_ref, w_sems.at[1])
+    for copy in copies:
+        copy.start()
+    wait_all(arriving)
     width = grad_ref.shape[1]
     upper = grad_ref[...].astype(bf16)
-    low = low_ref[0]
     back = None
+    groups = w1_ref.shape[0]
     for q in range(4):
         pre = u_ref[:, q * width : (q + 1) * width]
         cdf = normal_cdf(pre)
@@ -411,10 +517,12 @@
         second = dot_tn(act, upper)
         for i in range(per):
             put_chunk(dw2, low, q * per + i, second[i * rows : (i + 1) * rows].astype(bf16))
+            leave_chunk(dw2, low, q * per + i, keep2_ref, send2_ref, out_sems.at[0, q * per + i])
+        if q == 0:
+            wait_all(copies)
         dact = dot_nt(upper, matrix(w2_ref, q))
         dpre = (dact * (cdf + pre * density(pre))).astype(bf16)
         first = dot_tn(b_ref[...], dpre).astype(bf16)
-        groups = w1_ref.shape[0]
         rows = width // groups
         for i in range(groups):
             piece = first[i * rows : (i + 1) * rows]
@@ -424,13 +532,19 @@
                 dw1_ref[i, q * rows : (q + 1) * rows, :] = piece
         part = dot_nt(dpre, quarter_in(w1_ref, q))
         back = part if back is None else back + part
-    flush(dw2, keep2_ref, send2_ref, sems)
     if by_core:
-        flush(dw1, keep1_ref, send1_ref, sems)
+        for i in range(groups):
+            leave_chunk(dw1, low, i, keep1_ref, send1_ref, out_sems.at[1, i])
     normed, inverse = norm_rows(stream_ref[...])
     addend, gain_grad = norm_back(back, normed, inverse, gain_ref[...])
-    out_ref[...] = grad_ref[...] + addend
+    held_out[...] = grad_ref[...] + addend
+    last = pltpu.make_async_copy(held_out, out_ref, last_sem)
+    last.start()
     gain_out[...] = gain_grad
+    wait_chunks(dw2, low, keep2_ref, out_sems.at[0])
+    if by_core:
+        wait_chunks(dw1, low, keep1_ref, out_sems.at[1])
+    last.wait()
 
 
 def pick_hots(picks, experts):
@@ -443,11 +557,23 @@
     return raised / jnp.sum(raised, axis=-1, keepdims=True)
 
 
-def dispatch_kernel(stream_ref, gain_ref, wr_ref, picks_ref, rows_ref, c_ref, probs_ref, x_ref):
+def router_matrix(flat, width, experts):
+    block = width // experts
+    row = lax.broadcasted_iota(jnp.int32, (block, width), 0)
+    lane = lax.broadcasted_iota(jnp.int32, (block, width), 1)
+    mine = (lane // experts == row).astype(f32)
+    lane = lax.broadcasted_iota(jnp.int32, (width, experts), 0)
+    column = lax.broadcasted_iota(jnp.int32, (width, experts), 1)
+    pick = (lax.rem(lane, experts) == column).astype(f32).astype(bf16)
+    parts = [dot((mine * flat[i : i + 1]).astype(bf16), pick) for i in range(experts)]
+    return jnp.concatenate(parts).astype(bf16)
+
+
+def dispatch(stream_ref, gain, wr_ref, picks_ref, rows_ref, c_ref, probs_ref, x_ref):
     width = stream_ref.shape[1]
     experts = wr_ref.shape[1]
     normed, _ = norm_rows(stream_ref[...])
-    c_ref[...] = (normed * gain_ref[...]).astype(bf16)
+    c_ref[...] = (normed * gain).astype(bf16)
     probs = softmax_rows(dot(c_ref[...], wr_ref[...]))
     probs_ref[...] = probs
     hots = pick_hots(picks_ref, experts)
@@ -616,6 +742,12 @@
     return (left.astype(f32) + right.astype(f32)).astype(bf16)
 
 
+def pack_sets_kernel(*refs):
+    out_ref = refs[-1]
+    for i, ref in enumerate(refs[:-1]):
+        out_ref[i // 4, i % 4] = ref[...]
+
+
 def fold_layers_kernel(cut, top_ref, *refs):
     layers, refs = [refs[2 * i : 2 * i + 2] for i in range(4)], refs[8:]
     uppers, (send_x, keep_x, send_y, keep_y, scratch) = refs[:4], refs[4:]
@@ -679,6 +811,15 @@
 
 def after(value, *others):
     return lax.optimization_barrier((value, others))[0]
+
+
+class Order:
+    def __init__(self):
+        self.latest = ()
+
+    def land(self, value):
+        self.latest = after(value, self.latest)
+        return self.latest
 
 
 def bit_groups(bits):
@@ -761,15 +902,13 @@
         cost_estimate=cost(0, 6 * dense_master.size),
         name="pack_dense",
     )(me_arr, tail_from, dense_flat)
-    gathered = lax.all_gather(chunk, both, axis=0, tiled=True)
-    gathered = gathered.reshape(devices, rows + tail_rows, width)
 
     expert_wide = (dp_me < dp_ranks // 2).astype(jnp.int32).reshape(1)
-    halves = pl.pallas_call(
+    expert_chunk = pl.pallas_call(
         functools.partial(pack_expert_kernel, (expert_rows, tiles)),
         in_specs=[SMEM, VMEM],
-        out_specs=[VMEM, VMEM],
-        out_shape=[shape((expert_rows // 2, width), bf16)] * 2,
+        out_specs=VMEM,
+        out_shape=shape((expert_rows, width), bf16),
         compiler_params=params(),
         cost_estimate=cost(0, 6 * expert_master.size),
         name="pack_expert",
@@ -779,18 +918,6 @@
 
     def gather_step(parts, bit):
         return {**parts, **{at | (1 << bit): swap(part, dp_axis, 1 << bit) for at, part in parts.items()}}
-
-    half_rows = expert_rows // 2
-    orders = (dp_order, dp_order[::-1])
-    sides = [gather_step({0: half}, bits[0]) for half, bits in zip(halves, orders)]
-    gathered, sides = lax.optimization_barrier((gathered, sides))
-    sides = [gather_step(side, bits[1]) for side, bits in zip(sides, orders)]
-    for i, bits in enumerate(orders):
-        for bit in bits[2:]:
-            sides[i] = gather_step(sides[i], bit)
-    expert_parts = [side[at] for side in sides for at in sorted(side)]
-    expert_spans = [(at, i * half_rows) for i, side in enumerate(sides) for at in sorted(side)]
-    soon = [sides[i][1 << bits[1]] for i, bits in enumerate(orders)]
 
     capacity = 2 * seq // experts
     stride = -(-capacity // 8) * 8
@@ -820,27 +947,86 @@
         value = lax.all_to_all(value, "expert", split_axis=0, concat_axis=0, tiled=True)
         return value.reshape(dims)
 
-    arriving_cot = exchange(outgoing_cot)
-
-    tail_flat = gathered[devices - 1, rows:, :].reshape(-1)
-    router = tail_flat[: width * experts].reshape(width, experts)
-    gains = tail_flat[width * experts : width * (experts + 4)].reshape(4, width).astype(f32)
-    gain = [gains[i : i + 1] for i in range(4)]
-
     per = devices // 4
-    dense_block = (per, rows + tail_rows, width)
+    per_bits = per.bit_length() - 1
+    top_bits = (per_bits, per_bits + 1)
+    chunk_rows = rows + tail_rows
+    half_rows = expert_rows // 2
+    orders = (dp_order, dp_order[::-1])
+    expert_parts, expert_spans = [], []
+    if per_bits == 3 and dp_bits == 2:
+        masks = [1 << bit for bit in top_bits]
+        order = Order()
+
+        def spread(value):
+            return [swap(value, both, mask) for mask in masks]
+
+        sets = [chunk, swap(chunk, both, 2), swap(chunk, both, 4), None]
+        near, far = [spread(chunk)] + [None] * 3, [None] * 4
+        sets[1] = order.land(sets[1])
+        near[1] = spread(sets[1])
+        near[0] = order.land((near[0], expert_chunk, outgoing_cot, stream))[0]
+        far[0] = swap(near[0][1], both, masks[0])
+        near[1] = order.land(near[1])
+        far[1] = swap(near[1][0], both, masks[1])
+        sets[2] = order.land(sets[2])
+        sets[3] = swap(sets[2], both, 2)
+        near[2] = spread(sets[2])
+        far[0], far[1] = order.land((far[0], far[1]))
+        sets[3] = order.land(sets[3])
+        near[3] = spread(sets[3])
+        arriving_cot = exchange(after(outgoing_cot, sets[3]))
+        near[2] = order.land(near[2])
+        far[2] = swap(near[2][1], both, masks[0])
+        near[3] = order.land(near[3])
+        far[3] = swap(near[3][0], both, masks[1])
+
+        def pack_sets(which):
+            ins = [part for s in which for part in (sets[s], *near[s], far[s])]
+            return pl.pallas_call(
+                pack_sets_kernel,
+                in_specs=[VMEM] * len(ins),
+                out_specs=VMEM,
+                out_shape=shape((len(which), 4, chunk_rows, width), bf16),
+                compiler_params=params(),
+                cost_estimate=cost(),
+                name="pack_sets",
+            )(*ins)
+
+        packed = [pack_sets([0, 1])]
+        far[2:], packed, arriving_cot = lax.optimization_barrier((far[2:], packed, arriving_cot))
+        far[2], far[3] = order.land((far[2], far[3]))
+        packed.append(pack_sets([2, 3]))
+        arrays = packed + [swap(value, both, 1) for value in packed]
+        spots = [((j >> 2) + 2 * (j & 1), ((j >> 1) & 1,), ()) for j in range(per)]
+        own_shard = after(expert_chunk, near[3])
+        beside = [swap(own_shard, dp_axis, mask) for mask in (1, 2)]
+        across = [swap(beside[0][:half_rows], dp_axis, 2), swap(beside[1][half_rows:], dp_axis, 1)]
+        expert_parts = [expert_chunk, *beside, *across]
+        expert_spans = [(0, 0), (1, 0), (2, 0), (3, 0), (3, half_rows)]
+    else:
+        gathered = chunk[None]
+        for bit in range(all_bits):
+            gathered = jnp.concatenate([gathered, swap(gathered, both, 1 << bit)])
+        arrays = [gathered.reshape(4, per, chunk_rows, width)]
+        spots = [(0, (), (j,)) for j in range(per)]
+        for side, bits in enumerate(orders):
+            parts, places = [expert_chunk[side * half_rows : (side + 1) * half_rows]], [0]
+            for bit in bits:
+                parts = parts + [swap(part, dp_axis, 1 << bit) for part in parts]
+                places = places + [place | (1 << bit) for place in places]
+            expert_parts += parts
+            expert_spans += [(place, side * half_rows) for place in places]
+        arriving_cot = exchange(outgoing_cot)
+
     low = me & (per - 1)
     low_arr = low.reshape(1)
-
-    def layer_spec(index):
-        return pl.BlockSpec(dense_block, lambda *_: (index, 0, 0), pipeline_mode=pl.Buffered(1))
-
-    if wide_ok:
-        first_in, first_spec = gathered, layer_spec(2)
-    else:
-        first_in = gathered[2 * per : 3 * per, :rows].reshape(width, 4, width)
+    place_arr = jnp.stack([low, me >> per_bits])
+    layer_w = pltpu.VMEM((per, rows, width), bf16)
+    if not wide_ok:
+        first_in = lax.dynamic_index_in_dim(arrays[0], 2 ^ (me >> per_bits), 0, keepdims=False)
+        first_in = jnp.take(first_in, jnp.arange(per) ^ low, axis=0)[:, :rows].reshape(width, 4, width)
         first_in = first_in.transpose(1, 0, 2).reshape(1, 4 * width, width)
-        first_spec = None
 
     act_shape = shape((padded, width), bf16)
     stream_shape = shape((padded, width), f32)
@@ -867,68 +1053,84 @@
             name=name,
         )(*ins)
 
-    def attn_fwd(value, layer, which):
-        return call(
-            functools.partial(attn_fwd_kernel, seq),
-            (value, gain[which], gathered),
-            (None, None, layer_spec(layer)),
-            [stream_shape] + [act_shape] * 5,
-            "attn_fwd",
-            5 * tok_flops,
-            4 * weight_bytes,
-        )
-
     places = per // 2
     core_shape = shape((places, rows, width), bf16)
     by_core = pltpu.VMEM((2, places, rows, width), bf16)
-    sems = pltpu.SemaphoreType.DMA((2,))
+    stream_vmem, act_vmem = pltpu.VMEM((padded, width), f32), pltpu.VMEM((padded, width), bf16)
 
     def attn_bwd(grad, value, kept, layer, which):
         return call(
-            functools.partial(attn_bwd_kernel, seq),
-            (grad, value, gain[which], gathered, *kept[1:4]),
-            (None, None, None, layer_spec(layer)) + (None,) * 3,
+            functools.partial(attn_bwd_kernel, seq, spots, layer),
+            (place_arr, gain[which], grad, value, *kept[1:4], *arrays),
+            (SMEM, None) + (ANY,) * (5 + len(arrays)),
             [stream_shape, gain_shape] + [act_shape] * 3,
             "attn_bwd",
             0,
             0,
-            scratch=[pltpu.VMEM((padded, width), bf16)],
+            out_specs=[ANY, None, ANY, ANY, ANY],
+            scratch=[
+                stream_vmem,
+                stream_vmem,
+                *[act_vmem] * 3,
+                stream_vmem,
+                *[act_vmem] * 4,
+                layer_w,
+                pltpu.SemaphoreType.DMA((per,)),
+                pltpu.SemaphoreType.DMA((5,)),
+                pltpu.SemaphoreType.DMA((4,)),
+            ],
         )
 
     def attn_weights(grad, kept, found):
         return call(
             attn_weights_kernel,
             (low_arr, grad, kept[0], kept[4], *found),
-            (SMEM,) + (None,) * 6,
+            (SMEM,) + (ANY,) * 6,
             [core_shape, core_shape],
             "attn_weights",
             0,
             0,
             out_specs=[ANY] * 2,
-            scratch=[by_core, sems],
+            scratch=[
+                stream_vmem,
+                *[act_vmem] * 5,
+                by_core,
+                pltpu.SemaphoreType.DMA((6,)),
+                pltpu.SemaphoreType.DMA((per,)),
+            ],
         )
 
-    stream_one, *kept_one = attn_fwd(stream, 0, 0)
-    stream_two, mlp_in, mlp_pre = call(
-        mlp_fwd_kernel,
-        (stream_one, gain[1], first_in, gathered),
-        (None, None, first_spec, layer_spec(3)),
-        [stream_shape, act_shape, shape((padded, hidden), f32)],
-        "mlp_fwd",
-        8 * tok_flops,
-        8 * weight_bytes,
+    outs = [stream_shape] + [act_shape] * 5 + [stream_shape, act_shape, shape((padded, hidden), f32)]
+    outs += [stream_shape] + [act_shape] * 5
+    *results, gains, router, moe_in, probs, outgoing = call(
+        functools.partial(forward_kernel, seq, spots, (rows, experts, len(arrays)), wide_ok),
+        (place_arr, stream, picks, rows_slots, *arrays, *([] if wide_ok else [first_in])),
+        (SMEM, None, None, None) + (ANY,) * len(arrays) + (() if wide_ok else (None,)),
+        outs
+        + [
+            shape((4, width)),
+            shape((width, experts), bf16),
+            act_shape,
+            shape((padded, experts)),
+            shape((slots, width + LANES), bf16),
+        ],
+        "forward",
+        0,
+        0,
+        out_specs=[ANY] * 15 + [None] * 5,
+        scratch=[pltpu.VMEM(o.shape, o.dtype) for o in outs]
+        + [
+            pltpu.VMEM((4, per, rows, width), bf16),
+            pltpu.VMEM((per, tail_rows, width), bf16),
+            pltpu.SemaphoreType.DMA((4, per)),
+            pltpu.SemaphoreType.DMA((per,)),
+            pltpu.SemaphoreType.DMA((15,)),
+        ],
     )
-    stream_three, *kept_two = attn_fwd(stream_two, 1, 2)
-    stream_three = after(stream_three, soon)
-    moe_in, probs, outgoing = call(
-        dispatch_kernel,
-        (stream_three, gain[3], router, picks, rows_slots),
-        (None,) * 5,
-        [act_shape, shape((padded, experts)), shape((slots, width + LANES), bf16)],
-        "dispatch",
-        0,
-        0,
-    )
+    stream_one, kept_one = results[0], results[1:6]
+    stream_two, mlp_in, mlp_pre = results[6:9]
+    stream_three, kept_two = results[9], results[10:]
+    gain = [gains[i : i + 1] for i in range(4)]
     arriving = exchange(outgoing)
 
     quarter = expert_rows // 4
@@ -976,10 +1178,8 @@
     expert_first = [expert_first[i * count : (i + 1) * count] for i in range(4)]
     returned_grad = after(returned_grad, expert_first)
 
-    per_bits = per.bit_length() - 1
     cut = max(16, rows // 96 * 16)
     middle = (rows - cut) // 2
-    top_bits = (per_bits, per_bits + 1)
     top = (me >> per_bits).reshape(1)
     z_bits = list(range(1, per_bits))
     z_masks = [2 * j for j in (1, 2, 3)]
@@ -1019,15 +1219,23 @@
     mlp_out = [core_shape, core_shape]
     mlp_out = mlp_out * 2 if wide_ok else mlp_out + [shape((1, 4 * width, width), bf16)]
     grad, gain_two, *mlp_dw = call(
-        functools.partial(mlp_bwd_kernel, wide_ok),
-        (low_arr, grad, stream_one, gain[1], first_in, gathered, mlp_in, mlp_pre),
-        (SMEM, None, None, None, first_spec, layer_spec(3), None, None),
+        functools.partial(mlp_bwd_kernel, wide_ok, spots, len(arrays)),
+        (place_arr, gain[1], grad, stream_one, mlp_in, mlp_pre, *arrays, *([] if wide_ok else [first_in])),
+        (SMEM, None) + (ANY,) * (4 + len(arrays)) + (() if wide_ok else (None,)),
         [stream_shape, gain_shape] + mlp_out,
         "mlp_bwd",
         0,
         0,
-        out_specs=[None, None] + ([ANY] * 4 if wide_ok else [ANY] * 2 + [None]),
-        scratch=[by_core] * (2 if wide_ok else 1) + [sems],
+        out_specs=[ANY, None] + ([ANY] * 4 if wide_ok else [ANY] * 2 + [None]),
+        scratch=[by_core] * (2 if wide_ok else 1)
+        + [layer_w] * (2 if wide_ok else 1)
+        + [stream_vmem, stream_vmem, act_vmem, pltpu.VMEM((padded, hidden), f32), stream_vmem]
+        + [
+            pltpu.SemaphoreType.DMA((2, per)),
+            pltpu.SemaphoreType.DMA((4,)),
+            pltpu.SemaphoreType.DMA((2, per)),
+            pltpu.SemaphoreType.DMA,
+        ],
     )
     if not wide_ok:
         wide_grad = mlp_dw[2].reshape(4, width, width).transpose(1, 0, 2).reshape(per, rows, width)
@@ -1038,9 +1246,6 @@
 
     upper = grad
     grad, gain_one, *found = attn_bwd(upper, stream, kept_one, 0, 0)
-    found, expert_got = lax.optimization_barrier((found, expert_got))
-    first_dw = to_other_core(attn_weights(upper, kept_one, found))
-
     small = call(
         stack_rows_kernel,
         (router_grad, gain_one, gain_two, gain_three, gain_four),
@@ -1050,8 +1255,10 @@
         0,
         0,
     )[0]
-    found_small = small
-    small = jnp.sum(lax.all_gather(small, both, axis=0, tiled=False), axis=0)
+    found, expert_got, small = lax.optimization_barrier((found, expert_got, small))
+    first_dw = to_other_core(attn_weights(upper, kept_one, found))
+
+    small = lax.all_gather(small, both, axis=0, tiled=False)
 
     plane_shape = shape((2, places, middle, width), bf16)
     plane_spec = pl.BlockSpec((2, 1, middle, width), lambda i: (0, i, 0, 0))
@@ -1124,7 +1331,7 @@
         0,
         0,
     )
-    lower_rows, other_out, expert_second, _ = lax.optimization_barrier((lower_rows, other_out, expert_second, found_small))
+    lower_rows, other_out, expert_second = lax.optimization_barrier((lower_rows, other_out, expert_second))
     lower_rows = over_z(lower_rows)
     half = count // 2
     expert_groups = []
@@ -1154,18 +1361,6 @@
         scratch=[pltpu.VMEM((slots, width), f32)],
     )[0]
 
-    lower_rows, output = lax.optimization_barrier((lower_rows, output))
-    lower_rows = rest_of_z(lower_rows)
-    upper_rows = [upper_rows[0]] + [
-        swap(value, both, masks[0] * j) for j, value in enumerate(upper_rows) if j
-    ]
-    dense_groups = [upper_rows, [value.reshape(rows - cut, width) for value in lower_rows]]
-
-    gain_grads = small[experts:]
-    small_square = jnp.sum(small * small)
-    small = jnp.concatenate([small[:experts].T.reshape(-1, LANES), gain_grads.reshape(-1, LANES)])
-    small = jnp.pad(small, ((0, tail - small.shape[0]), (0, 0)))
-
     def unpack(wide, groups, count, name):
         pieces = [piece for group in groups for piece in group]
         return pl.pallas_call(
@@ -1180,21 +1375,25 @@
         )(wide, *pieces)
 
     expert_grad, expert_square = unpack(expert_wide, expert_groups, expert_rows, "unpack_expert")
+    lower_rows, output, expert_grad, expert_square = lax.optimization_barrier(
+        (lower_rows, output, expert_grad, expert_square)
+    )
+    lower_rows = rest_of_z(lower_rows)
+    upper_rows = [upper_rows[0]] + [
+        swap(value, both, masks[0] * j) for j, value in enumerate(upper_rows) if j
+    ]
+    dense_groups = [upper_rows, [value.reshape(rows - cut, width) for value in lower_rows]]
+
     dense_wide = (me >= devices // 2) & (me < 3 * devices // 4) & wide_ok
     dense_rows, dense_square = unpack(dense_wide.astype(jnp.int32).reshape(1), dense_groups, rows, "unpack_dense")
+    small = jnp.sum(after(small, dense_square), axis=0)
+    gain_grads = small[experts:]
+    small_square = jnp.sum(small * small)
+    small = jnp.concatenate([small[:experts].T.reshape(-1, LANES), gain_grads.reshape(-1, LANES)])
+    small = jnp.pad(small, ((0, tail - small.shape[0]), (0, 0)))
+
     head = lax.ppermute(dense_rows[:tail], both, backward_ring)
     head = jnp.where(me == devices - 1, small, head)
-    dense_grad = pl.pallas_call(
-        functools.partial(shift_kernel, (step, own)),
-        in_specs=[SMEM, VMEM, VMEM],
-        out_specs=VMEM,
-        out_shape=shape((own, LANES)),
-        scratch_shapes=[pltpu.VMEM((-(-(rows * tiles + tail) // 8) * 8, LANES), f32)],
-        compiler_params=params(),
-        cost_estimate=cost(0, 8 * rows * width),
-        name="shift_dense",
-    )(me_arr, dense_rows, head)
-
     square = dense_square + expert_square
     for bits in bit_groups(list(range(all_bits))):
         square = all_sum_step(square, both, bits)
@@ -1202,12 +1401,22 @@
     param_count = (dense_master.size + expert_master.size) * devices
     clip_factor = jnp.minimum(1.0, jnp.sqrt(param_count / (square_sum + 1e-06))).reshape(1)
 
-    dense_update, momentum_dense, variance_dense = adam(
+    dense_update, momentum_dense, variance_dense, dense_grad = pl.pallas_call(
+        functools.partial(adam_shift_kernel, (step, own)),
+        in_specs=[SMEM, SMEM] + [VMEM] * 4,
+        out_specs=[VMEM] * 4,
+        out_shape=[shape((own, LANES))] * 4,
+        scratch_shapes=[pltpu.VMEM((-(-(rows * tiles + tail) // 8) * 8, LANES), f32)],
+        compiler_params=params(),
+        cost_estimate=cost(),
+        name="adam_dense",
+    )(
         clip_factor,
-        dense_grad,
+        me_arr,
+        dense_rows,
+        head,
         dense_momentum.reshape(own, LANES),
         dense_variance.reshape(own, LANES),
-        own,
     )
     expert_update, momentum_expert, variance_expert = adam(
         clip_factor,

time: 549 us -> 510 us (0.929); the launches traced: 550 us -> 505 us
  waiting for transfers between devices: 266 us -> 210 us
  starting transfers between devices: 66.6 us -> 73.4 us
    all_gather x2 -> x1, waiting for transfers between devices: 115 us -> 0.01 us  [on_device(): small = lax.all_gather(small, both, axis=0, tiled=False)]
    ppermute x40 -> x55, waiting for transfers between devices: 138 us -> 198 us  [swap(): return lax.ppermute(value, axes, [(i, i ^ mask) for i in range(size)])]
    ppermute x40 -> x55, starting transfers between devices: 40.5 us -> 61.2 us  [swap(): return lax.ppermute(value, axes, [(i, i ^ mask) for i in range(size)])]
    all_to_all x3, starting transfers between devices: 24.1 us -> 11.2 us  [exchange(): lax.all_to_all(value, 'expert', split_axis=0, concat_axis=0, tiled=True)]
    pallas_call x1 -> x3, Pallas kernels: 2.45 us -> 14.9 us  [the longest x2 10 us: pack_sets(): pl.pallas_call(pack_sets_kernel, in_specs=[VMEM] * len(ins), out_specs=VM...]
    pallas_call x15 -> x12, Pallas kernels: 92.5 us -> 83.5 us  [call(): pl.pallas_call(kernel, grid=(1,), in_specs=[s or whole(a) for a, s in zip...]
    pallas_call x2 -> x1, Pallas kernels: 16.5 us -> 12.5 us  [adam(): pl.pallas_call(adam_kernel, grid=(pl.cdiv(count, block),), in_specs=[SMEM...]
    unnamed x75 -> x99, local copies, waits for them, and re-layouts: 9.47 us -> 12.5 us
  transfers between devices with their start and end apart: 47 -> 61, of which waited for: 26 -> 31; matrix products, arithmetic and copies ran while one was open for 3% -> 3% of each run, Pallas kernels for 20% -> 25%
where the time goes in v4:
time: 510 us; the launch traced here: 505 us
  waiting for transfers between devices  210 us (41%)
  Pallas kernels  177 us (35%)
  starting transfers between devices  73.4 us (14%)
  local copies, waits for them, and re-layouts  21.3 us (4%)
  between operations  16.2 us (3%)
  other arithmetic  7.1 us (1%)
    ppermute x55, waiting for transfers between devices, swap(): return lax.ppermute(value, axes, [(i, i ^ mask) for i in range(size)])  198 us
    pallas_call x12, Pallas kernels, call(): pl.pallas_call(kernel, grid=(1,), in_specs=[s or whole(a) for a, s in zip...  83.5 us
    ppermute x55, starting transfers between devices, swap(): return lax.ppermute(value, axes, [(i, i ^ mask) for i in range(size)])  61.2 us
    pallas_call x1, Pallas kernels, on_device(): pl.pallas_call(functools.partial(expert_kernel, (dp_ranks, quarter, exper...  17.9 us
    pallas_call x1, Pallas kernels, adam(): pl.pallas_call(adam_kernel, grid=(pl.cdiv(count, block),), in_specs=[SMEM...  12.5 us
    unnamed x99, local copies, waits for them, and re-layouts  12.5 us
    pallas_call x1, Pallas kernels, on_device(): pl.pallas_call(functools.partial(fold_layers_kernel, cut), grid=(places,)...  12.2 us
    pallas_call x1, Pallas kernels, on_device(): pl.pallas_call(functools.partial(expert_grad_kernel, (dp_ranks, quarter))...  11.8 us
  transfers between devices with their start and end apart: 61, of which 31 were waited for; matrix products, arithmetic and copies ran while one was open for 3% of the time, Pallas kernels for 25%

profile of v4, /device:TPU:0, one launch (start us, length us, event | category | flops | bytes accessed | tf_op | source)
XLA Modules:
  0.0 505.5 jit_solution(9931724065038683455)
XLA Ops:
  8.4 7.7 %collective-permute-done.tail_ref = f32[96,128]{1,0:T(8,128)S(1)} collective-permute-done((f32[96,128]{1,0:T(8,128)S(1)}, f32[96,128]{1,0:T(8,128)S(1)}, u32[]{:S(2)}, u32[]{:S(2)}) %collective-permute-start) | collective-permute-done | bytes 49184 | tf_op jit(solution)/shard_map/ppermute | solution.py:891
  21.6 9.6 %collective-permute-done.2.refs_4_ = bf16[400,768]{1,0:T(8,128)(2,1)S(1)} collective-permute-done((bf16[400,768]{1,0:T(8,128)(2,1)}, bf16[400,768]{1,0:T(8,128)(2,1)S(1)}, u32[]{:S(2)}, u32[]{:S(2)}) %collective-permute-start.2) | collective-permute-done | bytes 614432 | tf_op jit(solution)/shard_map/ppermute | solution.py:809
  50.6 11.4 %collective-permute-done.1.refs_0_ = bf16[400,768]{1,0:T(8,128)(2,1)S(1)} collective-permute-done((bf16[400,768]{1,0:T(8,128)(2,1)}, bf16[400,768]{1,0:T(8,128)(2,1)S(1)}, u32[]{:S(2)}, u32[]{:S(2)}) %collective-permute-start.1) | collective-permute-done | bytes 614432 | tf_op jit(solution)/shard_map/ppermute | solution.py:809
  63.9 13.9 %collective-permute-done.9.refs_4_ = bf16[400,768]{1,0:T(8,128)(2,1)S(1)} collective-permute-done((bf16[400,768]{1,0:T(8,128)(2,1)S(1)}, bf16[400,768]{1,0:T(8,128)(2,1)S(1)}, u32[]{:S(2)}, u32[]{:S(2)}) %collective-permute-start.9) | collective-permute-done | bytes 614432 | tf_op jit(solution)/shard_map/ppermute | solution.py:809
  84.1 10.6 %collective-permute-done.13.refs_5_ = bf16[400,768]{1,0:T(8,128)(2,1)} collective-permute-done((bf16[400,768]{1,0:T(8,128)(2,1)S(1)}, bf16[400,768]{1,0:T(8,128)(2,1)}, u32[]{:S(2)}, u32[]{:S(2)}) %collective-permute-start.13) | collective-permute-done | bytes 614432 | tf_op jit(solution)/shard_map/ppermute | solution.py:809
  121.0 7.0 %collective-permute-done.16.refs_2_.refs_7_.refs_6_ = bf16[2,4,400,768]{3,2,1,0:T(8,128)(2,1)} collective-permute-done((bf16[2,4,400,768]{3,2,1,0:T(8,128)(2,1)}, bf16[2,4,400,768]{3,2,1,0:T(8,128)(2,1)}, u32[]{:S(2)}, u32[]{:S(2)}) %collective-permute-start.16) | collective-permute-done | bytes 4915232 | tf_op jit(solution)/shard_map/ppermute | solution.py:809
  128.1 15.9 %forward.1 = (f32[208,768]{1,0:T(8,128)}, bf16[208,768]{1,0:T(8,128)(2,1)}, bf16[208,768]{1,0:T(8,128)(2,1)}, bf16[208,768]{1,0:T(8,128)(2,1)}, bf16[208,768]{1,...) custom-call(s32[2]{0:T(128)} %pad_add_fusion.place_ref, ...), custom_call_target="tpu_custom_call" | custom-call | flops 1 | bytes 1 | tf_op jit(solution)/shard_map/forward/pallas_call | solution.py:1044
  148.0 18.3 %collective-permute-done.18.refs_1_ = bf16[1536,768]{1,0:T(8,128)(2,1)} collective-permute-done((bf16[1536,768]{1,0:T(8,128)(2,1)S(1)}, bf16[1536,768]{1,0:T(8,128)(2,1)}, u32[]{:S(2)}, u32[]{:S(2)}) %collective-permute-start.18) | collective-permute-done | bytes 2359328 | tf_op jit(solution)/shard_map/ppermute | solution.py:809
  171.5 23.3 %collective-permute-done.20.refs_3_ = bf16[768,768]{1,0:T(8,128)(2,1)S(1)} collective-permute-done((bf16[768,768]{1,0:T(8,128)(2,1)S(1)}, bf16[768,768]{1,0:T(8,128)(2,1)S(1)}, u32[]{:S(2)}, u32[]{:S(2)}) %collective-permute-start.20) | collective-permute-done | bytes 1179680 | tf_op jit(solution)/shard_map/ppermute | solution.py:809
  197.4 17.9 %expert.1 = (bf16[2,56,768]{2,1,0:T(8,128)(2,1)}, bf16[2,56,768]{2,1,0:T(8,128)(2,1)}, bf16[2,56,768]{2,1,0:T(8,128)(2,1)}, bf16[2,56,768]{2,1,0:T(8,128)(2,1)},...) custom-call(s32[2]{0:T(128)} %pad_add_fusion.1.me_ref, ...), custom_call_target="tpu_custom_call" | custom-call | flops 1 | bytes 1 | tf_op jit(solution)/shard_map/expert/pallas_call | solution.py:1142
  219.0 11.8 %expert_grad.1 = (bf16[768,768]{1,0:T(8,128)(2,1)}, bf16[768,768]{1,0:T(8,128)(2,1)}, bf16[768,768]{1,0:T(8,128)(2,1)}, bf16[768,768]{1,0:T(8,128)(2,1)}, bf16[7...) custom-call(s32[1]{0:T(128)} %bitcast.14.dp_ref, ...), custom_call_target="tpu_custom_call" | custom-call | flops 1 | bytes 1 | tf_op jit(solution)/shard_map/expert_grad/pallas_call | solution.py:1163
  245.0 11.8 %attn_bwd.2 = (f32[208,768]{1,0:T(8,128)}, f32[1,768]{1,0:T(1,128)}, bf16[208,768]{1,0:T(8,128)(2,1)}, bf16[208,768]{1,0:T(8,128)(2,1)}, bf16[208,768]{1,0:T(8,128)(2,1)}) custom-call(s32[2]{0:T(128)} %pad_add_fusion.place_ref, f32[1,768]{1,0:T(1,128)} %get-tuple-element.400.gain_ref, f32[208,768]{1,0:T(8,128)} %get-tuple-element.229.refs_0_, ...), custom_call_target="tpu_custom_call" | custom-call | flops 1 | bytes 1 | tf_op jit(solution)/shard_map/attn_bwd/pallas_call | solution.py:1044
  256.8 14.8 %mlp_bwd.1 = (f32[208,768]{1,0:T(8,128)}, f32[1,768]{1,0:T(1,128)}, bf16[4,384,768]{2,1,0:T(8,128)(2,1)}, bf16[4,384,768]{2,1,0:T(8,128)(2,1)}, bf16[4,384,768]{...) custom-call(s32[2]{0:T(128)} %pad_add_fusion.place_ref, f32[1,768]{1,0:T(1,128)} %get-tuple-element.401.gain_ref, ...), custom_call_target="tpu_custom_call" | custom-call | flops 1 | bytes 1 | tf_op jit(solution)/shard_map/mlp_bwd/pallas_call | solution.py:1044
  271.7 11.8 %attn_bwd.3 = (f32[208,768]{1,0:T(8,128)}, f32[1,768]{1,0:T(1,128)}, bf16[208,768]{1,0:T(8,128)(2,1)}, bf16[208,768]{1,0:T(8,128)(2,1)}, bf16[208,768]{1,0:T(8,128)(2,1)}) custom-call(s32[2]{0:T(128)} %pad_add_fusion.place_ref, f32[1,768]{1,0:T(1,128)} %get-tuple-element.398.gain_ref, f32[208,768]{1,0:T(8,128)} %get-tuple-element.238.refs_0_, ...), custom_call_target="tpu_custom_call" | custom-call | flops 1 | bytes 1 | tf_op jit(solution)/shard_map/attn_bwd/pallas_call | solution.py:1044
  299.8 6.7 %collective-permute-done.28.refs_5_ = bf16[4,384,768]{2,1,0:T(8,128)(2,1)S(1)} collective-permute-done((bf16[4,384,768]{2,1,0:T(8,128)(2,1)}, bf16[4,384,768]{2,1,0:T(8,128)(2,1)S(1)}, u32[]{:S(2)}, u32[]{:S(2)}) %collective-permute-start.28) | collective-permute-done | bytes 2359328 | tf_op jit(solution)/shard_map/ppermute | solution.py:809
  308.0 12.2 %fold_layers.1 = (bf16[4,1,64,768]{3,2,1,0:T(8,128)(2,1)}, bf16[4,1,64,768]{3,2,1,0:T(8,128)(2,1)}, bf16[4,1,64,768]{3,2,1,0:T(8,128)(2,1)}, bf16[4,1,64,768]{3,...) custom-call(s32[1]{0:T(128)} %bitcast.top_ref, ...), custom_call_target="tpu_custom_call" | custom-call | flops 1 | bytes 1 | tf_op jit(solution)/shard_map/fold_layers/pallas_call | solution.py:1270
  327.9 6.2 %fold_expert.1 = (bf16[768,768]{1,0:T(8,128)(2,1)}, bf16[768,768]{1,0:T(8,128)(2,1)}, bf16[768,768]{1,0:T(8,128)(2,1)}, bf16[768,768]{1,0:T(8,128)(2,1)}) custom-call(bf16[768,768]{1,0:T(8,128)(2,1)} %get-tuple-element.222.refs_0_, bf16[768,768]{1,0:T(8,128)(2,1)} %get-tuple-element.223.refs_1_, bf16[768,768]{1,0:T(8,128)(2,1)} %copy-done.10, ...), custom_call_target="tpu_custom_call" | custom-call | flops 1 | bytes 1 | tf_op jit(solution)/shard_map/fold_expert/pallas_call | solution.py:1044
  334.1 8.0 %collective-permute-done.32 = bf16[4,1,64,768]{3,2,0,1:T(8,128)(2,1)S(1)} collective-permute-done((bf16[4,1,64,768]{3,2,0,1:T(8,128)(2,1)}, bf16[4,1,64,768]{3,2,0,1:T(8,128)(2,1)S(1)}, u32[]{:S(2)}, u32[]{:S(2)}) %collective-permute-start.32) | collective-permute-done | bytes 393248 | tf_op jit(solution)/shard_map/ppermute | solution.py:809
  342.1 13.0 %collective-permute-done.33 = bf16[4,1,64,768]{3,2,0,1:T(8,128)(2,1)S(1)} collective-permute-done((bf16[4,1,64,768]{3,2,0,1:T(8,128)(2,1)}, bf16[4,1,64,768]{3,2,0,1:T(8,128)(2,1)S(1)}, u32[]{:S(2)}, u32[]{:S(2)}) %collective-permute-start.33) | collective-permute-done | bytes 393248 | tf_op jit(solution)/shard_map/ppermute | solution.py:809
  358.4 7.2 %collective-permute-done.30.got_x = bf16[2,4,160,768]{3,2,1,0:T(8,128)(2,1)S(1)} collective-permute-done((bf16[2,4,160,768]{3,2,1,0:T(8,128)(2,1)}, bf16[2,4,160,768]{3,2,1,0:T(8,128)(2,1)S(1)}, u32[]{:S(2)}, u32[]{:S(2)}) %collective-permute-start.30) | collective-permute-done | bytes 1966112 | tf_op jit(solution)/shard_map/ppermute | solution.py:809
  384.1 9.8 %collective-permute-done.38.refs_2_ = bf16[2,56,768]{2,1,0:T(8,128)(2,1)S(1)} collective-permute-done((bf16[2,56,768]{2,1,0:T(8,128)(2,1)S(1)}, bf16[2,56,768]{2,1,0:T(8,128)(2,1)S(1)}, u32[]{:S(2)}, u32[]{:S(2)}) %collective-permute-start.38) | collective-permute-done | bytes 172064 | tf_op jit(solution)/shard_map/ppermute | solution.py:809
  410.3 23.6 %collective-permute-done.44.refs_1_ = bf16[768,768]{1,0:T(8,128)(2,1)S(1)} collective-permute-done((bf16[768,768]{1,0:T(8,128)(2,1)}, bf16[768,768]{1,0:T(8,128)(2,1)S(1)}, u32[]{:S(2)}, u32[]{:S(2)}) %collective-permute-start.44) | collective-permute-done | bytes 1179680 | tf_op jit(solution)/shard_map/ppermute | solution.py:809
  454.1 8.4 %collective-permute-start.50 = (f32[1,128]{1,0:T(1,128)S(1)}, f32[1,128]{1,0:T(1,128)S(1)}, u32[]{:S(2)}, u32[]{:S(2)}) collective-permute-start(f32[1,128]{1,0:T(1,128)S(1)} %add.44), channel_id=1, source_target_pairs={{0,2},{1,3},{2,0},{3,1},{4,6},{5,7},{6,4},{7,5},{8,10},{9,11},{10,... | collective-permute-start | bytes 1544 | tf_op jit(solution)/shard_map/ppermute | solution.py:809
  480.4 12.5 %adam.1 = (f32[9216,128]{1,0:T(8,128)}, f32[9216,128]{1,0:T(8,128)}, f32[9216,128]{1,0:T(8,128)}) custom-call(f32[1]{0:T(128)} %bitcast.34.clip_ref, f32[9216,128]{1,0:T(8,128)} %get-tuple-element.356.grad_ref, f32[9216,128]{1,0:T(8,128)} %bitcast.56, f32[9216,128]{1,0:T(8,128)} %bitcast.57), custom_call_target="tpu_custom_call" | custom-call | flops 1 | bytes 1 | tf_op jit(solution)/shard_map/adam/pallas_call | solution.py:206
  (254 shorter events, 195.5 us)
Async XLA Ops:
  19.1 30.7 %collective-permute-start.5 = (bf16[400,768]{1,0:T(8,128)(2,1)}, bf16[400,768]{1,0:T(8,128)(2,1)S(1)}, u32[]{:S(2)}, u32[]{:S(2)}) collective-permute-start(bf16[400,768]{1,0:T(8,128)(2,1)} %pack_dense.1.refs_0_), channel_id=1, source_target_pairs={{0,8},{1,9},{2,10},{3,11},{4,12},{5,13},{6,14},{7,15},{8,0},{9,1},... | collective-permute-start | bytes 1843208 | tf_op jit(solution)/shard_map/ppermute | solution.py:809
  20.1 29.7 %collective-permute-start.6 = (bf16[400,768]{1,0:T(8,128)(2,1)}, bf16[400,768]{1,0:T(8,128)(2,1)S(1)}, u32[]{:S(2)}, u32[]{:S(2)}) collective-permute-start(bf16[400,768]{1,0:T(8,128)(2,1)} %pack_dense.1.refs_0_), channel_id=1, source_target_pairs={{0,16},{1,17},{2,18},{3,19},{4,20},{5,21},{6,22},{7,23},{8,24},{9,... | collective-permute-start | bytes 1843208 | tf_op jit(solution)/shard_map/ppermute | solution.py:809
  34.2 27.8 %collective-permute-start.1 = (bf16[400,768]{1,0:T(8,128)(2,1)}, bf16[400,768]{1,0:T(8,128)(2,1)S(1)}, u32[]{:S(2)}, u32[]{:S(2)}) collective-permute-start(bf16[400,768]{1,0:T(8,128)(2,1)} %pack_dense.1.refs_0_), channel_id=1, source_target_pairs={{0,4},{1,5},{2,6},{3,7},{4,0},{5,1},{6,2},{7,3},{8,12},{9,13},{10,... | collective-permute-start | bytes 1843208 | tf_op jit(solution)/shard_map/ppermute | solution.py:809
  78.8 27.4 %all-to-all-start = ((bf16[8,56,768]{2,1,0:T(8,128)(2,1)}), bf16[8,56,768]{2,1,0:T(8,128)(2,1)S(1)}, u32[]{:S(2)}, u32[]{:S(2)}) async-start(bf16[8,56,768]{2,1,0:T(8,128)(2,1)} %bitcast.67), calls=%async_computation | async-start | bytes 1376256 | tf_op jit(solution)/shard_map/all_to_all | solution.py:947
  113.0 53.3 %collective-permute-start.18 = (bf16[1536,768]{1,0:T(8,128)(2,1)S(1)}, bf16[1536,768]{1,0:T(8,128)(2,1)}, u32[]{:S(2)}, u32[]{:S(2)}) collective-permute-start(bf16[1536,768]{1,0:T(8,128)(2,1)S(1)} %copy-done), channel_id=1, source_target_pairs={{0,8},{8,0},{16,24},{24,16},{1,9},{9,1},{17,25},{25,17},{2,10},{10... | collective-permute-start | bytes 7077896 | tf_op jit(solution)/shard_map/ppermute | solution.py:809
  114.5 53.5 %collective-permute-start.19 = (bf16[1536,768]{1,0:T(8,128)(2,1)S(1)}, bf16[1536,768]{1,0:T(8,128)(2,1)}, u32[]{:S(2)}, u32[]{:S(2)}) collective-permute-start(bf16[1536,768]{1,0:T(8,128)(2,1)S(1)} %copy-done), channel_id=1, source_target_pairs={{0,16},{8,24},{16,0},{24,8},{1,17},{9,25},{17,1},{25,9},{2,18},{10... | collective-permute-start | bytes 7077896 | tf_op jit(solution)/shard_map/ppermute | solution.py:809
  144.0 52.1 %all-to-all-start.1 = ((bf16[8,56,896]{2,1,0:T(8,128)(2,1)}), bf16[8,56,896]{2,1,0:T(8,128)(2,1)S(1)}, u32[]{:S(2)}, u32[]{:S(2)}) async-start(bf16[8,56,896]{2,1,0:T(8,128)(2,1)} %bitcast.66), calls=%async_computation.1 | async-start | bytes 1605632 | tf_op jit(solution)/shard_map/all_to_all | solution.py:947
  167.6 27.1 %collective-permute-start.20 = (bf16[768,768]{1,0:T(8,128)(2,1)S(1)}, bf16[768,768]{1,0:T(8,128)(2,1)S(1)}, u32[]{:S(2)}, u32[]{:S(2)}) collective-permute-start(bf16[768,768]{1,0:T(8,128)(2,1)S(1)} %slice.72), channel_id=1, source_target_pairs={{0,16},{8,24},{16,0},{24,8},{1,17},{9,25},{17,1},{25,9},{2,18},{10... | collective-permute-start | bytes 3538952 | tf_op jit(solution)/shard_map/ppermute | solution.py:809
  169.3 26.8 %collective-permute-start.21 = (bf16[768,768]{1,0:T(8,128)(2,1)S(1)}, bf16[768,768]{1,0:T(8,128)(2,1)S(1)}, u32[]{:S(2)}, u32[]{:S(2)}) collective-permute-start(bf16[768,768]{1,0:T(8,128)(2,1)S(1)} %slice.73), channel_id=1, source_target_pairs={{0,8},{8,0},{16,24},{24,16},{1,9},{9,1},{17,25},{25,17},{2,10},{10... | collective-permute-start | bytes 3538952 | tf_op jit(solution)/shard_map/ppermute | solution.py:809
  215.4 24.8 %all-to-all-start.2 = ((bf16[8,56,896]{2,1,0:T(8,128)(2,1)}), bf16[8,56,896]{2,1,0:T(8,128)(2,1)S(1)}, u32[]{:S(2)}, u32[]{:S(2)}) async-start(bf16[8,56,896]{2,1,0:T(8,128)(2,1)} %bitcast.65), calls=%async_computation.2 | async-start | bytes 1605632 | tf_op jit(solution)/shard_map/all_to_all | solution.py:947
  218.9 245.1 %all-gather.4.cloned.1.call-start = ((), (), s32[]{:S(2)}) async-start(), calls=%async_computation.3 | async-start | bytes 1622016 | tf_op jit(solution)/shard_map/all_gather | solution.py:1261
  230.8 54.1 %collective-permute-start.22 = (bf16[768,768]{1,0:T(8,128)(2,1)}, bf16[768,768]{1,0:T(8,128)(2,1)S(1)}, u32[]{:S(2)}, u32[]{:S(2)}) collective-permute-start(bf16[768,768]{1,0:T(8,128)(2,1)} %get-tuple-element.220), channel_id=1, source_target_pairs={{0,8},{8,0},{16,24},{24,16},{1,9},{9,1},{17,25},{25,17},{2,10},{10... | collective-permute-start | bytes 3538952 | tf_op jit(solution)/shard_map/ppermute | solution.py:809
  232.3 52.6 %collective-permute-start.23 = (bf16[768,768]{1,0:T(8,128)(2,1)}, bf16[768,768]{1,0:T(8,128)(2,1)S(1)}, u32[]{:S(2)}, u32[]{:S(2)}) collective-permute-start(bf16[768,768]{1,0:T(8,128)(2,1)} %get-tuple-element.221), channel_id=1, source_target_pairs={{0,8},{8,0},{16,24},{24,16},{1,9},{9,1},{17,25},{25,17},{2,10},{10... | collective-permute-start | bytes 3538952 | tf_op jit(solution)/shard_map/ppermute | solution.py:809
  232.9 52.1 %collective-permute-start.24 = (bf16[768,768]{1,0:T(8,128)(2,1)}, bf16[768,768]{1,0:T(8,128)(2,1)}, u32[]{:S(2)}, u32[]{:S(2)}) collective-permute-start(bf16[768,768]{1,0:T(8,128)(2,1)} %get-tuple-element.224), channel_id=1, source_target_pairs={{0,16},{8,24},{16,0},{24,8},{1,17},{9,25},{17,1},{25,9},{2,18},{10... | collective-permute-start | bytes 3538952 | tf_op jit(solution)/shard_map/ppermute | solution.py:809
  234.6 51.5 %collective-permute-start.25 = (bf16[768,768]{1,0:T(8,128)(2,1)}, bf16[768,768]{1,0:T(8,128)(2,1)}, u32[]{:S(2)}, u32[]{:S(2)}) collective-permute-start(bf16[768,768]{1,0:T(8,128)(2,1)} %get-tuple-element.225), channel_id=1, source_target_pairs={{0,16},{8,24},{16,0},{24,8},{1,17},{9,25},{17,1},{25,9},{2,18},{10... | collective-permute-start | bytes 3538952 | tf_op jit(solution)/shard_map/ppermute | solution.py:809
  320.2 45.4 %collective-permute-start.30 = (bf16[2,4,160,768]{3,2,1,0:T(8,128)(2,1)}, bf16[2,4,160,768]{3,2,1,0:T(8,128)(2,1)S(1)}, u32[]{:S(2)}, u32[]{:S(2)}) collective-permute-start(bf16[2,4,160,768]{3,2,1,0:T(8,128)(2,1)} %get-tuple-element.269), channel_id=1, source_target_pairs={{0,8},{1,9},{2,10},{3,11},{4,12},{5,13},{6,14},{7,15},{8,0},{9,1},... | collective-permute-start | bytes 5898248 | tf_op jit(solution)/shard_map/ppermute | solution.py:809
  321.8 45.0 %collective-permute-start.31 = (bf16[2,4,160,768]{3,2,1,0:T(8,128)(2,1)}, bf16[2,4,160,768]{3,2,1,0:T(8,128)(2,1)S(1)}, u32[]{:S(2)}, u32[]{:S(2)}) collective-permute-start(bf16[2,4,160,768]{3,2,1,0:T(8,128)(2,1)} %get-tuple-element.270), channel_id=1, source_target_pairs={{0,16},{1,17},{2,18},{3,19},{4,20},{5,21},{6,22},{7,23},{8,24},{9,... | collective-permute-start | bytes 5898248 | tf_op jit(solution)/shard_map/ppermute | solution.py:809
  325.1 30.0 %collective-permute-start.33 = (bf16[4,1,64,768]{3,2,0,1:T(8,128)(2,1)}, bf16[4,1,64,768]{3,2,0,1:T(8,128)(2,1)S(1)}, u32[]{:S(2)}, u32[]{:S(2)}) collective-permute-start(bf16[4,1,64,768]{3,2,0,1:T(8,128)(2,1)} %bitcast.85), channel_id=1, source_target_pairs={{0,4},{1,5},{2,6},{3,7},{4,0},{5,1},{6,2},{7,3},{8,12},{9,13},{10,... | collective-permute-start | bytes 1179656 | tf_op jit(solution)/shard_map/ppermute | solution.py:809
  327.5 27.6 %collective-permute-start.34 = (bf16[4,1,64,768]{3,2,0,1:T(8,128)(2,1)}, bf16[4,1,64,768]{3,2,0,1:T(8,128)(2,1)S(1)}, u32[]{:S(2)}, u32[]{:S(2)}) collective-permute-start(bf16[4,1,64,768]{3,2,0,1:T(8,128)(2,1)} %bitcast.84), channel_id=1, source_target_pairs={{0,6},{1,7},{2,4},{3,5},{4,2},{5,3},{6,0},{7,1},{8,14},{9,15},{10,... | collective-permute-start | bytes 1179656 | tf_op jit(solution)/shard_map/ppermute | solution.py:809
  403.4 30.5 %collective-permute-start.44 = (bf16[768,768]{1,0:T(8,128)(2,1)}, bf16[768,768]{1,0:T(8,128)(2,1)S(1)}, u32[]{:S(2)}, u32[]{:S(2)}) collective-permute-start(bf16[768,768]{1,0:T(8,128)(2,1)} %get-tuple-element.331), channel_id=1, source_target_pairs={{0,16},{8,24},{16,0},{24,8},{1,17},{9,25},{17,1},{25,9},{2,18},{10... | collective-permute-start | bytes 3538952 | tf_op jit(solution)/shard_map/ppermute | solution.py:809
  405.1 30.4 %collective-permute-start.45 = (bf16[768,768]{1,0:T(8,128)(2,1)}, bf16[768,768]{1,0:T(8,128)(2,1)S(1)}, u32[]{:S(2)}, u32[]{:S(2)}) collective-permute-start(bf16[768,768]{1,0:T(8,128)(2,1)} %get-tuple-element.333), channel_id=1, source_target_pairs={{0,8},{8,0},{16,24},{24,16},{1,9},{9,1},{17,25},{25,17},{2,10},{10... | collective-permute-start | bytes 3538952 | tf_op jit(solution)/shard_map/ppermute | solution.py:809
  405.9 30.7 %collective-permute-start.41 = (bf16[1,320,768]{2,1,0:T(8,128)(2,1)}, bf16[1,320,768]{2,1,0:T(8,128)(2,1)S(1)}, u32[]{:S(2)}, u32[]{:S(2)}) collective-permute-start(bf16[1,320,768]{2,1,0:T(8,128)(2,1)} %get-tuple-element.325), channel_id=1, source_target_pairs={{0,2},{1,3},{2,0},{3,1},{4,6},{5,7},{6,4},{7,5},{8,10},{9,11},{10,... | collective-permute-start | bytes 1474568 | tf_op jit(solution)/shard_map/ppermute | solution.py:809
  407.6 42.0 %collective-permute-start.42 = (bf16[1,320,768]{2,1,0:T(8,128)(2,1)}, bf16[1,320,768]{2,1,0:T(8,128)(2,1)}, u32[]{:S(2)}, u32[]{:S(2)}) collective-permute-start(bf16[1,320,768]{2,1,0:T(8,128)(2,1)} %get-tuple-element.326), channel_id=1, source_target_pairs={{0,4},{1,5},{2,6},{3,7},{4,0},{5,1},{6,2},{7,3},{8,12},{9,13},{10,... | collective-permute-start | bytes 1474568 | tf_op jit(solution)/shard_map/ppermute | solution.py:809
  410.0 39.6 %collective-permute-start.43 = (bf16[1,320,768]{2,1,0:T(8,128)(2,1)}, bf16[1,320,768]{2,1,0:T(8,128)(2,1)}, u32[]{:S(2)}, u32[]{:S(2)}) collective-permute-start(bf16[1,320,768]{2,1,0:T(8,128)(2,1)} %get-tuple-element.327), channel_id=1, source_target_pairs={{0,6},{1,7},{2,4},{3,5},{4,2},{5,3},{6,0},{7,1},{8,14},{9,15},{10,... | collective-permute-start | bytes 1474568 | tf_op jit(solution)/shard_map/ppermute | solution.py:809
  (85 other events, 935.8 us)
Sparse Core Ops, SparseCore 0:
  376.5 77.6 all-gather.3

commit v5 on v4

--- a/solution.py
+++ b/solution.py
@@ -29,8 +29,8 @@
     return pltpu.CompilerParams(vmem_limit_bytes=mib << 20)
 
 
-def cost(*_):
-    return pl.CostEstimate(flops=1, bytes_accessed=1, transcendentals=0)
+def cost(rows=0):
+    return pl.CostEstimate(flops=1 + int(rows * 16.45e6), bytes_accessed=1, transcendentals=0)
 
 
 def dot(a, b):
@@ -138,6 +138,10 @@
 def unpack_kernel(dims, groups, wide_ref, *refs):
     rows, tiles = dims
     refs, (out_ref, square_ref, rows_ref) = refs[:-3], refs[-3:]
+    if len(refs) > sum(groups):
+        refs, (small_ref, before_ref) = refs[:-2], refs[-2:]
+    else:
+        small_ref = None
     at = 0
     for count in groups:
         value = add_up(refs[:count])
@@ -153,11 +157,18 @@
             for j in range(tiles):
                 piece = rows_ref[q * quarter : (q + 1) * quarter, LANES * j : LANES * (j + 1)]
                 if is_wide:
-                    out_ref[pl.ds(tiles * q + j, quarter, stride=4 * tiles), :] = piece
+                    at = pl.ds(tiles * q + j, quarter, stride=4 * tiles)
                 else:
-                    out_ref[pl.ds(tiles * quarter * q + j, quarter, stride=tiles), :] = piece
+                    at = pl.ds(tiles * quarter * q + j, quarter, stride=tiles)
+                out_ref[at, :] = piece
                 total = total + jnp.sum(piece * piece, axis=0, keepdims=True)
-        square_ref[...] = total
+        if small_ref is None:
+            square_ref[...] = total
+        else:
+            count = small_ref.shape[0]
+            square_ref[0:count] = small_ref[...]
+            square_ref[count:] = jnp.zeros((square_ref.shape[0] - count, LANES), f32)
+            square_ref[count : count + 1] = total + before_ref[...]
 
     @pl.when(wide)
     def _():
@@ -168,51 +179,86 @@
         store(False)
 
 
-def stack_rows_kernel(*refs):
-    out_ref = refs[-1]
-    at = 0
-    for ref in refs[:-1]:
-        out_ref[at : at + ref.shape[0]] = ref[...]
-        at += ref.shape[0]
-
-
-def adam_shift_kernel(
-    dims, clip_ref, k_ref, flat_ref, head_ref, momentum_ref, variance_ref,
-    update_ref, momentum_out, variance_out, grad_ref, buf,
-):
-    step, own = dims
-    count = flat_ref.shape[0]
-    buf[0:count] = flat_ref[...]
-    buf[count : count + head_ref.shape[0]] = head_ref[...]
-    grad_ref[...] = buf[pl.ds(step * k_ref[0], own), :]
-    adam_kernel(clip_ref, grad_ref, momentum_ref, variance_ref, update_ref, momentum_out, variance_out)
-
-
-def adam_kernel(clip_ref, grad_ref, momentum_ref, variance_ref, update_ref, momentum_out, variance_out):
-    clipped = grad_ref[...] * clip_ref[0]
-    momentum_new = beta_first * momentum_ref[...] + (1.0 - beta_first) * clipped
-    variance_new = beta_second * variance_ref[...] + (1.0 - beta_second) * clipped * clipped
+def adam_values(clip, grad, momentum, variance):
+    clipped = grad * clip
+    momentum_new = beta_first * momentum + (1.0 - beta_first) * clipped
+    variance_new = beta_second * variance + (1.0 - beta_second) * clipped * clipped
     first_hat = momentum_new / (1.0 - beta_first**adam_step)
     second_hat = variance_new / (1.0 - beta_second**adam_step)
-    update_ref[...] = -first_hat / (jnp.sqrt(second_hat) + adam_eps)
-    momentum_out[...] = momentum_new
-    variance_out[...] = variance_new
-
-
-def adam(clip, grad, momentum, variance, block):
-    count = grad.shape[0]
-    spec = pl.BlockSpec((block, LANES), lambda i: (i, 0))
-    shape = jax.ShapeDtypeStruct(grad.shape, f32)
-    return pl.pallas_call(
-        adam_kernel,
-        grid=(pl.cdiv(count, block),),
-        in_specs=[SMEM, spec, spec, spec],
-        out_specs=[spec] * 3,
-        out_shape=[shape] * 3,
-        compiler_params=params(),
-        cost_estimate=cost(),
-        name="adam",
-    )(clip, grad, momentum, variance)
+    return -first_hat / (jnp.sqrt(second_hat) + adam_eps), momentum_new, variance_new
+
+
+def adam_kernel(dims, k_ref, total_ref, head_ref, *refs):
+    step, chunks, devices, param_count, router_rows = dims
+    sources, refs = refs[:6], refs[6:]
+    outs, dense_outs, gains_ref, refs = refs[:3], refs[3:7], refs[7], refs[8:]
+    held, slots, buf, dense_slots, in_sems, sems, dense_in, dense_sems = refs[:3], *refs[3:]
+    flat_ref, dense_m, dense_v = dense_slots.at[0], dense_slots.at[1], dense_slots.at[2]
+    rows = slots.shape[2]
+
+    def arriving(c, i):
+        at = slice(c * rows, (c + 1) * rows)
+        return pltpu.make_async_copy(sources[i].at[at], held[i].at[at], in_sems.at[c, i])
+
+    def leaving(c, i):
+        target = outs[i].at[c * rows : (c + 1) * rows]
+        return pltpu.make_async_copy(slots.at[c % 4, i], target, sems.at[c % 4, i])
+
+    for c in range(chunks):
+        for i in range(3):
+            arriving(c, i).start()
+    count, own = sources[3].shape[0], sources[4].shape[0]
+    dense_copies = [pltpu.make_async_copy(sources[3], buf.at[0:count], dense_in.at[0])]
+    for i in (1, 2):
+        dense_copies.append(pltpu.make_async_copy(sources[3 + i], dense_slots.at[i], dense_in.at[i]))
+    for copy in dense_copies:
+        copy.start()
+
+    summed = head_ref.shape[0]
+    squares = total_ref[summed : summed + 1]
+    for at in range(0, summed, 8):
+        part = total_ref[at : at + 8]
+        squares = squares + jnp.sum(part * part, axis=0, keepdims=True)
+    square_sum = jnp.sum(squares, axis=1, keepdims=True)
+    clip = jnp.minimum(1.0, jnp.sqrt(param_count / (square_sum + 1e-06)))
+    tiles = gains_ref.shape[1] // LANES
+    for which in range(gains_ref.shape[0]):
+        for j in range(tiles):
+            at = router_rows + which * tiles + j
+            gains_ref[which : which + 1, LANES * j : LANES * (j + 1)] = total_ref[at : at + 1]
+
+    for c in range(chunks):
+        at = slice(c * rows, (c + 1) * rows)
+        for i in range(3):
+            arriving(c, i).wait()
+            if c >= 4:
+                leaving(c - 4, i).wait()
+        values = adam_values(clip, held[0][at], held[1][at], held[2][at])
+        for i, value in enumerate(values):
+            slots[c % 4, i] = value
+            leaving(c, i).start()
+    for copy in dense_copies:
+        copy.wait()
+    last = k_ref[0] == devices - 1
+
+    @pl.when(last)
+    def _():
+        buf[count : count + summed] = total_ref[0:summed]
+
+    @pl.when(jnp.logical_not(last))
+    def _():
+        buf[count : count + summed] = head_ref[...]
+
+    grad = buf[pl.ds(step * k_ref[0], own), :]
+    values = adam_values(clip, grad, dense_m[...], dense_v[...])
+    for i, value in enumerate((grad, *values)):
+        dense_slots[i] = value
+    targets = (dense_outs[3], *dense_outs[:3])
+    copies = start_all([dense_slots.at[i] for i in range(4)], targets, dense_sems)
+    for c in range(max(0, chunks - 4), chunks):
+        for i in range(3):
+            leaving(c, i).wait()
+    wait_all(copies)
 
 
 def route_kernel(
@@ -335,17 +381,7 @@
     out_ref[...] = stream_ref[...] + dot(o_ref[...], matrix(w_ref, 3))
 
 
-def attn_bwd_kernel(seq, spots, layer, place_ref, gain_ref, *refs):
-    ins, arrays, refs = refs[:5], refs[5 : 5 + len(refs) - 24], refs[len(refs) - 19 :]
-    out_ref, gain_out, *outs = refs[:5]
-    grad_ref, stream_ref, q_ref, k_ref, v_ref = refs[5:10]
-    held_out, dq_ref, dk_ref, dv_ref, do_ref, w_ref, w_sems, in_sems, out_sems = refs[10:]
-    copies = layer_copies(spots, arrays, place_ref, layer, w_ref, w_sems)
-    for copy in copies:
-        copy.start()
-    arriving = start_all(ins, (grad_ref, stream_ref, q_ref, k_ref, v_ref), in_sems)
-    wait_all(copies)
-    wait_all(arriving)
+def attn_bwd(seq, grad_ref, stream_ref, gain, w_ref, q_ref, k_ref, v_ref, out_ref, dq_ref, dk_ref, dv_ref, do_ref):
     do_ref[...] = dot_nt(grad_ref[...].astype(bf16), matrix(w_ref, 3)).astype(bf16)
     count = grad_ref.shape[0]
     key_ok = lax.broadcasted_iota(jnp.int32, (count, count), 1) < seq
@@ -371,22 +407,17 @@
         dq_ref[:, lanes] = (dq * scale).astype(bf16)
         dk_ref[:, lanes] = (dk * scale).astype(bf16)
         dv_ref[:, lanes] = dv.astype(bf16)
-    leaving = start_all((dq_ref, dk_ref, dv_ref), outs, out_sems)
     back = None
     for index, ref in enumerate((dq_ref, dk_ref, dv_ref)):
         part = dot_nt(ref[...], matrix(w_ref, index))
         back = part if back is None else back + part
     normed, inverse = norm_rows(stream_ref[...])
-    addend, gain_grad = norm_back(back, normed, inverse, gain_ref[...])
-    held_out[...] = grad_ref[...] + addend
-    last = pltpu.make_async_copy(held_out, out_ref, out_sems.at[3])
-    last.start()
-    gain_out[...] = gain_grad
-    wait_all(leaving)
-    last.wait()
-
-
-def leave_chunk(scratch, low, chunk, keep_ref, send_ref, sem):
+    addend, gain_grad = norm_back(back, normed, inverse, gain)
+    out_ref[...] = grad_ref[...] + addend
+    return gain_grad
+
+
+def leave_chunk(scratch, low, chunk, keep_ref, send_refs, sem):
     place = chunk ^ low
     source = scratch.at[place & 1, place >> 1]
 
@@ -394,9 +425,14 @@
     def _():
         pltpu.make_async_copy(source, keep_ref.at[place >> 1], sem).start()
 
-    @pl.when((place & 1) == 1)
-    def _():
-        pltpu.make_async_copy(source, send_ref.at[place >> 1], sem).start()
+    at = 0
+    for ref, count in send_refs:
+
+        @pl.when(((place & 1) == 1) & ((place >> 1) >= at) & ((place >> 1) < at + count))
+        def _():
+            pltpu.make_async_copy(source, ref.at[(place >> 1) - at], sem).start()
+
+        at += count
 
 
 def wait_chunks(scratch, low, keep_ref, sems):
@@ -405,14 +441,9 @@
         pltpu.make_async_copy(scratch.at[place & 1, place >> 1], keep_ref.at[place >> 1], sems.at[chunk]).wait()
 
 
-def attn_weights_kernel(low_ref, *refs):
-    ins, keep_ref, send_ref, refs = refs[:6], refs[6], refs[7], refs[8:]
-    (grad_ref, a_ref, o_ref, dq_ref, dk_ref, dv_ref), (dw, in_sems, sems) = refs[:6], refs[6:]
-    low = low_ref[0]
+def attn_weights(low, grad_ref, a_ref, o_ref, dq_ref, dk_ref, dv_ref, dw, keep_ref, send_ref, sems):
     rows = dw.shape[2]
     per = grad_ref.shape[1] // rows
-    arriving = start_all(ins, refs[:6], in_sems)
-    wait_all(arriving)
     branch = grad_ref[...].astype(bf16)
     for index in range(4):
         left = o_ref if index == 3 else a_ref
@@ -421,7 +452,14 @@
         for i in range(per):
             put_chunk(dw, low, index * per + i, value[i * rows : (i + 1) * rows].astype(bf16))
             leave_chunk(dw, low, index * per + i, keep_ref, send_ref, sems.at[index * per + i])
-    wait_chunks(dw, low, keep_ref, sems)
+
+
+def attn_weights_kernel(low_ref, *refs):
+    ins, keep_ref, send_ref, refs = refs[:6], refs[6], refs[7], refs[8:]
+    held, (dw, in_sems, sems) = refs[:6], refs[6:]
+    wait_all(start_all(ins, held, in_sems))
+    attn_weights(low_ref[0], *held, dw, keep_ref, [(send_ref, dw.shape[1])], sems)
+    wait_chunks(dw, low_ref[0], keep_ref, sems)
 
 
 def mlp_fwd(stream_ref, gain, w1_ref, w2_ref, out_ref, b_ref, u_ref):
@@ -487,64 +525,24 @@
         copy.wait()
 
 
-def mlp_bwd_kernel(by_core, spots, count, place_ref, gain_ref, *refs):
-    ins, arrays, refs = refs[:4], refs[4 : 4 + count], refs[4 + count :]
-    if by_core:
-        out_ref, gain_out, keep2_ref, send2_ref, keep1_ref, send1_ref, *refs = refs
-        dw2, dw1, w2_ref, w1_ref, *refs = refs
-    else:
-        w1_ref, out_ref, gain_out, keep2_ref, send2_ref, dw1_ref, *refs = refs
-        dw2, w2_ref, *refs = refs
-    grad_ref, stream_ref, b_ref, u_ref, held_out, w_sems, in_sems, out_sems, last_sem = refs
-    low = place_ref[0]
-    arriving = start_all(ins, (grad_ref, stream_ref, b_ref, u_ref), in_sems)
-    copies = layer_copies(spots, arrays, place_ref, 3, w2_ref, w_sems.at[0])
-    if by_core:
-        copies += layer_copies(spots, arrays, place_ref, 2, w1_ref, w_sems.at[1])
-    for copy in copies:
-        copy.start()
-    wait_all(arriving)
+def mlp_bwd(low, grad_ref, stream_ref, gain, w1_ref, w2_ref, b_ref, u_ref, out_ref, put_first, put_second):
     width = grad_ref.shape[1]
     upper = grad_ref[...].astype(bf16)
     back = None
-    groups = w1_ref.shape[0]
     for q in range(4):
         pre = u_ref[:, q * width : (q + 1) * width]
         cdf = normal_cdf(pre)
         act = (pre * cdf).astype(bf16)
-        rows = dw2.shape[2]
-        per = width // rows
-        second = dot_tn(act, upper)
-        for i in range(per):
-            put_chunk(dw2, low, q * per + i, second[i * rows : (i + 1) * rows].astype(bf16))
-            leave_chunk(dw2, low, q * per + i, keep2_ref, send2_ref, out_sems.at[0, q * per + i])
-        if q == 0:
-            wait_all(copies)
+        put_second(q, dot_tn(act, upper).astype(bf16))
         dact = dot_nt(upper, matrix(w2_ref, q))
         dpre = (dact * (cdf + pre * density(pre))).astype(bf16)
-        first = dot_tn(b_ref[...], dpre).astype(bf16)
-        rows = width // groups
-        for i in range(groups):
-            piece = first[i * rows : (i + 1) * rows]
-            if by_core:
-                put_chunk(dw1, low, i, piece, q * rows)
-            else:
-                dw1_ref[i, q * rows : (q + 1) * rows, :] = piece
+        put_first(q, dot_tn(b_ref[...], dpre).astype(bf16))
         part = dot_nt(dpre, quarter_in(w1_ref, q))
         back = part if back is None else back + part
-    if by_core:
-        for i in range(groups):
-            leave_chunk(dw1, low, i, keep1_ref, send1_ref, out_sems.at[1, i])
     normed, inverse = norm_rows(stream_ref[...])
-    addend, gain_grad = norm_back(back, normed, inverse, gain_ref[...])
-    held_out[...] = grad_ref[...] + addend
-    last = pltpu.make_async_copy(held_out, out_ref, last_sem)
-    last.start()
-    gain_out[...] = gain_grad
-    wait_chunks(dw2, low, keep2_ref, out_sems.at[0])
-    if by_core:
-        wait_chunks(dw1, low, keep1_ref, out_sems.at[1])
-    last.wait()
+    addend, gain_grad = norm_back(back, normed, inverse, gain)
+    out_ref[...] = grad_ref[...] + addend
+    return gain_grad
 
 
 def pick_hots(picks, experts):
@@ -601,17 +599,33 @@
     half = parts // 2
     me = me_ref[0]
 
+    rows = weights.shape[1] // 2
+
+    def copies(side):
+        found = []
+        for i, ((place, first), ref) in enumerate(zip(spans, weight_refs)):
+            low, high = max(first, side * rows), min(first + ref.shape[0], (side + 1) * rows)
+            if low < high:
+                target = weights.at[place ^ me, low:high]
+                found.append(pltpu.make_async_copy(ref.at[low - first : high - first], target, sems.at[side, i]))
+        return found
+
+    staged = 2 * quarter >= width // half and rows >= width
+
     @pl.when(q == 0)
     def _():
-        copies = [
-            pltpu.make_async_copy(ref, weights.at[place ^ me, first : first + ref.shape[0]], sems.at[i])
-            for i, ((place, first), ref) in enumerate(zip(spans, weight_refs))
-        ]
-        for copy in copies:
+        for copy in copies(0) + copies(1):
             copy.start()
         dy_ref[...] = (add_lanes(x_ref[:, width:]) * g_ref[...].astype(f32)).astype(bf16)
-        for copy in copies:
+        for copy in copies(0) if staged else copies(0) + copies(1):
             copy.wait()
+
+    if staged:
+
+        @pl.when(q == 1)
+        def _():
+            for copy in copies(1):
+                copy.wait()
 
     first = weights[0:half, pl.ds(pl.multiple_of(q * quarter, 16), quarter), :].reshape(width, width)
     if 4 * quarter >= width:
@@ -656,51 +670,51 @@
 
 def expert_grad_kernel(dims, dp_ref, x_ref, dy_ref, act_ref, dpre_ref, *refs):
     parts, quarter = dims
-    out_refs, scratch, sems = refs[: 2 * parts], refs[-2], refs[-1]
+    out_refs, scratch, sems = refs[:4], refs[-2], refs[-1]
     q = pl.program_id(0)
     me = dp_ref[0]
     width = dy_ref.shape[1]
     half = parts // 2
     rows = scratch.shape[1]
+    side_rows = rows // 2
+
+    def leave(owner, first, count, sem):
+        place = owner ^ me
+        side = first // side_rows
+        source = scratch.at[place, pl.ds(first, count)]
+        at = pl.ds(pl.multiple_of(lax.rem(first, side_rows), 16), count)
+        for which, (bit, index) in enumerate(((1, place >> 1), (half, place & (half - 1)))):
+            for taken, ref in enumerate((out_refs[2 * which + 1], out_refs[2 * which])):
+
+                @pl.when((side == which) & (((place & bit) > 0) == (taken == 1)))
+                def _():
+                    pltpu.make_async_copy(source, ref.at[index, at], sem).start()
+
     first = dot_tn(x_ref[:, 0:width], dpre_ref[...]).astype(bf16)
     count = width // half
+    at = pl.multiple_of(q * quarter, 16)
     for i in range(half):
-        at = pl.ds(pl.multiple_of(q * quarter, 16), quarter)
-        scratch[i ^ me, at, :] = first[i * count : (i + 1) * count]
+        scratch[i ^ me, pl.ds(at, quarter), :] = first[i * count : (i + 1) * count]
+        leave(i, at, quarter, sems.at[i])
     second = dot_tn(act_ref[...], dy_ref[...]).astype(bf16)
-    if rows >= width:
-        per = rows // width
-        at = pl.ds(pl.multiple_of(lax.rem(q, per) * width, 16), width)
-        scratch[(half + q // per) ^ me, at, :] = second
-    else:
-        per = width // rows
-        for i in range(per):
-            scratch[(half + q * per + i) ^ me] = second[i * rows : (i + 1) * rows]
+    step = min(width, side_rows)
+    for i in range(width // step):
+        flat = q * width + i * step
+        owner, at = half + flat // rows, pl.multiple_of(lax.rem(flat, rows), 16)
+        scratch[owner ^ me, pl.ds(at, step), :] = second[i * step : (i + 1) * step]
+        leave(owner, at, step, sems.at[half + i])
 
     @pl.when(q == pl.num_programs(0) - 1)
     def _():
-        copies = []
-        for side, bit in ((0, 1), (1, parts // 2)):
-            lists = [r for r in range(parts) if r & bit], [r for r in range(parts) if not r & bit]
-            for which, group in enumerate(lists):
-                for i, r in enumerate(group):
-                    copies.append(
-                        pltpu.make_async_copy(
-                            scratch.at[r, side * rows // 2 : (side + 1) * rows // 2],
-                            out_refs[side * parts + which * half + i],
-                            sems.at[side * parts + r],
-                        )
-                    )
-        for copy in copies:
-            copy.start()
-        for copy in copies:
-            copy.wait()
-
-
-def combine_kernel(
-    stream_ref, gain_ref, wr_ref, picks_ref, cols_ref, cot_ref, c_ref, probs_ref, dx_ref,
-    grad_ref, gain_out, router_out,
-):
+        whole = out_refs[0].at[0]
+        for _ in range(4):
+            for i in range(half):
+                pltpu.make_async_copy(scratch.at[0, 0:quarter], whole.at[0:quarter], sems.at[i]).wait()
+            for i in range(width // step):
+                pltpu.make_async_copy(scratch.at[0, 0:step], whole.at[0:step], sems.at[half + i]).wait()
+
+
+def combine(stream_ref, gain, wr_ref, picks_ref, cols_ref, cot_ref, c_ref, probs_ref, dx_ref, grad_ref):
     width = stream_ref.shape[1]
     experts = wr_ref.shape[1]
     probs = probs_ref[...]
@@ -712,22 +726,148 @@
         prob_grad = part if prob_grad is None else prob_grad + part
     logit_grad = probs * (prob_grad - jnp.sum(prob_grad * probs, axis=-1, keepdims=True))
     logit_grad = logit_grad.astype(bf16)
-    router_out[...] = dot_tn(logit_grad, c_ref[...])
+    router_grad = dot_tn(c_ref[...], logit_grad)
     back = dot(selects[0] + selects[1], dx_ref[:, 0:width]) + dot_nt(logit_grad, wr_ref[...])
     normed, inverse = norm_rows(stream_ref[...])
-    addend, gain_grad = norm_back(back, normed, inverse, gain_ref[...])
+    addend, gain_grad = norm_back(back, normed, inverse, gain)
     grad_ref[...] = cot_ref[...].astype(f32) + addend
-    gain_out[...] = gain_grad
-
-
-def output_kernel(stream_ref, picks_ref, near_ref, probs_ref, *refs):
-    y_refs, (other_ref, out_ref, wide) = refs[:-3], refs[-3:]
+    return gain_grad, router_grad
+
+
+def put_router(out_ref, value, scratch):
+    width, experts = value.shape
+    many = LANES // experts
+    scratch[...] = jnp.zeros_like(scratch)
+    scratch[:, 0:experts] = value
+    total = None
+    for m in range(many):
+        rows = scratch[pl.ds(m, width // many, stride=many), :]
+        rows = pltpu.roll(rows, m * experts, 1) if m else rows
+        total = rows if total is None else total + rows
+    out_ref[0 : width // many, :] = total
+
+
+def backward_kernel(
+    seq, spots, count, by_core, place_ref, gains_ref, wr_ref, picks_ref, cols_ref, cot_ref, probs_ref, dx_ref, *refs
+):
+    ins, refs = refs[:15], refs[15:]
+    arrays, refs = refs[:count], refs[count:]
+    if not by_core:
+        w1_ref, refs = refs[0], refs[1:]
+    small_ref, upper_out, dq_out, dk_out, dv_out, grad_out, *refs = refs
+    keep_ref, send_ref, keeps_ref, send2_ref, send_rest, *refs = refs
+    places = send_ref.shape[0]
+    most, rest = send2_ref.shape[0], places - send2_ref.shape[0]
+    keeps = (keep_ref, keeps_ref.at[0])
+    sends = ([(send_ref, places)], [(send2_ref, most), (send_rest.at[0], rest)])
+    if by_core:
+        send1_ref, *refs = refs
+        keep1_ref, send1 = keeps_ref.at[1], [(send1_ref, most), (send_rest.at[1], rest)]
+    else:
+        dw1_ref, *refs = refs
+    held, refs = refs[:15], refs[15:]
+    grads, refs = refs[:4], refs[4:]
+    dq_ref, dk_ref, dv_ref, do_ref, dw, dw2, w2_ref, w_attn, *refs = refs
+    if by_core:
+        dw1, w1_ref, *refs = refs
+    router_scratch, in_sems, w_sems, out_sems, last_sems = refs
+    low = place_ref[0]
+    experts = wr_ref.shape[1]
+
+    def fetch(first, last):
+        copies = [pltpu.make_async_copy(ins[i], held[i], in_sems.at[i]) for i in range(first, last)]
+        for copy in copies:
+            copy.start()
+        return copies
+
+    def fetch_layer(layer, target, at):
+        copies = layer_copies(spots, arrays, place_ref, layer, target, w_sems.at[at])
+        for copy in copies:
+            copy.start()
+        return copies
+
+    part = fetch(0, 2)
+    second = fetch_layer(1, w_attn.at[0], 0) + fetch(2, 8)
+    wait_all(part)
+    gain_four, router_grad = combine(
+        held[0], gains_ref[3:4], wr_ref, picks_ref, cols_ref, cot_ref, held[1], probs_ref, dx_ref, grads[0]
+    )
+    tiles = router_grad.shape[0] // LANES
+    router_rows = router_grad.shape[0] * experts // LANES
+    small_ref[...] = jnp.zeros_like(small_ref)
+    put_router(small_ref, router_grad, router_scratch)
+
+    def put_gain(which, value):
+        at = router_rows + which * tiles
+        for j in range(tiles):
+            small_ref[at + j : at + j + 1, :] = value[:, LANES * j : LANES * (j + 1)]
+
+    put_gain(3, gain_four)
+    middle = fetch(8, 11) + fetch_layer(3, w2_ref, 1)
+    if by_core:
+        middle += fetch_layer(2, w1_ref, 2)
+    wait_all(second)
+    stream, q, k, v, a, o = held[2:8]
+    gain_three = attn_bwd(
+        seq, grads[0], stream, gains_ref[2:3], w_attn.at[0], q, k, v, grads[1], dq_ref, dk_ref, dv_ref, do_ref
+    )
+    put_gain(2, gain_three)
+    attn_weights(low, grads[0], a, o, dq_ref, dk_ref, dv_ref, dw, keeps[0], sends[0], out_sems.at[0])
+    first = fetch(11, 15) + fetch_layer(0, w_attn.at[1], 3)
+    wait_all(middle)
+    stream, b, u = held[8:11]
+    width = stream.shape[1]
+    groups = w1_ref.shape[0]
+
+    def put_first(q, value):
+        rows = width // groups
+        for i in range(groups):
+            piece = value[i * rows : (i + 1) * rows]
+            if by_core:
+                put_chunk(dw1, low, i, piece, q * rows)
+                if q == 3:
+                    leave_chunk(dw1, low, i, keep1_ref, send1, out_sems.at[2, i])
+            else:
+                dw1_ref[i, q * rows : (q + 1) * rows, :] = piece
+
+    def put_second(q, value):
+        rows = dw2.shape[2]
+        per = width // rows
+        for i in range(per):
+            put_chunk(dw2, low, q * per + i, value[i * rows : (i + 1) * rows])
+            leave_chunk(dw2, low, q * per + i, keeps[1], sends[1], out_sems.at[1, q * per + i])
+
+    gain_two = mlp_bwd(
+        low, grads[1], stream, gains_ref[1:2], w1_ref, w2_ref, b, u, grads[2], put_first, put_second
+    )
+    put_gain(1, gain_two)
+    leaving = start_all((grads[2],), (upper_out,), last_sems)
+    wait_all(first)
+    wait_chunks(dw, low, keeps[0], out_sems.at[0])
+    stream, q, k, v = held[11:15]
+    gain_one = attn_bwd(
+        seq, grads[2], stream, gains_ref[0:1], w_attn.at[1], q, k, v, grads[3], dq_ref, dk_ref, dv_ref, do_ref
+    )
+    put_gain(0, gain_one)
+    outs = ((dq_ref, dq_out), (dk_ref, dk_out), (dv_ref, dv_out), (grads[3], grad_out))
+    for i, (source, target) in enumerate(outs):
+        leaving.append(pltpu.make_async_copy(source, target, last_sems.at[1 + i]))
+        leaving[-1].start()
+    wait_chunks(dw2, low, keeps[1], out_sems.at[1])
+    if by_core:
+        wait_chunks(dw1, low, keep1_ref, out_sems.at[2])
+    wait_all(leaving)
+
+
+def output_kernel(stream_ref, picks_ref, near_ref, probs_ref, grad_ref, *refs):
+    y_refs, (other_ref, out_ref, grad_out, wide) = refs[:-4], refs[-4:]
     stride = other_ref.shape[1]
     for pair, ref in enumerate(y_refs):
         wide[2 * pair * stride : (2 * pair + 1) * stride] = ref[0].astype(f32)
         wide[(2 * pair + 1) * stride : (2 * pair + 2) * stride] = other_ref[pair].astype(f32)
     y = wide[...].astype(bf16)
-    seq = out_ref.shape[0]
+    tiles = stream_ref.shape[1] // LANES
+    seq = out_ref.shape[0] // tiles
     probs = probs_ref[...]
     hots = pick_hots(picks_ref, probs.shape[1])
     selects = token_selects(near_ref, y.shape[0])
@@ -735,7 +875,9 @@
     for j in range(2):
         gate = jnp.sum(probs * hots[j], axis=-1, keepdims=True)
         total = total + gate * dot(selects[j], y)
-    out_ref[...] = total[0:seq]
+    for value, ref in ((total, out_ref), (grad_ref, grad_out)):
+        for j in range(tiles):
+            ref[pl.ds(j, seq, stride=tiles), :] = value[0:seq, LANES * j : LANES * (j + 1)]
 
 
 def add_pair(left, right):
@@ -748,25 +890,49 @@
         out_ref[i // 4, i % 4] = ref[...]
 
 
-def fold_layers_kernel(cut, top_ref, *refs):
-    layers, refs = [refs[2 * i : 2 * i + 2] for i in range(4)], refs[8:]
-    uppers, (send_x, keep_x, send_y, keep_y, scratch) = refs[:4], refs[4:]
+def fold_layer_kernel(cut, layer, at, sources, top_ref, keep_ref, *refs):
+    refs_in, uppers, (send_x, keep_x, send_y, keep_y), refs = refs, refs[-14:-10], refs[-10:-6], refs[-6:]
+    kept, got, total, keep_sems, got_sems, out_sems = refs
+    if at is not None:
+        keep_ref = keep_ref.at[at]
+    got_refs = []
+    for ref, (index, many) in zip(refs_in, sources):
+        ref = ref if index is None else ref.at[index]
+        got_refs += [ref.at[i] for i in range(many)]
+    count = kept.shape[0]
     middle = send_x.shape[2]
-    place = pl.program_id(0)
-    for layer, (keep, got) in enumerate(layers):
-        value = add_pair(keep[0], got[0])
-        for j, upper in enumerate(uppers):
-
-            @pl.when(lax.rem(place, 4) == j)
-            def _():
-                upper[layer, place // 4] = value[:cut]
-
-        scratch[layer ^ top_ref[0]] = value[cut:]
-    for i in range(2):
-        keep_x[i, 0] = scratch[2 * i, 0:middle]
-        send_x[i, 0] = scratch[2 * i + 1, 0:middle]
-        keep_y[i, 0] = scratch[i, middle:]
-        send_y[i, 0] = scratch[i + 2, middle:]
+    place = layer ^ top_ref[0]
+    for i in range(count):
+        pltpu.make_async_copy(keep_ref.at[i], kept.at[i], keep_sems.at[i]).start()
+        pltpu.make_async_copy(got_refs[i], got.at[i], got_sems.at[i]).start()
+    for i in range(count):
+        pltpu.make_async_copy(keep_ref.at[i], kept.at[i], keep_sems.at[i]).wait()
+        pltpu.make_async_copy(got_refs[i], got.at[i], got_sems.at[i]).wait()
+        total[i] = add_pair(kept[i], got[i])
+        pltpu.make_async_copy(total.at[i, 0:cut], uppers[i % 4].at[layer, i // 4], out_sems.at[0, i]).start()
+        for bit, send, keep, at, where, sem in (
+            (place & 1, send_x, keep_x, place >> 1, slice(cut, cut + middle), out_sems.at[1, i]),
+            (place >> 1, send_y, keep_y, place & 1, slice(cut + middle, cut + 2 * middle), out_sems.at[2, i]),
+        ):
+            for value, target in ((0, keep), (1, send)):
+
+                @pl.when(bit == value)
+                def _():
+                    pltpu.make_async_copy(total.at[i, where], target.at[at, i], sem).start()
+
+    for i in range(count):
+        pltpu.make_async_copy(total.at[i, 0:cut], uppers[i % 4].at[layer, i // 4], out_sems.at[0, i]).wait()
+        for sem in (out_sems.at[1, i], out_sems.at[2, i]):
+            pltpu.make_async_copy(total.at[i, cut : cut + middle], keep_x.at[0, i], sem).wait()
+
+
+def add_kernel(left, right, out_ref):
+    out_ref[...] = add_pair(left[...], right[...])
+
+
+def pause_kernel(ref, out_ref):
+    for i in range(ref.shape[0]):
+        out_ref[i] = ref[i]
 
 
 def fold_plane_kernel(keep_x, got_x, keep_y, got_y, own_a, send_y, own_b, send_x):
@@ -792,14 +958,13 @@
 
 
 def fold_expert_kernel(highs, *refs):
-    count = len(refs) // 6
-    ins, outs = refs[: 4 * count], refs[4 * count :]
+    ins, outs = refs[:4], refs[4:]
+    count = ins[0].shape[0]
     for side, high in enumerate(highs):
         half = count // 2
         for i in range(count):
             which, at = (i // half, i % half) if high else (i % 2, i // 2)
-            keep, got = ins[2 * side * count + i], ins[(2 * side + 1) * count + i]
-            outs[side * count + which * half + at][...] = add_pair(keep[...], got[...])
+            outs[side * count + which * half + at][...] = add_pair(ins[2 * side][i], ins[2 * side + 1][i])
 
 
 def swap(value, axes, mask):
@@ -811,6 +976,20 @@
 
 def after(value, *others):
     return lax.optimization_barrier((value, others))[0]
+
+
+def pause(scalars, rows, others):
+    scalars, others = lax.optimization_barrier((scalars, others))
+    scalars = pl.pallas_call(
+        pause_kernel,
+        in_specs=[SMEM],
+        out_specs=SMEM,
+        out_shape=shape(scalars.shape, jnp.int32),
+        compiler_params=params(),
+        cost_estimate=cost(rows),
+        name="pause",
+    )(scalars)
+    return scalars, others
 
 
 class Order:
@@ -899,7 +1078,7 @@
         out_shape=shape((rows + tail_rows, width), bf16),
         scratch_shapes=[pltpu.VMEM((buf_rows, LANES), f32)],
         compiler_params=params(),
-        cost_estimate=cost(0, 6 * dense_master.size),
+        cost_estimate=cost(),
         name="pack_dense",
     )(me_arr, tail_from, dense_flat)
 
@@ -910,7 +1089,7 @@
         out_specs=VMEM,
         out_shape=shape((expert_rows, width), bf16),
         compiler_params=params(),
-        cost_estimate=cost(0, 6 * expert_master.size),
+        cost_estimate=cost(),
         name="pack_expert",
     )(expert_wide, expert_master.reshape(expert_flat, LANES))
     dp_axis = ("dp",)
@@ -951,35 +1130,44 @@
     per_bits = per.bit_length() - 1
     top_bits = (per_bits, per_bits + 1)
     chunk_rows = rows + tail_rows
+    low = me & (per - 1)
+    low_arr = low.reshape(1)
+    place_arr = jnp.stack([low, me >> per_bits])
+    expert_me = jnp.concatenate([dp_arr, e_me])
     half_rows = expert_rows // 2
     orders = (dp_order, dp_order[::-1])
     expert_parts, expert_spans = [], []
     if per_bits == 3 and dp_bits == 2:
         masks = [1 << bit for bit in top_bits]
+        split = chunk_rows // 32 * 16 + 16
         order = Order()
 
         def spread(value):
             return [swap(value, both, mask) for mask in masks]
 
-        sets = [chunk, swap(chunk, both, 2), swap(chunk, both, 4), None]
+        sets = [chunk, swap(chunk, both, 2), None, None]
         near, far = [spread(chunk)] + [None] * 3, [None] * 4
+        near[0] = order.land(near[0])
         sets[1] = order.land(sets[1])
         near[1] = spread(sets[1])
-        near[0] = order.land((near[0], expert_chunk, outgoing_cot, stream))[0]
-        far[0] = swap(near[0][1], both, masks[0])
+        sets[2] = swap(after(chunk, sets[1]), both, 4)
+        halves = [swap(near[0][1][:split], both, masks[0]), swap(near[0][0][split:], both, masks[1])]
         near[1] = order.land(near[1])
-        far[1] = swap(near[1][0], both, masks[1])
+        halves, expert_chunk, outgoing_cot, stream = order.land((halves, expert_chunk, outgoing_cot, stream))
         sets[2] = order.land(sets[2])
         sets[3] = swap(sets[2], both, 2)
         near[2] = spread(sets[2])
-        far[0], far[1] = order.land((far[0], far[1]))
+        far[0] = jnp.concatenate(halves)
+        far[1], far[2] = swap(far[0], both, 2), swap(far[0], both, 4)
         sets[3] = order.land(sets[3])
         near[3] = spread(sets[3])
-        arriving_cot = exchange(after(outgoing_cot, sets[3]))
         near[2] = order.land(near[2])
-        far[2] = swap(near[2][1], both, masks[0])
         near[3] = order.land(near[3])
-        far[3] = swap(near[3][0], both, masks[1])
+        far[1] = order.land(far[1])
+        far[2] = order.land(far[2])
+        place_arr, far[2] = pause(place_arr, 800, far[2])
+        far[3] = swap(far[2], both, 2)
+        arriving_cot = exchange(after(outgoing_cot, far[2]))
 
         def pack_sets(which):
             ins = [part for s in which for part in (sets[s], *near[s], far[s])]
@@ -994,14 +1182,18 @@
             )(*ins)
 
         packed = [pack_sets([0, 1])]
-        far[2:], packed, arriving_cot = lax.optimization_barrier((far[2:], packed, arriving_cot))
-        far[2], far[3] = order.land((far[2], far[3]))
+        far[3], packed = lax.optimization_barrier((far[3], packed))
+        far[3] = order.land(far[3])
         packed.append(pack_sets([2, 3]))
         arrays = packed + [swap(value, both, 1) for value in packed]
         spots = [((j >> 2) + 2 * (j & 1), ((j >> 1) & 1,), ()) for j in range(per)]
         own_shard = after(expert_chunk, near[3])
         beside = [swap(own_shard, dp_axis, mask) for mask in (1, 2)]
+        place_arr, beside = pause(place_arr, 650, beside)
+        place_arr, arriving_cot = pause(place_arr, 1900, arriving_cot)
+        place_arr, arrays[2] = pause(place_arr, 300, arrays[2])
         across = [swap(beside[0][:half_rows], dp_axis, 2), swap(beside[1][half_rows:], dp_axis, 1)]
+        expert_me, across = pause(expert_me, 400, across)
         expert_parts = [expert_chunk, *beside, *across]
         expert_spans = [(0, 0), (1, 0), (2, 0), (3, 0), (3, half_rows)]
     else:
@@ -1019,9 +1211,6 @@
             expert_spans += [(place, side * half_rows) for place in places]
         arriving_cot = exchange(outgoing_cot)
 
-    low = me & (per - 1)
-    low_arr = low.reshape(1)
-    place_arr = jnp.stack([low, me >> per_bits])
     layer_w = pltpu.VMEM((per, rows, width), bf16)
     if not wide_ok:
         first_in = lax.dynamic_index_in_dim(arrays[0], 2 ^ (me >> per_bits), 0, keepdims=False)
@@ -1035,7 +1224,7 @@
     weight_bytes = 2 * width * width
     ANY = pl.BlockSpec(memory_space=pl.ANY)
 
-    def call(kernel, ins, in_specs, outs, name, flops, nbytes, out_specs=None, scratch=()):
+    def call(kernel, ins, in_specs, outs, name, rows=0, mib=56, out_specs=None, scratch=(), aliases=None):
         out_specs = out_specs or [None] * len(outs)
 
         def whole(a):
@@ -1048,8 +1237,9 @@
             out_specs=[s or whole(a) for a, s in zip(outs, out_specs, strict=True)],
             out_shape=outs,
             scratch_shapes=list(scratch),
-            compiler_params=params(),
-            cost_estimate=cost(flops, nbytes),
+            compiler_params=params(mib),
+            cost_estimate=cost(rows),
+            input_output_aliases=aliases or {},
             name=name,
         )(*ins)
 
@@ -1058,37 +1248,13 @@
     by_core = pltpu.VMEM((2, places, rows, width), bf16)
     stream_vmem, act_vmem = pltpu.VMEM((padded, width), f32), pltpu.VMEM((padded, width), bf16)
 
-    def attn_bwd(grad, value, kept, layer, which):
-        return call(
-            functools.partial(attn_bwd_kernel, seq, spots, layer),
-            (place_arr, gain[which], grad, value, *kept[1:4], *arrays),
-            (SMEM, None) + (ANY,) * (5 + len(arrays)),
-            [stream_shape, gain_shape] + [act_shape] * 3,
-            "attn_bwd",
-            0,
-            0,
-            out_specs=[ANY, None, ANY, ANY, ANY],
-            scratch=[
-                stream_vmem,
-                stream_vmem,
-                *[act_vmem] * 3,
-                stream_vmem,
-                *[act_vmem] * 4,
-                layer_w,
-                pltpu.SemaphoreType.DMA((per,)),
-                pltpu.SemaphoreType.DMA((5,)),
-                pltpu.SemaphoreType.DMA((4,)),
-            ],
-        )
-
-    def attn_weights(grad, kept, found):
+    def attn_weights_call(grad, kept, found):
         return call(
             attn_weights_kernel,
             (low_arr, grad, kept[0], kept[4], *found),
             (SMEM,) + (ANY,) * 6,
             [core_shape, core_shape],
             "attn_weights",
-            0,
             0,
             out_specs=[ANY] * 2,
             scratch=[
@@ -1116,7 +1282,6 @@
         ],
         "forward",
         0,
-        0,
         out_specs=[ANY] * 15 + [None] * 5,
         scratch=[pltpu.VMEM(o.shape, o.dtype) for o in outs]
         + [
@@ -1130,7 +1295,6 @@
     stream_one, kept_one = results[0], results[1:6]
     stream_two, mlp_in, mlp_pre = results[6:9]
     stream_three, kept_two = results[9], results[10:]
-    gain = [gains[i : i + 1] for i in range(4)]
     arriving = exchange(outgoing)
 
     quarter = expert_rows // 4
@@ -1152,20 +1316,21 @@
             pltpu.VMEM((experts, stride, width), bf16),
             pltpu.VMEM((slots, width), f32),
             pltpu.VMEM((slots, width), f32),
-            pltpu.SemaphoreType.DMA((len(expert_parts),)),
+            pltpu.SemaphoreType.DMA((2, len(expert_parts))),
         ],
         compiler_params=params(),
         cost_estimate=cost(),
         name="expert",
-    )(jnp.concatenate([dp_arr, e_me]), arriving, arriving_cot, *expert_parts)
+    )(expert_me, arriving, arriving_cot, *expert_parts)
     returned_grad = exchange(input_back)
     part_shape = shape((expert_rows // 2, width), bf16)
+    count = dp_ranks // 2
     expert_first = pl.pallas_call(
         functools.partial(expert_grad_kernel, (dp_ranks, quarter)),
         grid=(4,),
         in_specs=[SMEM, wide_spec, slot_spec, hidden_spec, hidden_spec],
-        out_specs=[ANY] * (2 * dp_ranks),
-        out_shape=[part_shape] * (2 * dp_ranks),
+        out_specs=[ANY] * 4,
+        out_shape=[shape((count,) + part_shape.shape, bf16)] * 4,
         scratch_shapes=[
             pltpu.VMEM((dp_ranks, expert_rows, width), bf16),
             pltpu.SemaphoreType.DMA((2 * dp_ranks,)),
@@ -1174,19 +1339,24 @@
         cost_estimate=cost(),
         name="expert_grad",
     )(dp_arr, arriving, slot_grad, expert_act, pre_grad)
-    count = dp_ranks // 2
-    expert_first = [expert_first[i * count : (i + 1) * count] for i in range(4)]
     returned_grad = after(returned_grad, expert_first)
 
-    cut = max(16, rows // 96 * 16)
+    cut = max(16, rows // 64 * 16)
     middle = (rows - cut) // 2
     top = (me >> per_bits).reshape(1)
     z_bits = list(range(1, per_bits))
     z_masks = [2 * j for j in (1, 2, 3)]
     assert places % 4 == 0
 
-    def over_z(values):
-        return [values[0]] + [swap(value, both, mask) for value, mask in zip(values[1:], z_masks)]
+    def add_call(left, right):
+        return call(add_kernel, (left, right), (None, None), [shape(left.shape, bf16)], "add", mib=12)[0]
+
+    def over_z(values, meanwhile=None):
+        farthest = swap(values[3], both, 2)
+        near = swap(values[1], both, 2)
+        if meanwhile is not None:
+            farthest, *meanwhile[:] = lax.optimization_barrier((farthest, *meanwhile))
+        return [values[0], near, swap(add_call(values[2], farthest), both, 4)]
 
     def rest_of_z(values):
         if len(z_bits) == 2:
@@ -1196,92 +1366,93 @@
         total = jnp.moveaxis(total, lead, 0)
         return [reduce_bits(total, both, z_bits[2:])]
 
-    grad, gain_four, router_grad = call(
-        combine_kernel,
-        (stream_three, gain[3], router, picks, cols, cot, moe_in, probs, returned_grad),
-        (None,) * 9,
-        [stream_shape, gain_shape, shape((experts, width))],
-        "combine",
-        0,
-        0,
-    )
     def to_other_core(parts):
         return [parts[0], swap(parts[1], both, 1)]
 
-    expert_got = [
-        [swap(value[i], dp_axis, mask) for i in range(dp_ranks // 2)]
-        for value, mask in ((expert_first[0], 1), (expert_first[2], dp_ranks // 2))
-    ]
-    upper = grad
-    grad, gain_three, *found = attn_bwd(upper, stream_two, kept_two, 1, 2)
-    second_dw = to_other_core(attn_weights(upper, kept_two, found))
-
-    mlp_out = [core_shape, core_shape]
-    mlp_out = mlp_out * 2 if wide_ok else mlp_out + [shape((1, 4 * width, width), bf16)]
-    grad, gain_two, *mlp_dw = call(
-        functools.partial(mlp_bwd_kernel, wide_ok, spots, len(arrays)),
-        (place_arr, gain[1], grad, stream_one, mlp_in, mlp_pre, *arrays, *([] if wide_ok else [first_in])),
-        (SMEM, None) + (ANY,) * (4 + len(arrays)) + (() if wide_ok else (None,)),
-        [stream_shape, gain_shape] + mlp_out,
-        "mlp_bwd",
-        0,
-        0,
-        out_specs=[ANY, None] + ([ANY] * 4 if wide_ok else [ANY] * 2 + [None]),
-        scratch=[by_core] * (2 if wide_ok else 1)
-        + [layer_w] * (2 if wide_ok else 1)
-        + [stream_vmem, stream_vmem, act_vmem, pltpu.VMEM((padded, hidden), f32), stream_vmem]
+    expert_got = [swap(expert_first[0], dp_axis, 1), swap(expert_first[2], dp_axis, dp_ranks // 2)]
+    backward_ins = (
+        (stream_three, moe_in, stream_two, *kept_two[1:4], kept_two[0], kept_two[4])
+        + (stream_one, mlp_in, mlp_pre, stream, *kept_one[1:4])
+    )
+    held_vmem = [stream_vmem, act_vmem, stream_vmem] + [act_vmem] * 5
+    held_vmem += [stream_vmem, act_vmem, pltpu.VMEM((padded, hidden), f32), stream_vmem] + [act_vmem] * 3
+    kinds = 2 if wide_ok else 1
+    most, rest = places * 3 // 4, places // 4
+    keeps_shape = shape((kinds,) + core_shape.shape, bf16)
+    most_shape, rest_shape = shape((most, rows, width), bf16), shape((kinds, rest, rows, width), bf16)
+    first_dw_out = [most_shape] if wide_ok else [shape((1, 4 * width, width), bf16)]
+    small, upper, dq, dk, dv, grad, *dws = call(
+        functools.partial(backward_kernel, seq, spots, len(arrays), wide_ok),
+        (place_arr, gains, router, picks, cols, cot, probs, returned_grad, *backward_ins, *arrays)
+        + (() if wide_ok else (first_in,)),
+        (SMEM,) + (None,) * 7 + (ANY,) * (15 + len(arrays)) + (() if wide_ok else (None,)),
+        [shape((tail, LANES)), stream_shape, act_shape, act_shape, act_shape, stream_shape]
+        + [core_shape, core_shape, keeps_shape, most_shape, rest_shape]
+        + first_dw_out,
+        "backward",
+        out_specs=[None] + [ANY] * 10 + ([ANY] if wide_ok else [None]),
+        scratch=held_vmem
+        + [stream_vmem] * 4
+        + [act_vmem] * 4
+        + [by_core, by_core, layer_w, pltpu.VMEM((2, per, rows, width), bf16)]
+        + ([by_core, layer_w] if wide_ok else [])
         + [
-            pltpu.SemaphoreType.DMA((2, per)),
-            pltpu.SemaphoreType.DMA((4,)),
-            pltpu.SemaphoreType.DMA((2, per)),
-            pltpu.SemaphoreType.DMA,
+            pltpu.VMEM((width, LANES), f32),
+            pltpu.SemaphoreType.DMA((15,)),
+            pltpu.SemaphoreType.DMA((4, per)),
+            pltpu.SemaphoreType.DMA((3, per)),
+            pltpu.SemaphoreType.DMA((5,)),
         ],
     )
     if not wide_ok:
-        wide_grad = mlp_dw[2].reshape(4, width, width).transpose(1, 0, 2).reshape(per, rows, width)
+        wide_grad = dws[5].reshape(4, width, width).transpose(1, 0, 2).reshape(per, rows, width)
         wide_grad = jnp.take(wide_grad, jnp.arange(per) ^ low, axis=0)
         wide_grad = wide_grad.reshape(places, 2, rows, width)
-        mlp_dw = mlp_dw[:2] + [wide_grad[:, 0], wide_grad[:, 1]]
-    mlp_dw = [to_other_core(mlp_dw[i : i + 2]) for i in (0, 2)]
-
-    upper = grad
-    grad, gain_one, *found = attn_bwd(upper, stream, kept_one, 0, 0)
-    small = call(
-        stack_rows_kernel,
-        (router_grad, gain_one, gain_two, gain_three, gain_four),
-        (None,) * 5,
-        [shape((experts + 4, width))],
-        "stack_rows",
-        0,
-        0,
-    )[0]
-    found, expert_got, small = lax.optimization_barrier((found, expert_got, small))
-    first_dw = to_other_core(attn_weights(upper, kept_one, found))
-
-    small = lax.all_gather(small, both, axis=0, tiled=False)
+        dws[2] = jnp.concatenate([dws[2], wide_grad[None, :, 0]])
+        dws[4] = jnp.concatenate([dws[4], wide_grad[None, most:, 1]])
+        dws[5] = wide_grad[:most, 1]
+    most_got = [swap(dws[3], both, 1), swap(dws[5], both, 1)]
+    rest_got = swap(dws[4], both, 1)
+    first_dw = attn_weights_call(upper, kept_one, (dq, dk, dv))
+    layer_got = {0: [(swap(first_dw[1], both, 1), None, places)], 1: [(swap(dws[1], both, 1), None, places)]}
+    for i, layer in enumerate((3, 2)):
+        layer_got[layer] = [(most_got[i], None, most), (rest_got, i, rest)]
+    layer_keep = {3: (dws[2], 0), 2: (dws[2], 1), 1: (dws[0], None), 0: (first_dw[0], None)}
 
     plane_shape = shape((2, places, middle, width), bf16)
     plane_spec = pl.BlockSpec((2, 1, middle, width), lambda i: (0, i, 0, 0))
     line_shape = shape((places, middle, width), bf16)
     line_spec = pl.BlockSpec((1, middle, width), lambda i: (i, 0, 0))
     upper_shape = shape((4, places // 4, cut, width), bf16)
-    part_spec = pl.BlockSpec((1, rows, width), lambda i: (i, 0, 0))
-    layers = (first_dw, second_dw, mlp_dw[1], mlp_dw[0])
-    *uppers, send_x, keep_x, send_y, keep_y = pl.pallas_call(
-        functools.partial(fold_layers_kernel, cut),
-        grid=(places,),
-        in_specs=[SMEM] + [part_spec] * 8,
-        out_specs=[pl.BlockSpec(upper_shape.shape, lambda i: (0, 0, 0, 0))] * 4 + [plane_spec] * 4,
-        out_shape=[upper_shape] * 4 + [plane_shape] * 4,
-        scratch_shapes=[pltpu.VMEM((4, rows - cut, width), bf16)],
-        compiler_params=params(),
-        cost_estimate=cost(),
-        name="fold_layers",
-    )(top, *[part for layer in layers for part in layer])
+    sums = ()
+    for layer in (3, 2, 1, 0):
+        keep, at = layer_keep[layer]
+        parts = layer_got[layer]
+        if layer == 3:
+            keep = after(keep, first_dw)
+        if layer == 1:
+            expert_got, sums = lax.optimization_barrier((expert_got, sums))
+            top, expert_got = pause(top, 1600, expert_got)
+        sums = call(
+            functools.partial(fold_layer_kernel, cut, layer, at, [part[1:] for part in parts]),
+            (top, keep, *[part[0] for part in parts], *sums),
+            (SMEM,) + (ANY,) * (1 + len(parts) + len(sums)),
+            [upper_shape] * 4 + [plane_shape] * 4,
+            "fold_layer",
+            out_specs=[ANY] * 8,
+            scratch=[pltpu.VMEM((places, rows, width), bf16)] * 3
+            + [
+                pltpu.SemaphoreType.DMA((places,)),
+                pltpu.SemaphoreType.DMA((places,)),
+                pltpu.SemaphoreType.DMA((3, places)),
+            ],
+            aliases={2 + len(parts) + i: i for i in range(len(sums))},
+        )
+    *uppers, send_x, keep_x, send_y, keep_y = sums
     masks = [1 << bit for bit in top_bits]
     got_x, got_y = swap(send_x, both, masks[0]), swap(send_y, both, masks[1])
     uppers = over_z(uppers)
-    expert_ins = [part for i in (0, 1) for group in (expert_first[2 * i + 1], expert_got[i]) for part in group]
+    expert_ins = (expert_first[1], expert_got[0], expert_first[3], expert_got[1])
     expert_second = call(
         functools.partial(fold_expert_kernel, (dp_bits == 1, True)),
         expert_ins,
@@ -1289,25 +1460,20 @@
         [part_shape] * (2 * count),
         "fold_expert",
         0,
-        0,
     )
 
     uppers = [value.reshape(4, -1, cut, width) for value in uppers]
     uppers = [value.reshape(4, cut, width) for value in rest_of_z(uppers)]
-    uppers, expert_second = lax.optimization_barrier((uppers, expert_second))
     upper_rows = call(
         fold_uppers_kernel,
         (top, *uppers),
         (SMEM,) + (None,) * len(uppers),
         [shape((cut, width), bf16)] * 4,
         "fold_uppers",
-        0,
-        0,
+        100,
         scratch=[pltpu.VMEM((4, cut, width), bf16)],
     )
-    got_x, got_y, upper_rows = lax.optimization_barrier((got_x, got_y, upper_rows))
-
-    expert_out = after(expert_out, upper_rows)
+    got_x, got_y, expert_second = lax.optimization_barrier((got_x, got_y, expert_second))
     expert_out = [expert_out[0]] + [swap(v, ("expert",), 2 * j) for j, v in enumerate(expert_out) if j]
     own_a, send_y, own_b, send_x = pl.pallas_call(
         fold_plane_kernel,
@@ -1320,7 +1486,7 @@
         name="fold_plane",
     )(keep_x, got_x, keep_y, got_y)
     got_y, got_x = swap(send_y, both, masks[1]), swap(send_x, both, masks[0])
-    got_x, got_y, expert_out = lax.optimization_barrier((got_x, got_y, expert_out))
+    expert_second, expert_out, upper_rows = lax.optimization_barrier((expert_second, expert_out, upper_rows))
     other_out = swap(jnp.stack([value[1] for value in expert_out]), ("expert",), 1)
     lower_rows = call(
         fold_rows_kernel,
@@ -1329,10 +1495,21 @@
         [shape((places // 4, rows - cut, width), bf16)] * 4,
         "fold_rows",
         0,
-        0,
     )
-    lower_rows, other_out, expert_second = lax.optimization_barrier((lower_rows, other_out, expert_second))
-    lower_rows = over_z(lower_rows)
+    lower_rows, other_out = lax.optimization_barrier((lower_rows, other_out))
+    output, grad = call(
+        output_kernel,
+        (stream_three, picks, near_cols, probs, grad, *expert_out, other_out),
+        (None,) * (6 + pairs),
+        [shape((seq * tiles, LANES))] * 2,
+        "output",
+        mib=16,
+        scratch=[pltpu.VMEM((slots, width), f32)],
+    )
+    image = (1, seq, width)
+    meanwhile = [output.reshape(image), grad.reshape(image)]
+    lower_rows = over_z(lower_rows, meanwhile)
+    output, grad = meanwhile
     half = count // 2
     expert_groups = []
     for side, bits in enumerate(orders):
@@ -1350,27 +1527,16 @@
     expert_groups = [side[0] for side in expert_groups]
     upper_rows, expert_groups = lax.optimization_barrier((upper_rows, expert_groups))
 
-    output = call(
-        output_kernel,
-        (stream_three, picks, near_cols, probs, *expert_out, other_out),
-        (None,) * (5 + pairs),
-        [shape((seq, width))],
-        "output",
-        0,
-        0,
-        scratch=[pltpu.VMEM((slots, width), f32)],
-    )[0]
-
-    def unpack(wide, groups, count, name):
-        pieces = [piece for group in groups for piece in group]
+    def unpack(wide, groups, count, name, extra=(), square_shape=(1, LANES)):
+        pieces = [piece for group in groups for piece in group] + list(extra)
         return pl.pallas_call(
             functools.partial(unpack_kernel, (count, tiles), [len(group) for group in groups]),
             in_specs=[SMEM] + [VMEM] * len(pieces),
             out_specs=[VMEM, VMEM],
-            out_shape=[shape((count * tiles, LANES)), shape((1, LANES))],
+            out_shape=[shape((count * tiles, LANES)), shape(square_shape)],
             scratch_shapes=[pltpu.VMEM((count, width), f32)],
             compiler_params=params(),
-            cost_estimate=cost(0, 6 * count * width),
+            cost_estimate=cost(),
             name=name,
         )(wide, *pieces)
 
@@ -1385,50 +1551,58 @@
     dense_groups = [upper_rows, [value.reshape(rows - cut, width) for value in lower_rows]]
 
     dense_wide = (me >= devices // 2) & (me < 3 * devices // 4) & wide_ok
-    dense_rows, dense_square = unpack(dense_wide.astype(jnp.int32).reshape(1), dense_groups, rows, "unpack_dense")
-    small = jnp.sum(after(small, dense_square), axis=0)
-    gain_grads = small[experts:]
-    small_square = jnp.sum(small * small)
-    small = jnp.concatenate([small[:experts].T.reshape(-1, LANES), gain_grads.reshape(-1, LANES)])
-    small = jnp.pad(small, ((0, tail - small.shape[0]), (0, 0)))
-
+    dense_rows, total = unpack(
+        dense_wide.astype(jnp.int32).reshape(1),
+        dense_groups,
+        rows,
+        "unpack_dense",
+        (small, expert_square),
+        (tail + 8, LANES),
+    )
     head = lax.ppermute(dense_rows[:tail], both, backward_ring)
-    head = jnp.where(me == devices - 1, small, head)
-    square = dense_square + expert_square
-    for bits in bit_groups(list(range(all_bits))):
-        square = all_sum_step(square, both, bits)
-    square_sum = jnp.sum(square) + small_square
+    groups = bit_groups(list(range(all_bits)))
+    for bits in groups[:-1]:
+        total = all_sum_step(total, both, bits)
+    total, head = lax.optimization_barrier((total, head))
+    total = all_sum_step(total, both, groups[-1])
     param_count = (dense_master.size + expert_master.size) * devices
-    clip_factor = jnp.minimum(1.0, jnp.sqrt(param_count / (square_sum + 1e-06))).reshape(1)
-
-    dense_update, momentum_dense, variance_dense, dense_grad = pl.pallas_call(
-        functools.partial(adam_shift_kernel, (step, own)),
-        in_specs=[SMEM, SMEM] + [VMEM] * 4,
-        out_specs=[VMEM] * 4,
-        out_shape=[shape((own, LANES))] * 4,
-        scratch_shapes=[pltpu.VMEM((-(-(rows * tiles + tail) // 8) * 8, LANES), f32)],
+
+    chunks = 16
+    results = pl.pallas_call(
+        functools.partial(adam_kernel, (step, chunks, devices, param_count, width * experts // LANES)),
+        in_specs=[SMEM, VMEM, VMEM] + [ANY] * 6,
+        out_specs=[ANY] * 7 + [VMEM],
+        out_shape=[shape((expert_flat, LANES))] * 3 + [shape((own, LANES))] * 4 + [shape((4, width))],
+        scratch_shapes=[pltpu.VMEM((expert_flat, LANES), f32)] * 3
+        + [
+            pltpu.VMEM((4, 3, expert_flat // chunks, LANES), f32),
+            pltpu.VMEM((-(-(rows * tiles + tail) // 8) * 8, LANES), f32),
+            pltpu.VMEM((4, own, LANES), f32),
+            pltpu.SemaphoreType.DMA((chunks, 3)),
+            pltpu.SemaphoreType.DMA((4, 3)),
+            pltpu.SemaphoreType.DMA((3,)),
+            pltpu.SemaphoreType.DMA((4,)),
+        ],
         compiler_params=params(),
         cost_estimate=cost(),
-        name="adam_dense",
+        name="adam",
     )(
-        clip_factor,
         me_arr,
+        total,
+        head,
+        expert_grad,
+        expert_momentum.reshape(expert_flat, LANES),
+        expert_variance.reshape(expert_flat, LANES),
         dense_rows,
-        head,
         dense_momentum.reshape(own, LANES),
         dense_variance.reshape(own, LANES),
     )
-    expert_update, momentum_expert, variance_expert = adam(
-        clip_factor,
-        expert_grad,
-        expert_momentum.reshape(expert_flat, LANES),
-        expert_variance.reshape(expert_flat, LANES),
-        expert_flat // 8,
-    )
-    image = (1, seq, width)
+    gain_grads = results[7]
+    expert_update, momentum_expert, variance_expert = results[:3]
+    dense_update, momentum_dense, variance_dense, dense_grad = results[3:7]
     return (
-        output.reshape(image),
-        grad[:seq].reshape(image),
+        output,
+        grad,
         dense_grad.reshape(dense_master.shape),
         expert_grad.reshape(expert_master.shape),
         dense_update.reshape(dense_master.shape),

time: 510 us -> 446 us (0.87)
  waiting for transfers between devices: 210 us -> 183 us
  Pallas kernels: 177 us -> 159 us
  between operations: 16.2 us -> 1.57 us
  starting transfers between devices: 73.4 us -> 64.7 us
  local copies, waits for them, and re-layouts: 21.3 us -> 27.2 us
    ppermute x55, waiting for transfers between devices: 198 us -> 146 us  [swap(): return lax.ppermute(value, axes, [(i, i ^ mask) for i in range(size)])]
    all_to_all x3, waiting for transfers between devices: 4.69 us -> 29 us  [exchange(): lax.all_to_all(value, 'expert', split_axis=0, concat_axis=0, tiled=True)]
    ppermute x55, starting transfers between devices: 61.2 us -> 51.3 us  [swap(): return lax.ppermute(value, axes, [(i, i ^ mask) for i in range(size)])]
    pallas_call x3 -> x7, Pallas kernels: 29.5 us -> 22.5 us  [the longest x1 16.1 us: on_device(): pl.pallas_call(functools.partial(adam_kernel, (step, chunks, devices, par...]
    pallas_call x12 -> x13, Pallas kernels: 83.5 us -> 77.1 us  [call(): pl.pallas_call(kernel, grid=(1,), in_specs=[s or whole(a) for a, s in zip...]
    unnamed x99 -> x98, local copies, waits for them, and re-layouts: 12.5 us -> 13.6 us
  transfers between devices with their start and end apart: 61 -> 60, of which waited for: 31 -> 31; matrix products, arithmetic and copies ran while one was open for 3% -> 4% of each run, Pallas kernels for 25% -> 27%
where the time goes in v5:
time: 446 us; the launch traced here: 441 us
  waiting for transfers between devices  183 us (41%)
  Pallas kernels  159 us (36%)
  starting transfers between devices  64.7 us (15%)
  local copies, waits for them, and re-layouts  27.2 us (6%)
  other arithmetic  4.55 us (1%)
    ppermute x55, waiting for transfers between devices, swap(): return lax.ppermute(value, axes, [(i, i ^ mask) for i in range(size)])  146 us
    pallas_call x13, Pallas kernels, call(): pl.pallas_call(kernel, grid=(1,), in_specs=[s or whole(a) for a, s in zip...  77.1 us
    ppermute x55, starting transfers between devices, swap(): return lax.ppermute(value, axes, [(i, i ^ mask) for i in range(size)])  51.3 us
    all_to_all x3, waiting for transfers between devices, exchange(): lax.all_to_all(value, 'expert', split_axis=0, concat_axis=0, tiled=True)  29 us
    pallas_call x1, Pallas kernels, on_device(): pl.pallas_call(functools.partial(expert_kernel, (dp_ranks, quarter, exper...  16.6 us
    pallas_call x1, Pallas kernels, on_device(): pl.pallas_call(functools.partial(adam_kernel, (step, chunks, devices, par...  16.1 us
    unnamed x98, local copies, waits for them, and re-layouts  13.6 us
    all_to_all x3, starting transfers between devices, exchange(): lax.all_to_all(value, 'expert', split_axis=0, concat_axis=0, tiled=True)  11.2 us
  transfers between devices with their start and end apart: 60, of which 31 were waited for; matrix products, arithmetic and copies ran while one was open for 4% of the time, Pallas kernels for 27%

profile of v5, /device:TPU:0, one launch (start us, length us, event | category | flops | bytes accessed | tf_op | source)
XLA Modules:
  0.0 440.8 jit_solution(3021822353088096908)
XLA Ops:
  1.9 7.7 %collective-permute-done.tail_ref = f32[96,128]{1,0:T(8,128)S(1)} collective-permute-done((f32[96,128]{1,0:T(8,128)S(1)}, f32[96,128]{1,0:T(8,128)S(1)}, u32[]{:S(2)}, u32[]{:S(2)}) %collective-permute-start) | collective-permute-done | bytes 49184 | tf_op jit(solution)/shard_map/ppermute | solution.py:1070
  15.1 9.6 %collective-permute-done.1.refs_1_ = bf16[400,768]{1,0:T(8,128)(2,1)S(1)} collective-permute-done((bf16[400,768]{1,0:T(8,128)(2,1)}, bf16[400,768]{1,0:T(8,128)(2,1)S(1)}, u32[]{:S(2)}, u32[]{:S(2)}) %collective-permute-start.1) | collective-permute-done | bytes 614432 | tf_op jit(solution)/shard_map/ppermute | solution.py:974
  49.2 6.7 %collective-permute-done.10.refs_0_ = bf16[400,768]{1,0:T(8,128)(2,1)} collective-permute-done((bf16[400,768]{1,0:T(8,128)(2,1)}, bf16[400,768]{1,0:T(8,128)(2,1)}, u32[]{:S(2)}, u32[]{:S(2)}) %collective-permute-start.10) | collective-permute-done | bytes 614432 | tf_op jit(solution)/shard_map/ppermute | solution.py:974
  58.6 12.2 %collective-permute-done.11.refs_4_ = bf16[400,768]{1,0:T(8,128)(2,1)S(1)} collective-permute-done((bf16[400,768]{1,0:T(8,128)(2,1)}, bf16[400,768]{1,0:T(8,128)(2,1)S(1)}, u32[]{:S(2)}, u32[]{:S(2)}) %collective-permute-start.11) | collective-permute-done | bytes 614432 | tf_op jit(solution)/shard_map/ppermute | solution.py:974
  77.0 7.5 %collective-permute-done.12.refs_5_ = bf16[400,768]{1,0:T(8,128)(2,1)S(1)} collective-permute-done((bf16[400,768]{1,0:T(8,128)(2,1)S(1)}, bf16[400,768]{1,0:T(8,128)(2,1)S(1)}, u32[]{:S(2)}, u32[]{:S(2)}) %collective-permute-start.12) | collective-permute-done | bytes 614432 | tf_op jit(solution)/shard_map/ppermute | solution.py:974
  90.4 10.4 %collective-permute-done.9.refs_7_ = bf16[400,768]{1,0:T(8,128)(2,1)} collective-permute-done((bf16[400,768]{1,0:T(8,128)(2,1)S(1)}, bf16[400,768]{1,0:T(8,128)(2,1)}, u32[]{:S(2)}, u32[]{:S(2)}) %collective-permute-start.9) | collective-permute-done | bytes 614432 | tf_op jit(solution)/shard_map/ppermute | solution.py:974
  113.0 6.3 %collective-permute-done.18.refs_7_ = bf16[400,768]{1,0:T(8,128)(2,1)} collective-permute-done((bf16[400,768]{1,0:T(8,128)(2,1)}, bf16[400,768]{1,0:T(8,128)(2,1)}, u32[]{:S(2)}, u32[]{:S(2)}) %collective-permute-start.18) | collective-permute-done | bytes 614432 | tf_op jit(solution)/shard_map/ppermute | solution.py:974
  119.3 5.0 %pack_sets.3.refs_1_.refs_16_ = bf16[2,4,400,768]{3,2,1,0:T(8,128)(2,1)} custom-call(bf16[400,768]{1,0:T(8,128)(2,1)} %collective-permute-done.10.refs_0_, bf16[400,768]{1,0:T(8,128)(2,1)} %copy-done.26, bf16[400,768]{1,0:T(8,128)(2,1)} %copy-done.27, bf16[400,768]{1,0:T(8,128)(2,1)} %collective-permute-done.8.refs_3_, bf16[400,768]{1,0:T(8,128)(2,1)} %copy-done.25, ...), custom_call_target="tpu_custom_call" | custom-call | flops 1 | bytes 1 | tf_op jit(solution)/shard_map/pack_sets/pallas_call | solution.py:1174
  125.9 12.7 %collective-permute-done.16.refs_1_ = bf16[1536,768]{1,0:T(8,128)(2,1)} collective-permute-done((bf16[1536,768]{1,0:T(8,128)(2,1)S(1)}, bf16[1536,768]{1,0:T(8,128)(2,1)}, u32[]{:S(2)}, u32[]{:S(2)}) %collective-permute-start.16) | collective-permute-done | bytes 2359328 | tf_op jit(solution)/shard_map/ppermute | solution.py:974
  149.5 16.0 %forward.1 = (f32[208,768]{1,0:T(8,128)}, bf16[208,768]{1,0:T(8,128)(2,1)}, bf16[208,768]{1,0:T(8,128)(2,1)}, bf16[208,768]{1,0:T(8,128)(2,1)}, bf16[208,768]{1,...) custom-call(s32[2]{0:T(128)} %pause.9.place_ref, ...), custom_call_target="tpu_custom_call" | custom-call | flops 1 | bytes 1 | tf_op jit(solution)/shard_map/forward/pallas_call | solution.py:1233
  172.0 18.7 %all-to-all-done.1 = bf16[8,56,896]{2,1,0:T(8,128)(2,1)S(1)} async-done(((bf16[8,56,896]{2,1,0:T(8,128)(2,1)}), bf16[8,56,896]{2,1,0:T(8,128)(2,1)S(1)}, u32[]{:S(2)}, u32[]{:S(2)}) %all-to-all-start.1) | async-done | bytes 802848 | tf_op jit(solution)/shard_map/all_to_all | solution.py:1126
  191.6 16.6 %expert.1 = (bf16[2,56,768]{2,1,0:T(8,128)(2,1)}, bf16[2,56,768]{2,1,0:T(8,128)(2,1)}, bf16[2,56,768]{2,1,0:T(8,128)(2,1)}, bf16[2,56,768]{2,1,0:T(8,128)(2,1)},...) custom-call(s32[2]{0:T(128)} %pause.10.me_ref, ...), custom_call_target="tpu_custom_call" | custom-call | flops 1 | bytes 1 | tf_op jit(solution)/shard_map/expert/pallas_call | solution.py:1306
  211.8 9.3 %expert_grad.1 = (bf16[2,768,768]{2,1,0:T(8,128)(2,1)}, bf16[2,768,768]{2,1,0:T(8,128)(2,1)}, bf16[2,768,768]{2,1,0:T(8,128)(2,1)}, bf16[2,768,768]{2,1,0:T(8,128)(2,1)}) custom-call(s32[1]{0:T(128)} %bitcast.1.dp_ref, bf16[448,896]{1,0:T(8,128)(2,1)} %bitcast.45, bf16[448,768]{1,0:T(8,128)(2,1)} %get-tuple-element.255.dy_ref, ...), custom_call_target="tpu_custom_call" | custom-call | flops 1 | bytes 1 | tf_op jit(solution)/shard_map/expert_grad/pallas_call | solution.py:1328
  222.8 10.3 %all-to-all-done.2 = bf16[8,56,896]{2,1,0:T(8,128)(2,1)S(1)} async-done(((bf16[8,56,896]{2,1,0:T(8,128)(2,1)}), bf16[8,56,896]{2,1,0:T(8,128)(2,1)S(1)}, u32[]{:S(2)}, u32[]{:S(2)}) %all-to-all-start.2) | async-done | bytes 802848 | tf_op jit(solution)/shard_map/all_to_all | solution.py:1126
  234.0 27.6 %backward.1 = (f32[96,128]{1,0:T(8,128)}, f32[208,768]{1,0:T(8,128)}, bf16[208,768]{1,0:T(8,128)(2,1)}, bf16[208,768]{1,0:T(8,128)(2,1)}, bf16[208,768]{1,0:T(8,...) custom-call(s32[2]{0:T(128)} %pause.9.place_ref, ...), custom_call_target="tpu_custom_call" | custom-call | flops 1 | bytes 1 | tf_op jit(solution)/shard_map/backward/pallas_call | solution.py:1233
  294.0 14.4 %collective-permute-done.38.right = bf16[4,1,96,768]{3,2,1,0:T(8,128)(2,1)S(1)} collective-permute-done((bf16[4,1,96,768]{3,2,1,0:T(8,128)(2,1)}, bf16[4,1,96,768]{3,2,1,0:T(8,128)(2,1)S(1)}, u32[]{:S(2)}, u32[]{:S(2)}) %collective-permute-start.38) | collective-permute-done | bytes 589856 | tf_op jit(solution)/shard_map/ppermute | solution.py:974
  309.8 6.2 %fold_expert.1 = (bf16[768,768]{1,0:T(8,128)(2,1)}, bf16[768,768]{1,0:T(8,128)(2,1)}, bf16[768,768]{1,0:T(8,128)(2,1)}, bf16[768,768]{1,0:T(8,128)(2,1)}) custom-call(bf16[2,768,768]{2,1,0:T(8,128)(2,1)} %get-tuple-element.265.refs_0_, bf16[2,768,768]{2,1,0:T(8,128)(2,1)} %copy-done.14, bf16[2,768,768]{2,1,0:T(8,128)(2,1)} %get-tuple-element.266.refs_2_, ...), custom_call_target="tpu_custom_call" | custom-call | flops 1 | bytes 1 | tf_op jit(solution)/shard_map/fold_expert/pallas_call | solution.py:1233
  316.0 15.4 %collective-permute-done.30.got_x = bf16[2,4,144,768]{3,2,1,0:T(8,128)(2,1)S(1)} collective-permute-done((bf16[2,4,144,768]{3,2,1,0:T(8,128)(2,1)}, bf16[2,4,144,768]{3,2,1,0:T(8,128)(2,1)S(1)}, u32[]{:S(2)}, u32[]{:S(2)}) %collective-permute-start.30) | collective-permute-done | bytes 1769504 | tf_op jit(solution)/shard_map/ppermute | solution.py:974
  333.3 5.3 %fold_plane.1 = (bf16[4,144,768]{2,1,0:T(8,128)(2,1)}, bf16[4,144,768]{2,1,0:T(8,128)(2,1)}, bf16[4,144,768]{2,1,0:T(8,128)(2,1)}, bf16[4,144,768]{2,1,0:T(8,128)(2,1)}) custom-call(bf16[2,4,144,768]{3,2,1,0:T(8,128)(2,1)} %get-tuple-element.332.keep_x, bf16[2,4,144,768]{3,2,1,0:T(8,128)(2,1)} %copy-done.17, ...), custom_call_target="tpu_custom_call" | custom-call | flops 1 | bytes 1 | tf_op jit(solution)/shard_map/fold_plane/pallas_call | solution.py:1478
  348.0 7.2 %collective-permute-done.35.refs_2_ = bf16[2,56,768]{2,1,0:T(8,128)(2,1)S(1)} collective-permute-done((bf16[2,56,768]{2,1,0:T(8,128)(2,1)S(1)}, bf16[2,56,768]{2,1,0:T(8,128)(2,1)S(1)}, u32[]{:S(2)}, u32[]{:S(2)}) %collective-permute-start.35) | collective-permute-done | bytes 172064 | tf_op jit(solution)/shard_map/ppermute | solution.py:974
  370.0 14.3 %collective-permute-done.42.right = bf16[1,288,768]{2,1,0:T(8,128)(2,1)S(1)} collective-permute-done((bf16[1,288,768]{2,1,0:T(8,128)(2,1)}, bf16[1,288,768]{2,1,0:T(8,128)(2,1)S(1)}, u32[]{:S(2)}, u32[]{:S(2)}) %collective-permute-start.42) | collective-permute-done | bytes 442400 | tf_op jit(solution)/shard_map/ppermute | solution.py:974
  388.7 6.1 %unpack_expert.1 = (f32[9216,128]{1,0:T(8,128)}, f32[1,128]{1,0:T(1,128)}) custom-call(s32[1]{0:T(128)} %bitcast.6.wide_ref, bf16[768,768]{1,0:T(8,128)(2,1)} %get-tuple-element.391.refs_0_, bf16[768,768]{1,0:T(8,128)(2,1)} %collective-permute-done.44.refs_1_, bf16[768,768]{1,0:T(8,128)(2,1)} %get-tuple-element.393.refs_2_, ...), custom_call_target="tpu_custom_call" | custom-call | flops 1 | bytes 1 | tf_op jit(solution)/shard_map/unpack_expert/pallas_call | solution.py:1532
  394.8 6.1 %collective-permute-done.43 = bf16[1,288,768]{2,1,0:T(8,128)(2,1)S(1)} collective-permute-done((bf16[1,288,768]{2,1,0:T(8,128)(2,1)S(1)}, bf16[1,288,768]{2,1,0:T(8,128)(2,1)S(1)}, u32[]{:S(2)}, u32[]{:S(2)}) %collective-permute-start.43) | collective-permute-done | bytes 442400 | tf_op jit(solution)/shard_map/ppermute | solution.py:974
  424.5 16.1 %adam.1 = (f32[9216,128]{1,0:T(8,128)}, f32[9216,128]{1,0:T(8,128)}, f32[9216,128]{1,0:T(8,128)}, f32[2307,128]{1,0:T(8,128)}, f32[2307,128]{1,0:T(8,128)}, /*in...) custom-call(s32[1]{0:T(128)} %bitcast.3.k_ref, f32[104,128]{1,0:T(8,128)} %add.41.total_ref, ...), custom_call_target="tpu_custom_call" | custom-call | flops 1 | bytes 1 | tf_op jit(solution)/shard_map/adam/pallas_call | solution.py:1571
  (249 shorter events, 171.6 us)
Async XLA Ops:
  27.2 22.0 %collective-permute-start.6 = (bf16[400,768]{1,0:T(8,128)(2,1)S(1)}, bf16[400,768]{1,0:T(8,128)(2,1)}, u32[]{:S(2)}, u32[]{:S(2)}) collective-permute-start(bf16[400,768]{1,0:T(8,128)(2,1)S(1)} %collective-permute-done.5.refs_4_), channel_id=1, source_target_pairs={{0,8},{1,9},{2,10},{3,11},{4,12},{5,13},{6,14},{7,15},{8,0},{9,1},... | collective-permute-start | bytes 1843208 | tf_op jit(solution)/shard_map/ppermute | solution.py:974
  29.0 26.9 %collective-permute-start.10 = (bf16[400,768]{1,0:T(8,128)(2,1)}, bf16[400,768]{1,0:T(8,128)(2,1)}, u32[]{:S(2)}, u32[]{:S(2)}) collective-permute-start(bf16[400,768]{1,0:T(8,128)(2,1)} %pack_dense.1.refs_0_), channel_id=1, source_target_pairs={{0,4},{1,5},{2,6},{3,7},{4,0},{5,1},{6,2},{7,3},{8,12},{9,13},{10,... | collective-permute-start | bytes 1843208 | tf_op jit(solution)/shard_map/ppermute | solution.py:974
  75.4 25.3 %collective-permute-start.9 = (bf16[400,768]{1,0:T(8,128)(2,1)S(1)}, bf16[400,768]{1,0:T(8,128)(2,1)}, u32[]{:S(2)}, u32[]{:S(2)}) collective-permute-start(bf16[400,768]{1,0:T(8,128)(2,1)S(1)} %constant_dynamic-update-slice_fusion.refs_3_), channel_id=1, source_target_pairs={{0,2},{1,3},{2,0},{3,1},{4,6},{5,7},{6,4},{7,5},{8,10},{9,11},{10,... | collective-permute-start | bytes 1843208 | tf_op jit(solution)/shard_map/ppermute | solution.py:974
  75.8 28.5 %collective-permute-start.8 = (bf16[400,768]{1,0:T(8,128)(2,1)S(1)}, bf16[400,768]{1,0:T(8,128)(2,1)}, u32[]{:S(2)}, u32[]{:S(2)}) collective-permute-start(bf16[400,768]{1,0:T(8,128)(2,1)S(1)} %constant_dynamic-update-slice_fusion.refs_3_), channel_id=1, source_target_pairs={{0,4},{1,5},{2,6},{3,7},{4,0},{5,1},{6,2},{7,3},{8,12},{9,13},{10,... | collective-permute-start | bytes 1843208 | tf_op jit(solution)/shard_map/ppermute | solution.py:974
  87.1 51.5 %collective-permute-start.16 = (bf16[1536,768]{1,0:T(8,128)(2,1)S(1)}, bf16[1536,768]{1,0:T(8,128)(2,1)}, u32[]{:S(2)}, u32[]{:S(2)}) collective-permute-start(bf16[1536,768]{1,0:T(8,128)(2,1)S(1)} %copy-done.8), channel_id=1, source_target_pairs={{0,8},{8,0},{16,24},{24,16},{1,9},{9,1},{17,25},{25,17},{2,10},{10... | collective-permute-start | bytes 7077896 | tf_op jit(solution)/shard_map/ppermute | solution.py:974
  88.0 51.4 %collective-permute-start.17 = (bf16[1536,768]{1,0:T(8,128)(2,1)S(1)}, bf16[1536,768]{1,0:T(8,128)(2,1)}, u32[]{:S(2)}, u32[]{:S(2)}) collective-permute-start(bf16[1536,768]{1,0:T(8,128)(2,1)S(1)} %copy-done.8), channel_id=1, source_target_pairs={{0,16},{8,24},{16,0},{24,8},{1,17},{9,25},{17,1},{25,9},{2,18},{10... | collective-permute-start | bytes 7077896 | tf_op jit(solution)/shard_map/ppermute | solution.py:974
  109.3 31.3 %all-to-all-start = ((bf16[8,56,768]{2,1,0:T(8,128)(2,1)}), bf16[8,56,768]{2,1,0:T(8,128)(2,1)S(1)}, u32[]{:S(2)}, u32[]{:S(2)}) async-start(bf16[8,56,768]{2,1,0:T(8,128)(2,1)} %bitcast.59), calls=%async_computation | async-start | bytes 1376256 | tf_op jit(solution)/shard_map/all_to_all | solution.py:1126
  124.2 25.3 %collective-permute-start.20 = (bf16[2,4,400,768]{3,2,1,0:T(8,128)(2,1)}, bf16[2,4,400,768]{3,2,1,0:T(8,128)(2,1)}, u32[]{:S(2)}, u32[]{:S(2)}) collective-permute-start(bf16[2,4,400,768]{3,2,1,0:T(8,128)(2,1)} %pack_sets.3.refs_1_.refs_16_), channel_id=1, source_target_pairs={{0,1},{1,0},{2,3},{3,2},{4,5},{5,4},{6,7},{7,6},{8,9},{9,8},{10,11... | collective-permute-start | bytes 14745608 | tf_op jit(solution)/shard_map/ppermute | solution.py:974
  124.2 24.1 %collective-permute-start.19 = (bf16[2,4,400,768]{3,2,1,0:T(8,128)(2,1)}, bf16[2,4,400,768]{3,2,1,0:T(8,128)(2,1)}, u32[]{:S(2)}, u32[]{:S(2)}) collective-permute-start(bf16[2,4,400,768]{3,2,1,0:T(8,128)(2,1)} %pack_sets.2.refs_0_.refs_15_), channel_id=1, source_target_pairs={{0,1},{1,0},{2,3},{3,2},{4,5},{5,4},{6,7},{7,6},{8,9},{9,8},{10,11... | collective-permute-start | bytes 14745608 | tf_op jit(solution)/shard_map/ppermute | solution.py:974
  142.2 27.9 %collective-permute-start.21 = (bf16[768,768]{1,0:T(8,128)(2,1)S(1)}, bf16[768,768]{1,0:T(8,128)(2,1)}, u32[]{:S(2)}, u32[]{:S(2)}) collective-permute-start(bf16[768,768]{1,0:T(8,128)(2,1)S(1)} %slice.45), channel_id=1, source_target_pairs={{0,16},{8,24},{16,0},{24,8},{1,17},{9,25},{17,1},{25,9},{2,18},{10... | collective-permute-start | bytes 3538952 | tf_op jit(solution)/shard_map/ppermute | solution.py:974
  146.1 24.8 %collective-permute-start.22 = (bf16[768,768]{1,0:T(8,128)(2,1)}, bf16[768,768]{1,0:T(8,128)(2,1)}, u32[]{:S(2)}, u32[]{:S(2)}) collective-permute-start(bf16[768,768]{1,0:T(8,128)(2,1)} %slice.46), channel_id=1, source_target_pairs={{0,8},{8,0},{16,24},{24,16},{1,9},{9,1},{17,25},{25,17},{2,10},{10... | collective-permute-start | bytes 3538952 | tf_op jit(solution)/shard_map/ppermute | solution.py:974
  165.5 25.2 %all-to-all-start.1 = ((bf16[8,56,896]{2,1,0:T(8,128)(2,1)}), bf16[8,56,896]{2,1,0:T(8,128)(2,1)S(1)}, u32[]{:S(2)}, u32[]{:S(2)}) async-start(bf16[8,56,896]{2,1,0:T(8,128)(2,1)} %bitcast.57), calls=%async_computation.1 | async-start | bytes 1605632 | tf_op jit(solution)/shard_map/all_to_all | solution.py:1126
  208.3 24.8 %all-to-all-start.2 = ((bf16[8,56,896]{2,1,0:T(8,128)(2,1)}), bf16[8,56,896]{2,1,0:T(8,128)(2,1)S(1)}, u32[]{:S(2)}, u32[]{:S(2)}) async-start(bf16[8,56,896]{2,1,0:T(8,128)(2,1)} %bitcast.58), calls=%async_computation.2 | async-start | bytes 1605632 | tf_op jit(solution)/shard_map/all_to_all | solution.py:1126
  221.1 57.9 %collective-permute-start.23 = (bf16[2,768,768]{2,1,0:T(8,128)(2,1)}, bf16[2,768,768]{2,1,0:T(8,128)(2,1)S(1)}, u32[]{:S(2)}, u32[]{:S(2)}) collective-permute-start(bf16[2,768,768]{2,1,0:T(8,128)(2,1)} %get-tuple-element.258), channel_id=1, source_target_pairs={{0,8},{8,0},{16,24},{24,16},{1,9},{9,1},{17,25},{25,17},{2,10},{10... | collective-permute-start | bytes 7077896 | tf_op jit(solution)/shard_map/ppermute | solution.py:974
  222.2 56.8 %collective-permute-start.24 = (bf16[2,768,768]{2,1,0:T(8,128)(2,1)}, bf16[2,768,768]{2,1,0:T(8,128)(2,1)}, u32[]{:S(2)}, u32[]{:S(2)}) collective-permute-start(bf16[2,768,768]{2,1,0:T(8,128)(2,1)} %get-tuple-element.259), channel_id=1, source_target_pairs={{0,16},{8,24},{16,0},{24,8},{1,17},{9,25},{17,1},{25,9},{2,18},{10... | collective-permute-start | bytes 7077896 | tf_op jit(solution)/shard_map/ppermute | solution.py:974
  290.4 40.9 %collective-permute-start.30 = (bf16[2,4,144,768]{3,2,1,0:T(8,128)(2,1)}, bf16[2,4,144,768]{3,2,1,0:T(8,128)(2,1)S(1)}, u32[]{:S(2)}, u32[]{:S(2)}) collective-permute-start(bf16[2,4,144,768]{3,2,1,0:T(8,128)(2,1)} %get-tuple-element.333), channel_id=1, source_target_pairs={{0,8},{1,9},{2,10},{3,11},{4,12},{5,13},{6,14},{7,15},{8,0},{9,1},... | collective-permute-start | bytes 5308424 | tf_op jit(solution)/shard_map/ppermute | solution.py:974
  291.5 40.6 %collective-permute-start.31 = (bf16[2,4,144,768]{3,2,1,0:T(8,128)(2,1)}, bf16[2,4,144,768]{3,2,1,0:T(8,128)(2,1)S(1)}, u32[]{:S(2)}, u32[]{:S(2)}) collective-permute-start(bf16[2,4,144,768]{3,2,1,0:T(8,128)(2,1)} %get-tuple-element.334), channel_id=1, source_target_pairs={{0,16},{1,17},{2,18},{3,19},{4,20},{5,21},{6,22},{7,23},{8,24},{9,... | collective-permute-start | bytes 5308424 | tf_op jit(solution)/shard_map/ppermute | solution.py:974
  292.0 48.2 %collective-permute-start.37 = (bf16[4,1,96,768]{3,2,0,1:T(8,128)(2,1)}, bf16[4,1,96,768]{3,2,0,1:T(8,128)(2,1)S(1)}, u32[]{:S(2)}, u32[]{:S(2)}) collective-permute-start(bf16[4,1,96,768]{3,2,0,1:T(8,128)(2,1)} %bitcast.47), channel_id=1, source_target_pairs={{0,2},{1,3},{2,0},{3,1},{4,6},{5,7},{6,4},{7,5},{8,10},{9,11},{10,... | collective-permute-start | bytes 1769480 | tf_op jit(solution)/shard_map/ppermute | solution.py:974
  309.7 32.4 %collective-permute-start.39 = (bf16[4,1,96,768]{3,2,0,1:T(8,128)(2,1)S(1)}, bf16[4,1,96,768]{3,2,0,1:T(8,128)(2,1)S(1)}, u32[]{:S(2)}, u32[]{:S(2)}) collective-permute-start(bf16[4,1,96,768]{3,2,0,1:T(8,128)(2,1)S(1)} %bitcast.43), channel_id=1, source_target_pairs={{0,4},{1,5},{2,6},{3,7},{4,0},{5,1},{6,2},{7,3},{8,12},{9,13},{10,... | collective-permute-start | bytes 1769480 | tf_op jit(solution)/shard_map/ppermute | solution.py:974
  338.6 22.8 %collective-permute-start.32 = (bf16[4,144,768]{2,1,0:T(8,128)(2,1)}, bf16[4,144,768]{2,1,0:T(8,128)(2,1)S(1)}, u32[]{:S(2)}, u32[]{:S(2)}) collective-permute-start(bf16[4,144,768]{2,1,0:T(8,128)(2,1)} %get-tuple-element.345), channel_id=1, source_target_pairs={{0,16},{1,17},{2,18},{3,19},{4,20},{5,21},{6,22},{7,23},{8,24},{9,... | collective-permute-start | bytes 2654216 | tf_op jit(solution)/shard_map/ppermute | solution.py:974
  339.1 22.8 %collective-permute-start.33 = (bf16[4,144,768]{2,1,0:T(8,128)(2,1)}, bf16[4,144,768]{2,1,0:T(8,128)(2,1)S(1)}, u32[]{:S(2)}, u32[]{:S(2)}) collective-permute-start(bf16[4,144,768]{2,1,0:T(8,128)(2,1)} %get-tuple-element.347), channel_id=1, source_target_pairs={{0,8},{1,9},{2,10},{3,11},{4,12},{5,13},{6,14},{7,15},{8,0},{9,1},... | collective-permute-start | bytes 2654216 | tf_op jit(solution)/shard_map/ppermute | solution.py:974
  355.2 29.7 %collective-permute-start.44 = (bf16[768,768]{1,0:T(8,128)(2,1)}, bf16[768,768]{1,0:T(8,128)(2,1)}, u32[]{:S(2)}, u32[]{:S(2)}) collective-permute-start(bf16[768,768]{1,0:T(8,128)(2,1)} %get-tuple-element.388), channel_id=1, source_target_pairs={{0,16},{8,24},{16,0},{24,8},{1,17},{9,25},{17,1},{25,9},{2,18},{10... | collective-permute-start | bytes 3538952 | tf_op jit(solution)/shard_map/ppermute | solution.py:974
  356.7 28.5 %collective-permute-start.45 = (bf16[768,768]{1,0:T(8,128)(2,1)}, bf16[768,768]{1,0:T(8,128)(2,1)}, u32[]{:S(2)}, u32[]{:S(2)}) collective-permute-start(bf16[768,768]{1,0:T(8,128)(2,1)} %get-tuple-element.390), channel_id=1, source_target_pairs={{0,8},{8,0},{16,24},{24,16},{1,9},{9,1},{17,25},{25,17},{2,10},{10... | collective-permute-start | bytes 3538952 | tf_op jit(solution)/shard_map/ppermute | solution.py:974
  368.0 26.9 %collective-permute-start.41 = (bf16[1,288,768]{2,1,0:T(8,128)(2,1)}, bf16[1,288,768]{2,1,0:T(8,128)(2,1)S(1)}, u32[]{:S(2)}, u32[]{:S(2)}) collective-permute-start(bf16[1,288,768]{2,1,0:T(8,128)(2,1)} %get-tuple-element.373), channel_id=1, source_target_pairs={{0,2},{1,3},{2,0},{3,1},{4,6},{5,7},{6,4},{7,5},{8,10},{9,11},{10,... | collective-permute-start | bytes 1327112 | tf_op jit(solution)/shard_map/ppermute | solution.py:974
  (83 other events, 821.5 us)

commit v6 on v5

--- a/solution.py
+++ b/solution.py
@@ -111,14 +111,18 @@
         write(rows, tail_rows, j, read(own + j, tail_rows, tiles))
 
 
-def pack_expert_kernel(dims, wide_ref, own_ref, out_ref):
+def pack_expert_kernel(dims, cuts, wide_ref, own_ref, *out_refs):
     rows, tiles = dims
 
     def read(first, count, stride):
         return own_ref[pl.ds(first, count, stride=stride), :]
 
     def write(first, count, j, value):
-        out_ref[first : first + count, LANES * j : LANES * (j + 1)] = value.astype(bf16)
+        value = value.astype(bf16)
+        for (low, high), ref in zip(cuts, out_refs):
+            start, end = max(first, low), min(first + count, high)
+            if start < end:
+                ref[start - low : end - low, LANES * j : LANES * (j + 1)] = value[start - first : end - first]
 
     wide = wide_ref[0] > 0
 
@@ -137,11 +141,11 @@
 
 def unpack_kernel(dims, groups, wide_ref, *refs):
     rows, tiles = dims
-    refs, (out_ref, square_ref, rows_ref) = refs[:-3], refs[-3:]
-    if len(refs) > sum(groups):
-        refs, (small_ref, before_ref) = refs[:-2], refs[-2:]
+    (*refs, rows_ref), small_ref = refs, None
+    if len(refs) > sum(groups) + 2:
+        *refs, small_ref, before_ref, out_ref, square_ref, head_ref = refs
     else:
-        small_ref = None
+        *refs, out_ref, square_ref = refs
     at = 0
     for count in groups:
         value = add_up(refs[:count])
@@ -169,6 +173,7 @@
             square_ref[0:count] = small_ref[...]
             square_ref[count:] = jnp.zeros((square_ref.shape[0] - count, LANES), f32)
             square_ref[count : count + 1] = total + before_ref[...]
+            head_ref[...] = out_ref[0:count]
 
     @pl.when(wide)
     def _():
@@ -890,40 +895,55 @@
         out_ref[i // 4, i % 4] = ref[...]
 
 
-def fold_layer_kernel(cut, layer, at, sources, top_ref, keep_ref, *refs):
-    refs_in, uppers, (send_x, keep_x, send_y, keep_y), refs = refs, refs[-14:-10], refs[-10:-6], refs[-6:]
-    kept, got, total, keep_sems, got_sems, out_sems = refs
-    if at is not None:
-        keep_ref = keep_ref.at[at]
-    got_refs = []
-    for ref, (index, many) in zip(refs_in, sources):
-        ref = ref if index is None else ref.at[index]
-        got_refs += [ref.at[i] for i in range(many)]
-    count = kept.shape[0]
+def fold_layers_kernel(cut, plan, top_ref, *refs):
+    uppers, (send_x, keep_x, send_y, keep_y), scratch = refs[-14:-10], refs[-10:-6], refs[-6:]
+    kept, got, total, keep_sems, got_sems, out_sems = scratch
+    count = kept.shape[1]
     middle = send_x.shape[2]
-    place = layer ^ top_ref[0]
-    for i in range(count):
-        pltpu.make_async_copy(keep_ref.at[i], kept.at[i], keep_sems.at[i]).start()
-        pltpu.make_async_copy(got_refs[i], got.at[i], got_sems.at[i]).start()
-    for i in range(count):
-        pltpu.make_async_copy(keep_ref.at[i], kept.at[i], keep_sems.at[i]).wait()
-        pltpu.make_async_copy(got_refs[i], got.at[i], got_sems.at[i]).wait()
-        total[i] = add_pair(kept[i], got[i])
-        pltpu.make_async_copy(total.at[i, 0:cut], uppers[i % 4].at[layer, i // 4], out_sems.at[0, i]).start()
+    ins = []
+    for layer, at, sources in plan:
+        keep_ref, refs = refs[0], refs[1:]
+        keep_ref = keep_ref if at is None else keep_ref.at[at]
+        got_refs = []
+        for index, many in sources:
+            ref, refs = refs[0], refs[1:]
+            ref = ref if index is None else ref.at[index]
+            got_refs += [ref.at[i] for i in range(many)]
+        ins.append((layer, keep_ref, got_refs))
+
+    def arriving(n, i):
+        _, keep_ref, got_refs = ins[n]
+        return (
+            pltpu.make_async_copy(keep_ref.at[i], kept.at[n, i], keep_sems.at[n, i]),
+            pltpu.make_async_copy(got_refs[i], got.at[n, i], got_sems.at[n, i]),
+        )
+
+    steps = [(n, i) for n in range(len(ins)) for i in range(count)]
+    for n, i in steps:
+        for copy in arriving(n, i):
+            copy.start()
+    for n, i in steps:
+        layer = ins[n][0]
+        place = layer ^ top_ref[0]
+        for copy in arriving(n, i):
+            copy.wait()
+        total[n, i] = add_pair(kept[n, i], got[n, i])
+        pltpu.make_async_copy(total.at[n, i, 0:cut], uppers[i % 4].at[layer, i // 4], out_sems.at[n, 0, i]).start()
         for bit, send, keep, at, where, sem in (
-            (place & 1, send_x, keep_x, place >> 1, slice(cut, cut + middle), out_sems.at[1, i]),
-            (place >> 1, send_y, keep_y, place & 1, slice(cut + middle, cut + 2 * middle), out_sems.at[2, i]),
+            (place & 1, send_x, keep_x, place >> 1, slice(cut, cut + middle), out_sems.at[n, 1, i]),
+            (place >> 1, send_y, keep_y, place & 1, slice(cut + middle, cut + 2 * middle), out_sems.at[n, 2, i]),
         ):
             for value, target in ((0, keep), (1, send)):
 
                 @pl.when(bit == value)
                 def _():
-                    pltpu.make_async_copy(total.at[i, where], target.at[at, i], sem).start()
-
-    for i in range(count):
-        pltpu.make_async_copy(total.at[i, 0:cut], uppers[i % 4].at[layer, i // 4], out_sems.at[0, i]).wait()
-        for sem in (out_sems.at[1, i], out_sems.at[2, i]):
-            pltpu.make_async_copy(total.at[i, cut : cut + middle], keep_x.at[0, i], sem).wait()
+                    pltpu.make_async_copy(total.at[n, i, where], target.at[at, i], sem).start()
+
+    for n, i in steps:
+        layer = ins[n][0]
+        pltpu.make_async_copy(total.at[n, i, 0:cut], uppers[i % 4].at[layer, i // 4], out_sems.at[n, 0, i]).wait()
+        for part in (1, 2):
+            pltpu.make_async_copy(total.at[n, i, cut : cut + middle], keep_x.at[0, i], out_sems.at[n, part, i]).wait()
 
 
 def add_kernel(left, right, out_ref):
@@ -1083,11 +1103,14 @@
     )(me_arr, tail_from, dense_flat)
 
     expert_wide = (dp_me < dp_ranks // 2).astype(jnp.int32).reshape(1)
-    expert_chunk = pl.pallas_call(
-        functools.partial(pack_expert_kernel, (expert_rows, tiles)),
+    quarter = expert_rows // 4
+    cuts = [(0, 2), (2, 4), (0, 1), (1, 2), (2, 3), (3, 4)]
+    cuts = [(low * quarter, high * quarter) for low, high in cuts]
+    expert_chunks = pl.pallas_call(
+        functools.partial(pack_expert_kernel, (expert_rows, tiles), cuts),
         in_specs=[SMEM, VMEM],
-        out_specs=VMEM,
-        out_shape=shape((expert_rows, width), bf16),
+        out_specs=[VMEM] * 6,
+        out_shape=[shape((high - low, width), bf16) for low, high in cuts],
         compiler_params=params(),
         cost_estimate=cost(),
         name="pack_expert",
@@ -1153,19 +1176,22 @@
         sets[2] = swap(after(chunk, sets[1]), both, 4)
         halves = [swap(near[0][1][:split], both, masks[0]), swap(near[0][0][split:], both, masks[1])]
         near[1] = order.land(near[1])
-        halves, expert_chunk, outgoing_cot, stream = order.land((halves, expert_chunk, outgoing_cot, stream))
+        halves = order.land(halves)
+        x_half, y_half, *quarters = expert_chunks
+        early = [swap(quarters[2], dp_axis, 1), swap(quarters[0], dp_axis, 2)]
+        early, outgoing_cot, stream = order.land((early, outgoing_cot, stream))
         sets[2] = order.land(sets[2])
         sets[3] = swap(sets[2], both, 2)
         near[2] = spread(sets[2])
         far[0] = jnp.concatenate(halves)
+        sets[3], far[0] = order.land((sets[3], far[0]))
         far[1], far[2] = swap(far[0], both, 2), swap(far[0], both, 4)
-        sets[3] = order.land(sets[3])
         near[3] = spread(sets[3])
         near[2] = order.land(near[2])
         near[3] = order.land(near[3])
         far[1] = order.land(far[1])
         far[2] = order.land(far[2])
-        place_arr, far[2] = pause(place_arr, 800, far[2])
+        place_arr, far[2] = pause(place_arr, 200, far[2])
         far[3] = swap(far[2], both, 2)
         arriving_cot = exchange(after(outgoing_cot, far[2]))
 
@@ -1187,15 +1213,17 @@
         packed.append(pack_sets([2, 3]))
         arrays = packed + [swap(value, both, 1) for value in packed]
         spots = [((j >> 2) + 2 * (j & 1), ((j >> 1) & 1,), ()) for j in range(per)]
-        own_shard = after(expert_chunk, near[3])
-        beside = [swap(own_shard, dp_axis, mask) for mask in (1, 2)]
-        place_arr, beside = pause(place_arr, 650, beside)
-        place_arr, arriving_cot = pause(place_arr, 1900, arriving_cot)
+        x_out, y_out = after((x_half, y_half), near[3])
+        beside = [swap(x_out, dp_axis, 1), swap(y_out, dp_axis, 2)]
+        place_arr, beside = pause(place_arr, 3000, beside)
+        across = [swap(beside[0], dp_axis, 2), swap(beside[1], dp_axis, 1)]
+        late = after((quarters[3], quarters[1]), beside)
+        late = [swap(late[0], dp_axis, 1), swap(late[1], dp_axis, 2)]
         place_arr, arrays[2] = pause(place_arr, 300, arrays[2])
-        across = [swap(beside[0][:half_rows], dp_axis, 2), swap(beside[1][half_rows:], dp_axis, 1)]
-        expert_me, across = pause(expert_me, 400, across)
-        expert_parts = [expert_chunk, *beside, *across]
-        expert_spans = [(0, 0), (1, 0), (2, 0), (3, 0), (3, half_rows)]
+        expert_me, (across, arriving_cot) = pause(expert_me, 400, (across, arriving_cot))
+        expert_parts = [x_half, y_half, beside[0], early[0], late[0], beside[1], early[1], late[1], *across]
+        expert_spans = [(0, 0), (0, 2), (1, 0), (1, 2), (1, 3), (2, 2), (2, 0), (2, 1), (3, 0), (3, 2)]
+        expert_spans = [(place, first * quarter) for place, first in expert_spans]
     else:
         gathered = chunk[None]
         for bit in range(all_bits):
@@ -1203,7 +1231,7 @@
         arrays = [gathered.reshape(4, per, chunk_rows, width)]
         spots = [(0, (), (j,)) for j in range(per)]
         for side, bits in enumerate(orders):
-            parts, places = [expert_chunk[side * half_rows : (side + 1) * half_rows]], [0]
+            parts, places = [expert_chunks[side]], [0]
             for bit in bits:
                 parts = parts + [swap(part, dp_axis, 1 << bit) for part in parts]
                 places = places + [place | (1 << bit) for place in places]
@@ -1297,7 +1325,6 @@
     stream_three, kept_two = results[9], results[10:]
     arriving = exchange(outgoing)
 
-    quarter = expert_rows // 4
     slot_spec = pl.BlockSpec((slots, width), lambda q: (0, 0))
     wide_spec = pl.BlockSpec((slots, width + LANES), lambda q: (0, 0))
     pair_spec = pl.BlockSpec((2, stride, width), lambda q: (0, 0, 0))
@@ -1341,7 +1368,7 @@
     )(dp_arr, arriving, slot_grad, expert_act, pre_grad)
     returned_grad = after(returned_grad, expert_first)
 
-    cut = max(16, rows // 64 * 16)
+    cut = max(16, rows // 48 * 16)
     middle = (rows - cut) // 2
     top = (me >> per_bits).reshape(1)
     z_bits = list(range(1, per_bits))
@@ -1353,9 +1380,9 @@
 
     def over_z(values, meanwhile=None):
         farthest = swap(values[3], both, 2)
-        near = swap(values[1], both, 2)
         if meanwhile is not None:
             farthest, *meanwhile[:] = lax.optimization_barrier((farthest, *meanwhile))
+        near = swap(after(values[1], farthest), both, 2)
         return [values[0], near, swap(add_call(values[2], farthest), both, 4)]
 
     def rest_of_z(values):
@@ -1370,6 +1397,8 @@
         return [parts[0], swap(parts[1], both, 1)]
 
     expert_got = [swap(expert_first[0], dp_axis, 1), swap(expert_first[2], dp_axis, dp_ranks // 2)]
+    returned_grad, expert_out = lax.optimization_barrier((returned_grad, expert_out))
+    expert_out = [expert_out[0]] + [swap(v, ("expert",), 2 * j) for j, v in enumerate(expert_out) if j]
     backward_ins = (
         (stream_three, moe_in, stream_two, *kept_two[1:4], kept_two[0], kept_two[4])
         + (stream_one, mlp_in, mlp_pre, stream, *kept_one[1:4])
@@ -1411,6 +1440,7 @@
         dws[2] = jnp.concatenate([dws[2], wide_grad[None, :, 0]])
         dws[4] = jnp.concatenate([dws[4], wide_grad[None, most:, 1]])
         dws[5] = wide_grad[:most, 1]
+    dws, expert_out = lax.optimization_barrier((dws, expert_out))
     most_got = [swap(dws[3], both, 1), swap(dws[5], both, 1)]
     rest_got = swap(dws[4], both, 1)
     first_dw = attn_weights_call(upper, kept_one, (dq, dk, dv))
@@ -1425,28 +1455,30 @@
     line_spec = pl.BlockSpec((1, middle, width), lambda i: (i, 0, 0))
     upper_shape = shape((4, places // 4, cut, width), bf16)
     sums = ()
-    for layer in (3, 2, 1, 0):
-        keep, at = layer_keep[layer]
-        parts = layer_got[layer]
-        if layer == 3:
-            keep = after(keep, first_dw)
-        if layer == 1:
+    for pair in ((3, 2), (1, 0)):
+        if pair[0] == 1:
             expert_got, sums = lax.optimization_barrier((expert_got, sums))
             top, expert_got = pause(top, 1600, expert_got)
+        plan, ins = [], []
+        for layer in pair:
+            keep, at = layer_keep[layer]
+            parts = layer_got[layer]
+            plan.append((layer, at, [part[1:] for part in parts]))
+            ins += [after(keep, first_dw) if layer == 3 else keep] + [part[0] for part in parts]
         sums = call(
-            functools.partial(fold_layer_kernel, cut, layer, at, [part[1:] for part in parts]),
-            (top, keep, *[part[0] for part in parts], *sums),
-            (SMEM,) + (ANY,) * (1 + len(parts) + len(sums)),
+            functools.partial(fold_layers_kernel, cut, plan),
+            (top, *ins, *sums),
+            (SMEM,) + (ANY,) * (len(ins) + len(sums)),
             [upper_shape] * 4 + [plane_shape] * 4,
-            "fold_layer",
+            "fold_layers",
             out_specs=[ANY] * 8,
-            scratch=[pltpu.VMEM((places, rows, width), bf16)] * 3
+            scratch=[pltpu.VMEM((2, places, rows, width), bf16)] * 3
             + [
-                pltpu.SemaphoreType.DMA((places,)),
-                pltpu.SemaphoreType.DMA((places,)),
-                pltpu.SemaphoreType.DMA((3, places)),
+                pltpu.SemaphoreType.DMA((2, places)),
+                pltpu.SemaphoreType.DMA((2, places)),
+                pltpu.SemaphoreType.DMA((2, 3, places)),
             ],
-            aliases={2 + len(parts) + i: i for i in range(len(sums))},
+            aliases={1 + len(ins) + i: i for i in range(len(sums))},
         )
     *uppers, send_x, keep_x, send_y, keep_y = sums
     masks = [1 << bit for bit in top_bits]
@@ -1474,7 +1506,6 @@
         scratch=[pltpu.VMEM((4, cut, width), bf16)],
     )
     got_x, got_y, expert_second = lax.optimization_barrier((got_x, got_y, expert_second))
-    expert_out = [expert_out[0]] + [swap(v, ("expert",), 2 * j) for j, v in enumerate(expert_out) if j]
     own_a, send_y, own_b, send_x = pl.pallas_call(
         fold_plane_kernel,
         grid=(places,),
@@ -1486,7 +1517,7 @@
         name="fold_plane",
     )(keep_x, got_x, keep_y, got_y)
     got_y, got_x = swap(send_y, both, masks[1]), swap(send_x, both, masks[0])
-    expert_second, expert_out, upper_rows = lax.optimization_barrier((expert_second, expert_out, upper_rows))
+    expert_second, upper_rows = lax.optimization_barrier((expert_second, upper_rows))
     other_out = swap(jnp.stack([value[1] for value in expert_out]), ("expert",), 1)
     lower_rows = call(
         fold_rows_kernel,
@@ -1527,13 +1558,13 @@
     expert_groups = [side[0] for side in expert_groups]
     upper_rows, expert_groups = lax.optimization_barrier((upper_rows, expert_groups))
 
-    def unpack(wide, groups, count, name, extra=(), square_shape=(1, LANES)):
+    def unpack(wide, groups, count, name, extra=(), more_shapes=((1, LANES),)):
         pieces = [piece for group in groups for piece in group] + list(extra)
         return pl.pallas_call(
             functools.partial(unpack_kernel, (count, tiles), [len(group) for group in groups]),
             in_specs=[SMEM] + [VMEM] * len(pieces),
-            out_specs=[VMEM, VMEM],
-            out_shape=[shape((count * tiles, LANES)), shape(square_shape)],
+            out_specs=[VMEM] * (1 + len(more_shapes)),
+            out_shape=[shape((count * tiles, LANES))] + [shape(dims) for dims in more_shapes],
             scratch_shapes=[pltpu.VMEM((count, width), f32)],
             compiler_params=params(),
             cost_estimate=cost(),
@@ -1551,15 +1582,15 @@
     dense_groups = [upper_rows, [value.reshape(rows - cut, width) for value in lower_rows]]
 
     dense_wide = (me >= devices // 2) & (me < 3 * devices // 4) & wide_ok
-    dense_rows, total = unpack(
+    dense_rows, total, head = unpack(
         dense_wide.astype(jnp.int32).reshape(1),
         dense_groups,
         rows,
         "unpack_dense",
         (small, expert_square),
-        (tail + 8, LANES),
+        ((tail + 8, LANES), (tail, LANES)),
     )
-    head = lax.ppermute(dense_rows[:tail], both, backward_ring)
+    head = lax.ppermute(head, both, backward_ring)
     groups = bit_groups(list(range(all_bits)))
     for bits in groups[:-1]:
         total = all_sum_step(total, both, bits)

time: 446 us -> 422 us (0.946)
  waiting for transfers between devices: 183 us -> 157 us
  starting transfers between devices: 64.7 us -> 72.2 us
  local copies, waits for them, and re-layouts: 27.2 us -> 22.5 us
    all_to_all x3, waiting for transfers between devices: 29 us -> 13.6 us  [exchange(): lax.all_to_all(value, 'expert', split_axis=0, concat_axis=0, tiled=True)]
    ppermute x55 -> x59, waiting for transfers between devices: 146 us -> 136 us  [swap(): return lax.ppermute(value, axes, [(i, i ^ mask) for i in range(size)])]
    ppermute x55 -> x59, starting transfers between devices: 51.3 us -> 58.6 us  [swap(): return lax.ppermute(value, axes, [(i, i ^ mask) for i in range(size)])]
    slice x3 -> x0, local copies, waits for them, and re-layouts: 4.76 us -> none  [the longest x1 2.36 us: on_device(): beside[1][half_rows:]]
    unnamed x98 -> x115, local copies, waits for them, and re-layouts: 13.6 us -> 17.1 us
    pallas_call x13 -> x11, Pallas kernels: 77.1 us -> 74.9 us  [call(): pl.pallas_call(kernel, grid=(1,), in_specs=[s or whole(a) for a, s in zip...]
  transfers between devices with their start and end apart: 60 -> 64, of which waited for: 31 -> 34; matrix products, arithmetic and copies ran while one was open for 4% -> 3% of each run, Pallas kernels for 27% -> 27%
where the time goes in v6:
time: 422 us; the launch traced here: 416 us
  Pallas kernels  158 us (37%)
  waiting for transfers between devices  157 us (37%)
  starting transfers between devices  72.2 us (17%)
  local copies, waits for them, and re-layouts  22.5 us (5%)
  other arithmetic  5.64 us (1%)
    ppermute x59, waiting for transfers between devices, swap(): return lax.ppermute(value, axes, [(i, i ^ mask) for i in range(size)])  136 us
    pallas_call x11, Pallas kernels, call(): pl.pallas_call(kernel, grid=(1,), in_specs=[s or whole(a) for a, s in zip...  74.9 us
    ppermute x59, starting transfers between devices, swap(): return lax.ppermute(value, axes, [(i, i ^ mask) for i in range(size)])  58.6 us
    pallas_call x1, Pallas kernels, on_device(): pl.pallas_call(functools.partial(expert_kernel, (dp_ranks, quarter, exper...  17.4 us
    unnamed x115, local copies, waits for them, and re-layouts  17.1 us
    pallas_call x1, Pallas kernels, on_device(): pl.pallas_call(functools.partial(adam_kernel, (step, chunks, devices, par...  16.1 us
    all_to_all x3, waiting for transfers between devices, exchange(): lax.all_to_all(value, 'expert', split_axis=0, concat_axis=0, tiled=True)  13.6 us
    all_to_all x3, starting transfers between devices, exchange(): lax.all_to_all(value, 'expert', split_axis=0, concat_axis=0, tiled=True)  12.1 us
  transfers between devices with their start and end apart: 64, of which 34 were waited for; matrix products, arithmetic and copies ran while one was open for 3% of the time, Pallas kernels for 27%

profile of v6, /device:TPU:0, one launch (start us, length us, event | category | flops | bytes accessed | tf_op | source)
XLA Modules:
  0.0 416.5 jit_solution(15300881188161259830)
XLA Ops:
  1.9 7.7 %collective-permute-done.tail_ref = f32[96,128]{1,0:T(8,128)S(1)} collective-permute-done((f32[96,128]{1,0:T(8,128)S(1)}, f32[96,128]{1,0:T(8,128)S(1)}, u32[]{:S(2)}, u32[]{:S(2)}) %collective-permute-start) | collective-permute-done | bytes 49184 | tf_op jit(solution)/shard_map/ppermute | solution.py:1090
  15.1 9.6 %collective-permute-done.2.refs_1_ = bf16[400,768]{1,0:T(8,128)(2,1)S(1)} collective-permute-done((bf16[400,768]{1,0:T(8,128)(2,1)}, bf16[400,768]{1,0:T(8,128)(2,1)S(1)}, u32[]{:S(2)}, u32[]{:S(2)}) %collective-permute-start.2) | collective-permute-done | bytes 614432 | tf_op jit(solution)/shard_map/ppermute | solution.py:994
  30.8 5.8 %pack_expert.1 = (bf16[768,768]{1,0:T(8,128)(2,1)}, bf16[768,768]{1,0:T(8,128)(2,1)}, bf16[384,768]{1,0:T(8,128)(2,1)}, bf16[384,768]{1,0:T(8,128)(2,1)}, bf16[3...) custom-call(s32[1]{0:T(128)} %bitcast.6.wide_ref, f32[9216,128]{1,0:T(8,128)} %bitcast.46), custom_call_target="tpu_custom_call" | custom-call | flops 1 | bytes 1 | tf_op jit(solution)/shard_map/pack_expert/pallas_call | solution.py:1109
  51.6 6.5 %collective-permute-done.8 = bf16[192,768]{1,0:T(8,128)(2,1)S(1)} collective-permute-done((bf16[192,768]{1,0:T(8,128)(2,1)S(1)}, bf16[192,768]{1,0:T(8,128)(2,1)S(1)}, u32[]{:S(2)}, u32[]{:S(2)}) %collective-permute-start.8) | collective-permute-done | bytes 294944 | tf_op jit(solution)/shard_map/ppermute | solution.py:994
  65.1 8.9 %collective-permute-done.11.refs_4_ = bf16[400,768]{1,0:T(8,128)(2,1)S(1)} collective-permute-done((bf16[400,768]{1,0:T(8,128)(2,1)}, bf16[400,768]{1,0:T(8,128)(2,1)S(1)}, u32[]{:S(2)}, u32[]{:S(2)}) %collective-permute-start.11) | collective-permute-done | bytes 614432 | tf_op jit(solution)/shard_map/ppermute | solution.py:994
  79.2 9.3 %collective-permute-done.14.refs_5_ = bf16[400,768]{1,0:T(8,128)(2,1)S(1)} collective-permute-done((bf16[400,768]{1,0:T(8,128)(2,1)S(1)}, bf16[400,768]{1,0:T(8,128)(2,1)S(1)}, u32[]{:S(2)}, u32[]{:S(2)}) %collective-permute-start.14) | collective-permute-done | bytes 614432 | tf_op jit(solution)/shard_map/ppermute | solution.py:994
  91.3 9.1 %collective-permute-done.13.refs_7_ = bf16[400,768]{1,0:T(8,128)(2,1)} collective-permute-done((bf16[400,768]{1,0:T(8,128)(2,1)S(1)}, bf16[400,768]{1,0:T(8,128)(2,1)}, u32[]{:S(2)}, u32[]{:S(2)}) %collective-permute-start.13) | collective-permute-done | bytes 614432 | tf_op jit(solution)/shard_map/ppermute | solution.py:994
  105.3 5.0 %pack_sets.2.refs_0_.refs_15_ = bf16[2,4,400,768]{3,2,1,0:T(8,128)(2,1)} custom-call(bf16[400,768]{1,0:T(8,128)(2,1)} %pack_dense.1.refs_0_, bf16[400,768]{1,0:T(8,128)(2,1)} %copy-done.21, bf16[400,768]{1,0:T(8,128)(2,1)} %copy-done.20, bf16[400,768]{1,0:T(8,128)(2,1)} %copy-done.13, bf16[400,768]{1,0:T(8,128)(2,1)} %copy-done.27, ...), custom_call_target="tpu_custom_call" | custom-call | flops 1 | bytes 1 | tf_op jit(solution)/shard_map/pack_sets/pallas_call | solution.py:1200
  130.3 16.0 %forward.1 = (f32[208,768]{1,0:T(8,128)}, bf16[208,768]{1,0:T(8,128)(2,1)}, bf16[208,768]{1,0:T(8,128)(2,1)}, bf16[208,768]{1,0:T(8,128)(2,1)}, bf16[208,768]{1,...) custom-call(s32[2]{0:T(128)} %pause.7.place_ref, ...), custom_call_target="tpu_custom_call" | custom-call | flops 1 | bytes 1 | tf_op jit(solution)/shard_map/forward/pallas_call | solution.py:1261
  154.9 12.8 %collective-permute-done.25.refs_4_ = bf16[384,768]{1,0:T(8,128)(2,1)S(1)} collective-permute-done((bf16[384,768]{1,0:T(8,128)(2,1)}, bf16[384,768]{1,0:T(8,128)(2,1)S(1)}, u32[]{:S(2)}, u32[]{:S(2)}) %collective-permute-start.25) | collective-permute-done | bytes 589856 | tf_op jit(solution)/shard_map/ppermute | solution.py:994
  173.3 17.4 %expert.1 = (bf16[2,56,768]{2,1,0:T(8,128)(2,1)}, bf16[2,56,768]{2,1,0:T(8,128)(2,1)}, bf16[2,56,768]{2,1,0:T(8,128)(2,1)}, bf16[2,56,768]{2,1,0:T(8,128)(2,1)},...) custom-call(s32[2]{0:T(128)} %pause.8.me_ref, ...), custom_call_target="tpu_custom_call" | custom-call | flops 1 | bytes 1 | tf_op jit(solution)/shard_map/expert/pallas_call | solution.py:1333
  194.3 9.4 %expert_grad.1 = (bf16[2,768,768]{2,1,0:T(8,128)(2,1)}, bf16[2,768,768]{2,1,0:T(8,128)(2,1)}, bf16[2,768,768]{2,1,0:T(8,128)(2,1)}, bf16[2,768,768]{2,1,0:T(8,128)(2,1)}) custom-call(s32[1]{0:T(128)} %bitcast.1.dp_ref, bf16[448,896]{1,0:T(8,128)(2,1)} %bitcast.45, bf16[448,768]{1,0:T(8,128)(2,1)} %get-tuple-element.273.dy_ref, ...), custom_call_target="tpu_custom_call" | custom-call | flops 1 | bytes 1 | tf_op jit(solution)/shard_map/expert_grad/pallas_call | solution.py:1355
  205.7 9.8 %all-to-all-done.2 = bf16[8,56,896]{2,1,0:T(8,128)(2,1)S(1)} async-done(((bf16[8,56,896]{2,1,0:T(8,128)(2,1)}), bf16[8,56,896]{2,1,0:T(8,128)(2,1)S(1)}, u32[]{:S(2)}, u32[]{:S(2)}) %all-to-all-start.2) | async-done | bytes 802848 | tf_op jit(solution)/shard_map/all_to_all | solution.py:1149
  219.9 27.7 %backward.1 = (f32[96,128]{1,0:T(8,128)}, f32[208,768]{1,0:T(8,128)}, bf16[208,768]{1,0:T(8,128)(2,1)}, bf16[208,768]{1,0:T(8,128)(2,1)}, bf16[208,768]{1,0:T(8,...) custom-call(s32[2]{0:T(128)} %pause.7.place_ref, ...), custom_call_target="tpu_custom_call" | custom-call | flops 1 | bytes 1 | tf_op jit(solution)/shard_map/backward/pallas_call | solution.py:1261
  257.5 6.0 %fold_layers.2 = (bf16[4,1,128,768]{3,2,1,0:T(8,128)(2,1)}, bf16[4,1,128,768]{3,2,1,0:T(8,128)(2,1)}, bf16[4,1,128,768]{3,2,1,0:T(8,128)(2,1)}, bf16[4,1,128,768...) custom-call(s32[1]{0:T(128)} %bitcast.top_ref.ref, ...), custom_call_target="tpu_custom_call" | custom-call | flops 1 | bytes 1 | tf_op jit(solution)/shard_map/fold_layers/pallas_call | solution.py:1261
  266.8 6.9 %fold_layers.3 = (bf16[4,1,128,768]{3,2,1,0:T(8,128)(2,1)}, bf16[4,1,128,768]{3,2,1,0:T(8,128)(2,1)}, bf16[4,1,128,768]{3,2,1,0:T(8,128)(2,1)}, bf16[4,1,128,768...) custom-call(s32[1]{0:T(128)} %pause.9.top_ref, ...), custom_call_target="tpu_custom_call", output_to_operand_aliasing={{0}: (5, {}), {1}: (6, {}), {2}: (7, {}), {3}: (8, {}), {4}... | custom-call | flops 1 | bytes 1 | tf_op jit(solution)/shard_map/fold_layers/pallas_call | solution.py:1261
  275.6 19.2 %collective-permute-done.45.right = bf16[4,1,128,768]{3,2,1,0:T(8,128)(2,1)S(1)} collective-permute-done((bf16[4,1,128,768]{3,2,1,0:T(8,128)(2,1)}, bf16[4,1,128,768]{3,2,1,0:T(8,128)(2,1)S(1)}, u32[]{:S(2)}, u32[]{:S(2)}) %collective-permute-start.45) | collective-permute-done | bytes 786464 | tf_op jit(solution)/shard_map/ppermute | solution.py:994
  298.0 6.2 %fold_expert.1 = (bf16[768,768]{1,0:T(8,128)(2,1)}, bf16[768,768]{1,0:T(8,128)(2,1)}, bf16[768,768]{1,0:T(8,128)(2,1)}, bf16[768,768]{1,0:T(8,128)(2,1)}) custom-call(bf16[2,768,768]{2,1,0:T(8,128)(2,1)} %get-tuple-element.283.refs_0_, bf16[2,768,768]{2,1,0:T(8,128)(2,1)} %collective-permute-done.27.refs_1_, ...), custom_call_target="tpu_custom_call" | custom-call | flops 1 | bytes 1 | tf_op jit(solution)/shard_map/fold_expert/pallas_call | solution.py:1261
  304.2 6.2 %collective-permute-done.37.got_x = bf16[2,4,128,768]{3,2,1,0:T(8,128)(2,1)S(1)} collective-permute-done((bf16[2,4,128,768]{3,2,1,0:T(8,128)(2,1)}, bf16[2,4,128,768]{3,2,1,0:T(8,128)(2,1)S(1)}, u32[]{:S(2)}, u32[]{:S(2)}) %collective-permute-start.37) | collective-permute-done | bytes 1572896 | tf_op jit(solution)/shard_map/ppermute | solution.py:994
  319.1 13.0 %collective-permute-done.47 = bf16[4,1,128,768]{3,2,0,1:T(8,128)(2,1)S(1)} collective-permute-done((bf16[4,1,128,768]{3,2,0,1:T(8,128)(2,1)S(1)}, bf16[4,1,128,768]{3,2,0,1:T(8,128)(2,1)S(1)}, u32[]{:S(2)}, u32[]{:S(2)}) %collective-permute-start.47) | collective-permute-done | bytes 786464 | tf_op jit(solution)/shard_map/ppermute | solution.py:994
  345.5 10.0 %collective-permute-done.42.right = bf16[1,256,768]{2,1,0:T(8,128)(2,1)S(1)} collective-permute-done((bf16[1,256,768]{2,1,0:T(8,128)(2,1)}, bf16[1,256,768]{2,1,0:T(8,128)(2,1)S(1)}, u32[]{:S(2)}, u32[]{:S(2)}) %collective-permute-start.42) | collective-permute-done | bytes 393248 | tf_op jit(solution)/shard_map/ppermute | solution.py:994
  357.6 7.5 %collective-permute-done.48.refs_1_ = bf16[768,768]{1,0:T(8,128)(2,1)} collective-permute-done((bf16[768,768]{1,0:T(8,128)(2,1)}, bf16[768,768]{1,0:T(8,128)(2,1)}, u32[]{:S(2)}, u32[]{:S(2)}) %collective-permute-start.48) | collective-permute-done | bytes 1179680 | tf_op jit(solution)/shard_map/ppermute | solution.py:994
  369.5 6.1 %unpack_expert.1 = (f32[9216,128]{1,0:T(8,128)}, f32[1,128]{1,0:T(1,128)}) custom-call(s32[1]{0:T(128)} %bitcast.6.wide_ref, bf16[768,768]{1,0:T(8,128)(2,1)} %get-tuple-element.406.refs_0_, bf16[768,768]{1,0:T(8,128)(2,1)} %collective-permute-done.48.refs_1_, bf16[768,768]{1,0:T(8,128)(2,1)} %get-tuple-element.408.refs_2_, ...), custom_call_target="tpu_custom_call" | custom-call | flops 1 | bytes 1 | tf_op jit(solution)/shard_map/unpack_expert/pallas_call | solution.py:1563
  400.1 16.1 %adam.1 = (f32[9216,128]{1,0:T(8,128)}, f32[9216,128]{1,0:T(8,128)}, f32[9216,128]{1,0:T(8,128)}, f32[2307,128]{1,0:T(8,128)}, f32[2307,128]{1,0:T(8,128)}, /*in...) custom-call(s32[1]{0:T(128)} %bitcast.3.k_ref, f32[104,128]{1,0:T(8,128)} %add.41.total_ref, ...), custom_call_target="tpu_custom_call" | custom-call | flops 1 | bytes 1 | tf_op jit(solution)/shard_map/adam/pallas_call | solution.py:1602
  (268 shorter events, 162.9 us)
Async XLA Ops:
  30.2 29.1 %collective-permute-start.4 = (bf16[400,768]{1,0:T(8,128)(2,1)}, bf16[400,768]{1,0:T(8,128)(2,1)}, u32[]{:S(2)}, u32[]{:S(2)}) collective-permute-start(bf16[400,768]{1,0:T(8,128)(2,1)} %pack_dense.1.refs_0_), channel_id=1, source_target_pairs={{0,4},{1,5},{2,6},{3,7},{4,0},{5,1},{6,2},{7,3},{8,12},{9,13},{10,... | collective-permute-start | bytes 1843208 | tf_op jit(solution)/shard_map/ppermute | solution.py:994
  36.6 22.0 %collective-permute-start.5 = (bf16[384,768]{1,0:T(8,128)(2,1)}, bf16[384,768]{1,0:T(8,128)(2,1)}, u32[]{:S(2)}, u32[]{:S(2)}) collective-permute-start(bf16[384,768]{1,0:T(8,128)(2,1)} %get-tuple-element.228), channel_id=1, source_target_pairs={{0,8},{8,0},{16,24},{24,16},{1,9},{9,1},{17,25},{25,17},{2,10},{10... | collective-permute-start | bytes 1769480 | tf_op jit(solution)/shard_map/ppermute | solution.py:994
  75.3 25.1 %collective-permute-start.13 = (bf16[400,768]{1,0:T(8,128)(2,1)S(1)}, bf16[400,768]{1,0:T(8,128)(2,1)}, u32[]{:S(2)}, u32[]{:S(2)}) collective-permute-start(bf16[400,768]{1,0:T(8,128)(2,1)S(1)} %pad_maximum_fusion.refs_3_), channel_id=1, source_target_pairs={{0,2},{1,3},{2,0},{3,1},{4,6},{5,7},{6,4},{7,5},{8,10},{9,11},{10,... | collective-permute-start | bytes 1843208 | tf_op jit(solution)/shard_map/ppermute | solution.py:994
  78.0 22.3 %collective-permute-start.12 = (bf16[400,768]{1,0:T(8,128)(2,1)S(1)}, bf16[400,768]{1,0:T(8,128)(2,1)}, u32[]{:S(2)}, u32[]{:S(2)}) collective-permute-start(bf16[400,768]{1,0:T(8,128)(2,1)S(1)} %pad_maximum_fusion.refs_3_), channel_id=1, source_target_pairs={{0,4},{1,5},{2,6},{3,7},{4,0},{5,1},{6,2},{7,3},{8,12},{9,13},{10,... | collective-permute-start | bytes 1843208 | tf_op jit(solution)/shard_map/ppermute | solution.py:994
  89.2 32.2 %collective-permute-start.18 = (bf16[768,768]{1,0:T(8,128)(2,1)S(1)}, bf16[768,768]{1,0:T(8,128)(2,1)}, u32[]{:S(2)}, u32[]{:S(2)}) collective-permute-start(bf16[768,768]{1,0:T(8,128)(2,1)S(1)} %copy-done.22), channel_id=1, source_target_pairs={{0,8},{8,0},{16,24},{24,16},{1,9},{9,1},{17,25},{25,17},{2,10},{10... | collective-permute-start | bytes 3538952 | tf_op jit(solution)/shard_map/ppermute | solution.py:994
  90.3 31.1 %collective-permute-start.19 = (bf16[768,768]{1,0:T(8,128)(2,1)}, bf16[768,768]{1,0:T(8,128)(2,1)}, u32[]{:S(2)}, u32[]{:S(2)}) collective-permute-start(bf16[768,768]{1,0:T(8,128)(2,1)} %get-tuple-element.252.refs_1_), channel_id=1, source_target_pairs={{0,16},{8,24},{16,0},{24,8},{1,17},{9,25},{17,1},{25,9},{2,18},{10... | collective-permute-start | bytes 3538952 | tf_op jit(solution)/shard_map/ppermute | solution.py:994
  110.2 36.1 %all-to-all-start.1 = ((bf16[8,56,768]{2,1,0:T(8,128)(2,1)}), bf16[8,56,768]{2,1,0:T(8,128)(2,1)S(1)}, u32[]{:S(2)}, u32[]{:S(2)}) async-start(bf16[8,56,768]{2,1,0:T(8,128)(2,1)} %bitcast.59), calls=%async_computation.1 | async-start | bytes 1376256 | tf_op jit(solution)/shard_map/all_to_all | solution.py:1149
  121.4 32.2 %collective-permute-start.23 = (bf16[768,768]{1,0:T(8,128)(2,1)}, bf16[768,768]{1,0:T(8,128)(2,1)S(1)}, u32[]{:S(2)}, u32[]{:S(2)}) collective-permute-start(bf16[768,768]{1,0:T(8,128)(2,1)} %collective-permute-done.18.refs_2_), channel_id=1, source_target_pairs={{0,16},{8,24},{16,0},{24,8},{1,17},{9,25},{17,1},{25,9},{2,18},{10... | collective-permute-start | bytes 3538952 | tf_op jit(solution)/shard_map/ppermute | solution.py:994
  122.2 31.4 %collective-permute-start.24 = (bf16[768,768]{1,0:T(8,128)(2,1)}, bf16[768,768]{1,0:T(8,128)(2,1)}, u32[]{:S(2)}, u32[]{:S(2)}) collective-permute-start(bf16[768,768]{1,0:T(8,128)(2,1)} %collective-permute-done.19.refs_5_), channel_id=1, source_target_pairs={{0,8},{8,0},{16,24},{24,16},{1,9},{9,1},{17,25},{25,17},{2,10},{10... | collective-permute-start | bytes 3538952 | tf_op jit(solution)/shard_map/ppermute | solution.py:994
  146.3 26.1 %all-to-all-start = ((bf16[8,56,896]{2,1,0:T(8,128)(2,1)}), bf16[8,56,896]{2,1,0:T(8,128)(2,1)S(1)}, u32[]{:S(2)}, u32[]{:S(2)}) async-start(bf16[8,56,896]{2,1,0:T(8,128)(2,1)} %bitcast.55), calls=%async_computation | async-start | bytes 1605632 | tf_op jit(solution)/shard_map/all_to_all | solution.py:1149
  190.7 24.8 %all-to-all-start.2 = ((bf16[8,56,896]{2,1,0:T(8,128)(2,1)}), bf16[8,56,896]{2,1,0:T(8,128)(2,1)S(1)}, u32[]{:S(2)}, u32[]{:S(2)}) async-start(bf16[8,56,896]{2,1,0:T(8,128)(2,1)} %bitcast.56), calls=%async_computation.2 | async-start | bytes 1605632 | tf_op jit(solution)/shard_map/all_to_all | solution.py:1149
  203.6 59.9 %collective-permute-start.27 = (bf16[2,768,768]{2,1,0:T(8,128)(2,1)}, bf16[2,768,768]{2,1,0:T(8,128)(2,1)}, u32[]{:S(2)}, u32[]{:S(2)}) collective-permute-start(bf16[2,768,768]{2,1,0:T(8,128)(2,1)} %get-tuple-element.276), channel_id=1, source_target_pairs={{0,8},{8,0},{16,24},{24,16},{1,9},{9,1},{17,25},{25,17},{2,10},{10... | collective-permute-start | bytes 7077896 | tf_op jit(solution)/shard_map/ppermute | solution.py:994
  204.9 58.6 %collective-permute-start.28 = (bf16[2,768,768]{2,1,0:T(8,128)(2,1)}, bf16[2,768,768]{2,1,0:T(8,128)(2,1)}, u32[]{:S(2)}, u32[]{:S(2)}) collective-permute-start(bf16[2,768,768]{2,1,0:T(8,128)(2,1)} %get-tuple-element.277), channel_id=1, source_target_pairs={{0,16},{8,24},{16,0},{24,8},{1,17},{9,25},{17,1},{25,9},{2,18},{10... | collective-permute-start | bytes 7077896 | tf_op jit(solution)/shard_map/ppermute | solution.py:994
  215.5 32.1 %collective-permute-start.29 = (bf16[2,56,768]{2,1,0:T(8,128)(2,1)S(1)}, bf16[2,56,768]{2,1,0:T(8,128)(2,1)S(1)}, u32[]{:S(2)}, u32[]{:S(2)}) collective-permute-start(bf16[2,56,768]{2,1,0:T(8,128)(2,1)S(1)} %copy-done.55), channel_id=1, source_target_pairs={{0,2},{1,3},{2,0},{3,1},{4,6},{5,7},{6,4},{7,5},{8,10},{9,11},{10,... | collective-permute-start | bytes 516104 | tf_op jit(solution)/shard_map/ppermute | solution.py:994
  215.5 32.1 %collective-permute-start.30 = (bf16[2,56,768]{2,1,0:T(8,128)(2,1)S(1)}, bf16[2,56,768]{2,1,0:T(8,128)(2,1)S(1)}, u32[]{:S(2)}, u32[]{:S(2)}) collective-permute-start(bf16[2,56,768]{2,1,0:T(8,128)(2,1)S(1)} %copy-done.54), channel_id=1, source_target_pairs={{0,4},{1,5},{2,6},{3,7},{4,0},{5,1},{6,2},{7,3},{8,12},{9,13},{10,... | collective-permute-start | bytes 516104 | tf_op jit(solution)/shard_map/ppermute | solution.py:994
  217.3 30.4 %collective-permute-start.31 = (bf16[2,56,768]{2,1,0:T(8,128)(2,1)S(1)}, bf16[2,56,768]{2,1,0:T(8,128)(2,1)S(1)}, u32[]{:S(2)}, u32[]{:S(2)}) collective-permute-start(bf16[2,56,768]{2,1,0:T(8,128)(2,1)S(1)} %copy-done.53), channel_id=1, source_target_pairs={{0,6},{1,7},{2,4},{3,5},{4,2},{5,3},{6,0},{7,1},{8,14},{9,15},{10,... | collective-permute-start | bytes 516104 | tf_op jit(solution)/shard_map/ppermute | solution.py:994
  273.7 36.7 %collective-permute-start.37 = (bf16[2,4,128,768]{3,2,1,0:T(8,128)(2,1)}, bf16[2,4,128,768]{3,2,1,0:T(8,128)(2,1)S(1)}, u32[]{:S(2)}, u32[]{:S(2)}) collective-permute-start(bf16[2,4,128,768]{3,2,1,0:T(8,128)(2,1)} %get-tuple-element.350), channel_id=1, source_target_pairs={{0,8},{1,9},{2,10},{3,11},{4,12},{5,13},{6,14},{7,15},{8,0},{9,1},... | collective-permute-start | bytes 4718600 | tf_op jit(solution)/shard_map/ppermute | solution.py:994
  274.8 36.4 %collective-permute-start.38 = (bf16[2,4,128,768]{3,2,1,0:T(8,128)(2,1)}, bf16[2,4,128,768]{3,2,1,0:T(8,128)(2,1)S(1)}, u32[]{:S(2)}, u32[]{:S(2)}) collective-permute-start(bf16[2,4,128,768]{3,2,1,0:T(8,128)(2,1)} %get-tuple-element.351), channel_id=1, source_target_pairs={{0,16},{1,17},{2,18},{3,19},{4,20},{5,21},{6,22},{7,23},{8,24},{9,... | collective-permute-start | bytes 4718600 | tf_op jit(solution)/shard_map/ppermute | solution.py:994
  296.1 35.9 %collective-permute-start.47 = (bf16[4,1,128,768]{3,2,0,1:T(8,128)(2,1)S(1)}, bf16[4,1,128,768]{3,2,0,1:T(8,128)(2,1)S(1)}, u32[]{:S(2)}, u32[]{:S(2)}) collective-permute-start(bf16[4,1,128,768]{3,2,0,1:T(8,128)(2,1)S(1)} %bitcast.43), channel_id=1, source_target_pairs={{0,4},{1,5},{2,6},{3,7},{4,0},{5,1},{6,2},{7,3},{8,12},{9,13},{10,... | collective-permute-start | bytes 2359304 | tf_op jit(solution)/shard_map/ppermute | solution.py:994
  297.1 35.0 %collective-permute-start.46 = (bf16[4,1,128,768]{3,2,0,1:T(8,128)(2,1)S(1)}, bf16[4,1,128,768]{3,2,0,1:T(8,128)(2,1)S(1)}, u32[]{:S(2)}, u32[]{:S(2)}) collective-permute-start(bf16[4,1,128,768]{3,2,0,1:T(8,128)(2,1)S(1)} %bitcast.58), channel_id=1, source_target_pairs={{0,2},{1,3},{2,0},{3,1},{4,6},{5,7},{6,4},{7,5},{8,10},{9,11},{10,... | collective-permute-start | bytes 2359304 | tf_op jit(solution)/shard_map/ppermute | solution.py:994
  317.2 22.1 %collective-permute-start.39 = (bf16[4,128,768]{2,1,0:T(8,128)(2,1)}, bf16[4,128,768]{2,1,0:T(8,128)(2,1)S(1)}, u32[]{:S(2)}, u32[]{:S(2)}) collective-permute-start(bf16[4,128,768]{2,1,0:T(8,128)(2,1)} %get-tuple-element.362), channel_id=1, source_target_pairs={{0,16},{1,17},{2,18},{3,19},{4,20},{5,21},{6,22},{7,23},{8,24},{9,... | collective-permute-start | bytes 2359304 | tf_op jit(solution)/shard_map/ppermute | solution.py:994
  318.0 21.4 %collective-permute-start.40 = (bf16[4,128,768]{2,1,0:T(8,128)(2,1)}, bf16[4,128,768]{2,1,0:T(8,128)(2,1)S(1)}, u32[]{:S(2)}, u32[]{:S(2)}) collective-permute-start(bf16[4,128,768]{2,1,0:T(8,128)(2,1)} %get-tuple-element.364), channel_id=1, source_target_pairs={{0,8},{1,9},{2,10},{3,11},{4,12},{5,13},{6,14},{7,15},{8,0},{9,1},... | collective-permute-start | bytes 2359304 | tf_op jit(solution)/shard_map/ppermute | solution.py:994
  336.9 28.2 %collective-permute-start.48 = (bf16[768,768]{1,0:T(8,128)(2,1)}, bf16[768,768]{1,0:T(8,128)(2,1)}, u32[]{:S(2)}, u32[]{:S(2)}) collective-permute-start(bf16[768,768]{1,0:T(8,128)(2,1)} %get-tuple-element.403), channel_id=1, source_target_pairs={{0,16},{8,24},{16,0},{24,8},{1,17},{9,25},{17,1},{25,9},{2,18},{10... | collective-permute-start | bytes 3538952 | tf_op jit(solution)/shard_map/ppermute | solution.py:994
  338.1 27.9 %collective-permute-start.49 = (bf16[768,768]{1,0:T(8,128)(2,1)}, bf16[768,768]{1,0:T(8,128)(2,1)}, u32[]{:S(2)}, u32[]{:S(2)}) collective-permute-start(bf16[768,768]{1,0:T(8,128)(2,1)} %get-tuple-element.405), channel_id=1, source_target_pairs={{0,8},{8,0},{16,24},{24,16},{1,9},{9,1},{17,25},{25,17},{2,10},{10... | collective-permute-start | bytes 3538952 | tf_op jit(solution)/shard_map/ppermute | solution.py:994
  (96 other events, 911.3 us)

commit v7 on v6

--- a/solution.py
+++ b/solution.py
@@ -209,15 +209,15 @@
         target = outs[i].at[c * rows : (c + 1) * rows]
         return pltpu.make_async_copy(slots.at[c % 4, i], target, sems.at[c % 4, i])
 
-    for c in range(chunks):
-        for i in range(3):
-            arriving(c, i).start()
     count, own = sources[3].shape[0], sources[4].shape[0]
     dense_copies = [pltpu.make_async_copy(sources[3], buf.at[0:count], dense_in.at[0])]
     for i in (1, 2):
         dense_copies.append(pltpu.make_async_copy(sources[3 + i], dense_slots.at[i], dense_in.at[i]))
     for copy in dense_copies:
         copy.start()
+    for c in range(chunks):
+        for i in range(3):
+            arriving(c, i).start()
 
     summed = head_ref.shape[0]
     squares = total_ref[summed : summed + 1]
@@ -232,6 +232,24 @@
             at = router_rows + which * tiles + j
             gains_ref[which : which + 1, LANES * j : LANES * (j + 1)] = total_ref[at : at + 1]
 
+    for copy in dense_copies:
+        copy.wait()
+    last = k_ref[0] == devices - 1
+
+    @pl.when(last)
+    def _():
+        buf[count : count + summed] = total_ref[0:summed]
+
+    @pl.when(jnp.logical_not(last))
+    def _():
+        buf[count : count + summed] = head_ref[...]
+
+    grad = buf[pl.ds(step * k_ref[0], own), :]
+    values = adam_values(clip, grad, dense_m[...], dense_v[...])
+    for i, value in enumerate((grad, *values)):
+        dense_slots[i] = value
+    targets = (dense_outs[3], *dense_outs[:3])
+    copies = start_all([dense_slots.at[i] for i in range(4)], targets, dense_sems)
     for c in range(chunks):
         at = slice(c * rows, (c + 1) * rows)
         for i in range(3):
@@ -242,24 +260,6 @@
         for i, value in enumerate(values):
             slots[c % 4, i] = value
             leaving(c, i).start()
-    for copy in dense_copies:
-        copy.wait()
-    last = k_ref[0] == devices - 1
-
-    @pl.when(last)
-    def _():
-        buf[count : count + summed] = total_ref[0:summed]
-
-    @pl.when(jnp.logical_not(last))
-    def _():
-        buf[count : count + summed] = head_ref[...]
-
-    grad = buf[pl.ds(step * k_ref[0], own), :]
-    values = adam_values(clip, grad, dense_m[...], dense_v[...])
-    for i, value in enumerate((grad, *values)):
-        dense_slots[i] = value
-    targets = (dense_outs[3], *dense_outs[:3])
-    copies = start_all([dense_slots.at[i] for i in range(4)], targets, dense_sems)
     for c in range(max(0, chunks - 4), chunks):
         for i in range(3):
             leaving(c, i).wait()
@@ -467,15 +467,17 @@
     wait_chunks(dw, low_ref[0], keep_ref, sems)
 
 
-def mlp_fwd(stream_ref, gain, w1_ref, w2_ref, out_ref, b_ref, u_ref):
+def mlp_fwd(stream_ref, gain, w1_ref, w2_ref, out_ref, b_ref, u_ref, cdf_ref):
     width = stream_ref.shape[1]
     normed, _ = norm_rows(stream_ref[...])
     b_ref[...] = (normed * gain).astype(bf16)
     total = None
     for q in range(4):
         pre = dot(b_ref[...], quarter_in(w1_ref, q))
+        cdf = normal_cdf(pre)
         u_ref[:, q * width : (q + 1) * width] = pre
-        part = dot((pre * normal_cdf(pre)).astype(bf16), matrix(w2_ref, q))
+        cdf_ref[:, q * width : (q + 1) * width] = cdf
+        part = dot((pre * cdf).astype(bf16), matrix(w2_ref, q))
         total = part if total is None else total + part
     out_ref[...] = stream_ref[...] + total
 
@@ -485,9 +487,9 @@
     arrays, refs = refs[:count], refs[count:]
     if not by_core:
         w1_ref, refs = refs[0], refs[1:]
-    outs, refs = refs[:15], refs[15:]
+    outs, refs = refs[:16], refs[16:]
     gains_ref, wr_ref, c_ref, probs_ref, x_ref = refs[:5]
-    held, (weights, tails, w_sems, tail_sems, out_sems) = refs[5:20], refs[20:]
+    held, (weights, tails, w_sems, tail_sems, out_sems) = refs[5:21], refs[21:]
     low, top = place_ref[0], place_ref[1]
     per = weights.shape[1]
     copies = {
@@ -518,25 +520,25 @@
     leave(0, 6)
     for copy in copies[2] + copies[3]:
         copy.wait()
-    mlp_fwd(held[0], gains[1], weights.at[2] if by_core else w1_ref, weights.at[3], *held[6:9])
-    leave(6, 9)
+    mlp_fwd(held[0], gains[1], weights.at[2] if by_core else w1_ref, weights.at[3], *held[6:10])
+    leave(6, 10)
     for copy in copies[1]:
         copy.wait()
-    attn_fwd(seq, held[6], gains[2], weights.at[1], *held[9:15])
-    leave(9, 15)
+    attn_fwd(seq, held[6], gains[2], weights.at[1], *held[10:16])
+    leave(10, 16)
     wr_ref[...] = router_matrix(tail, stream_ref.shape[1], experts)
-    dispatch(held[9], gains[3], wr_ref, picks_ref, rows_ref, c_ref, probs_ref, x_ref)
+    dispatch(held[10], gains[3], wr_ref, picks_ref, rows_ref, c_ref, probs_ref, x_ref)
     for copy in leaving:
         copy.wait()
 
 
-def mlp_bwd(low, grad_ref, stream_ref, gain, w1_ref, w2_ref, b_ref, u_ref, out_ref, put_first, put_second):
+def mlp_bwd(grad_ref, stream_ref, gain, w1_ref, w2_ref, b_ref, u_ref, cdf_ref, out_ref, put_first, put_second):
     width = grad_ref.shape[1]
     upper = grad_ref[...].astype(bf16)
     back = None
     for q in range(4):
         pre = u_ref[:, q * width : (q + 1) * width]
-        cdf = normal_cdf(pre)
+        cdf = cdf_ref[:, q * width : (q + 1) * width]
         act = (pre * cdf).astype(bf16)
         put_second(q, dot_tn(act, upper).astype(bf16))
         dact = dot_nt(upper, matrix(w2_ref, q))
@@ -755,7 +757,7 @@
 def backward_kernel(
     seq, spots, count, by_core, place_ref, gains_ref, wr_ref, picks_ref, cols_ref, cot_ref, probs_ref, dx_ref, *refs
 ):
-    ins, refs = refs[:15], refs[15:]
+    ins, refs = refs[:16], refs[16:]
     arrays, refs = refs[:count], refs[count:]
     if not by_core:
         w1_ref, refs = refs[0], refs[1:]
@@ -770,7 +772,7 @@
         keep1_ref, send1 = keeps_ref.at[1], [(send1_ref, most), (send_rest.at[1], rest)]
     else:
         dw1_ref, *refs = refs
-    held, refs = refs[:15], refs[15:]
+    held, refs = refs[:16], refs[16:]
     grads, refs = refs[:4], refs[4:]
     dq_ref, dk_ref, dv_ref, do_ref, dw, dw2, w2_ref, w_attn, *refs = refs
     if by_core:
@@ -808,7 +810,7 @@
             small_ref[at + j : at + j + 1, :] = value[:, LANES * j : LANES * (j + 1)]
 
     put_gain(3, gain_four)
-    middle = fetch(8, 11) + fetch_layer(3, w2_ref, 1)
+    middle = fetch(8, 12) + fetch_layer(3, w2_ref, 1)
     if by_core:
         middle += fetch_layer(2, w1_ref, 2)
     wait_all(second)
@@ -818,9 +820,9 @@
     )
     put_gain(2, gain_three)
     attn_weights(low, grads[0], a, o, dq_ref, dk_ref, dv_ref, dw, keeps[0], sends[0], out_sems.at[0])
-    first = fetch(11, 15) + fetch_layer(0, w_attn.at[1], 3)
+    first = fetch(12, 16) + fetch_layer(0, w_attn.at[1], 3)
     wait_all(middle)
-    stream, b, u = held[8:11]
+    stream, b, u, cdf = held[8:12]
     width = stream.shape[1]
     groups = w1_ref.shape[0]
 
@@ -843,13 +845,13 @@
             leave_chunk(dw2, low, q * per + i, keeps[1], sends[1], out_sems.at[1, q * per + i])
 
     gain_two = mlp_bwd(
-        low, grads[1], stream, gains_ref[1:2], w1_ref, w2_ref, b, u, grads[2], put_first, put_second
+        grads[1], stream, gains_ref[1:2], w1_ref, w2_ref, b, u, cdf, grads[2], put_first, put_second
     )
     put_gain(1, gain_two)
     leaving = start_all((grads[2],), (upper_out,), last_sems)
     wait_all(first)
     wait_chunks(dw, low, keeps[0], out_sems.at[0])
-    stream, q, k, v = held[11:15]
+    stream, q, k, v = held[12:16]
     gain_one = attn_bwd(
         seq, grads[2], stream, gains_ref[0:1], w_attn.at[1], q, k, v, grads[3], dq_ref, dk_ref, dv_ref, do_ref
     )
@@ -890,9 +892,8 @@
 
 
 def pack_sets_kernel(*refs):
-    out_ref = refs[-1]
-    for i, ref in enumerate(refs[:-1]):
-        out_ref[i // 4, i % 4] = ref[...]
+    *parts, out_ref, sems = refs
+    wait_all(start_all(parts, [out_ref.at[i // 4, i % 4] for i in range(len(parts))], sems))
 
 
 def fold_layers_kernel(cut, plan, top_ref, *refs):
@@ -1177,21 +1178,22 @@
         halves = [swap(near[0][1][:split], both, masks[0]), swap(near[0][0][split:], both, masks[1])]
         near[1] = order.land(near[1])
         halves = order.land(halves)
+        far[0] = jnp.concatenate(halves)
         x_half, y_half, *quarters = expert_chunks
-        early = [swap(quarters[2], dp_axis, 1), swap(quarters[0], dp_axis, 2)]
-        early, outgoing_cot, stream = order.land((early, outgoing_cot, stream))
-        sets[2] = order.land(sets[2])
+        first, second = after((quarters[2], quarters[0]), halves)
+        early = [swap(first, dp_axis, 1), swap(second, dp_axis, 2)]
+        sets[2], outgoing_cot, stream = order.land((sets[2], outgoing_cot, stream))
         sets[3] = swap(sets[2], both, 2)
         near[2] = spread(sets[2])
-        far[0] = jnp.concatenate(halves)
-        sets[3], far[0] = order.land((sets[3], far[0]))
+        early = order.land(early)
+        place_arr, early = pause(place_arr, 100, early)
+        sets[3], far[0], place_arr = order.land((sets[3], far[0], place_arr))
         far[1], far[2] = swap(far[0], both, 2), swap(far[0], both, 4)
         near[3] = spread(sets[3])
         near[2] = order.land(near[2])
         near[3] = order.land(near[3])
         far[1] = order.land(far[1])
         far[2] = order.land(far[2])
-        place_arr, far[2] = pause(place_arr, 200, far[2])
         far[3] = swap(far[2], both, 2)
         arriving_cot = exchange(after(outgoing_cot, far[2]))
 
@@ -1199,23 +1201,25 @@
             ins = [part for s in which for part in (sets[s], *near[s], far[s])]
             return pl.pallas_call(
                 pack_sets_kernel,
-                in_specs=[VMEM] * len(ins),
+                in_specs=[pl.BlockSpec(memory_space=pl.ANY)] * len(ins),
                 out_specs=VMEM,
                 out_shape=shape((len(which), 4, chunk_rows, width), bf16),
+                scratch_shapes=[pltpu.SemaphoreType.DMA((len(ins),))],
                 compiler_params=params(),
                 cost_estimate=cost(),
                 name="pack_sets",
             )(*ins)
 
-        packed = [pack_sets([0, 1])]
-        far[3], packed = lax.optimization_barrier((far[3], packed))
-        far[3] = order.land(far[3])
-        packed.append(pack_sets([2, 3]))
-        arrays = packed + [swap(value, both, 1) for value in packed]
-        spots = [((j >> 2) + 2 * (j & 1), ((j >> 1) & 1,), ()) for j in range(per)]
         x_out, y_out = after((x_half, y_half), near[3])
         beside = [swap(x_out, dp_axis, 1), swap(y_out, dp_axis, 2)]
-        place_arr, beside = pause(place_arr, 3000, beside)
+        packed = [pack_sets([0, 1, 2])]
+        first_swap = swap(packed[0], both, 1)
+        far[3], beside = order.land(after((far[3], beside), packed))
+        packed.append(pack_sets([3]))
+        arrays = [*packed, first_swap, swap(packed[1], both, 1)]
+        at = ((0, 0), (0, 1), (0, 2), (1, 0))
+        spots = [(at[j >> 1][0] + 2 * (j & 1), (at[j >> 1][1],), ()) for j in range(per)]
+        place_arr, beside = pause(place_arr, 4400, beside)
         across = [swap(beside[0], dp_axis, 2), swap(beside[1], dp_axis, 1)]
         late = after((quarters[3], quarters[1]), beside)
         late = [swap(late[0], dp_axis, 1), swap(late[1], dp_axis, 2)]
@@ -1294,7 +1298,7 @@
             ],
         )
 
-    outs = [stream_shape] + [act_shape] * 5 + [stream_shape, act_shape, shape((padded, hidden), f32)]
+    outs = [stream_shape] + [act_shape] * 5 + [stream_shape, act_shape] + [shape((padded, hidden))] * 2
     outs += [stream_shape] + [act_shape] * 5
     *results, gains, router, moe_in, probs, outgoing = call(
         functools.partial(forward_kernel, seq, spots, (rows, experts, len(arrays)), wide_ok),
@@ -1310,19 +1314,19 @@
         ],
         "forward",
         0,
-        out_specs=[ANY] * 15 + [None] * 5,
+        out_specs=[ANY] * 16 + [None] * 5,
         scratch=[pltpu.VMEM(o.shape, o.dtype) for o in outs]
         + [
             pltpu.VMEM((4, per, rows, width), bf16),
             pltpu.VMEM((per, tail_rows, width), bf16),
             pltpu.SemaphoreType.DMA((4, per)),
             pltpu.SemaphoreType.DMA((per,)),
-            pltpu.SemaphoreType.DMA((15,)),
+            pltpu.SemaphoreType.DMA((16,)),
         ],
     )
     stream_one, kept_one = results[0], results[1:6]
-    stream_two, mlp_in, mlp_pre = results[6:9]
-    stream_three, kept_two = results[9], results[10:]
+    stream_two, mlp_in, mlp_pre, mlp_cdf = results[6:10]
+    stream_three, kept_two = results[10], results[11:]
     arriving = exchange(outgoing)
 
     slot_spec = pl.BlockSpec((slots, width), lambda q: (0, 0))
@@ -1401,10 +1405,10 @@
     expert_out = [expert_out[0]] + [swap(v, ("expert",), 2 * j) for j, v in enumerate(expert_out) if j]
     backward_ins = (
         (stream_three, moe_in, stream_two, *kept_two[1:4], kept_two[0], kept_two[4])
-        + (stream_one, mlp_in, mlp_pre, stream, *kept_one[1:4])
+        + (stream_one, mlp_in, mlp_pre, mlp_cdf, stream, *kept_one[1:4])
     )
     held_vmem = [stream_vmem, act_vmem, stream_vmem] + [act_vmem] * 5
-    held_vmem += [stream_vmem, act_vmem, pltpu.VMEM((padded, hidden), f32), stream_vmem] + [act_vmem] * 3
+    held_vmem += [stream_vmem, act_vmem] + [pltpu.VMEM((padded, hidden), f32)] * 2 + [stream_vmem] + [act_vmem] * 3
     kinds = 2 if wide_ok else 1
     most, rest = places * 3 // 4, places // 4
     keeps_shape = shape((kinds,) + core_shape.shape, bf16)
@@ -1414,7 +1418,7 @@
         functools.partial(backward_kernel, seq, spots, len(arrays), wide_ok),
         (place_arr, gains, router, picks, cols, cot, probs, returned_grad, *backward_ins, *arrays)
         + (() if wide_ok else (first_in,)),
-        (SMEM,) + (None,) * 7 + (ANY,) * (15 + len(arrays)) + (() if wide_ok else (None,)),
+        (SMEM,) + (None,) * 7 + (ANY,) * (16 + len(arrays)) + (() if wide_ok else (None,)),
         [shape((tail, LANES)), stream_shape, act_shape, act_shape, act_shape, stream_shape]
         + [core_shape, core_shape, keeps_shape, most_shape, rest_shape]
         + first_dw_out,
@@ -1427,7 +1431,7 @@
         + ([by_core, layer_w] if wide_ok else [])
         + [
             pltpu.VMEM((width, LANES), f32),
-            pltpu.SemaphoreType.DMA((15,)),
+            pltpu.SemaphoreType.DMA((16,)),
             pltpu.SemaphoreType.DMA((4, per)),
             pltpu.SemaphoreType.DMA((3, per)),
             pltpu.SemaphoreType.DMA((5,)),

time: 422 us -> 415 us (0.983)
    unnamed x115 -> x113, local copies, waits for them, and re-layouts: 17.1 us -> 15.3 us
where the time goes in v7:
time: 415 us; the launch traced here: 409 us
  Pallas kernels  157 us (38%)
  waiting for transfers between devices  154 us (37%)
  starting transfers between devices  70.1 us (17%)
  local copies, waits for them, and re-layouts  22.4 us (5%)
  other arithmetic  4.69 us (1%)
    ppermute x59, waiting for transfers between devices, swap(): return lax.ppermute(value, axes, [(i, i ^ mask) for i in range(size)])  133 us
    pallas_call x11, Pallas kernels, call(): pl.pallas_call(kernel, grid=(1,), in_specs=[s or whole(a) for a, s in zip...  75 us
    ppermute x59, starting transfers between devices, swap(): return lax.ppermute(value, axes, [(i, i ^ mask) for i in range(size)])  57.1 us
    pallas_call x1, Pallas kernels, on_device(): pl.pallas_call(functools.partial(expert_kernel, (dp_ranks, quarter, exper...  16.7 us
    pallas_call x1, Pallas kernels, on_device(): pl.pallas_call(functools.partial(adam_kernel, (step, chunks, devices, par...  16.1 us
    unnamed x113, local copies, waits for them, and re-layouts  15.3 us
    all_to_all x3, waiting for transfers between devices, exchange(): lax.all_to_all(value, 'expert', split_axis=0, concat_axis=0, tiled=True)  13.3 us
    all_to_all x3, starting transfers between devices, exchange(): lax.all_to_all(value, 'expert', split_axis=0, concat_axis=0, tiled=True)  11.3 us
  transfers between devices with their start and end apart: 64, of which 34 were waited for; matrix products, arithmetic and copies ran while one was open for 3% of the time, Pallas kernels for 27%

profile of v7, /device:TPU:0, one launch (start us, length us, event | category | flops | bytes accessed | tf_op | source)
XLA Modules:
  0.0 409.2 jit_solution(2563655061480140503)
XLA Ops:
  1.9 7.7 %collective-permute-done.tail_ref = f32[96,128]{1,0:T(8,128)S(1)} collective-permute-done((f32[96,128]{1,0:T(8,128)S(1)}, f32[96,128]{1,0:T(8,128)S(1)}, u32[]{:S(2)}, u32[]{:S(2)}) %collective-permute-start) | collective-permute-done | bytes 49184 | tf_op jit(solution)/shard_map/ppermute | solution.py:1091
  15.1 9.6 %collective-permute-done.2.refs_1_ = bf16[400,768]{1,0:T(8,128)(2,1)S(1)} collective-permute-done((bf16[400,768]{1,0:T(8,128)(2,1)}, bf16[400,768]{1,0:T(8,128)(2,1)S(1)}, u32[]{:S(2)}, u32[]{:S(2)}) %collective-permute-start.2) | collective-permute-done | bytes 614432 | tf_op jit(solution)/shard_map/ppermute | solution.py:995
  34.6 5.8 %pack_expert.1 = (bf16[768,768]{1,0:T(8,128)(2,1)}, bf16[768,768]{1,0:T(8,128)(2,1)}, bf16[384,768]{1,0:T(8,128)(2,1)}, bf16[384,768]{1,0:T(8,128)(2,1)}, bf16[3...) custom-call(s32[1]{0:T(128)} %bitcast.11.wide_ref, f32[9216,128]{1,0:T(8,128)} %bitcast.46), custom_call_target="tpu_custom_call" | custom-call | flops 1 | bytes 1 | tf_op jit(solution)/shard_map/pack_expert/pallas_call | solution.py:1110
  63.8 7.0 %collective-permute-done.9.refs_0_ = bf16[400,768]{1,0:T(8,128)(2,1)S(1)} collective-permute-done((bf16[400,768]{1,0:T(8,128)(2,1)}, bf16[400,768]{1,0:T(8,128)(2,1)S(1)}, u32[]{:S(2)}, u32[]{:S(2)}) %collective-permute-start.9) | collective-permute-done | bytes 614432 | tf_op jit(solution)/shard_map/ppermute | solution.py:995
  77.7 7.0 %collective-permute-done.14.refs_1_ = bf16[400,768]{1,0:T(8,128)(2,1)S(1)} collective-permute-done((bf16[400,768]{1,0:T(8,128)(2,1)S(1)}, bf16[400,768]{1,0:T(8,128)(2,1)S(1)}, u32[]{:S(2)}, u32[]{:S(2)}) %collective-permute-start.14) | collective-permute-done | bytes 614432 | tf_op jit(solution)/shard_map/ppermute | solution.py:995
  89.0 9.5 %collective-permute-done.13.refs_7_ = bf16[400,768]{1,0:T(8,128)(2,1)S(1)} collective-permute-done((bf16[400,768]{1,0:T(8,128)(2,1)S(1)}, bf16[400,768]{1,0:T(8,128)(2,1)S(1)}, u32[]{:S(2)}, u32[]{:S(2)}) %collective-permute-start.13) | collective-permute-done | bytes 614432 | tf_op jit(solution)/shard_map/ppermute | solution.py:995
  103.0 6.2 %pack_sets.2.refs_0_.refs_16_ = bf16[3,4,400,768]{3,2,1,0:T(8,128)(2,1)} custom-call(bf16[400,768]{1,0:T(8,128)(2,1)} %pack_dense.1.refs_0_, bf16[400,768]{1,0:T(8,128)(2,1)} %copy-done.20, bf16[400,768]{1,0:T(8,128)(2,1)} %copy-done.19, bf16[400,768]{1,0:T(8,128)(2,1)} %copy-done.13, bf16[400,768]{1,0:T(8,128)(2,1)} %copy-done.26, ...), custom_call_target="tpu_custom_call" | custom-call | flops 1 | bytes 1 | tf_op jit(solution)/shard_map/pack_sets/pallas_call | solution.py:1202
  126.4 16.0 %forward.1 = (f32[208,768]{1,0:T(8,128)}, bf16[208,768]{1,0:T(8,128)(2,1)}, bf16[208,768]{1,0:T(8,128)(2,1)}, bf16[208,768]{1,0:T(8,128)(2,1)}, bf16[208,768]{1,...) custom-call(s32[2]{0:T(128)} %pause.7.place_ref, ...), custom_call_target="tpu_custom_call" | custom-call | flops 1 | bytes 1 | tf_op jit(solution)/shard_map/forward/pallas_call | solution.py:1265
  150.8 12.1 %collective-permute-done.25.refs_4_ = bf16[384,768]{1,0:T(8,128)(2,1)S(1)} collective-permute-done((bf16[384,768]{1,0:T(8,128)(2,1)}, bf16[384,768]{1,0:T(8,128)(2,1)S(1)}, u32[]{:S(2)}, u32[]{:S(2)}) %collective-permute-start.25) | collective-permute-done | bytes 589856 | tf_op jit(solution)/shard_map/ppermute | solution.py:995
  168.6 16.7 %expert.1 = (bf16[2,56,768]{2,1,0:T(8,128)(2,1)}, bf16[2,56,768]{2,1,0:T(8,128)(2,1)}, bf16[2,56,768]{2,1,0:T(8,128)(2,1)}, bf16[2,56,768]{2,1,0:T(8,128)(2,1)},...) custom-call(s32[2]{0:T(128)} %pause.8.me_ref, ...), custom_call_target="tpu_custom_call" | custom-call | flops 1 | bytes 1 | tf_op jit(solution)/shard_map/expert/pallas_call | solution.py:1337
  188.9 9.3 %expert_grad.1 = (bf16[2,768,768]{2,1,0:T(8,128)(2,1)}, bf16[2,768,768]{2,1,0:T(8,128)(2,1)}, bf16[2,768,768]{2,1,0:T(8,128)(2,1)}, bf16[2,768,768]{2,1,0:T(8,128)(2,1)}) custom-call(s32[1]{0:T(128)} %bitcast.1.dp_ref, bf16[448,896]{1,0:T(8,128)(2,1)} %bitcast.45, bf16[448,768]{1,0:T(8,128)(2,1)} %get-tuple-element.288.dy_ref, ...), custom_call_target="tpu_custom_call" | custom-call | flops 1 | bytes 1 | tf_op jit(solution)/shard_map/expert_grad/pallas_call | solution.py:1359
  200.9 9.2 %all-to-all-done.2 = bf16[8,56,896]{2,1,0:T(8,128)(2,1)S(1)} async-done(((bf16[8,56,896]{2,1,0:T(8,128)(2,1)}), bf16[8,56,896]{2,1,0:T(8,128)(2,1)S(1)}, u32[]{:S(2)}, u32[]{:S(2)}) %all-to-all-start.2) | async-done | bytes 802848 | tf_op jit(solution)/shard_map/all_to_all | solution.py:1150
  214.5 27.8 %backward.1 = (f32[96,128]{1,0:T(8,128)}, f32[208,768]{1,0:T(8,128)}, bf16[208,768]{1,0:T(8,128)(2,1)}, bf16[208,768]{1,0:T(8,128)(2,1)}, bf16[208,768]{1,0:T(8,...) custom-call(s32[2]{0:T(128)} %pause.7.place_ref, ...), custom_call_target="tpu_custom_call" | custom-call | flops 1 | bytes 1 | tf_op jit(solution)/shard_map/backward/pallas_call | solution.py:1265
  250.7 6.0 %fold_layers.2 = (bf16[4,1,128,768]{3,2,1,0:T(8,128)(2,1)}, bf16[4,1,128,768]{3,2,1,0:T(8,128)(2,1)}, bf16[4,1,128,768]{3,2,1,0:T(8,128)(2,1)}, bf16[4,1,128,768...) custom-call(s32[1]{0:T(128)} %bitcast.top_ref.ref, ...), custom_call_target="tpu_custom_call" | custom-call | flops 1 | bytes 1 | tf_op jit(solution)/shard_map/fold_layers/pallas_call | solution.py:1265
  259.5 6.9 %fold_layers.3 = (bf16[4,1,128,768]{3,2,1,0:T(8,128)(2,1)}, bf16[4,1,128,768]{3,2,1,0:T(8,128)(2,1)}, bf16[4,1,128,768]{3,2,1,0:T(8,128)(2,1)}, bf16[4,1,128,768...) custom-call(s32[1]{0:T(128)} %pause.9.top_ref, ...), custom_call_target="tpu_custom_call", output_to_operand_aliasing={{0}: (5, {}), {1}: (6, {}), {2}: (7, {}), {3}: (8, {}), {4}... | custom-call | flops 1 | bytes 1 | tf_op jit(solution)/shard_map/fold_layers/pallas_call | solution.py:1265
  268.9 19.2 %collective-permute-done.45.right = bf16[4,1,128,768]{3,2,1,0:T(8,128)(2,1)S(1)} collective-permute-done((bf16[4,1,128,768]{3,2,1,0:T(8,128)(2,1)}, bf16[4,1,128,768]{3,2,1,0:T(8,128)(2,1)S(1)}, u32[]{:S(2)}, u32[]{:S(2)}) %collective-permute-start.45) | collective-permute-done | bytes 786464 | tf_op jit(solution)/shard_map/ppermute | solution.py:995
  291.3 6.2 %fold_expert.1 = (bf16[768,768]{1,0:T(8,128)(2,1)}, bf16[768,768]{1,0:T(8,128)(2,1)}, bf16[768,768]{1,0:T(8,128)(2,1)}, bf16[768,768]{1,0:T(8,128)(2,1)}) custom-call(bf16[2,768,768]{2,1,0:T(8,128)(2,1)} %get-tuple-element.298.refs_0_, bf16[2,768,768]{2,1,0:T(8,128)(2,1)} %copy-done.15, bf16[2,768,768]{2,1,0:T(8,128)(2,1)} %get-tuple-element.299.refs_2_, ...), custom_call_target="tpu_custom_call" | custom-call | flops 1 | bytes 1 | tf_op jit(solution)/shard_map/fold_expert/pallas_call | solution.py:1265
  297.5 5.6 %collective-permute-done.37.got_x = bf16[2,4,128,768]{3,2,1,0:T(8,128)(2,1)S(1)} collective-permute-done((bf16[2,4,128,768]{3,2,1,0:T(8,128)(2,1)}, bf16[2,4,128,768]{3,2,1,0:T(8,128)(2,1)S(1)}, u32[]{:S(2)}, u32[]{:S(2)}) %collective-permute-start.37) | collective-permute-done | bytes 1572896 | tf_op jit(solution)/shard_map/ppermute | solution.py:995
  304.8 4.9 %fold_plane.1 = (bf16[4,128,768]{2,1,0:T(8,128)(2,1)}, bf16[4,128,768]{2,1,0:T(8,128)(2,1)}, bf16[4,128,768]{2,1,0:T(8,128)(2,1)}, bf16[4,128,768]{2,1,0:T(8,128)(2,1)}) custom-call(bf16[2,4,128,768]{3,2,1,0:T(8,128)(2,1)} %get-tuple-element.365.keep_x, bf16[2,4,128,768]{3,2,1,0:T(8,128)(2,1)} %copy-done.17, ...), custom_call_target="tpu_custom_call" | custom-call | flops 1 | bytes 1 | tf_op jit(solution)/shard_map/fold_plane/pallas_call | solution.py:1513
  312.1 13.2 %collective-permute-done.47 = bf16[4,1,128,768]{3,2,0,1:T(8,128)(2,1)S(1)} collective-permute-done((bf16[4,1,128,768]{3,2,0,1:T(8,128)(2,1)S(1)}, bf16[4,1,128,768]{3,2,0,1:T(8,128)(2,1)S(1)}, u32[]{:S(2)}, u32[]{:S(2)}) %collective-permute-start.47) | collective-permute-done | bytes 786464 | tf_op jit(solution)/shard_map/ppermute | solution.py:995
  338.1 10.0 %collective-permute-done.42.right = bf16[1,256,768]{2,1,0:T(8,128)(2,1)S(1)} collective-permute-done((bf16[1,256,768]{2,1,0:T(8,128)(2,1)}, bf16[1,256,768]{2,1,0:T(8,128)(2,1)S(1)}, u32[]{:S(2)}, u32[]{:S(2)}) %collective-permute-start.42) | collective-permute-done | bytes 393248 | tf_op jit(solution)/shard_map/ppermute | solution.py:995
  350.2 8.1 %collective-permute-done.48.refs_1_ = bf16[768,768]{1,0:T(8,128)(2,1)} collective-permute-done((bf16[768,768]{1,0:T(8,128)(2,1)}, bf16[768,768]{1,0:T(8,128)(2,1)}, u32[]{:S(2)}, u32[]{:S(2)}) %collective-permute-start.48) | collective-permute-done | bytes 1179680 | tf_op jit(solution)/shard_map/ppermute | solution.py:995
  361.9 6.1 %unpack_expert.1 = (f32[9216,128]{1,0:T(8,128)}, f32[1,128]{1,0:T(1,128)}) custom-call(s32[1]{0:T(128)} %bitcast.11.wide_ref, bf16[768,768]{1,0:T(8,128)(2,1)} %get-tuple-element.422.refs_0_, bf16[768,768]{1,0:T(8,128)(2,1)} %collective-permute-done.48.refs_1_, bf16[768,768]{1,0:T(8,128)(2,1)} %get-tuple-element.424.refs_2_, ...), custom_call_target="tpu_custom_call" | custom-call | flops 1 | bytes 1 | tf_op jit(solution)/shard_map/unpack_expert/pallas_call | solution.py:1567
  392.8 16.1 %adam.1 = (f32[9216,128]{1,0:T(8,128)}, f32[9216,128]{1,0:T(8,128)}, f32[9216,128]{1,0:T(8,128)}, f32[2307,128]{1,0:T(8,128)}, f32[2307,128]{1,0:T(8,128)}, /*in...) custom-call(s32[1]{0:T(128)} %bitcast.2.k_ref, f32[104,128]{1,0:T(8,128)} %add.41.total_ref, ...), custom_call_target="tpu_custom_call" | custom-call | flops 1 | bytes 1 | tf_op jit(solution)/shard_map/adam/pallas_call | solution.py:1606
  (266 shorter events, 161.1 us)
Async XLA Ops:
  29.0 28.0 %collective-permute-start.4 = (bf16[400,768]{1,0:T(8,128)(2,1)}, bf16[400,768]{1,0:T(8,128)(2,1)}, u32[]{:S(2)}, u32[]{:S(2)}) collective-permute-start(bf16[400,768]{1,0:T(8,128)(2,1)} %pack_dense.1.refs_0_), channel_id=1, source_target_pairs={{0,4},{1,5},{2,6},{3,7},{4,0},{5,1},{6,2},{7,3},{8,12},{9,13},{10,... | collective-permute-start | bytes 1843208 | tf_op jit(solution)/shard_map/ppermute | solution.py:995
  74.4 24.1 %collective-permute-start.13 = (bf16[400,768]{1,0:T(8,128)(2,1)S(1)}, bf16[400,768]{1,0:T(8,128)(2,1)S(1)}, u32[]{:S(2)}, u32[]{:S(2)}) collective-permute-start(bf16[400,768]{1,0:T(8,128)(2,1)S(1)} %pad_maximum_fusion.refs_3_), channel_id=1, source_target_pairs={{0,2},{1,3},{2,0},{3,1},{4,6},{5,7},{6,4},{7,5},{8,10},{9,11},{10,... | collective-permute-start | bytes 1843208 | tf_op jit(solution)/shard_map/ppermute | solution.py:995
  74.7 27.5 %collective-permute-start.12 = (bf16[400,768]{1,0:T(8,128)(2,1)S(1)}, bf16[400,768]{1,0:T(8,128)(2,1)S(1)}, u32[]{:S(2)}, u32[]{:S(2)}) collective-permute-start(bf16[400,768]{1,0:T(8,128)(2,1)S(1)} %pad_maximum_fusion.refs_3_), channel_id=1, source_target_pairs={{0,4},{1,5},{2,6},{3,7},{4,0},{5,1},{6,2},{7,3},{8,12},{9,13},{10,... | collective-permute-start | bytes 1843208 | tf_op jit(solution)/shard_map/ppermute | solution.py:995
  86.4 28.9 %collective-permute-start.19 = (bf16[768,768]{1,0:T(8,128)(2,1)S(1)}, bf16[768,768]{1,0:T(8,128)(2,1)}, u32[]{:S(2)}, u32[]{:S(2)}) collective-permute-start(bf16[768,768]{1,0:T(8,128)(2,1)S(1)} %copy-done.21), channel_id=1, source_target_pairs={{0,8},{8,0},{16,24},{24,16},{1,9},{9,1},{17,25},{25,17},{2,10},{10... | collective-permute-start | bytes 3538952 | tf_op jit(solution)/shard_map/ppermute | solution.py:995
  87.2 28.1 %collective-permute-start.20 = (bf16[768,768]{1,0:T(8,128)(2,1)}, bf16[768,768]{1,0:T(8,128)(2,1)}, u32[]{:S(2)}, u32[]{:S(2)}) collective-permute-start(bf16[768,768]{1,0:T(8,128)(2,1)} %get-tuple-element.263.refs_1_), channel_id=1, source_target_pairs={{0,16},{8,24},{16,0},{24,8},{1,17},{9,25},{17,1},{25,9},{2,18},{10... | collective-permute-start | bytes 3538952 | tf_op jit(solution)/shard_map/ppermute | solution.py:995
  109.4 33.1 %all-to-all-start.1 = ((bf16[8,56,768]{2,1,0:T(8,128)(2,1)}), bf16[8,56,768]{2,1,0:T(8,128)(2,1)S(1)}, u32[]{:S(2)}, u32[]{:S(2)}) async-start(bf16[8,56,768]{2,1,0:T(8,128)(2,1)} %bitcast.15), calls=%async_computation.1 | async-start | bytes 1376256 | tf_op jit(solution)/shard_map/all_to_all | solution.py:1150
  115.4 34.2 %collective-permute-start.23 = (bf16[768,768]{1,0:T(8,128)(2,1)}, bf16[768,768]{1,0:T(8,128)(2,1)S(1)}, u32[]{:S(2)}, u32[]{:S(2)}) collective-permute-start(bf16[768,768]{1,0:T(8,128)(2,1)} %collective-permute-done.19.refs_2_), channel_id=1, source_target_pairs={{0,16},{8,24},{16,0},{24,8},{1,17},{9,25},{17,1},{25,9},{2,18},{10... | collective-permute-start | bytes 3538952 | tf_op jit(solution)/shard_map/ppermute | solution.py:995
  115.7 33.9 %collective-permute-start.24 = (bf16[768,768]{1,0:T(8,128)(2,1)}, bf16[768,768]{1,0:T(8,128)(2,1)}, u32[]{:S(2)}, u32[]{:S(2)}) collective-permute-start(bf16[768,768]{1,0:T(8,128)(2,1)} %collective-permute-done.20.refs_5_), channel_id=1, source_target_pairs={{0,8},{8,0},{16,24},{24,16},{1,9},{9,1},{17,25},{25,17},{2,10},{10... | collective-permute-start | bytes 3538952 | tf_op jit(solution)/shard_map/ppermute | solution.py:995
  142.5 25.2 %all-to-all-start = ((bf16[8,56,896]{2,1,0:T(8,128)(2,1)}), bf16[8,56,896]{2,1,0:T(8,128)(2,1)S(1)}, u32[]{:S(2)}, u32[]{:S(2)}) async-start(bf16[8,56,896]{2,1,0:T(8,128)(2,1)} %bitcast.55), calls=%async_computation | async-start | bytes 1605632 | tf_op jit(solution)/shard_map/all_to_all | solution.py:1150
  185.3 24.8 %all-to-all-start.2 = ((bf16[8,56,896]{2,1,0:T(8,128)(2,1)}), bf16[8,56,896]{2,1,0:T(8,128)(2,1)S(1)}, u32[]{:S(2)}, u32[]{:S(2)}) async-start(bf16[8,56,896]{2,1,0:T(8,128)(2,1)} %bitcast.56), calls=%async_computation.2 | async-start | bytes 1605632 | tf_op jit(solution)/shard_map/all_to_all | solution.py:1150
  198.2 58.5 %collective-permute-start.27 = (bf16[2,768,768]{2,1,0:T(8,128)(2,1)}, bf16[2,768,768]{2,1,0:T(8,128)(2,1)S(1)}, u32[]{:S(2)}, u32[]{:S(2)}) collective-permute-start(bf16[2,768,768]{2,1,0:T(8,128)(2,1)} %get-tuple-element.291), channel_id=1, source_target_pairs={{0,8},{8,0},{16,24},{24,16},{1,9},{9,1},{17,25},{25,17},{2,10},{10... | collective-permute-start | bytes 7077896 | tf_op jit(solution)/shard_map/ppermute | solution.py:995
  199.2 57.5 %collective-permute-start.28 = (bf16[2,768,768]{2,1,0:T(8,128)(2,1)}, bf16[2,768,768]{2,1,0:T(8,128)(2,1)}, u32[]{:S(2)}, u32[]{:S(2)}) collective-permute-start(bf16[2,768,768]{2,1,0:T(8,128)(2,1)} %get-tuple-element.292), channel_id=1, source_target_pairs={{0,16},{8,24},{16,0},{24,8},{1,17},{9,25},{17,1},{25,9},{2,18},{10... | collective-permute-start | bytes 7077896 | tf_op jit(solution)/shard_map/ppermute | solution.py:995
  210.1 32.2 %collective-permute-start.29 = (bf16[2,56,768]{2,1,0:T(8,128)(2,1)}, bf16[2,56,768]{2,1,0:T(8,128)(2,1)S(1)}, u32[]{:S(2)}, u32[]{:S(2)}) collective-permute-start(bf16[2,56,768]{2,1,0:T(8,128)(2,1)} %get-tuple-element.328), channel_id=1, source_target_pairs={{0,2},{1,3},{2,0},{3,1},{4,6},{5,7},{6,4},{7,5},{8,10},{9,11},{10,... | collective-permute-start | bytes 516104 | tf_op jit(solution)/shard_map/ppermute | solution.py:995
  210.1 32.2 %collective-permute-start.30 = (bf16[2,56,768]{2,1,0:T(8,128)(2,1)S(1)}, bf16[2,56,768]{2,1,0:T(8,128)(2,1)S(1)}, u32[]{:S(2)}, u32[]{:S(2)}) collective-permute-start(bf16[2,56,768]{2,1,0:T(8,128)(2,1)S(1)} %copy-done.54), channel_id=1, source_target_pairs={{0,4},{1,5},{2,6},{3,7},{4,0},{5,1},{6,2},{7,3},{8,12},{9,13},{10,... | collective-permute-start | bytes 516104 | tf_op jit(solution)/shard_map/ppermute | solution.py:995
  211.9 30.4 %collective-permute-start.31 = (bf16[2,56,768]{2,1,0:T(8,128)(2,1)S(1)}, bf16[2,56,768]{2,1,0:T(8,128)(2,1)S(1)}, u32[]{:S(2)}, u32[]{:S(2)}) collective-permute-start(bf16[2,56,768]{2,1,0:T(8,128)(2,1)S(1)} %copy-done.53), channel_id=1, source_target_pairs={{0,6},{1,7},{2,4},{3,5},{4,2},{5,3},{6,0},{7,1},{8,14},{9,15},{10,... | collective-permute-start | bytes 516104 | tf_op jit(solution)/shard_map/ppermute | solution.py:995
  266.4 36.7 %collective-permute-start.37 = (bf16[2,4,128,768]{3,2,1,0:T(8,128)(2,1)}, bf16[2,4,128,768]{3,2,1,0:T(8,128)(2,1)S(1)}, u32[]{:S(2)}, u32[]{:S(2)}) collective-permute-start(bf16[2,4,128,768]{3,2,1,0:T(8,128)(2,1)} %get-tuple-element.366), channel_id=1, source_target_pairs={{0,8},{1,9},{2,10},{3,11},{4,12},{5,13},{6,14},{7,15},{8,0},{9,1},... | collective-permute-start | bytes 4718600 | tf_op jit(solution)/shard_map/ppermute | solution.py:995
  267.2 36.4 %collective-permute-start.38 = (bf16[2,4,128,768]{3,2,1,0:T(8,128)(2,1)}, bf16[2,4,128,768]{3,2,1,0:T(8,128)(2,1)S(1)}, u32[]{:S(2)}, u32[]{:S(2)}) collective-permute-start(bf16[2,4,128,768]{3,2,1,0:T(8,128)(2,1)} %get-tuple-element.367), channel_id=1, source_target_pairs={{0,16},{1,17},{2,18},{3,19},{4,20},{5,21},{6,22},{7,23},{8,24},{9,... | collective-permute-start | bytes 4718600 | tf_op jit(solution)/shard_map/ppermute | solution.py:995
  289.4 35.9 %collective-permute-start.47 = (bf16[4,1,128,768]{3,2,0,1:T(8,128)(2,1)S(1)}, bf16[4,1,128,768]{3,2,0,1:T(8,128)(2,1)S(1)}, u32[]{:S(2)}, u32[]{:S(2)}) collective-permute-start(bf16[4,1,128,768]{3,2,0,1:T(8,128)(2,1)S(1)} %bitcast.43), channel_id=1, source_target_pairs={{0,4},{1,5},{2,6},{3,7},{4,0},{5,1},{6,2},{7,3},{8,12},{9,13},{10,... | collective-permute-start | bytes 2359304 | tf_op jit(solution)/shard_map/ppermute | solution.py:995
  290.4 35.0 %collective-permute-start.46 = (bf16[4,1,128,768]{3,2,0,1:T(8,128)(2,1)S(1)}, bf16[4,1,128,768]{3,2,0,1:T(8,128)(2,1)S(1)}, u32[]{:S(2)}, u32[]{:S(2)}) collective-permute-start(bf16[4,1,128,768]{3,2,0,1:T(8,128)(2,1)S(1)} %bitcast.58), channel_id=1, source_target_pairs={{0,2},{1,3},{2,0},{3,1},{4,6},{5,7},{6,4},{7,5},{8,10},{9,11},{10,... | collective-permute-start | bytes 2359304 | tf_op jit(solution)/shard_map/ppermute | solution.py:995
  309.7 22.3 %collective-permute-start.39 = (bf16[4,128,768]{2,1,0:T(8,128)(2,1)}, bf16[4,128,768]{2,1,0:T(8,128)(2,1)S(1)}, u32[]{:S(2)}, u32[]{:S(2)}) collective-permute-start(bf16[4,128,768]{2,1,0:T(8,128)(2,1)} %get-tuple-element.378), channel_id=1, source_target_pairs={{0,16},{1,17},{2,18},{3,19},{4,20},{5,21},{6,22},{7,23},{8,24},{9,... | collective-permute-start | bytes 2359304 | tf_op jit(solution)/shard_map/ppermute | solution.py:995
  311.3 20.7 %collective-permute-start.40 = (bf16[4,128,768]{2,1,0:T(8,128)(2,1)}, bf16[4,128,768]{2,1,0:T(8,128)(2,1)S(1)}, u32[]{:S(2)}, u32[]{:S(2)}) collective-permute-start(bf16[4,128,768]{2,1,0:T(8,128)(2,1)} %get-tuple-element.380), channel_id=1, source_target_pairs={{0,8},{1,9},{2,10},{3,11},{4,12},{5,13},{6,14},{7,15},{8,0},{9,1},... | collective-permute-start | bytes 2359304 | tf_op jit(solution)/shard_map/ppermute | solution.py:995
  330.2 28.2 %collective-permute-start.48 = (bf16[768,768]{1,0:T(8,128)(2,1)}, bf16[768,768]{1,0:T(8,128)(2,1)}, u32[]{:S(2)}, u32[]{:S(2)}) collective-permute-start(bf16[768,768]{1,0:T(8,128)(2,1)} %get-tuple-element.419), channel_id=1, source_target_pairs={{0,16},{8,24},{16,0},{24,8},{1,17},{9,25},{17,1},{25,9},{2,18},{10... | collective-permute-start | bytes 3538952 | tf_op jit(solution)/shard_map/ppermute | solution.py:995
  330.5 27.9 %collective-permute-start.49 = (bf16[768,768]{1,0:T(8,128)(2,1)}, bf16[768,768]{1,0:T(8,128)(2,1)}, u32[]{:S(2)}, u32[]{:S(2)}) collective-permute-start(bf16[768,768]{1,0:T(8,128)(2,1)} %get-tuple-element.421), channel_id=1, source_target_pairs={{0,8},{8,0},{16,24},{24,16},{1,9},{9,1},{17,25},{25,17},{2,10},{10... | collective-permute-start | bytes 3538952 | tf_op jit(solution)/shard_map/ppermute | solution.py:995
  348.2 20.1 %collective-permute-start.44 = (bf16[1,256,768]{2,1,0:T(8,128)(2,1)S(1)}, bf16[1,256,768]{2,1,0:T(8,128)(2,1)S(1)}, u32[]{:S(2)}, u32[]{:S(2)}) collective-permute-start(bf16[1,256,768]{2,1,0:T(8,128)(2,1)S(1)} %add.52), channel_id=1, source_target_pairs={{0,4},{1,5},{2,6},{3,7},{4,0},{5,1},{6,2},{7,3},{8,12},{9,13},{10,... | collective-permute-start | bytes 1179656 | tf_op jit(solution)/shard_map/ppermute | solution.py:995
  (95 other events, 952.9 us)

commit v8 on v7

--- a/solution.py
+++ b/solution.py
@@ -897,10 +897,11 @@
 
 
 def fold_layers_kernel(cut, plan, top_ref, *refs):
-    uppers, (send_x, keep_x, send_y, keep_y), scratch = refs[-14:-10], refs[-10:-6], refs[-6:]
+    uppers, (keep_x, send_y, keep_y, send_x), scratch = refs[-14:-10], refs[-10:-6], refs[-6:]
     kept, got, total, keep_sems, got_sems, out_sems = scratch
     count = kept.shape[1]
-    middle = send_x.shape[2]
+    x_part = slice(cut, cut + send_x.shape[1])
+    y_part = slice(x_part.stop, x_part.stop + send_y.shape[2])
     ins = []
     for layer, at, sources in plan:
         keep_ref, refs = refs[0], refs[1:]
@@ -930,21 +931,21 @@
             copy.wait()
         total[n, i] = add_pair(kept[n, i], got[n, i])
         pltpu.make_async_copy(total.at[n, i, 0:cut], uppers[i % 4].at[layer, i // 4], out_sems.at[n, 0, i]).start()
-        for bit, send, keep, at, where, sem in (
-            (place & 1, send_x, keep_x, place >> 1, slice(cut, cut + middle), out_sems.at[n, 1, i]),
-            (place >> 1, send_y, keep_y, place & 1, slice(cut + middle, cut + 2 * middle), out_sems.at[n, 2, i]),
+        for bit, send, keep, where, sem in (
+            (place & 1, send_x.at[i], keep_x.at[place >> 1, i], x_part, out_sems.at[n, 1, i]),
+            (place >> 1, send_y.at[place & 1, i], keep_y.at[place & 1, i], y_part, out_sems.at[n, 2, i]),
         ):
             for value, target in ((0, keep), (1, send)):
 
                 @pl.when(bit == value)
                 def _():
-                    pltpu.make_async_copy(total.at[n, i, where], target.at[at, i], sem).start()
+                    pltpu.make_async_copy(total.at[n, i, where], target, sem).start()
 
     for n, i in steps:
         layer = ins[n][0]
         pltpu.make_async_copy(total.at[n, i, 0:cut], uppers[i % 4].at[layer, i // 4], out_sems.at[n, 0, i]).wait()
-        for part in (1, 2):
-            pltpu.make_async_copy(total.at[n, i, cut : cut + middle], keep_x.at[0, i], out_sems.at[n, part, i]).wait()
+        pltpu.make_async_copy(total.at[n, i, x_part], keep_x.at[0, i], out_sems.at[n, 1, i]).wait()
+        pltpu.make_async_copy(total.at[n, i, y_part], keep_y.at[0, i], out_sems.at[n, 2, i]).wait()
 
 
 def add_kernel(left, right, out_ref):
@@ -956,10 +957,17 @@
         out_ref[i] = ref[i]
 
 
-def fold_plane_kernel(keep_x, got_x, keep_y, got_y, own_a, send_y, own_b, send_x):
-    for keep, got, own, send in ((keep_x, got_x, own_a, send_y), (keep_y, got_y, own_b, send_x)):
-        own[...] = add_pair(keep[0], got[0])
-        send[...] = add_pair(keep[1], got[1])
+def fold_plane_kernel(top_ref, keep_x, got_one, got_two, keep_y, got_y, own_a, send_y, own_b, send_x):
+    for place in range(2):
+
+        @pl.when(top_ref[0] >> 1 == place)
+        def _():
+            near, far = (got_two, got_one) if place == 0 else (got_one, got_two)
+            own_a[...] = add_pair(keep_x[0], near[...])
+            send_y[...] = add_pair(keep_x[1], far[...])
+
+    own_b[...] = add_pair(keep_y[0], got_y[0])
+    send_x[...] = add_pair(keep_y[1], got_y[1])
 
 
 def fold_rows_kernel(own_a, got_a, own_b, got_b, *outs):
@@ -1023,7 +1031,8 @@
 
 
 def bit_groups(bits):
-    return [bits[i : i + 2] for i in range(0, len(bits), 2)]
+    odd = len(bits) % 2
+    return [bits[:odd]] * odd + [bits[i : i + 2] for i in range(odd, len(bits), 2)]
 
 
 def all_sum_step(value, axes, bits):
@@ -1373,21 +1382,21 @@
     returned_grad = after(returned_grad, expert_first)
 
     cut = max(16, rows // 48 * 16)
-    middle = (rows - cut) // 2
+    x_rows = max(16, (rows - cut) * 9 // 256 * 16)
+    y_rows = rows - cut - x_rows
     top = (me >> per_bits).reshape(1)
     z_bits = list(range(1, per_bits))
     z_masks = [2 * j for j in (1, 2, 3)]
     assert places % 4 == 0
 
-    def add_call(left, right):
-        return call(add_kernel, (left, right), (None, None), [shape(left.shape, bf16)], "add", mib=12)[0]
-
-    def over_z(values, meanwhile=None):
+    def add_call(left, right, weight):
+        return call(add_kernel, (left, right), (None, None), [shape(left.shape, bf16)], "add", weight, mib=12)[0]
+
+    def over_z(values, meanwhile, weight=0):
         farthest = swap(values[3], both, 2)
-        if meanwhile is not None:
-            farthest, *meanwhile[:] = lax.optimization_barrier((farthest, *meanwhile))
+        farthest, *meanwhile[:] = lax.optimization_barrier((farthest, *meanwhile))
         near = swap(after(values[1], farthest), both, 2)
-        return [values[0], near, swap(add_call(values[2], farthest), both, 4)]
+        return [values[0], near, swap(add_call(values[2], farthest, weight), both, 4)]
 
     def rest_of_z(values):
         if len(z_bits) == 2:
@@ -1453,12 +1462,13 @@
         layer_got[layer] = [(most_got[i], None, most), (rest_got, i, rest)]
     layer_keep = {3: (dws[2], 0), 2: (dws[2], 1), 1: (dws[0], None), 0: (first_dw[0], None)}
 
-    plane_shape = shape((2, places, middle, width), bf16)
-    plane_spec = pl.BlockSpec((2, 1, middle, width), lambda i: (0, i, 0, 0))
-    line_shape = shape((places, middle, width), bf16)
-    line_spec = pl.BlockSpec((1, middle, width), lambda i: (i, 0, 0))
+    x_plane, y_plane = (shape((2, places, part, width), bf16) for part in (x_rows, y_rows))
+    x_line, y_line = (shape((places, part, width), bf16) for part in (x_rows, y_rows))
+    plane_specs = [pl.BlockSpec((2, 1, part, width), lambda i: (0, i, 0, 0)) for part in (x_rows, y_rows)]
+    line_specs = [pl.BlockSpec((1, part, width), lambda i: (i, 0, 0)) for part in (x_rows, y_rows)]
     upper_shape = shape((4, places // 4, cut, width), bf16)
-    sums = ()
+    sums, got_x = (), []
+    masks = [1 << bit for bit in top_bits]
     for pair in ((3, 2), (1, 0)):
         if pair[0] == 1:
             expert_got, sums = lax.optimization_barrier((expert_got, sums))
@@ -1469,11 +1479,11 @@
             parts = layer_got[layer]
             plan.append((layer, at, [part[1:] for part in parts]))
             ins += [after(keep, first_dw) if layer == 3 else keep] + [part[0] for part in parts]
-        sums = call(
+        *sums, out = call(
             functools.partial(fold_layers_kernel, cut, plan),
             (top, *ins, *sums),
             (SMEM,) + (ANY,) * (len(ins) + len(sums)),
-            [upper_shape] * 4 + [plane_shape] * 4,
+            [upper_shape] * 4 + [x_plane, y_plane, y_plane, x_line],
             "fold_layers",
             out_specs=[ANY] * 8,
             scratch=[pltpu.VMEM((2, places, rows, width), bf16)] * 3
@@ -1484,10 +1494,12 @@
             ],
             aliases={1 + len(ins) + i: i for i in range(len(sums))},
         )
-    *uppers, send_x, keep_x, send_y, keep_y = sums
-    masks = [1 << bit for bit in top_bits]
-    got_x, got_y = swap(send_x, both, masks[0]), swap(send_y, both, masks[1])
-    uppers = over_z(uppers)
+        got_x.append(swap(out, both, masks[0]))
+    *uppers, keep_x, send_y, keep_y = sums
+    got_y = swap(send_y, both, masks[1])
+    me_top, landed = top, [got_x[0]]
+    uppers = over_z(uppers, landed, 300)
+    got_x[:1] = landed
     expert_ins = (expert_first[1], expert_got[0], expert_first[3], expert_got[1])
     expert_second = call(
         functools.partial(fold_expert_kernel, (dp_bits == 1, True)),
@@ -1498,6 +1510,7 @@
         0,
     )
 
+    top, uppers = pause(top, 250, uppers)
     uppers = [value.reshape(4, -1, cut, width) for value in uppers]
     uppers = [value.reshape(4, cut, width) for value in rest_of_z(uppers)]
     upper_rows = call(
@@ -1513,15 +1526,16 @@
     own_a, send_y, own_b, send_x = pl.pallas_call(
         fold_plane_kernel,
         grid=(places,),
-        in_specs=[plane_spec] * 4,
-        out_specs=[line_spec] * 4,
-        out_shape=[line_shape] * 4,
+        in_specs=[SMEM, plane_specs[0], line_specs[0], line_specs[0], plane_specs[1], plane_specs[1]],
+        out_specs=[line_specs[0]] * 2 + [line_specs[1]] * 2,
+        out_shape=[x_line] * 2 + [y_line] * 2,
         compiler_params=params(),
         cost_estimate=cost(),
         name="fold_plane",
-    )(keep_x, got_x, keep_y, got_y)
+    )(me_top, keep_x, *got_x, keep_y, got_y)
     got_y, got_x = swap(send_y, both, masks[1]), swap(send_x, both, masks[0])
-    expert_second, upper_rows = lax.optimization_barrier((expert_second, upper_rows))
+    got_y, got_x = after((got_y, got_x), top)
+    expert_second = after(expert_second, got_y, got_x)
     other_out = swap(jnp.stack([value[1] for value in expert_out]), ("expert",), 1)
     lower_rows = call(
         fold_rows_kernel,
@@ -1542,9 +1556,9 @@
         scratch=[pltpu.VMEM((slots, width), f32)],
     )
     image = (1, seq, width)
-    meanwhile = [output.reshape(image), grad.reshape(image)]
-    lower_rows = over_z(lower_rows, meanwhile)
-    output, grad = meanwhile
+    meanwhile = [output.reshape(image), grad.reshape(image), upper_rows]
+    lower_rows = over_z(lower_rows, meanwhile, 250)
+    output, grad, upper_rows = meanwhile
     half = count // 2
     expert_groups = []
     for side, bits in enumerate(orders):

time: 415 us -> 411 us (level)
  waiting for transfers between devices: 154 us -> 146 us
    ppermute x59 -> x60, waiting for transfers between devices: 133 us -> 125 us  [swap(): return lax.ppermute(value, axes, [(i, i ^ mask) for i in range(size)])]
    ppermute x59 -> x60, starting transfers between devices: 57.1 us -> 59.9 us  [swap(): return lax.ppermute(value, axes, [(i, i ^ mask) for i in range(size)])]
    unnamed x113 -> x119, local copies, waits for them, and re-layouts: 15.3 us -> 15.5 us
  transfers between devices with their start and end apart: 64 -> 65, of which waited for: 34 -> 31; matrix products, arithmetic and copies ran while one was open for 3% -> 3% of each run, Pallas kernels for 27% -> 30%
where the time goes in v8:
time: 411 us; the launch traced here: 405 us
  Pallas kernels  158 us (38%)
  waiting for transfers between devices  146 us (36%)
  starting transfers between devices  71.6 us (17%)
  local copies, waits for them, and re-layouts  22.6 us (5%)
  other arithmetic  4.68 us (1%)
    ppermute x60, waiting for transfers between devices, swap(): return lax.ppermute(value, axes, [(i, i ^ mask) for i in range(size)])  125 us
    pallas_call x11, Pallas kernels, call(): pl.pallas_call(kernel, grid=(1,), in_specs=[s or whole(a) for a, s in zip...  74.8 us
    ppermute x60, starting transfers between devices, swap(): return lax.ppermute(value, axes, [(i, i ^ mask) for i in range(size)])  59.9 us
    pallas_call x1, Pallas kernels, on_device(): pl.pallas_call(functools.partial(expert_kernel, (dp_ranks, quarter, exper...  16.7 us
    pallas_call x1, Pallas kernels, on_device(): pl.pallas_call(functools.partial(adam_kernel, (step, chunks, devices, par...  16.1 us
    unnamed x119, local copies, waits for them, and re-layouts  15.5 us
    all_to_all x3, waiting for transfers between devices, exchange(): lax.all_to_all(value, 'expert', split_axis=0, concat_axis=0, tiled=True)  13.3 us
    all_to_all x3, starting transfers between devices, exchange(): lax.all_to_all(value, 'expert', split_axis=0, concat_axis=0, tiled=True)  11.3 us
  transfers between devices with their start and end apart: 65, of which 31 were waited for; matrix products, arithmetic and copies ran while one was open for 3% of the time, Pallas kernels for 30%

profile of v8, /device:TPU:0, one launch (start us, length us, event | category | flops | bytes accessed | tf_op | source)
XLA Modules:
  0.0 405.1 jit_solution(17510992153140040024)
XLA Ops:
  1.9 7.7 %collective-permute-done.tail_ref = f32[96,128]{1,0:T(8,128)S(1)} collective-permute-done((f32[96,128]{1,0:T(8,128)S(1)}, f32[96,128]{1,0:T(8,128)S(1)}, u32[]{:S(2)}, u32[]{:S(2)}) %collective-permute-start) | collective-permute-done | bytes 49184 | tf_op jit(solution)/shard_map/ppermute | solution.py:1100
  15.1 9.6 %collective-permute-done.2.refs_1_ = bf16[400,768]{1,0:T(8,128)(2,1)S(1)} collective-permute-done((bf16[400,768]{1,0:T(8,128)(2,1)}, bf16[400,768]{1,0:T(8,128)(2,1)S(1)}, u32[]{:S(2)}, u32[]{:S(2)}) %collective-permute-start.2) | collective-permute-done | bytes 614432 | tf_op jit(solution)/shard_map/ppermute | solution.py:1003
  34.6 5.8 %pack_expert.1 = (bf16[768,768]{1,0:T(8,128)(2,1)}, bf16[768,768]{1,0:T(8,128)(2,1)}, bf16[384,768]{1,0:T(8,128)(2,1)}, bf16[384,768]{1,0:T(8,128)(2,1)}, bf16[3...) custom-call(s32[1]{0:T(128)} %bitcast.11.wide_ref, f32[9216,128]{1,0:T(8,128)} %bitcast.46), custom_call_target="tpu_custom_call" | custom-call | flops 1 | bytes 1 | tf_op jit(solution)/shard_map/pack_expert/pallas_call | solution.py:1119
  42.2 4.4 %collective-permute-done.6 = bf16[192,768]{1,0:T(8,128)(2,1)} collective-permute-done((bf16[192,768]{1,0:T(8,128)(2,1)}, bf16[192,768]{1,0:T(8,128)(2,1)}, u32[]{:S(2)}, u32[]{:S(2)}) %collective-permute-start.6) | collective-permute-done | bytes 294944 | tf_op jit(solution)/shard_map/ppermute | solution.py:1003
  63.8 7.0 %collective-permute-done.9.refs_0_ = bf16[400,768]{1,0:T(8,128)(2,1)S(1)} collective-permute-done((bf16[400,768]{1,0:T(8,128)(2,1)}, bf16[400,768]{1,0:T(8,128)(2,1)S(1)}, u32[]{:S(2)}, u32[]{:S(2)}) %collective-permute-start.9) | collective-permute-done | bytes 614432 | tf_op jit(solution)/shard_map/ppermute | solution.py:1003
  77.7 7.0 %collective-permute-done.14.refs_1_ = bf16[400,768]{1,0:T(8,128)(2,1)S(1)} collective-permute-done((bf16[400,768]{1,0:T(8,128)(2,1)S(1)}, bf16[400,768]{1,0:T(8,128)(2,1)S(1)}, u32[]{:S(2)}, u32[]{:S(2)}) %collective-permute-start.14) | collective-permute-done | bytes 614432 | tf_op jit(solution)/shard_map/ppermute | solution.py:1003
  89.0 9.6 %collective-permute-done.13.refs_7_ = bf16[400,768]{1,0:T(8,128)(2,1)S(1)} collective-permute-done((bf16[400,768]{1,0:T(8,128)(2,1)S(1)}, bf16[400,768]{1,0:T(8,128)(2,1)S(1)}, u32[]{:S(2)}, u32[]{:S(2)}) %collective-permute-start.13) | collective-permute-done | bytes 614432 | tf_op jit(solution)/shard_map/ppermute | solution.py:1003
  103.1 6.2 %pack_sets.2.refs_0_.refs_16_ = bf16[3,4,400,768]{3,2,1,0:T(8,128)(2,1)} custom-call(bf16[400,768]{1,0:T(8,128)(2,1)} %pack_dense.1.refs_0_, bf16[400,768]{1,0:T(8,128)(2,1)} %copy-done.20, bf16[400,768]{1,0:T(8,128)(2,1)} %copy-done.18, bf16[400,768]{1,0:T(8,128)(2,1)} %copy-done.13, bf16[400,768]{1,0:T(8,128)(2,1)} %copy-done.28, ...), custom_call_target="tpu_custom_call" | custom-call | flops 1 | bytes 1 | tf_op jit(solution)/shard_map/pack_sets/pallas_call | solution.py:1211
  126.4 16.0 %forward.1 = (f32[208,768]{1,0:T(8,128)}, bf16[208,768]{1,0:T(8,128)(2,1)}, bf16[208,768]{1,0:T(8,128)(2,1)}, bf16[208,768]{1,0:T(8,128)(2,1)}, bf16[208,768]{1,...) custom-call(s32[2]{0:T(128)} %pause.8.place_ref, ...), custom_call_target="tpu_custom_call" | custom-call | flops 1 | bytes 1 | tf_op jit(solution)/shard_map/forward/pallas_call | solution.py:1274
  150.8 12.1 %collective-permute-done.25.refs_4_ = bf16[384,768]{1,0:T(8,128)(2,1)S(1)} collective-permute-done((bf16[384,768]{1,0:T(8,128)(2,1)}, bf16[384,768]{1,0:T(8,128)(2,1)S(1)}, u32[]{:S(2)}, u32[]{:S(2)}) %collective-permute-start.25) | collective-permute-done | bytes 589856 | tf_op jit(solution)/shard_map/ppermute | solution.py:1003
  168.6 16.7 %expert.1 = (bf16[2,56,768]{2,1,0:T(8,128)(2,1)}, bf16[2,56,768]{2,1,0:T(8,128)(2,1)}, bf16[2,56,768]{2,1,0:T(8,128)(2,1)}, bf16[2,56,768]{2,1,0:T(8,128)(2,1)},...) custom-call(s32[2]{0:T(128)} %pause.9.me_ref, ...), custom_call_target="tpu_custom_call" | custom-call | flops 1 | bytes 1 | tf_op jit(solution)/shard_map/expert/pallas_call | solution.py:1346
  188.9 9.4 %expert_grad.1 = (bf16[2,768,768]{2,1,0:T(8,128)(2,1)}, bf16[2,768,768]{2,1,0:T(8,128)(2,1)}, bf16[2,768,768]{2,1,0:T(8,128)(2,1)}, bf16[2,768,768]{2,1,0:T(8,128)(2,1)}) custom-call(s32[1]{0:T(128)} %bitcast.1.dp_ref, bf16[448,896]{1,0:T(8,128)(2,1)} %bitcast.45, bf16[448,768]{1,0:T(8,128)(2,1)} %get-tuple-element.296.dy_ref, ...), custom_call_target="tpu_custom_call" | custom-call | flops 1 | bytes 1 | tf_op jit(solution)/shard_map/expert_grad/pallas_call | solution.py:1368
  201.0 9.1 %all-to-all-done.2 = bf16[8,56,896]{2,1,0:T(8,128)(2,1)S(1)} async-done(((bf16[8,56,896]{2,1,0:T(8,128)(2,1)}), bf16[8,56,896]{2,1,0:T(8,128)(2,1)S(1)}, u32[]{:S(2)}, u32[]{:S(2)}) %all-to-all-start.2) | async-done | bytes 802848 | tf_op jit(solution)/shard_map/all_to_all | solution.py:1159
  214.5 27.9 %backward.1 = (f32[96,128]{1,0:T(8,128)}, f32[208,768]{1,0:T(8,128)}, bf16[208,768]{1,0:T(8,128)(2,1)}, bf16[208,768]{1,0:T(8,128)(2,1)}, bf16[208,768]{1,0:T(8,...) custom-call(s32[2]{0:T(128)} %pause.8.place_ref, ...), custom_call_target="tpu_custom_call" | custom-call | flops 1 | bytes 1 | tf_op jit(solution)/shard_map/backward/pallas_call | solution.py:1274
  252.2 6.0 %fold_layers.2 = (bf16[4,1,128,768]{3,2,1,0:T(8,128)(2,1)}, bf16[4,1,128,768]{3,2,1,0:T(8,128)(2,1)}, bf16[4,1,128,768]{3,2,1,0:T(8,128)(2,1)}, bf16[4,1,128,768...) custom-call(s32[1]{0:T(128)} %bitcast.top_ref.ref, ...), custom_call_target="tpu_custom_call" | custom-call | flops 1 | bytes 1 | tf_op jit(solution)/shard_map/fold_layers/pallas_call | solution.py:1274
  262.4 6.7 %fold_layers.3 = (bf16[4,1,128,768]{3,2,1,0:T(8,128)(2,1)}, bf16[4,1,128,768]{3,2,1,0:T(8,128)(2,1)}, bf16[4,1,128,768]{3,2,1,0:T(8,128)(2,1)}, bf16[4,1,128,768...) custom-call(s32[1]{0:T(128)} %pause.10.top_ref.ref, ...), custom_call_target="tpu_custom_call", output_to_operand_aliasing={{0}: (5, {}), {1}: (6, {}), {2}: (7, {}), {3}: (8, {}), {4}... | custom-call | flops 1 | bytes 1 | tf_op jit(solution)/shard_map/fold_layers/pallas_call | solution.py:1274
  271.7 9.3 %collective-permute-done.38.got_one = bf16[4,144,768]{2,1,0:T(8,128)(2,1)S(1)} collective-permute-done((bf16[4,144,768]{2,1,0:T(8,128)(2,1)}, bf16[4,144,768]{2,1,0:T(8,128)(2,1)S(1)}, u32[]{:S(2)}, u32[]{:S(2)}) %collective-permute-start.38) | collective-permute-done | bytes 884768 | tf_op jit(solution)/shard_map/ppermute | solution.py:1003
  281.1 7.6 %collective-permute-done.37.right = bf16[4,1,128,768]{3,2,1,0:T(8,128)(2,1)S(1)} collective-permute-done((bf16[4,1,128,768]{3,2,1,0:T(8,128)(2,1)}, bf16[4,1,128,768]{3,2,1,0:T(8,128)(2,1)S(1)}, u32[]{:S(2)}, u32[]{:S(2)}) %collective-permute-start.37) | collective-permute-done | bytes 786464 | tf_op jit(solution)/shard_map/ppermute | solution.py:1003
  291.8 6.2 %fold_expert.1 = (bf16[768,768]{1,0:T(8,128)(2,1)}, bf16[768,768]{1,0:T(8,128)(2,1)}, bf16[768,768]{1,0:T(8,128)(2,1)}, bf16[768,768]{1,0:T(8,128)(2,1)}) custom-call(bf16[2,768,768]{2,1,0:T(8,128)(2,1)} %get-tuple-element.306.refs_0_, bf16[2,768,768]{2,1,0:T(8,128)(2,1)} %collective-permute-done.27.refs_1_, ...), custom_call_target="tpu_custom_call" | custom-call | flops 1 | bytes 1 | tf_op jit(solution)/shard_map/fold_expert/pallas_call | solution.py:1274
  302.5 5.7 %fold_plane.1 = (bf16[4,144,768]{2,1,0:T(8,128)(2,1)}, bf16[4,144,768]{2,1,0:T(8,128)(2,1)}, bf16[4,112,768]{2,1,0:T(8,128)(2,1)}, bf16[4,112,768]{2,1,0:T(8,128)(2,1)}) custom-call(s32[1]{0:T(128)} %pause.10.top_ref.ref, bf16[2,4,144,768]{3,2,1,0:T(8,128)(2,1)} %get-tuple-element.371.keep_x, bf16[4,144,768]{2,1,0:T(8,128)(2,1)} %copy-done.23, ...), custom_call_target="tpu_custom_call" | custom-call | flops 1 | bytes 1 | tf_op jit(solution)/shard_map/fold_plane/pallas_call | solution.py:1526
  310.8 15.4 %collective-permute-done.44 = bf16[4,1,128,768]{3,2,0,1:T(8,128)(2,1)S(1)} collective-permute-done((bf16[4,1,128,768]{3,2,0,1:T(8,128)(2,1)S(1)}, bf16[4,1,128,768]{3,2,0,1:T(8,128)(2,1)S(1)}, u32[]{:S(2)}, u32[]{:S(2)}) %collective-permute-start.44) | collective-permute-done | bytes 786464 | tf_op jit(solution)/shard_map/ppermute | solution.py:1003
  345.8 9.9 %collective-permute-done.49.refs_1_ = bf16[768,768]{1,0:T(8,128)(2,1)} collective-permute-done((bf16[768,768]{1,0:T(8,128)(2,1)}, bf16[768,768]{1,0:T(8,128)(2,1)}, u32[]{:S(2)}, u32[]{:S(2)}) %collective-permute-start.49) | collective-permute-done | bytes 1179680 | tf_op jit(solution)/shard_map/ppermute | solution.py:1003
  360.7 6.1 %unpack_expert.1 = (f32[9216,128]{1,0:T(8,128)}, f32[1,128]{1,0:T(1,128)}) custom-call(s32[1]{0:T(128)} %bitcast.11.wide_ref, bf16[768,768]{1,0:T(8,128)(2,1)} %get-tuple-element.438.refs_0_, bf16[768,768]{1,0:T(8,128)(2,1)} %collective-permute-done.49.refs_1_, bf16[768,768]{1,0:T(8,128)(2,1)} %get-tuple-element.440.refs_2_, ...), custom_call_target="tpu_custom_call" | custom-call | flops 1 | bytes 1 | tf_op jit(solution)/shard_map/unpack_expert/pallas_call | solution.py:1581
  388.7 16.1 %adam.1 = (f32[9216,128]{1,0:T(8,128)}, f32[9216,128]{1,0:T(8,128)}, f32[9216,128]{1,0:T(8,128)}, f32[2307,128]{1,0:T(8,128)}, f32[2307,128]{1,0:T(8,128)}, /*in...) custom-call(s32[1]{0:T(128)} %bitcast.2.k_ref, f32[104,128]{1,0:T(8,128)} %add_add_fusion.total_ref, ...), custom_call_target="tpu_custom_call" | custom-call | flops 1 | bytes 1 | tf_op jit(solution)/shard_map/adam/pallas_call | solution.py:1620
  (275 shorter events, 166.1 us)
Async XLA Ops:
  29.0 28.0 %collective-permute-start.4 = (bf16[400,768]{1,0:T(8,128)(2,1)}, bf16[400,768]{1,0:T(8,128)(2,1)}, u32[]{:S(2)}, u32[]{:S(2)}) collective-permute-start(bf16[400,768]{1,0:T(8,128)(2,1)} %pack_dense.1.refs_0_), channel_id=1, source_target_pairs={{0,4},{1,5},{2,6},{3,7},{4,0},{5,1},{6,2},{7,3},{8,12},{9,13},{10,... | collective-permute-start | bytes 1843208 | tf_op jit(solution)/shard_map/ppermute | solution.py:1003
  74.4 24.1 %collective-permute-start.13 = (bf16[400,768]{1,0:T(8,128)(2,1)S(1)}, bf16[400,768]{1,0:T(8,128)(2,1)S(1)}, u32[]{:S(2)}, u32[]{:S(2)}) collective-permute-start(bf16[400,768]{1,0:T(8,128)(2,1)S(1)} %pad_maximum_fusion.refs_3_), channel_id=1, source_target_pairs={{0,2},{1,3},{2,0},{3,1},{4,6},{5,7},{6,4},{7,5},{8,10},{9,11},{10,... | collective-permute-start | bytes 1843208 | tf_op jit(solution)/shard_map/ppermute | solution.py:1003
  74.7 27.5 %collective-permute-start.12 = (bf16[400,768]{1,0:T(8,128)(2,1)S(1)}, bf16[400,768]{1,0:T(8,128)(2,1)S(1)}, u32[]{:S(2)}, u32[]{:S(2)}) collective-permute-start(bf16[400,768]{1,0:T(8,128)(2,1)S(1)} %pad_maximum_fusion.refs_3_), channel_id=1, source_target_pairs={{0,4},{1,5},{2,6},{3,7},{4,0},{5,1},{6,2},{7,3},{8,12},{9,13},{10,... | collective-permute-start | bytes 1843208 | tf_op jit(solution)/shard_map/ppermute | solution.py:1003
  86.4 28.9 %collective-permute-start.19 = (bf16[768,768]{1,0:T(8,128)(2,1)S(1)}, bf16[768,768]{1,0:T(8,128)(2,1)}, u32[]{:S(2)}, u32[]{:S(2)}) collective-permute-start(bf16[768,768]{1,0:T(8,128)(2,1)S(1)} %copy-done.21), channel_id=1, source_target_pairs={{0,8},{8,0},{16,24},{24,16},{1,9},{9,1},{17,25},{25,17},{2,10},{10... | collective-permute-start | bytes 3538952 | tf_op jit(solution)/shard_map/ppermute | solution.py:1003
  87.2 28.1 %collective-permute-start.20 = (bf16[768,768]{1,0:T(8,128)(2,1)}, bf16[768,768]{1,0:T(8,128)(2,1)}, u32[]{:S(2)}, u32[]{:S(2)}) collective-permute-start(bf16[768,768]{1,0:T(8,128)(2,1)} %get-tuple-element.271.refs_1_), channel_id=1, source_target_pairs={{0,16},{8,24},{16,0},{24,8},{1,17},{9,25},{17,1},{25,9},{2,18},{10... | collective-permute-start | bytes 3538952 | tf_op jit(solution)/shard_map/ppermute | solution.py:1003
  109.4 33.0 %all-to-all-start.1 = ((bf16[8,56,768]{2,1,0:T(8,128)(2,1)}), bf16[8,56,768]{2,1,0:T(8,128)(2,1)S(1)}, u32[]{:S(2)}, u32[]{:S(2)}) async-start(bf16[8,56,768]{2,1,0:T(8,128)(2,1)} %bitcast.15), calls=%async_computation.1 | async-start | bytes 1376256 | tf_op jit(solution)/shard_map/all_to_all | solution.py:1159
  115.3 34.3 %collective-permute-start.23 = (bf16[768,768]{1,0:T(8,128)(2,1)}, bf16[768,768]{1,0:T(8,128)(2,1)S(1)}, u32[]{:S(2)}, u32[]{:S(2)}) collective-permute-start(bf16[768,768]{1,0:T(8,128)(2,1)} %collective-permute-done.19.refs_2_), channel_id=1, source_target_pairs={{0,16},{8,24},{16,0},{24,8},{1,17},{9,25},{17,1},{25,9},{2,18},{10... | collective-permute-start | bytes 3538952 | tf_op jit(solution)/shard_map/ppermute | solution.py:1003
  115.6 34.0 %collective-permute-start.24 = (bf16[768,768]{1,0:T(8,128)(2,1)}, bf16[768,768]{1,0:T(8,128)(2,1)}, u32[]{:S(2)}, u32[]{:S(2)}) collective-permute-start(bf16[768,768]{1,0:T(8,128)(2,1)} %collective-permute-done.20.refs_5_), channel_id=1, source_target_pairs={{0,8},{8,0},{16,24},{24,16},{1,9},{9,1},{17,25},{25,17},{2,10},{10... | collective-permute-start | bytes 3538952 | tf_op jit(solution)/shard_map/ppermute | solution.py:1003
  142.5 25.2 %all-to-all-start = ((bf16[8,56,896]{2,1,0:T(8,128)(2,1)}), bf16[8,56,896]{2,1,0:T(8,128)(2,1)S(1)}, u32[]{:S(2)}, u32[]{:S(2)}) async-start(bf16[8,56,896]{2,1,0:T(8,128)(2,1)} %bitcast.55), calls=%async_computation | async-start | bytes 1605632 | tf_op jit(solution)/shard_map/all_to_all | solution.py:1159
  185.3 24.8 %all-to-all-start.2 = ((bf16[8,56,896]{2,1,0:T(8,128)(2,1)}), bf16[8,56,896]{2,1,0:T(8,128)(2,1)S(1)}, u32[]{:S(2)}, u32[]{:S(2)}) async-start(bf16[8,56,896]{2,1,0:T(8,128)(2,1)} %bitcast.56), calls=%async_computation.2 | async-start | bytes 1605632 | tf_op jit(solution)/shard_map/all_to_all | solution.py:1159
  198.3 60.0 %collective-permute-start.27 = (bf16[2,768,768]{2,1,0:T(8,128)(2,1)}, bf16[2,768,768]{2,1,0:T(8,128)(2,1)}, u32[]{:S(2)}, u32[]{:S(2)}) collective-permute-start(bf16[2,768,768]{2,1,0:T(8,128)(2,1)} %get-tuple-element.299), channel_id=1, source_target_pairs={{0,8},{8,0},{16,24},{24,16},{1,9},{9,1},{17,25},{25,17},{2,10},{10... | collective-permute-start | bytes 7077896 | tf_op jit(solution)/shard_map/ppermute | solution.py:1003
  199.2 59.1 %collective-permute-start.28 = (bf16[2,768,768]{2,1,0:T(8,128)(2,1)}, bf16[2,768,768]{2,1,0:T(8,128)(2,1)}, u32[]{:S(2)}, u32[]{:S(2)}) collective-permute-start(bf16[2,768,768]{2,1,0:T(8,128)(2,1)} %get-tuple-element.300), channel_id=1, source_target_pairs={{0,16},{8,24},{16,0},{24,8},{1,17},{9,25},{17,1},{25,9},{2,18},{10... | collective-permute-start | bytes 7077896 | tf_op jit(solution)/shard_map/ppermute | solution.py:1003
  210.1 32.3 %collective-permute-start.29 = (bf16[2,56,768]{2,1,0:T(8,128)(2,1)S(1)}, bf16[2,56,768]{2,1,0:T(8,128)(2,1)S(1)}, u32[]{:S(2)}, u32[]{:S(2)}) collective-permute-start(bf16[2,56,768]{2,1,0:T(8,128)(2,1)S(1)} %copy-done.57), channel_id=1, source_target_pairs={{0,2},{1,3},{2,0},{3,1},{4,6},{5,7},{6,4},{7,5},{8,10},{9,11},{10,... | collective-permute-start | bytes 516104 | tf_op jit(solution)/shard_map/ppermute | solution.py:1003
  210.1 32.3 %collective-permute-start.30 = (bf16[2,56,768]{2,1,0:T(8,128)(2,1)S(1)}, bf16[2,56,768]{2,1,0:T(8,128)(2,1)S(1)}, u32[]{:S(2)}, u32[]{:S(2)}) collective-permute-start(bf16[2,56,768]{2,1,0:T(8,128)(2,1)S(1)} %copy-done.56), channel_id=1, source_target_pairs={{0,4},{1,5},{2,6},{3,7},{4,0},{5,1},{6,2},{7,3},{8,12},{9,13},{10,... | collective-permute-start | bytes 516104 | tf_op jit(solution)/shard_map/ppermute | solution.py:1003
  211.9 30.5 %collective-permute-start.31 = (bf16[2,56,768]{2,1,0:T(8,128)(2,1)S(1)}, bf16[2,56,768]{2,1,0:T(8,128)(2,1)S(1)}, u32[]{:S(2)}, u32[]{:S(2)}) collective-permute-start(bf16[2,56,768]{2,1,0:T(8,128)(2,1)S(1)} %copy-done.55), channel_id=1, source_target_pairs={{0,6},{1,7},{2,4},{3,5},{4,2},{5,3},{6,0},{7,1},{8,14},{9,15},{10,... | collective-permute-start | bytes 516104 | tf_op jit(solution)/shard_map/ppermute | solution.py:1003
  258.3 22.8 %collective-permute-start.38 = (bf16[4,144,768]{2,1,0:T(8,128)(2,1)}, bf16[4,144,768]{2,1,0:T(8,128)(2,1)S(1)}, u32[]{:S(2)}, u32[]{:S(2)}) collective-permute-start(bf16[4,144,768]{2,1,0:T(8,128)(2,1)} %get-tuple-element.373), channel_id=1, source_target_pairs={{0,8},{1,9},{2,10},{3,11},{4,12},{5,13},{6,14},{7,15},{8,0},{9,1},... | collective-permute-start | bytes 2654216 | tf_op jit(solution)/shard_map/ppermute | solution.py:1003
  269.1 32.2 %collective-permute-start.40 = (bf16[2,4,112,768]{3,2,1,0:T(8,128)(2,1)}, bf16[2,4,112,768]{3,2,1,0:T(8,128)(2,1)S(1)}, u32[]{:S(2)}, u32[]{:S(2)}) collective-permute-start(bf16[2,4,112,768]{3,2,1,0:T(8,128)(2,1)} %get-tuple-element.376), channel_id=1, source_target_pairs={{0,16},{1,17},{2,18},{3,19},{4,20},{5,21},{6,22},{7,23},{8,24},{9,... | collective-permute-start | bytes 4128776 | tf_op jit(solution)/shard_map/ppermute | solution.py:1003
  271.0 28.2 %collective-permute-start.39 = (bf16[4,144,768]{2,1,0:T(8,128)(2,1)}, bf16[4,144,768]{2,1,0:T(8,128)(2,1)S(1)}, u32[]{:S(2)}, u32[]{:S(2)}) collective-permute-start(bf16[4,144,768]{2,1,0:T(8,128)(2,1)} %get-tuple-element.375), channel_id=1, source_target_pairs={{0,8},{1,9},{2,10},{3,11},{4,12},{5,13},{6,14},{7,15},{8,0},{9,1},... | collective-permute-start | bytes 2654216 | tf_op jit(solution)/shard_map/ppermute | solution.py:1003
  290.0 36.2 %collective-permute-start.44 = (bf16[4,1,128,768]{3,2,0,1:T(8,128)(2,1)S(1)}, bf16[4,1,128,768]{3,2,0,1:T(8,128)(2,1)S(1)}, u32[]{:S(2)}, u32[]{:S(2)}) collective-permute-start(bf16[4,1,128,768]{3,2,0,1:T(8,128)(2,1)S(1)} %bitcast.43), channel_id=1, source_target_pairs={{0,4},{1,5},{2,6},{3,7},{4,0},{5,1},{6,2},{7,3},{8,12},{9,13},{10,... | collective-permute-start | bytes 2359304 | tf_op jit(solution)/shard_map/ppermute | solution.py:1003
  290.9 35.3 %collective-permute-start.43 = (bf16[4,1,128,768]{3,2,0,1:T(8,128)(2,1)S(1)}, bf16[4,1,128,768]{3,2,0,1:T(8,128)(2,1)S(1)}, u32[]{:S(2)}, u32[]{:S(2)}) collective-permute-start(bf16[4,1,128,768]{3,2,0,1:T(8,128)(2,1)S(1)} %bitcast.58), channel_id=1, source_target_pairs={{0,2},{1,3},{2,0},{3,1},{4,6},{5,7},{6,4},{7,5},{8,10},{9,11},{10,... | collective-permute-start | bytes 2359304 | tf_op jit(solution)/shard_map/ppermute | solution.py:1003
  310.8 23.7 %collective-permute-start.45 = (bf16[4,56,768]{2,1,0:T(8,128)(2,1)S(1)}, bf16[4,56,768]{2,1,0:T(8,128)(2,1)S(1)}, u32[]{:S(2)}, u32[]{:S(2)}) collective-permute-start(bf16[4,56,768]{2,1,0:T(8,128)(2,1)S(1)} %pad_maximum_fusion.1), channel_id=1, source_target_pairs={{0,1},{1,0},{2,3},{3,2},{4,5},{5,4},{6,7},{7,6},{8,9},{9,8},{10,11... | collective-permute-start | bytes 1032200 | tf_op jit(solution)/shard_map/ppermute | solution.py:1003
  328.9 26.8 %collective-permute-start.49 = (bf16[768,768]{1,0:T(8,128)(2,1)}, bf16[768,768]{1,0:T(8,128)(2,1)}, u32[]{:S(2)}, u32[]{:S(2)}) collective-permute-start(bf16[768,768]{1,0:T(8,128)(2,1)} %get-tuple-element.435), channel_id=1, source_target_pairs={{0,16},{8,24},{16,0},{24,8},{1,17},{9,25},{17,1},{25,9},{2,18},{10... | collective-permute-start | bytes 3538952 | tf_op jit(solution)/shard_map/ppermute | solution.py:1003
  330.6 26.5 %collective-permute-start.50 = (bf16[768,768]{1,0:T(8,128)(2,1)}, bf16[768,768]{1,0:T(8,128)(2,1)}, u32[]{:S(2)}, u32[]{:S(2)}) collective-permute-start(bf16[768,768]{1,0:T(8,128)(2,1)} %get-tuple-element.437), channel_id=1, source_target_pairs={{0,8},{8,0},{16,24},{24,16},{1,9},{9,1},{17,25},{25,17},{2,10},{10... | collective-permute-start | bytes 3538952 | tf_op jit(solution)/shard_map/ppermute | solution.py:1003
  343.9 22.9 %collective-permute-start.48 = (bf16[1,256,768]{2,1,0:T(8,128)(2,1)S(1)}, bf16[1,256,768]{2,1,0:T(8,128)(2,1)S(1)}, u32[]{:S(2)}, u32[]{:S(2)}) collective-permute-start(bf16[1,256,768]{2,1,0:T(8,128)(2,1)S(1)} %add.53), channel_id=1, source_target_pairs={{0,4},{1,5},{2,6},{3,7},{4,0},{5,1},{6,2},{7,3},{8,12},{9,13},{10,... | collective-permute-start | bytes 1179656 | tf_op jit(solution)/shard_map/ppermute | solution.py:1003
  (99 other events, 988.6 us)

commit v9 on v8

--- a/solution.py
+++ b/solution.py
@@ -1616,7 +1616,7 @@
     total = all_sum_step(total, both, groups[-1])
     param_count = (dense_master.size + expert_master.size) * devices
 
-    chunks = 16
+    chunks = 8
     results = pl.pallas_call(
         functools.partial(adam_kernel, (step, chunks, devices, param_count, width * experts // LANES)),
         in_specs=[SMEM, VMEM, VMEM] + [ANY] * 6,

time: 411 us -> 410 us (level)
  no operation moved by 1% of the time
where the time goes in v9:
time: 410 us; the launch traced here: 405 us
  Pallas kernels  158 us (39%)
  waiting for transfers between devices  146 us (36%)
  starting transfers between devices  71.6 us (17%)
  local copies, waits for them, and re-layouts  22.6 us (6%)
  other arithmetic  4.68 us (1%)
    ppermute x60, waiting for transfers between devices, swap(): return lax.ppermute(value, axes, [(i, i ^ mask) for i in range(size)])  125 us
    pallas_call x11, Pallas kernels, call(): pl.pallas_call(kernel, grid=(1,), in_specs=[s or whole(a) for a, s in zip...  74.8 us
    ppermute x60, starting transfers between devices, swap(): return lax.ppermute(value, axes, [(i, i ^ mask) for i in range(size)])  59.9 us
    pallas_call x1, Pallas kernels, on_device(): pl.pallas_call(functools.partial(expert_kernel, (dp_ranks, quarter, exper...  16.7 us
    unnamed x119, local copies, waits for them, and re-layouts  15.5 us
    pallas_call x1, Pallas kernels, on_device(): pl.pallas_call(functools.partial(adam_kernel, (step, chunks, devices, par...  15.5 us
    all_to_all x3, waiting for transfers between devices, exchange(): lax.all_to_all(value, 'expert', split_axis=0, concat_axis=0, tiled=True)  13.3 us
    all_to_all x3, starting transfers between devices, exchange(): lax.all_to_all(value, 'expert', split_axis=0, concat_axis=0, tiled=True)  11.3 us
  transfers between devices with their start and end apart: 65, of which 31 were waited for; matrix products, arithmetic and copies ran while one was open for 3% of the time, Pallas kernels for 30%

profile of v9, /device:TPU:0, one launch (start us, length us, event | category | flops | bytes accessed | tf_op | source)
XLA Modules:
  0.0 404.5 jit_solution(12541174952812415758)
XLA Ops:
  1.9 7.7 %collective-permute-done.tail_ref = f32[96,128]{1,0:T(8,128)S(1)} collective-permute-done((f32[96,128]{1,0:T(8,128)S(1)}, f32[96,128]{1,0:T(8,128)S(1)}, u32[]{:S(2)}, u32[]{:S(2)}) %collective-permute-start) | collective-permute-done | bytes 49184 | tf_op jit(solution)/shard_map/ppermute | solution.py:1100
  15.1 9.6 %collective-permute-done.2.refs_1_ = bf16[400,768]{1,0:T(8,128)(2,1)S(1)} collective-permute-done((bf16[400,768]{1,0:T(8,128)(2,1)}, bf16[400,768]{1,0:T(8,128)(2,1)S(1)}, u32[]{:S(2)}, u32[]{:S(2)}) %collective-permute-start.2) | collective-permute-done | bytes 614432 | tf_op jit(solution)/shard_map/ppermute | solution.py:1003
  34.6 5.8 %pack_expert.1 = (bf16[768,768]{1,0:T(8,128)(2,1)}, bf16[768,768]{1,0:T(8,128)(2,1)}, bf16[384,768]{1,0:T(8,128)(2,1)}, bf16[384,768]{1,0:T(8,128)(2,1)}, bf16[3...) custom-call(s32[1]{0:T(128)} %bitcast.11.wide_ref, f32[9216,128]{1,0:T(8,128)} %bitcast.46), custom_call_target="tpu_custom_call" | custom-call | flops 1 | bytes 1 | tf_op jit(solution)/shard_map/pack_expert/pallas_call | solution.py:1119
  42.2 4.4 %collective-permute-done.6 = bf16[192,768]{1,0:T(8,128)(2,1)} collective-permute-done((bf16[192,768]{1,0:T(8,128)(2,1)}, bf16[192,768]{1,0:T(8,128)(2,1)}, u32[]{:S(2)}, u32[]{:S(2)}) %collective-permute-start.6) | collective-permute-done | bytes 294944 | tf_op jit(solution)/shard_map/ppermute | solution.py:1003
  63.8 7.0 %collective-permute-done.9.refs_0_ = bf16[400,768]{1,0:T(8,128)(2,1)S(1)} collective-permute-done((bf16[400,768]{1,0:T(8,128)(2,1)}, bf16[400,768]{1,0:T(8,128)(2,1)S(1)}, u32[]{:S(2)}, u32[]{:S(2)}) %collective-permute-start.9) | collective-permute-done | bytes 614432 | tf_op jit(solution)/shard_map/ppermute | solution.py:1003
  77.7 7.0 %collective-permute-done.14.refs_1_ = bf16[400,768]{1,0:T(8,128)(2,1)S(1)} collective-permute-done((bf16[400,768]{1,0:T(8,128)(2,1)S(1)}, bf16[400,768]{1,0:T(8,128)(2,1)S(1)}, u32[]{:S(2)}, u32[]{:S(2)}) %collective-permute-start.14) | collective-permute-done | bytes 614432 | tf_op jit(solution)/shard_map/ppermute | solution.py:1003
  89.0 9.6 %collective-permute-done.13.refs_7_ = bf16[400,768]{1,0:T(8,128)(2,1)S(1)} collective-permute-done((bf16[400,768]{1,0:T(8,128)(2,1)S(1)}, bf16[400,768]{1,0:T(8,128)(2,1)S(1)}, u32[]{:S(2)}, u32[]{:S(2)}) %collective-permute-start.13) | collective-permute-done | bytes 614432 | tf_op jit(solution)/shard_map/ppermute | solution.py:1003
  103.1 6.2 %pack_sets.2.refs_0_.refs_16_ = bf16[3,4,400,768]{3,2,1,0:T(8,128)(2,1)} custom-call(bf16[400,768]{1,0:T(8,128)(2,1)} %pack_dense.1.refs_0_, bf16[400,768]{1,0:T(8,128)(2,1)} %copy-done.20, bf16[400,768]{1,0:T(8,128)(2,1)} %copy-done.18, bf16[400,768]{1,0:T(8,128)(2,1)} %copy-done.13, bf16[400,768]{1,0:T(8,128)(2,1)} %copy-done.28, ...), custom_call_target="tpu_custom_call" | custom-call | flops 1 | bytes 1 | tf_op jit(solution)/shard_map/pack_sets/pallas_call | solution.py:1211
  126.4 16.0 %forward.1 = (f32[208,768]{1,0:T(8,128)}, bf16[208,768]{1,0:T(8,128)(2,1)}, bf16[208,768]{1,0:T(8,128)(2,1)}, bf16[208,768]{1,0:T(8,128)(2,1)}, bf16[208,768]{1,...) custom-call(s32[2]{0:T(128)} %pause.8.place_ref, ...), custom_call_target="tpu_custom_call" | custom-call | flops 1 | bytes 1 | tf_op jit(solution)/shard_map/forward/pallas_call | solution.py:1274
  150.8 12.1 %collective-permute-done.25.refs_4_ = bf16[384,768]{1,0:T(8,128)(2,1)S(1)} collective-permute-done((bf16[384,768]{1,0:T(8,128)(2,1)}, bf16[384,768]{1,0:T(8,128)(2,1)S(1)}, u32[]{:S(2)}, u32[]{:S(2)}) %collective-permute-start.25) | collective-permute-done | bytes 589856 | tf_op jit(solution)/shard_map/ppermute | solution.py:1003
  168.6 16.7 %expert.1 = (bf16[2,56,768]{2,1,0:T(8,128)(2,1)}, bf16[2,56,768]{2,1,0:T(8,128)(2,1)}, bf16[2,56,768]{2,1,0:T(8,128)(2,1)}, bf16[2,56,768]{2,1,0:T(8,128)(2,1)},...) custom-call(s32[2]{0:T(128)} %pause.9.me_ref, ...), custom_call_target="tpu_custom_call" | custom-call | flops 1 | bytes 1 | tf_op jit(solution)/shard_map/expert/pallas_call | solution.py:1346
  188.9 9.4 %expert_grad.1 = (bf16[2,768,768]{2,1,0:T(8,128)(2,1)}, bf16[2,768,768]{2,1,0:T(8,128)(2,1)}, bf16[2,768,768]{2,1,0:T(8,128)(2,1)}, bf16[2,768,768]{2,1,0:T(8,128)(2,1)}) custom-call(s32[1]{0:T(128)} %bitcast.1.dp_ref, bf16[448,896]{1,0:T(8,128)(2,1)} %bitcast.45, bf16[448,768]{1,0:T(8,128)(2,1)} %get-tuple-element.296.dy_ref, ...), custom_call_target="tpu_custom_call" | custom-call | flops 1 | bytes 1 | tf_op jit(solution)/shard_map/expert_grad/pallas_call | solution.py:1368
  201.0 9.1 %all-to-all-done.2 = bf16[8,56,896]{2,1,0:T(8,128)(2,1)S(1)} async-done(((bf16[8,56,896]{2,1,0:T(8,128)(2,1)}), bf16[8,56,896]{2,1,0:T(8,128)(2,1)S(1)}, u32[]{:S(2)}, u32[]{:S(2)}) %all-to-all-start.2) | async-done | bytes 802848 | tf_op jit(solution)/shard_map/all_to_all | solution.py:1159
  214.5 27.9 %backward.1 = (f32[96,128]{1,0:T(8,128)}, f32[208,768]{1,0:T(8,128)}, bf16[208,768]{1,0:T(8,128)(2,1)}, bf16[208,768]{1,0:T(8,128)(2,1)}, bf16[208,768]{1,0:T(8,...) custom-call(s32[2]{0:T(128)} %pause.8.place_ref, ...), custom_call_target="tpu_custom_call" | custom-call | flops 1 | bytes 1 | tf_op jit(solution)/shard_map/backward/pallas_call | solution.py:1274
  252.2 6.0 %fold_layers.2 = (bf16[4,1,128,768]{3,2,1,0:T(8,128)(2,1)}, bf16[4,1,128,768]{3,2,1,0:T(8,128)(2,1)}, bf16[4,1,128,768]{3,2,1,0:T(8,128)(2,1)}, bf16[4,1,128,768...) custom-call(s32[1]{0:T(128)} %bitcast.top_ref.ref, ...), custom_call_target="tpu_custom_call" | custom-call | flops 1 | bytes 1 | tf_op jit(solution)/shard_map/fold_layers/pallas_call | solution.py:1274
  262.4 6.7 %fold_layers.3 = (bf16[4,1,128,768]{3,2,1,0:T(8,128)(2,1)}, bf16[4,1,128,768]{3,2,1,0:T(8,128)(2,1)}, bf16[4,1,128,768]{3,2,1,0:T(8,128)(2,1)}, bf16[4,1,128,768...) custom-call(s32[1]{0:T(128)} %pause.10.top_ref.ref, ...), custom_call_target="tpu_custom_call", output_to_operand_aliasing={{0}: (5, {}), {1}: (6, {}), {2}: (7, {}), {3}: (8, {}), {4}... | custom-call | flops 1 | bytes 1 | tf_op jit(solution)/shard_map/fold_layers/pallas_call | solution.py:1274
  271.7 9.3 %collective-permute-done.38.got_one = bf16[4,144,768]{2,1,0:T(8,128)(2,1)S(1)} collective-permute-done((bf16[4,144,768]{2,1,0:T(8,128)(2,1)}, bf16[4,144,768]{2,1,0:T(8,128)(2,1)S(1)}, u32[]{:S(2)}, u32[]{:S(2)}) %collective-permute-start.38) | collective-permute-done | bytes 884768 | tf_op jit(solution)/shard_map/ppermute | solution.py:1003
  281.1 7.6 %collective-permute-done.37.right = bf16[4,1,128,768]{3,2,1,0:T(8,128)(2,1)S(1)} collective-permute-done((bf16[4,1,128,768]{3,2,1,0:T(8,128)(2,1)}, bf16[4,1,128,768]{3,2,1,0:T(8,128)(2,1)S(1)}, u32[]{:S(2)}, u32[]{:S(2)}) %collective-permute-start.37) | collective-permute-done | bytes 786464 | tf_op jit(solution)/shard_map/ppermute | solution.py:1003
  291.8 6.2 %fold_expert.1 = (bf16[768,768]{1,0:T(8,128)(2,1)}, bf16[768,768]{1,0:T(8,128)(2,1)}, bf16[768,768]{1,0:T(8,128)(2,1)}, bf16[768,768]{1,0:T(8,128)(2,1)}) custom-call(bf16[2,768,768]{2,1,0:T(8,128)(2,1)} %get-tuple-element.306.refs_0_, bf16[2,768,768]{2,1,0:T(8,128)(2,1)} %collective-permute-done.27.refs_1_, ...), custom_call_target="tpu_custom_call" | custom-call | flops 1 | bytes 1 | tf_op jit(solution)/shard_map/fold_expert/pallas_call | solution.py:1274
  302.5 5.7 %fold_plane.1 = (bf16[4,144,768]{2,1,0:T(8,128)(2,1)}, bf16[4,144,768]{2,1,0:T(8,128)(2,1)}, bf16[4,112,768]{2,1,0:T(8,128)(2,1)}, bf16[4,112,768]{2,1,0:T(8,128)(2,1)}) custom-call(s32[1]{0:T(128)} %pause.10.top_ref.ref, bf16[2,4,144,768]{3,2,1,0:T(8,128)(2,1)} %get-tuple-element.371.keep_x, bf16[4,144,768]{2,1,0:T(8,128)(2,1)} %copy-done.23, ...), custom_call_target="tpu_custom_call" | custom-call | flops 1 | bytes 1 | tf_op jit(solution)/shard_map/fold_plane/pallas_call | solution.py:1526
  310.8 15.4 %collective-permute-done.44 = bf16[4,1,128,768]{3,2,0,1:T(8,128)(2,1)S(1)} collective-permute-done((bf16[4,1,128,768]{3,2,0,1:T(8,128)(2,1)S(1)}, bf16[4,1,128,768]{3,2,0,1:T(8,128)(2,1)S(1)}, u32[]{:S(2)}, u32[]{:S(2)}) %collective-permute-start.44) | collective-permute-done | bytes 786464 | tf_op jit(solution)/shard_map/ppermute | solution.py:1003
  345.8 9.9 %collective-permute-done.49.refs_1_ = bf16[768,768]{1,0:T(8,128)(2,1)} collective-permute-done((bf16[768,768]{1,0:T(8,128)(2,1)}, bf16[768,768]{1,0:T(8,128)(2,1)}, u32[]{:S(2)}, u32[]{:S(2)}) %collective-permute-start.49) | collective-permute-done | bytes 1179680 | tf_op jit(solution)/shard_map/ppermute | solution.py:1003
  360.7 6.1 %unpack_expert.1 = (f32[9216,128]{1,0:T(8,128)}, f32[1,128]{1,0:T(1,128)}) custom-call(s32[1]{0:T(128)} %bitcast.11.wide_ref, bf16[768,768]{1,0:T(8,128)(2,1)} %get-tuple-element.438.refs_0_, bf16[768,768]{1,0:T(8,128)(2,1)} %collective-permute-done.49.refs_1_, bf16[768,768]{1,0:T(8,128)(2,1)} %get-tuple-element.440.refs_2_, ...), custom_call_target="tpu_custom_call" | custom-call | flops 1 | bytes 1 | tf_op jit(solution)/shard_map/unpack_expert/pallas_call | solution.py:1581
  388.7 15.5 %adam.1 = (f32[9216,128]{1,0:T(8,128)}, f32[9216,128]{1,0:T(8,128)}, f32[9216,128]{1,0:T(8,128)}, f32[2307,128]{1,0:T(8,128)}, f32[2307,128]{1,0:T(8,128)}, /*in...) custom-call(s32[1]{0:T(128)} %bitcast.2.k_ref, f32[104,128]{1,0:T(8,128)} %add_add_fusion.total_ref, ...), custom_call_target="tpu_custom_call" | custom-call | flops 1 | bytes 1 | tf_op jit(solution)/shard_map/adam/pallas_call | solution.py:1620
  (275 shorter events, 166.1 us)
Async XLA Ops:
  29.0 28.0 %collective-permute-start.4 = (bf16[400,768]{1,0:T(8,128)(2,1)}, bf16[400,768]{1,0:T(8,128)(2,1)}, u32[]{:S(2)}, u32[]{:S(2)}) collective-permute-start(bf16[400,768]{1,0:T(8,128)(2,1)} %pack_dense.1.refs_0_), channel_id=1, source_target_pairs={{0,4},{1,5},{2,6},{3,7},{4,0},{5,1},{6,2},{7,3},{8,12},{9,13},{10,... | collective-permute-start | bytes 1843208 | tf_op jit(solution)/shard_map/ppermute | solution.py:1003
  74.4 24.1 %collective-permute-start.13 = (bf16[400,768]{1,0:T(8,128)(2,1)S(1)}, bf16[400,768]{1,0:T(8,128)(2,1)S(1)}, u32[]{:S(2)}, u32[]{:S(2)}) collective-permute-start(bf16[400,768]{1,0:T(8,128)(2,1)S(1)} %pad_maximum_fusion.refs_3_), channel_id=1, source_target_pairs={{0,2},{1,3},{2,0},{3,1},{4,6},{5,7},{6,4},{7,5},{8,10},{9,11},{10,... | collective-permute-start | bytes 1843208 | tf_op jit(solution)/shard_map/ppermute | solution.py:1003
  74.7 27.5 %collective-permute-start.12 = (bf16[400,768]{1,0:T(8,128)(2,1)S(1)}, bf16[400,768]{1,0:T(8,128)(2,1)S(1)}, u32[]{:S(2)}, u32[]{:S(2)}) collective-permute-start(bf16[400,768]{1,0:T(8,128)(2,1)S(1)} %pad_maximum_fusion.refs_3_), channel_id=1, source_target_pairs={{0,4},{1,5},{2,6},{3,7},{4,0},{5,1},{6,2},{7,3},{8,12},{9,13},{10,... | collective-permute-start | bytes 1843208 | tf_op jit(solution)/shard_map/ppermute | solution.py:1003
  86.4 28.9 %collective-permute-start.19 = (bf16[768,768]{1,0:T(8,128)(2,1)S(1)}, bf16[768,768]{1,0:T(8,128)(2,1)}, u32[]{:S(2)}, u32[]{:S(2)}) collective-permute-start(bf16[768,768]{1,0:T(8,128)(2,1)S(1)} %copy-done.21), channel_id=1, source_target_pairs={{0,8},{8,0},{16,24},{24,16},{1,9},{9,1},{17,25},{25,17},{2,10},{10... | collective-permute-start | bytes 3538952 | tf_op jit(solution)/shard_map/ppermute | solution.py:1003
  87.2 28.1 %collective-permute-start.20 = (bf16[768,768]{1,0:T(8,128)(2,1)}, bf16[768,768]{1,0:T(8,128)(2,1)}, u32[]{:S(2)}, u32[]{:S(2)}) collective-permute-start(bf16[768,768]{1,0:T(8,128)(2,1)} %get-tuple-element.271.refs_1_), channel_id=1, source_target_pairs={{0,16},{8,24},{16,0},{24,8},{1,17},{9,25},{17,1},{25,9},{2,18},{10... | collective-permute-start | bytes 3538952 | tf_op jit(solution)/shard_map/ppermute | solution.py:1003
  109.4 33.0 %all-to-all-start.1 = ((bf16[8,56,768]{2,1,0:T(8,128)(2,1)}), bf16[8,56,768]{2,1,0:T(8,128)(2,1)S(1)}, u32[]{:S(2)}, u32[]{:S(2)}) async-start(bf16[8,56,768]{2,1,0:T(8,128)(2,1)} %bitcast.15), calls=%async_computation.1 | async-start | bytes 1376256 | tf_op jit(solution)/shard_map/all_to_all | solution.py:1159
  115.3 34.3 %collective-permute-start.23 = (bf16[768,768]{1,0:T(8,128)(2,1)}, bf16[768,768]{1,0:T(8,128)(2,1)S(1)}, u32[]{:S(2)}, u32[]{:S(2)}) collective-permute-start(bf16[768,768]{1,0:T(8,128)(2,1)} %collective-permute-done.19.refs_2_), channel_id=1, source_target_pairs={{0,16},{8,24},{16,0},{24,8},{1,17},{9,25},{17,1},{25,9},{2,18},{10... | collective-permute-start | bytes 3538952 | tf_op jit(solution)/shard_map/ppermute | solution.py:1003
  115.6 34.0 %collective-permute-start.24 = (bf16[768,768]{1,0:T(8,128)(2,1)}, bf16[768,768]{1,0:T(8,128)(2,1)}, u32[]{:S(2)}, u32[]{:S(2)}) collective-permute-start(bf16[768,768]{1,0:T(8,128)(2,1)} %collective-permute-done.20.refs_5_), channel_id=1, source_target_pairs={{0,8},{8,0},{16,24},{24,16},{1,9},{9,1},{17,25},{25,17},{2,10},{10... | collective-permute-start | bytes 3538952 | tf_op jit(solution)/shard_map/ppermute | solution.py:1003
  142.5 25.2 %all-to-all-start = ((bf16[8,56,896]{2,1,0:T(8,128)(2,1)}), bf16[8,56,896]{2,1,0:T(8,128)(2,1)S(1)}, u32[]{:S(2)}, u32[]{:S(2)}) async-start(bf16[8,56,896]{2,1,0:T(8,128)(2,1)} %bitcast.55), calls=%async_computation | async-start | bytes 1605632 | tf_op jit(solution)/shard_map/all_to_all | solution.py:1159
  185.3 24.8 %all-to-all-start.2 = ((bf16[8,56,896]{2,1,0:T(8,128)(2,1)}), bf16[8,56,896]{2,1,0:T(8,128)(2,1)S(1)}, u32[]{:S(2)}, u32[]{:S(2)}) async-start(bf16[8,56,896]{2,1,0:T(8,128)(2,1)} %bitcast.56), calls=%async_computation.2 | async-start | bytes 1605632 | tf_op jit(solution)/shard_map/all_to_all | solution.py:1159
  198.3 60.0 %collective-permute-start.27 = (bf16[2,768,768]{2,1,0:T(8,128)(2,1)}, bf16[2,768,768]{2,1,0:T(8,128)(2,1)}, u32[]{:S(2)}, u32[]{:S(2)}) collective-permute-start(bf16[2,768,768]{2,1,0:T(8,128)(2,1)} %get-tuple-element.299), channel_id=1, source_target_pairs={{0,8},{8,0},{16,24},{24,16},{1,9},{9,1},{17,25},{25,17},{2,10},{10... | collective-permute-start | bytes 7077896 | tf_op jit(solution)/shard_map/ppermute | solution.py:1003
  199.2 59.1 %collective-permute-start.28 = (bf16[2,768,768]{2,1,0:T(8,128)(2,1)}, bf16[2,768,768]{2,1,0:T(8,128)(2,1)}, u32[]{:S(2)}, u32[]{:S(2)}) collective-permute-start(bf16[2,768,768]{2,1,0:T(8,128)(2,1)} %get-tuple-element.300), channel_id=1, source_target_pairs={{0,16},{8,24},{16,0},{24,8},{1,17},{9,25},{17,1},{25,9},{2,18},{10... | collective-permute-start | bytes 7077896 | tf_op jit(solution)/shard_map/ppermute | solution.py:1003
  210.1 32.3 %collective-permute-start.29 = (bf16[2,56,768]{2,1,0:T(8,128)(2,1)S(1)}, bf16[2,56,768]{2,1,0:T(8,128)(2,1)S(1)}, u32[]{:S(2)}, u32[]{:S(2)}) collective-permute-start(bf16[2,56,768]{2,1,0:T(8,128)(2,1)S(1)} %copy-done.57), channel_id=1, source_target_pairs={{0,2},{1,3},{2,0},{3,1},{4,6},{5,7},{6,4},{7,5},{8,10},{9,11},{10,... | collective-permute-start | bytes 516104 | tf_op jit(solution)/shard_map/ppermute | solution.py:1003
  210.1 32.3 %collective-permute-start.30 = (bf16[2,56,768]{2,1,0:T(8,128)(2,1)S(1)}, bf16[2,56,768]{2,1,0:T(8,128)(2,1)S(1)}, u32[]{:S(2)}, u32[]{:S(2)}) collective-permute-start(bf16[2,56,768]{2,1,0:T(8,128)(2,1)S(1)} %copy-done.56), channel_id=1, source_target_pairs={{0,4},{1,5},{2,6},{3,7},{4,0},{5,1},{6,2},{7,3},{8,12},{9,13},{10,... | collective-permute-start | bytes 516104 | tf_op jit(solution)/shard_map/ppermute | solution.py:1003
  211.9 30.5 %collective-permute-start.31 = (bf16[2,56,768]{2,1,0:T(8,128)(2,1)S(1)}, bf16[2,56,768]{2,1,0:T(8,128)(2,1)S(1)}, u32[]{:S(2)}, u32[]{:S(2)}) collective-permute-start(bf16[2,56,768]{2,1,0:T(8,128)(2,1)S(1)} %copy-done.55), channel_id=1, source_target_pairs={{0,6},{1,7},{2,4},{3,5},{4,2},{5,3},{6,0},{7,1},{8,14},{9,15},{10,... | collective-permute-start | bytes 516104 | tf_op jit(solution)/shard_map/ppermute | solution.py:1003
  258.3 22.8 %collective-permute-start.38 = (bf16[4,144,768]{2,1,0:T(8,128)(2,1)}, bf16[4,144,768]{2,1,0:T(8,128)(2,1)S(1)}, u32[]{:S(2)}, u32[]{:S(2)}) collective-permute-start(bf16[4,144,768]{2,1,0:T(8,128)(2,1)} %get-tuple-element.373), channel_id=1, source_target_pairs={{0,8},{1,9},{2,10},{3,11},{4,12},{5,13},{6,14},{7,15},{8,0},{9,1},... | collective-permute-start | bytes 2654216 | tf_op jit(solution)/shard_map/ppermute | solution.py:1003
  269.1 32.2 %collective-permute-start.40 = (bf16[2,4,112,768]{3,2,1,0:T(8,128)(2,1)}, bf16[2,4,112,768]{3,2,1,0:T(8,128)(2,1)S(1)}, u32[]{:S(2)}, u32[]{:S(2)}) collective-permute-start(bf16[2,4,112,768]{3,2,1,0:T(8,128)(2,1)} %get-tuple-element.376), channel_id=1, source_target_pairs={{0,16},{1,17},{2,18},{3,19},{4,20},{5,21},{6,22},{7,23},{8,24},{9,... | collective-permute-start | bytes 4128776 | tf_op jit(solution)/shard_map/ppermute | solution.py:1003
  271.0 28.2 %collective-permute-start.39 = (bf16[4,144,768]{2,1,0:T(8,128)(2,1)}, bf16[4,144,768]{2,1,0:T(8,128)(2,1)S(1)}, u32[]{:S(2)}, u32[]{:S(2)}) collective-permute-start(bf16[4,144,768]{2,1,0:T(8,128)(2,1)} %get-tuple-element.375), channel_id=1, source_target_pairs={{0,8},{1,9},{2,10},{3,11},{4,12},{5,13},{6,14},{7,15},{8,0},{9,1},... | collective-permute-start | bytes 2654216 | tf_op jit(solution)/shard_map/ppermute | solution.py:1003
  290.0 36.2 %collective-permute-start.44 = (bf16[4,1,128,768]{3,2,0,1:T(8,128)(2,1)S(1)}, bf16[4,1,128,768]{3,2,0,1:T(8,128)(2,1)S(1)}, u32[]{:S(2)}, u32[]{:S(2)}) collective-permute-start(bf16[4,1,128,768]{3,2,0,1:T(8,128)(2,1)S(1)} %bitcast.43), channel_id=1, source_target_pairs={{0,4},{1,5},{2,6},{3,7},{4,0},{5,1},{6,2},{7,3},{8,12},{9,13},{10,... | collective-permute-start | bytes 2359304 | tf_op jit(solution)/shard_map/ppermute | solution.py:1003
  290.9 35.3 %collective-permute-start.43 = (bf16[4,1,128,768]{3,2,0,1:T(8,128)(2,1)S(1)}, bf16[4,1,128,768]{3,2,0,1:T(8,128)(2,1)S(1)}, u32[]{:S(2)}, u32[]{:S(2)}) collective-permute-start(bf16[4,1,128,768]{3,2,0,1:T(8,128)(2,1)S(1)} %bitcast.58), channel_id=1, source_target_pairs={{0,2},{1,3},{2,0},{3,1},{4,6},{5,7},{6,4},{7,5},{8,10},{9,11},{10,... | collective-permute-start | bytes 2359304 | tf_op jit(solution)/shard_map/ppermute | solution.py:1003
  310.8 23.7 %collective-permute-start.45 = (bf16[4,56,768]{2,1,0:T(8,128)(2,1)S(1)}, bf16[4,56,768]{2,1,0:T(8,128)(2,1)S(1)}, u32[]{:S(2)}, u32[]{:S(2)}) collective-permute-start(bf16[4,56,768]{2,1,0:T(8,128)(2,1)S(1)} %pad_maximum_fusion.1), channel_id=1, source_target_pairs={{0,1},{1,0},{2,3},{3,2},{4,5},{5,4},{6,7},{7,6},{8,9},{9,8},{10,11... | collective-permute-start | bytes 1032200 | tf_op jit(solution)/shard_map/ppermute | solution.py:1003
  328.9 26.8 %collective-permute-start.49 = (bf16[768,768]{1,0:T(8,128)(2,1)}, bf16[768,768]{1,0:T(8,128)(2,1)}, u32[]{:S(2)}, u32[]{:S(2)}) collective-permute-start(bf16[768,768]{1,0:T(8,128)(2,1)} %get-tuple-element.435), channel_id=1, source_target_pairs={{0,16},{8,24},{16,0},{24,8},{1,17},{9,25},{17,1},{25,9},{2,18},{10... | collective-permute-start | bytes 3538952 | tf_op jit(solution)/shard_map/ppermute | solution.py:1003
  330.6 26.5 %collective-permute-start.50 = (bf16[768,768]{1,0:T(8,128)(2,1)}, bf16[768,768]{1,0:T(8,128)(2,1)}, u32[]{:S(2)}, u32[]{:S(2)}) collective-permute-start(bf16[768,768]{1,0:T(8,128)(2,1)} %get-tuple-element.437), channel_id=1, source_target_pairs={{0,8},{8,0},{16,24},{24,16},{1,9},{9,1},{17,25},{25,17},{2,10},{10... | collective-permute-start | bytes 3538952 | tf_op jit(solution)/shard_map/ppermute | solution.py:1003
  343.9 22.9 %collective-permute-start.48 = (bf16[1,256,768]{2,1,0:T(8,128)(2,1)S(1)}, bf16[1,256,768]{2,1,0:T(8,128)(2,1)S(1)}, u32[]{:S(2)}, u32[]{:S(2)}) collective-permute-start(bf16[1,256,768]{2,1,0:T(8,128)(2,1)S(1)} %add.53), channel_id=1, source_target_pairs={{0,4},{1,5},{2,6},{3,7},{4,0},{5,1},{6,2},{7,3},{8,12},{9,13},{10,... | collective-permute-start | bytes 1179656 | tf_op jit(solution)/shard_map/ppermute | solution.py:1003
  (99 other events, 988.6 us)
